TPU v7x, 32 devices: a whole 2x2x4 slice. The times are simulated.
32 devices in a mesh: mol: 2 (over x), pair: 8 (over z, y), aux: 2 (over core).
Axes of the slice: x: 2, y: 2, z: 4, core: 2. Of those that a mesh axis runs over, the one named last changes fastest.
Arguments:
- three_index: bfloat16 [224, 256, 4096], P(('mol', 'pair'), None, 'aux'), parts along dimension 0, may hold values from -0.03125 to 0.03125
- density: bfloat16 [224, 256, 256], P(('mol', 'pair')), parts along dimension 0, may hold values from -6 to 6
- screen: int32 [224, 256], P(('mol', 'pair')), parts along dimension 0, may hold values 0 or 1
- pair_shells: int32 [224, 2], P(('mol', 'pair')), parts along dimension 0, may hold values from 0 to 1249, as said below
- home_slot: int32 [224], P('mol'), parts along dimension 0, may hold values from 0 to 111, as said below
- mirror_slot: int32 [224], P('mol'), parts along dimension 0, may hold values from 0 to 111, as said below
Outputs:
- coulomb_rows: bfloat16 [224, 256, 256], P(('mol', 'pair'), None, 'aux'), parts along dimension 0
- coulomb_cols: bfloat16 [224, 256, 256], P(('mol', 'pair'), None, 'aux'), parts along dimension 0
There are 2 independent parts, one for each index of `mol`. A program takes and returns all parts, laid end to end along the dimension named above; each array names one. Nothing has to cross between parts.
Inputs may be any that keep to these rules, and one draw needn't show every extreme that they name: `pair_shells`: the column shell is the row shell or one of the next two shells, modulo 1250. `home_slot`: a permutation; rows k * 14 to (k + 1) * 14 - 1 belong to device k, and of the 14 blocks of one device at most 3 have home rows on any one device, exactly 3 on some device. `mirror_slot`: as for home_slot.
All inputs are finite; a program needn't handle non-finite values. No bound on the sum of `screen` on one device may be relied on, other than what follows from the above.
Results may differ from a plain program's by a relative error of at most 0.0048.
Values may be sent and summed in bfloat16 or wider, within the bound.
No kernel may reach another device: no remote copies, remote signals or barrier semaphores. Data moves between devices by JAX's collectives and lax.ppermute only.
A program may use at most 192 MiB of HBM per device.

v0:
```python
import math

import jax
import jax.numpy as jnp
from jax import lax
from jax.sharding import PartitionSpec as P


def routing(slots, devices, blocks_dev, myself):
    total = slots.shape[0]
    capacity = 2 + (blocks_dev - 1) // devices
    numbers = jnp.arange(total, dtype=jnp.int32)
    source = numbers // blocks_dev
    target = slots // blocks_dev
    joined = source * devices + target
    earlier = (joined[:, None] == joined[None, :]) & (numbers[None, :] < numbers[:, None])
    ranking = jnp.sum(earlier.astype(jnp.int32), axis=1)
    columns = jnp.arange(devices * capacity, dtype=jnp.int32)
    lanes_all = jnp.arange(blocks_dev, dtype=jnp.int32)
    at_home = target == myself
    outgoing_hot = ((source * capacity + ranking)[:, None] == columns[None, :]) & at_home[:, None]
    local_hot = (slots % blocks_dev)[:, None] == lanes_all[None, :]
    sending = jnp.dot(outgoing_hot.T.astype(jnp.float32), local_hot.astype(jnp.float32)).astype(
        jnp.bfloat16
    )
    wanted = lax.dynamic_slice_in_dim(
        target * capacity + ranking, myself * blocks_dev, blocks_dev, 0
    )
    picking = (wanted[:, None] == columns[None, :]).astype(jnp.bfloat16)
    home_rows = lax.dynamic_slice_in_dim(slots, myself * blocks_dev, blocks_dev, 0)
    return (sending, picking, home_rows)


def local(three_index, density, screen, pair_shells, home_slot, mirror_slot):
    blocks_dev, pairs_fn, aux_dev = three_index.shape
    ndens = density.shape[2]
    shell_fn = math.isqrt(pairs_fn)
    devices = lax.axis_size("pair")
    myself = lax.axis_index("pair")
    capacity = 2 + (blocks_dev - 1) // devices
    home_send, home_pick, home_rows = routing(home_slot, devices, blocks_dev, myself)
    mirror_send, mirror_pick, unused_rows = routing(mirror_slot, devices, blocks_dev, myself)
    section = lax.all_gather(density, "pair", axis=0, tiled=True)
    length = section.shape[0]
    chosen = (home_rows[:, None] == jnp.arange(length, dtype=jnp.int32)[None, :]).astype(
        jnp.bfloat16
    )
    fetched = jnp.dot(
        chosen, section.reshape(length, -1), preferred_element_type=jnp.float32
    ).astype(jnp.bfloat16)
    weight = jnp.where(pair_shells[:, 0] != pair_shells[:, 1], 2.0, 1.0)
    factor = (screen.astype(jnp.float32) * weight[:, None]).astype(jnp.bfloat16)
    fitted = (fetched.reshape(blocks_dev, pairs_fn, ndens) * factor[:, :, None]).reshape(
        blocks_dev * pairs_fn, ndens
    )
    integrals = three_index.reshape(blocks_dev * pairs_fn, aux_dev)
    contract_rows = (((0,), (0,)), ((), ()))
    partial_fit = lax.dot_general(
        integrals, fitted, contract_rows, preferred_element_type=jnp.float32
    )
    coef = lax.psum(partial_fit, "pair").astype(jnp.bfloat16)
    summed = jnp.dot(integrals, coef, preferred_element_type=jnp.float32)
    halves = lax.psum_scatter(
        summed.reshape(blocks_dev, pairs_fn, ndens), "aux", scatter_dimension=2, tiled=True
    )
    coulomb = (halves * screen.astype(jnp.float32)[:, :, None]).astype(jnp.bfloat16)
    half_dens = coulomb.shape[2]
    turned = jnp.swapaxes(coulomb.reshape(blocks_dev, shell_fn, shell_fn, half_dens), 1, 2).reshape(
        blocks_dev, -1
    )
    to_rows = jnp.dot(
        home_pick.T, coulomb.reshape(blocks_dev, -1), preferred_element_type=jnp.float32
    ).astype(jnp.bfloat16)
    to_cols = jnp.dot(mirror_pick.T, turned, preferred_element_type=jnp.float32).astype(
        jnp.bfloat16
    )
    back_rows, back_cols = (
        lax.all_to_all(
            to_rows.reshape(devices, -1), "pair", split_axis=0, concat_axis=0, tiled=True
        ),
        lax.all_to_all(
            to_cols.reshape(devices, -1), "pair", split_axis=0, concat_axis=0, tiled=True
        ),
    )
    coulomb_rows = jnp.dot(
        home_send.T, back_rows.reshape(devices * capacity, -1), preferred_element_type=jnp.float32
    ).astype(jnp.bfloat16)
    coulomb_cols = jnp.dot(
        mirror_send.T, back_cols.reshape(devices * capacity, -1), preferred_element_type=jnp.float32
    ).astype(jnp.bfloat16)
    return (
        coulomb_rows.reshape(blocks_dev, pairs_fn, half_dens),
        coulomb_cols.reshape(blocks_dev, pairs_fn, half_dens),
    )


def solution(mesh):
    in_specs = (
        P(("mol", "pair"), None, "aux"),
        P(("mol", "pair"), None, None),
        P(("mol", "pair"), None),
        P(("mol", "pair"), None),
        P("mol"),
        P("mol"),
    )
    out_specs = (P(("mol", "pair"), None, "aux"), P(("mol", "pair"), None, "aux"))
    return jax.shard_map(local, mesh=mesh, in_specs=in_specs, out_specs=out_specs, check_vma=False)
```

profile of v0, /device:TPU:0, one launch (start us, length us, event | category | flops | bytes accessed | tf_op | source)
XLA Modules:
  0.0 493.1 jit_solution(17157770038559942855)
XLA Ops:
  8.2 206.8 %all-gather.2.cloned.1.call-done = bf16[112,256,256]{2,1,0:T(8,128)(2,1)} async-done(((bf16[14,256,256]{2,1,0:T(8,128)(2,1)}), bf16[112,256,256]{2,1,0:T(8,128)(2,1)}) %all-gather.2.cloned.1.call-update) | async-done | bytes 14680080 | tf_op jit(solution)/shard_map/all_gather | solution.py:43
  215.0 14.0 %copy.25 = bf16[14,8,256,256]{3,1,2,0:T(8,128)(2,1)S(1)} copy(bf16[14,8,256,256]{3,2,1,0:T(8,128)(2,1)} %bitcast.40) | data formatting | bytes 29360128
  231.8 2.6 copy.20
  234.4 7.8 %convolution_bitcast_fusion.1 = f32[2048,256]{0,1:T(8,128)S(1)} fusion(bf16[14,256,2048]{2,1,0:T(8,128)(2,1)} %param.6, bf16[14,256,256]{1,2,0:T(8,128)(2,1)} %copy.20, bf16[14,256]{1,0:T(8,128)(2,1)S(1)} %multiply_convert_fusion.1), kind=kOutput, calls=%fused_computation.6 | convolution fusion | flops 3759013888 | bytes 18619392 | tf_op jit(solution)/shard_map/dot_general | solution.py:58
  242.2 88.9 %all-reduce.1 = bf16[2048,256]{0,1:T(8,128)(2,1)S(1)} all-reduce(f32[2048,256]{0,1:T(8,128)S(1)} %convolution_bitcast_fusion.1), channel_id=1, replica_groups=mesh['mol'=2,'pair'=8,'aux'=2] {'pair'}, use_global_device_ids=true, to_apply=%region_1.2 | all-reduce | flops 524288 | bytes 3145728 | tf_op jit(solution)/shard_map/psum | solution.py:61
  331.1 9.1 %convolution_bitcast_fusion = f32[3584,256]{0,1:T(8,128)} fusion(bf16[3584,2048]{1,0:T(8,128)(2,1)} %bitcast.54, bf16[2048,256]{0,1:T(8,128)(2,1)S(1)} %all-reduce.1), kind=kOutput, calls=%fused_computation.5 | convolution fusion | flops 3758096384 | bytes 19398656 | tf_op jit(solution)/shard_map/dot_general | solution.py:62
  340.3 5.6 %copy.21 = f32[3584,256]{1,0:T(8,128)} copy(f32[3584,256]{0,1:T(8,128)} %convolution_bitcast_fusion) | data formatting | bytes 7340032 | tf_op jit(solution)/shard_map/dot_general | solution.py:62
  346.8 10.4 %reduce-scatter.2.cloned.1.call-done = f32[14,256,128]{2,1,0:T(8,128)} async-done(((f32[14,256,256]{2,1,0:T(8,128)}), f32[14,256,128]{2,1,0:T(8,128)}) %reduce-scatter.2.cloned.1.call-update) | async-done | bytes 1835024 | tf_op jit(solution)/shard_map/reduce_scatter | solution.py:63
  362.1 3.7 all_to_all.16
  366.3 11.6 %reduce.2 = bf16[8,98304]{1,0:T(8,128)(2,1)} reduce(bf16[8,1,98304]{2,1,0:T(2,128)(2,1)S(1)} %all_to_all.16, bf16[]{:T(256)} %broadcast.79), dimensions={1}, to_apply=%all_to_all.16.reduce_sub_computation | reduce | bytes 3145730 | tf_op jit(solution)/shard_map/all_to_all | solution.py:78
  377.9 3.9 reshape.97
  381.8 5.9 %all-to-all-start = ((bf16[8,2,49152]{2,1,0:T(2,128)(2,1)}), bf16[8,2,49152]{2,1,0:T(2,128)(2,1)}, u32[]{:S(2)}, u32[]{:S(2)}) async-start(bf16[8,2,49152]{2,1,0:T(2,128)(2,1)} %reshape.97), calls=%async_computation.1 | async-start | bytes 3145728 | tf_op jit(solution)/shard_map/all_to_all | solution.py:78
  390.8 3.7 all_to_all.17
  394.6 11.8 %reduce.3 = bf16[8,98304]{1,0:T(8,128)(2,1)} reduce(bf16[8,1,98304]{2,1,0:T(2,128)(2,1)S(1)} %all_to_all.17, bf16[]{:T(256)} %broadcast.79), dimensions={1}, to_apply=%all_to_all.17.reduce_sub_computation | reduce | bytes 3145730 | tf_op jit(solution)/shard_map/all_to_all | solution.py:81
  406.4 3.9 reshape.99
  410.3 15.0 %all-to-all-done = bf16[8,2,49152]{2,1,0:T(2,128)(2,1)} async-done(((bf16[8,2,49152]{2,1,0:T(2,128)(2,1)}), bf16[8,2,49152]{2,1,0:T(2,128)(2,1)}, u32[]{:S(2)}, u32[]{:S(2)}) %all-to-all-start) | async-done | bytes 1572896 | tf_op jit(solution)/shard_map/all_to_all | solution.py:78
  425.3 4.3 all-to-all-start.1
  429.6 4.7 reshape.98
  434.3 10.8 %reduce = bf16[8,98304]{1,0:T(8,128)(2,1)} reduce(bf16[8,1,98304]{2,1,0:T(2,128)(2,1)S(1)} %reshape.98, bf16[]{:T(256)} %constant.52), dimensions={1}, to_apply=%all_to_all.13.reduce_sub_computation | reduce | bytes 3145730 | tf_op jit(solution)/shard_map/all_to_all | solution.py:78
  445.1 2.3 reshape.88
  449.3 16.9 %all-to-all-done.1 = bf16[8,2,49152]{2,1,0:T(2,128)(2,1)} async-done(((bf16[8,2,49152]{2,1,0:T(2,128)(2,1)}), bf16[8,2,49152]{2,1,0:T(2,128)(2,1)}, u32[]{:S(2)}, u32[]{:S(2)}) %all-to-all-start.1) | async-done | bytes 1572896 | tf_op jit(solution)/shard_map/all_to_all | solution.py:81
  466.2 4.9 reshape.100
  471.1 10.8 %reduce.1 = bf16[8,98304]{1,0:T(8,128)(2,1)} reduce(bf16[8,1,98304]{2,1,0:T(2,128)(2,1)S(1)} %reshape.100, bf16[]{:T(256)} %constant.52), dimensions={1}, to_apply=%all_to_all.15.reduce_sub_computation | reduce | bytes 3145730 | tf_op jit(solution)/shard_map/all_to_all | solution.py:81
  481.8 2.3 reshape.92
  (49 shorter events, 16.9 us)
Async XLA Ops:
  7.2 0.8 copy-start.3
  7.2 0.9 copy-start.5
  7.2 0.9 copy-start.2
  7.2 207.8 %all-gather.2.cloned.1.call-start = ((), (), s32[]{:S(2)}) async-start(), calls=%async_computation.3 | async-start | bytes 16515072 | tf_op jit(solution)/shard_map/all_gather | solution.py:43
  7.9 349.3 %reduce-scatter.2.cloned.1.call-start = ((), (), s32[]{:S(2)}) async-start(), calls=%async_computation.4 | async-start | bytes 5505024 | tf_op jit(solution)/shard_map/reduce_scatter | solution.py:63
  345.8 0.7 copy-start.4
  359.3 0.9 copy-start
  381.8 6.2 %copy-start.1 = (bf16[14,256,128]{2,1,0:T(8,128)(2,1)S(1)}, bf16[14,256,128]{2,1,0:T(8,128)(2,1)}, u32[]{:S(2)}) copy-start(bf16[14,256,128]{2,1,0:T(8,128)(2,1)} %copy-done) | copy-start | bytes 2752516
  381.8 43.5 %all-to-all-start = ((bf16[8,2,49152]{2,1,0:T(2,128)(2,1)}), bf16[8,2,49152]{2,1,0:T(2,128)(2,1)}, u32[]{:S(2)}, u32[]{:S(2)}) async-start(bf16[8,2,49152]{2,1,0:T(2,128)(2,1)} %reshape.97), calls=%async_computation.1 | async-start | bytes 3145728 | tf_op jit(solution)/shard_map/all_to_all | solution.py:78
  425.3 40.9 %all-to-all-start.1 = ((bf16[8,2,49152]{2,1,0:T(2,128)(2,1)}), bf16[8,2,49152]{2,1,0:T(2,128)(2,1)}, u32[]{:S(2)}, u32[]{:S(2)}) async-start(bf16[8,2,49152]{2,1,0:T(2,128)(2,1)} %reshape.99), calls=%async_computation.2 | async-start | bytes 3145728 | tf_op jit(solution)/shard_map/all_to_all | solution.py:81
Sparse Core Ops, SparseCore 0:
  10.2 204.6 all-gather.1
  346.0 11.2 reduce-scatter.1
where the time goes:
time: 500 us; the launch traced here: 493 us
  waiting for transfers between devices  250 us (50%)
  blocking collectives  88.9 us (18%)
  local copies, waits for them, and re-layouts  57.9 us (12%)
  other arithmetic  47.5 us (10%)
  matrix products  24.2 us (5%)
  between operations  14.5 us (3%)
  starting transfers between devices  10.2 us (2%)
    all_gather x1, waiting for transfers between devices, local(): section = lax.all_gather(density, 'pair', axis=0, tiled=True)  207 us
    psum x1, blocking collectives, local(): coef = lax.psum(partial_fit, 'pair').astype(jnp.bfloat16)  88.9 us
    unnamed x24, local copies, waits for them, and re-layouts  34.5 us
    all_to_all x2, other arithmetic, local(): lax.all_to_all(to_cols.reshape(devices, -1), 'pair', split_axis=0, concat...  22.6 us
    all_to_all x2, other arithmetic, local(): lax.all_to_all(to_rows.reshape(devices, -1), 'pair', split_axis=0, concat...  22.3 us
    all_to_all x1, waiting for transfers between devices, local(): lax.all_to_all(to_cols.reshape(devices, -1), 'pair', split_axis=0, concat...  16.9 us
    all_to_all x1, waiting for transfers between devices, local(): lax.all_to_all(to_rows.reshape(devices, -1), 'pair', split_axis=0, concat...  15 us
    reduce_scatter x1, waiting for transfers between devices, local(): lax.psum_scatter(summed.reshape(blocks_dev, pairs_fn, ndens), 'aux', scat...  10.4 us
  transfers between devices with their start and end apart: 4, of which 4 were waited for; matrix products, arithmetic and copies ran while one was open for 8% of the time, Pallas kernels for 0%

commit v1 on v0

v1 whole, which is shorter than its diff:
```python
import functools
import math

import jax
import jax.numpy as jnp
from jax import lax
from jax.experimental import pallas as pl
from jax.experimental.pallas import tpu as pltpu
from jax.sharding import PartitionSpec as P

VMEM_BYTES = 48 * 1024 * 1024


def tables(slots, devices, blocks_dev, me):
    total = slots.shape[0]
    numbers = jnp.arange(total, dtype=jnp.int32)
    source = numbers // blocks_dev
    target = slots // blocks_dev
    joined = source * devices + target
    earlier = (joined[:, None] == joined[None, :]) & (numbers[None, :] < numbers[:, None])
    rank = jnp.sum(earlier.astype(jnp.int32), axis=1)
    own_target = lax.dynamic_slice_in_dim(target, me * blocks_dev, blocks_dev, 0)
    own_rank = lax.dynamic_slice_in_dim(rank, me * blocks_dev, blocks_dev, 0)
    rows = me * blocks_dev + jnp.arange(blocks_dev, dtype=jnp.int32)
    hot = slots[None, :] == rows[:, None]
    row_source = jnp.sum(jnp.where(hot, source[None, :], 0), axis=1)
    row_rank = jnp.sum(jnp.where(hot, rank[None, :], 0), axis=1)
    return own_target, own_rank, row_source, row_rank


def scatter_density_kernel(devices, blocks, width, table, density, *rest):
    sends, sems = rest[:devices], rest[devices]
    column = pl.multiple_of(table[2 * blocks] * width, width)

    def copy(row, step):
        return pltpu.make_async_copy(
            density.at[row, :, pl.ds(column, width)],
            sends[step].at[table[blocks + row]],
            sems.at[row],
        )

    for row in range(blocks):
        for step in range(devices):

            @pl.when(table[row] == step)
            def _():
                copy(row, step).start()

    for row in range(blocks):
        copy(row, 0).wait()


def gather_kernel(devices, blocks, groups, table, *rest):
    received, outs, sems = rest[:devices], rest[devices : devices + groups], rest[devices + groups]

    def copy(group, row, step):
        return pltpu.make_async_copy(
            received[step].at[table[(2 * group + 1) * blocks + row]],
            outs[group].at[row],
            sems.at[group, row],
        )

    for group in range(groups):
        for row in range(blocks):
            for step in range(devices):

                @pl.when(table[2 * group * blocks + row] == step)
                def _():
                    copy(group, row, step).start()

    for group in range(groups):
        for row in range(blocks):
            copy(group, row, 0).wait()


def fit_kernel(devices, some, steps, table, factor, own, other, integrals, *rest):
    own_part, sends, total = rest[0], rest[1:devices], rest[devices]
    step = pl.program_id(0)
    width = own_part.shape[1]

    @pl.when(step == 0)
    def _():
        total[...] = jnp.zeros_like(total)

    turned = []
    for b in range(some):
        both = jnp.concatenate([own[b], other[b]], axis=1)
        turned.append(both.T * factor[b])
    fitted = jnp.concatenate(turned, axis=1)
    flat = integrals.reshape(some * integrals.shape[1], integrals.shape[2])
    for chunk in range(devices):
        at = pl.ds(chunk * width, width)
        total[:, at] += jnp.dot(fitted, flat[:, at], preferred_element_type=jnp.float32)

    @pl.when(step == steps - 1)
    def _():
        for d in range(devices):
            chunk = lax.rem(table[0] + d, devices)
            value = total[:, pl.ds(pl.multiple_of(chunk * width, width), width)]
            if d == 0:
                own_part[...] = value
            else:
                sends[d - 1][...] = value.astype(jnp.bfloat16)


def apply_kernel(devices, some, table, integrals, *rest):
    chunks, own, other = rest[:devices], rest[devices], rest[devices + 1]
    width = chunks[0].shape[1]
    half = own.shape[2]
    flat = integrals.reshape(some * integrals.shape[1], integrals.shape[2])
    total = None
    for d in range(devices):
        chunk = lax.rem(table[0] + devices - d, devices)
        term = lax.dot_general(
            flat[:, pl.ds(pl.multiple_of(chunk * width, width), width)],
            chunks[d][...],
            (((1,), (1,)), ((), ())),
            preferred_element_type=jnp.float32,
        )
        total = term if total is None else total + term
    own[...] = total[:, :half].reshape(own.shape)
    other[...] = total[:, half:].reshape(other.shape)


def scatter_coulomb_kernel(devices, blocks, shell, cap, table, screen, own, other, *rest):
    sends = rest[:devices]
    turning, row_buf, col_buf, sems = rest[devices:]
    block = pl.program_id(0)
    pairs, half = own.shape[1], own.shape[2]
    keep = jnp.broadcast_to(screen[0], (half, pairs)).T
    value = (own[0] + other[0]) * keep
    turning[...] = value
    row_buf[block] = value.astype(jnp.bfloat16)
    for j in range(shell):
        col_buf[block, pl.ds(j * shell, shell), :] = turning[
            pl.ds(j, shell, stride=shell), :
        ].astype(jnp.bfloat16)

    def copy(group, b, step):
        buf = (row_buf, col_buf)[group]
        return pltpu.make_async_copy(
            buf.at[b],
            sends[step].at[group * cap + table[(2 * group + 1) * blocks + b]],
            sems.at[group, b],
        )

    for group in range(2):
        for step in range(devices):

            @pl.when(table[2 * group * blocks + block] == step)
            def _():
                copy(group, block, step).start()

    @pl.when(block == blocks - 1)
    def _():
        for group in range(2):
            for b in range(blocks):
                copy(group, b, 0).wait()


def local(three_index, density, screen, pair_shells, home_slot, mirror_slot):
    blocks, pairs, aux_dev = three_index.shape
    ndens = density.shape[2]
    shell = math.isqrt(pairs)
    n = lax.axis_size("pair")
    parts = lax.axis_size("aux")
    me = lax.axis_index("pair")
    core = lax.axis_index("aux")
    half = ndens // parts
    width = aux_dev // n
    cap = 2 + (blocks - 1) // n
    some = 2 if blocks % 2 == 0 else 1
    steps = blocks // some
    any_spec = pl.BlockSpec(memory_space=pl.ANY)
    params = pltpu.CompilerParams(vmem_limit_bytes=VMEM_BYTES)

    def shift(x, d):
        return lax.ppermute(x, "pair", [(s, (s + d) % n) for s in range(n)])

    def swap(x):
        return lax.ppermute(x, "aux", [(s, (s + 1) % parts) for s in range(parts)])

    home_target, home_rank, home_source, home_row_rank = tables(home_slot, n, blocks, me)
    mirror_target, mirror_rank, mirror_source, mirror_row_rank = tables(
        mirror_slot, n, blocks, me
    )
    ints = functools.partial(jnp.concatenate, axis=0)

    send_table = ints([(home_source - me) % n, home_row_rank, core[None].astype(jnp.int32)])
    slots = jax.ShapeDtypeStruct((cap, pairs, half), jnp.bfloat16)
    sends = pl.pallas_call(
        functools.partial(scatter_density_kernel, n, blocks, half),
        out_shape=[slots] * n,
        grid_spec=pltpu.PrefetchScalarGridSpec(
            num_scalar_prefetch=1,
            grid=(),
            in_specs=[any_spec],
            out_specs=[any_spec] * n,
            scratch_shapes=[pltpu.SemaphoreType.DMA((blocks,))],
        ),
        name="scatter_density",
    )(send_table, density)
    received = [sends[0]] + [shift(sends[d], d) for d in range(1, n)]
    pick_table = ints([(me - home_target) % n, home_rank])
    own = pl.pallas_call(
        functools.partial(gather_kernel, n, blocks, 1),
        out_shape=[jax.ShapeDtypeStruct((blocks, pairs, half), jnp.bfloat16)],
        grid_spec=pltpu.PrefetchScalarGridSpec(
            num_scalar_prefetch=1,
            grid=(),
            in_specs=[any_spec] * n,
            out_specs=[any_spec],
            scratch_shapes=[pltpu.SemaphoreType.DMA((1, blocks))],
        ),
        name="gather_density",
    )(pick_table, *received)[0]
    other = swap(own)

    weight = jnp.where(pair_shells[:, 0] != pair_shells[:, 1], 2.0, 1.0)
    factor = (screen.astype(jnp.float32) * weight[:, None]).astype(jnp.bfloat16)
    where = me[None].astype(jnp.int32)
    block_map = lambda i, t: (i, 0, 0)
    whole_map = lambda i, t: (0, 0)
    parts_fit = pl.pallas_call(
        functools.partial(fit_kernel, n, some, steps),
        out_shape=[jax.ShapeDtypeStruct((ndens, width), jnp.float32)]
        + [jax.ShapeDtypeStruct((ndens, width), jnp.bfloat16)] * (n - 1),
        grid_spec=pltpu.PrefetchScalarGridSpec(
            num_scalar_prefetch=1,
            grid=(steps,),
            in_specs=[
                pl.BlockSpec((some, 1, pairs), block_map),
                pl.BlockSpec((some, pairs, half), block_map),
                pl.BlockSpec((some, pairs, half), block_map),
                pl.BlockSpec((some, pairs, aux_dev), block_map),
            ],
            out_specs=[pl.BlockSpec((ndens, width), whole_map)] * n,
            scratch_shapes=[pltpu.VMEM((ndens, aux_dev), jnp.float32)],
        ),
        compiler_params=params,
        name="fit",
    )(where, factor[:, None, :], own, other, three_index)
    summed = parts_fit[0]
    for d in range(1, n):
        summed = summed + shift(parts_fit[d], d).astype(jnp.float32)
    coef = summed.astype(jnp.bfloat16)
    chunks = [coef] + [shift(coef, d) for d in range(1, n)]

    mine, theirs = pl.pallas_call(
        functools.partial(apply_kernel, n, some),
        out_shape=[jax.ShapeDtypeStruct((blocks, pairs, half), jnp.float32)] * 2,
        grid_spec=pltpu.PrefetchScalarGridSpec(
            num_scalar_prefetch=1,
            grid=(steps,),
            in_specs=[pl.BlockSpec((some, pairs, aux_dev), block_map)]
            + [pl.BlockSpec((ndens, width), whole_map)] * n,
            out_specs=[pl.BlockSpec((some, pairs, half), block_map)] * 2,
        ),
        compiler_params=params,
        name="apply",
    )(where, three_index, *chunks)
    added = swap(theirs)

    out_table = ints(
        [(home_target - me) % n, home_rank, (mirror_target - me) % n, mirror_rank]
    )
    slots = jax.ShapeDtypeStruct((2 * cap, pairs, half), jnp.bfloat16)
    sends = pl.pallas_call(
        functools.partial(scatter_coulomb_kernel, n, blocks, shell, cap),
        out_shape=[slots] * n,
        grid_spec=pltpu.PrefetchScalarGridSpec(
            num_scalar_prefetch=1,
            grid=(blocks,),
            in_specs=[
                pl.BlockSpec((1, 1, pairs), block_map),
                pl.BlockSpec((1, pairs, half), block_map),
                pl.BlockSpec((1, pairs, half), block_map),
            ],
            out_specs=[any_spec] * n,
            scratch_shapes=[
                pltpu.VMEM((pairs, half), jnp.float32),
                pltpu.VMEM((blocks, pairs, half), jnp.bfloat16),
                pltpu.VMEM((blocks, pairs, half), jnp.bfloat16),
                pltpu.SemaphoreType.DMA((2, blocks)),
            ],
        ),
        compiler_params=params,
        name="scatter_coulomb",
    )(out_table, screen.astype(jnp.float32)[:, None, :], mine, added)
    received = [sends[0]] + [shift(sends[d], d) for d in range(1, n)]
    in_table = ints(
        [
            (me - home_source) % n,
            home_row_rank,
            (me - mirror_source) % n,
            cap + mirror_row_rank,
        ]
    )
    rows, cols = pl.pallas_call(
        functools.partial(gather_kernel, n, blocks, 2),
        out_shape=[jax.ShapeDtypeStruct((blocks, pairs, half), jnp.bfloat16)] * 2,
        grid_spec=pltpu.PrefetchScalarGridSpec(
            num_scalar_prefetch=1,
            grid=(),
            in_specs=[any_spec] * n,
            out_specs=[any_spec] * 2,
            scratch_shapes=[pltpu.SemaphoreType.DMA((2, blocks))],
        ),
        name="gather_coulomb",
    )(in_table, *received)
    return rows, cols


def solution(mesh):
    in_specs = (
        P(("mol", "pair"), None, "aux"),
        P(("mol", "pair"), None, None),
        P(("mol", "pair"), None),
        P(("mol", "pair"), None),
        P("mol"),
        P("mol"),
    )
    out_specs = (P(("mol", "pair"), None, "aux"), P(("mol", "pair"), None, "aux"))
    return jax.shard_map(local, mesh=mesh, in_specs=in_specs, out_specs=out_specs, check_vma=False)
```

time: 500 us -> 327 us (0.65)
  the two profiles are of different devices: /device:TPU:0 before, /device:TPU:15 now
where the time goes in v1:
time: 327 us; the launch traced here: 326 us
  Pallas kernels  147 us (45%)
  waiting for transfers between devices  136 us (42%)
  starting transfers between devices  32.4 us (10%)
  other arithmetic  4.91 us (2%)
  local copies, waits for them, and re-layouts  4.89 us (1%)
    ppermute x28, waiting for transfers between devices, shift(): return lax.ppermute(x, 'pair', [(s, (s + d) % n) for s in range(n)])  130 us
    pallas_call x1, Pallas kernels, local(): pl.pallas_call(functools.partial(gather_kernel, n, blocks, 2), out_shape=...  57.6 us
    ppermute x28, starting transfers between devices, shift(): return lax.ppermute(x, 'pair', [(s, (s + d) % n) for s in range(n)])  30.2 us
    pallas_call x1, Pallas kernels, local(): pl.pallas_call(functools.partial(scatter_density_kernel, n, blocks, half)...  29.9 us
    pallas_call x1, Pallas kernels, local(): pl.pallas_call(functools.partial(gather_kernel, n, blocks, 1), out_shape=...  29.7 us
    pallas_call x1, Pallas kernels, local(): pl.pallas_call(functools.partial(scatter_coulomb_kernel, n, blocks, shell...  11 us
    pallas_call x1, Pallas kernels, local(): pl.pallas_call(functools.partial(fit_kernel, n, some, steps), out_shape=[...  9.77 us
    pallas_call x1, Pallas kernels, local(): pl.pallas_call(functools.partial(apply_kernel, n, some), out_shape=[jax.S...  9.54 us
  transfers between devices with their start and end apart: 30, of which 24 were waited for; matrix products, arithmetic and copies ran while one was open for 0% of the time, Pallas kernels for 0%

profile of v1, /device:TPU:15, one launch (start us, length us, event | category | flops | bytes accessed | tf_op | source)
XLA Modules:
  0.0 326.2 jit_solution(8805866942733963117)
XLA Ops:
  4.0 29.9 %scatter_density.1 = (bf16[3,256,128]{2,1,0:T(8,128)(2,1)}, bf16[3,256,128]{2,1,0:T(8,128)(2,1)}, bf16[3,256,128]{2,1,0:T(8,128)(2,1)}, bf16[3,256,128]{2,1,0:T(...) custom-call(s32[29]{0:T(128)} %pad_add_fusion.3.table, ...), custom_call_target="tpu_custom_call" | custom-call | tf_op jit(solution)/shard_map/scatter_density/pallas_call | solution.py:191
  41.0 3.0 collective-permute-done.1.rest_2_
  44.7 19.7 %collective-permute-done.2.rest_3_ = bf16[3,256,128]{2,1,0:T(8,128)(2,1)S(1)} collective-permute-done((bf16[3,256,128]{2,1,0:T(8,128)(2,1)}, bf16[3,256,128]{2,1,0:T(8,128)(2,1)S(1)}, u32[]{:S(2)}, u32[]{:S(2)}) %collective-permute-start.2) | collective-permute-done | bytes 196640 | tf_op jit(solution)/shard_map/ppermute | solution.py:178
  64.3 4.2 %collective-permute-done.3.rest_4_ = bf16[3,256,128]{2,1,0:T(8,128)(2,1)S(1)} collective-permute-done((bf16[3,256,128]{2,1,0:T(8,128)(2,1)}, bf16[3,256,128]{2,1,0:T(8,128)(2,1)S(1)}, u32[]{:S(2)}, u32[]{:S(2)}) %collective-permute-start.3) | collective-permute-done | bytes 196640 | tf_op jit(solution)/shard_map/ppermute | solution.py:178
  68.6 2.8 collective-permute-done.5.rest_6_
  73.1 29.7 %gather_density.1.own = bf16[14,256,128]{2,1,0:T(8,128)(2,1)} custom-call(s32[28]{0:T(128)} %pad_add_fusion.2.table, bf16[3,256,128]{2,1,0:T(8,128)(2,1)} %get-tuple-element.28.rest_0_, bf16[3,256,128]{2,1,0:T(8,128)(2,1)} %copy-done.10, bf16[3,256,128]{2,1,0:T(8,128)(2,1)} %copy-done.11, bf16[3,256,128]{2,1,0:T(8,128)(2,1)} %copy-done.12, ...), custom_call_target="tpu_custom_call" | custom-call | tf_op jit(solution)/shard_map/gather_density/pallas_call | solution.py:205
  106.9 9.8 %fit.1 = (f32[256,256]{1,0:T(8,128)S(1)}, bf16[256,256]{1,0:T(8,128)(2,1)S(1)}, bf16[256,256]{1,0:T(8,128)(2,1)S(1)}, bf16[256,256]{1,0:T(8,128)(2,1)S(1)}, bf16...) custom-call(s32[1]{0:T(128)} %bitcast.table, ...), custom_call_target="tpu_custom_call" | custom-call | tf_op jit(solution)/shard_map/fit/pallas_call | solution.py:224
  116.8 2.6 collective-permute-start.10
  124.5 11.9 %collective-permute-done.10 = bf16[256,256]{1,0:T(8,128)(2,1)S(1)} collective-permute-done((bf16[256,256]{1,0:T(8,128)(2,1)S(1)}, bf16[256,256]{1,0:T(8,128)(2,1)S(1)}, u32[]{:S(2)}, u32[]{:S(2)}) %collective-permute-start.10) | collective-permute-done | bytes 131104 | tf_op jit(solution)/shard_map/ppermute | solution.py:178
  136.4 2.8 collective-permute-done.11
  139.2 2.8 collective-permute-done.13
  153.2 5.5 %collective-permute-done.18.rest_4_ = bf16[256,256]{1,0:T(8,128)(2,1)S(1)} collective-permute-done((bf16[256,256]{1,0:T(8,128)(2,1)S(1)}, bf16[256,256]{1,0:T(8,128)(2,1)S(1)}, u32[]{:S(2)}, u32[]{:S(2)}) %collective-permute-start.18) | collective-permute-done | bytes 131104 | tf_op jit(solution)/shard_map/ppermute | solution.py:178
  158.7 3.0 collective-permute-done.17.rest_3_
  161.7 2.8 collective-permute-done.16.rest_2_
  164.5 2.6 collective-permute-done.15.rest_1_
  167.0 9.5 %apply.1 = (f32[14,256,128]{2,1,0:T(8,128)S(1)}, f32[14,256,128]{2,1,0:T(8,128)S(1)}) custom-call(s32[1]{0:T(128)} %bitcast.table, bf16[14,256,2048]{2,1,0:T(8,128)(2,1)} %integrals.3, bf16[256,256]{1,0:T(8,128)(2,1)S(1)} %add_convert_fusion.rest_0_, bf16[256,256]{1,0:T(8,128)(2,1)S(1)} %collective-permute-done.15.rest_1_, ...), custom_call_target="tpu_custom_call" | custom-call | tf_op jit(solution)/shard_map/apply/pallas_call | solution.py:249
  178.5 3.1 collective-permute-done.22.other
  182.9 11.0 %scatter_coulomb.1 = (bf16[6,256,128]{2,1,0:T(8,128)(2,1)S(1)}, bf16[6,256,128]{2,1,0:T(8,128)(2,1)S(1)}, bf16[6,256,128]{2,1,0:T(8,128)(2,1)S(1)}, bf16[6,256,1...) custom-call(s32[56]{0:T(128)S(1)} %pad_add_fusion.1.table, ...), custom_call_target="tpu_custom_call" | custom-call | tf_op jit(solution)/shard_map/scatter_coulomb/pallas_call | solution.py:268
  202.9 3.6 %collective-permute-done.23.rest_1_ = bf16[6,256,128]{2,1,0:T(8,128)(2,1)S(1)} collective-permute-done((bf16[6,256,128]{2,1,0:T(8,128)(2,1)S(1)}, bf16[6,256,128]{2,1,0:T(8,128)(2,1)S(1)}, u32[]{:S(2)}, u32[]{:S(2)}) %collective-permute-start.23) | collective-permute-done | bytes 393248 | tf_op jit(solution)/shard_map/ppermute | solution.py:178
  206.6 9.2 %collective-permute-done.24.rest_2_ = bf16[6,256,128]{2,1,0:T(8,128)(2,1)S(1)} collective-permute-done((bf16[6,256,128]{2,1,0:T(8,128)(2,1)S(1)}, bf16[6,256,128]{2,1,0:T(8,128)(2,1)S(1)}, u32[]{:S(2)}, u32[]{:S(2)}) %collective-permute-start.24) | collective-permute-done | bytes 393248 | tf_op jit(solution)/shard_map/ppermute | solution.py:178
  216.4 39.5 %collective-permute-done.25.rest_3_ = bf16[6,256,128]{2,1,0:T(8,128)(2,1)S(1)} collective-permute-done((bf16[6,256,128]{2,1,0:T(8,128)(2,1)S(1)}, bf16[6,256,128]{2,1,0:T(8,128)(2,1)S(1)}, u32[]{:S(2)}, u32[]{:S(2)}) %collective-permute-start.25) | collective-permute-done | bytes 393248 | tf_op jit(solution)/shard_map/ppermute | solution.py:178
  255.8 8.4 %collective-permute-done.26.rest_4_ = bf16[6,256,128]{2,1,0:T(8,128)(2,1)S(1)} collective-permute-done((bf16[6,256,128]{2,1,0:T(8,128)(2,1)S(1)}, bf16[6,256,128]{2,1,0:T(8,128)(2,1)S(1)}, u32[]{:S(2)}, u32[]{:S(2)}) %collective-permute-start.26) | collective-permute-done | bytes 393248 | tf_op jit(solution)/shard_map/ppermute | solution.py:178
  264.3 3.5 %collective-permute-done.28.rest_6_ = bf16[6,256,128]{2,1,0:T(8,128)(2,1)S(1)} collective-permute-done((bf16[6,256,128]{2,1,0:T(8,128)(2,1)S(1)}, bf16[6,256,128]{2,1,0:T(8,128)(2,1)S(1)}, u32[]{:S(2)}, u32[]{:S(2)}) %collective-permute-start.28) | collective-permute-done | bytes 393248 | tf_op jit(solution)/shard_map/ppermute | solution.py:178
  268.6 57.6 %gather_coulomb.1 = (bf16[14,256,128]{2,1,0:T(8,128)(2,1)}, bf16[14,256,128]{2,1,0:T(8,128)(2,1)}) custom-call(s32[56]{0:T(128)} %pad_add_fusion.table, bf16[6,256,128]{2,1,0:T(8,128)(2,1)} %copy-done.1, bf16[6,256,128]{2,1,0:T(8,128)(2,1)} %copy-done.3, bf16[6,256,128]{2,1,0:T(8,128)(2,1)} %copy-done.4, bf16[6,256,128]{2,1,0:T(8,128)(2,1)} %copy-done.5, ...), custom_call_target="tpu_custom_call" | custom-call | tf_op jit(solution)/shard_map/gather_coulomb/pallas_call | solution.py:299
  (102 shorter events, 47.0 us)
Async XLA Ops:
  35.2 8.8 %collective-permute-start.1 = (bf16[3,256,128]{2,1,0:T(8,128)(2,1)}, bf16[3,256,128]{2,1,0:T(8,128)(2,1)S(1)}, u32[]{:S(2)}, u32[]{:S(2)}) collective-permute-start(bf16[3,256,128]{2,1,0:T(8,128)(2,1)} %get-tuple-element.30), channel_id=1, source_target_pairs={{0,4},{2,6},{4,8},{6,10},{8,12},{10,14},{12,0},{14,2},{1,5},{3,7},... | collective-permute-start | bytes 589832 | tf_op jit(solution)/shard_map/ppermute | solution.py:178
  36.5 27.9 %collective-permute-start.2 = (bf16[3,256,128]{2,1,0:T(8,128)(2,1)}, bf16[3,256,128]{2,1,0:T(8,128)(2,1)S(1)}, u32[]{:S(2)}, u32[]{:S(2)}) collective-permute-start(bf16[3,256,128]{2,1,0:T(8,128)(2,1)} %get-tuple-element.31), channel_id=1, source_target_pairs={{0,6},{2,8},{4,10},{6,12},{8,14},{10,0},{12,2},{14,4},{1,7},{3,9},... | collective-permute-start | bytes 589832 | tf_op jit(solution)/shard_map/ppermute | solution.py:178
  37.4 31.2 %collective-permute-start.3 = (bf16[3,256,128]{2,1,0:T(8,128)(2,1)}, bf16[3,256,128]{2,1,0:T(8,128)(2,1)S(1)}, u32[]{:S(2)}, u32[]{:S(2)}) collective-permute-start(bf16[3,256,128]{2,1,0:T(8,128)(2,1)} %get-tuple-element.32), channel_id=1, source_target_pairs={{0,8},{2,10},{4,12},{6,14},{8,0},{10,2},{12,4},{14,6},{1,9},{3,11}... | collective-permute-start | bytes 589832 | tf_op jit(solution)/shard_map/ppermute | solution.py:178
  38.8 29.8 %collective-permute-start.4 = (bf16[3,256,128]{2,1,0:T(8,128)(2,1)}, bf16[3,256,128]{2,1,0:T(8,128)(2,1)S(1)}, u32[]{:S(2)}, u32[]{:S(2)}) collective-permute-start(bf16[3,256,128]{2,1,0:T(8,128)(2,1)} %get-tuple-element.33), channel_id=1, source_target_pairs={{0,10},{2,12},{4,14},{6,0},{8,2},{10,4},{12,6},{14,8},{1,11},{3,13... | collective-permute-start | bytes 589832 | tf_op jit(solution)/shard_map/ppermute | solution.py:178
  39.9 31.5 %collective-permute-start.5 = (bf16[3,256,128]{2,1,0:T(8,128)(2,1)}, bf16[3,256,128]{2,1,0:T(8,128)(2,1)S(1)}, u32[]{:S(2)}, u32[]{:S(2)}) collective-permute-start(bf16[3,256,128]{2,1,0:T(8,128)(2,1)} %get-tuple-element.34), channel_id=1, source_target_pairs={{0,12},{2,14},{4,0},{6,2},{8,4},{10,6},{12,8},{14,10},{1,13},{3,15... | collective-permute-start | bytes 589832 | tf_op jit(solution)/shard_map/ppermute | solution.py:178
  44.0 28.4 %collective-permute-start.6 = (bf16[3,256,128]{2,1,0:T(8,128)(2,1)}, bf16[3,256,128]{2,1,0:T(8,128)(2,1)S(1)}, u32[]{:S(2)}, u32[]{:S(2)}) collective-permute-start(bf16[3,256,128]{2,1,0:T(8,128)(2,1)} %get-tuple-element.35), channel_id=1, source_target_pairs={{0,14},{2,0},{4,2},{6,4},{8,6},{10,8},{12,10},{14,12},{1,15},{3,1}... | collective-permute-start | bytes 589832 | tf_op jit(solution)/shard_map/ppermute | solution.py:178
  116.7 6.3 %collective-permute-start.9 = (bf16[256,256]{1,0:T(8,128)(2,1)S(1)}, bf16[256,256]{1,0:T(8,128)(2,1)S(1)}, u32[]{:S(2)}, u32[]{:S(2)}) collective-permute-start(bf16[256,256]{1,0:T(8,128)(2,1)S(1)} %get-tuple-element.38), channel_id=1, source_target_pairs={{0,4},{2,6},{4,8},{6,10},{8,12},{10,14},{12,0},{14,2},{1,5},{3,7},... | collective-permute-start | bytes 393224 | tf_op jit(solution)/shard_map/ppermute | solution.py:178
  116.8 19.6 %collective-permute-start.10 = (bf16[256,256]{1,0:T(8,128)(2,1)S(1)}, bf16[256,256]{1,0:T(8,128)(2,1)S(1)}, u32[]{:S(2)}, u32[]{:S(2)}) collective-permute-start(bf16[256,256]{1,0:T(8,128)(2,1)S(1)} %get-tuple-element.39), channel_id=1, source_target_pairs={{0,6},{2,8},{4,10},{6,12},{8,14},{10,0},{12,2},{14,4},{1,7},{3,9},... | collective-permute-start | bytes 393224 | tf_op jit(solution)/shard_map/ppermute | solution.py:178
  119.4 19.7 %collective-permute-start.11 = (bf16[256,256]{1,0:T(8,128)(2,1)S(1)}, bf16[256,256]{1,0:T(8,128)(2,1)S(1)}, u32[]{:S(2)}, u32[]{:S(2)}) collective-permute-start(bf16[256,256]{1,0:T(8,128)(2,1)S(1)} %get-tuple-element.40), channel_id=1, source_target_pairs={{0,8},{2,10},{4,12},{6,14},{8,0},{10,2},{12,4},{14,6},{1,9},{3,11}... | collective-permute-start | bytes 393224 | tf_op jit(solution)/shard_map/ppermute | solution.py:178
  120.3 18.9 %collective-permute-start.12 = (bf16[256,256]{1,0:T(8,128)(2,1)S(1)}, bf16[256,256]{1,0:T(8,128)(2,1)S(1)}, u32[]{:S(2)}, u32[]{:S(2)}) collective-permute-start(bf16[256,256]{1,0:T(8,128)(2,1)S(1)} %get-tuple-element.41), channel_id=1, source_target_pairs={{0,10},{2,12},{4,14},{6,0},{8,2},{10,4},{12,6},{14,8},{1,11},{3,13... | collective-permute-start | bytes 393224 | tf_op jit(solution)/shard_map/ppermute | solution.py:178
  121.4 20.6 %collective-permute-start.13 = (bf16[256,256]{1,0:T(8,128)(2,1)S(1)}, bf16[256,256]{1,0:T(8,128)(2,1)S(1)}, u32[]{:S(2)}, u32[]{:S(2)}) collective-permute-start(bf16[256,256]{1,0:T(8,128)(2,1)S(1)} %get-tuple-element.42), channel_id=1, source_target_pairs={{0,12},{2,14},{4,0},{6,2},{8,4},{10,6},{12,8},{14,10},{1,13},{3,15... | collective-permute-start | bytes 393224 | tf_op jit(solution)/shard_map/ppermute | solution.py:178
  123.1 20.0 %collective-permute-start.14 = (bf16[256,256]{1,0:T(8,128)(2,1)S(1)}, bf16[256,256]{1,0:T(8,128)(2,1)S(1)}, u32[]{:S(2)}, u32[]{:S(2)}) collective-permute-start(bf16[256,256]{1,0:T(8,128)(2,1)S(1)} %get-tuple-element.43), channel_id=1, source_target_pairs={{0,14},{2,0},{4,2},{6,4},{8,6},{10,8},{12,10},{14,12},{1,15},{3,1}... | collective-permute-start | bytes 393224 | tf_op jit(solution)/shard_map/ppermute | solution.py:178
  143.4 9.8 %collective-permute-start.19 = (bf16[256,256]{1,0:T(8,128)(2,1)S(1)}, bf16[256,256]{1,0:T(8,128)(2,1)S(1)}, u32[]{:S(2)}, u32[]{:S(2)}) collective-permute-start(bf16[256,256]{1,0:T(8,128)(2,1)S(1)} %add_convert_fusion.rest_0_), channel_id=1, source_target_pairs={{0,10},{2,12},{4,14},{6,0},{8,2},{10,4},{12,6},{14,8},{1,11},{3,13... | collective-permute-start | bytes 393224 | tf_op jit(solution)/shard_map/ppermute | solution.py:178
  145.4 13.3 %collective-permute-start.18 = (bf16[256,256]{1,0:T(8,128)(2,1)S(1)}, bf16[256,256]{1,0:T(8,128)(2,1)S(1)}, u32[]{:S(2)}, u32[]{:S(2)}) collective-permute-start(bf16[256,256]{1,0:T(8,128)(2,1)S(1)} %add_convert_fusion.rest_0_), channel_id=1, source_target_pairs={{0,8},{2,10},{4,12},{6,14},{8,0},{10,2},{12,4},{14,6},{1,9},{3,11}... | collective-permute-start | bytes 393224 | tf_op jit(solution)/shard_map/ppermute | solution.py:178
  146.8 14.8 %collective-permute-start.17 = (bf16[256,256]{1,0:T(8,128)(2,1)S(1)}, bf16[256,256]{1,0:T(8,128)(2,1)S(1)}, u32[]{:S(2)}, u32[]{:S(2)}) collective-permute-start(bf16[256,256]{1,0:T(8,128)(2,1)S(1)} %add_convert_fusion.rest_0_), channel_id=1, source_target_pairs={{0,6},{2,8},{4,10},{6,12},{8,14},{10,0},{12,2},{14,4},{1,7},{3,9},... | collective-permute-start | bytes 393224 | tf_op jit(solution)/shard_map/ppermute | solution.py:178
  148.8 15.7 %collective-permute-start.16 = (bf16[256,256]{1,0:T(8,128)(2,1)S(1)}, bf16[256,256]{1,0:T(8,128)(2,1)S(1)}, u32[]{:S(2)}, u32[]{:S(2)}) collective-permute-start(bf16[256,256]{1,0:T(8,128)(2,1)S(1)} %add_convert_fusion.rest_0_), channel_id=1, source_target_pairs={{0,4},{2,6},{4,8},{6,10},{8,12},{10,14},{12,0},{14,2},{1,5},{3,7},... | collective-permute-start | bytes 393224 | tf_op jit(solution)/shard_map/ppermute | solution.py:178
  149.2 17.8 %collective-permute-start.15 = (bf16[256,256]{1,0:T(8,128)(2,1)S(1)}, bf16[256,256]{1,0:T(8,128)(2,1)S(1)}, u32[]{:S(2)}, u32[]{:S(2)}) collective-permute-start(bf16[256,256]{1,0:T(8,128)(2,1)S(1)} %add_convert_fusion.rest_0_), channel_id=1, source_target_pairs={{0,2},{2,4},{4,6},{6,8},{8,10},{10,12},{12,14},{14,0},{1,3},{3,5},... | collective-permute-start | bytes 393224 | tf_op jit(solution)/shard_map/ppermute | solution.py:178
  194.6 11.8 %collective-permute-start.23 = (bf16[6,256,128]{2,1,0:T(8,128)(2,1)S(1)}, bf16[6,256,128]{2,1,0:T(8,128)(2,1)S(1)}, u32[]{:S(2)}, u32[]{:S(2)}) collective-permute-start(bf16[6,256,128]{2,1,0:T(8,128)(2,1)S(1)} %get-tuple-element.47), channel_id=1, source_target_pairs={{0,2},{2,4},{4,6},{6,8},{8,10},{10,12},{12,14},{14,0},{1,3},{3,5},... | collective-permute-start | bytes 1179656 | tf_op jit(solution)/shard_map/ppermute | solution.py:178
  197.1 18.6 %collective-permute-start.24 = (bf16[6,256,128]{2,1,0:T(8,128)(2,1)S(1)}, bf16[6,256,128]{2,1,0:T(8,128)(2,1)S(1)}, u32[]{:S(2)}, u32[]{:S(2)}) collective-permute-start(bf16[6,256,128]{2,1,0:T(8,128)(2,1)S(1)} %get-tuple-element.48), channel_id=1, source_target_pairs={{0,4},{2,6},{4,8},{6,10},{8,12},{10,14},{12,0},{14,2},{1,5},{3,7},... | collective-permute-start | bytes 1179656 | tf_op jit(solution)/shard_map/ppermute | solution.py:178
  197.1 58.7 %collective-permute-start.25 = (bf16[6,256,128]{2,1,0:T(8,128)(2,1)S(1)}, bf16[6,256,128]{2,1,0:T(8,128)(2,1)S(1)}, u32[]{:S(2)}, u32[]{:S(2)}) collective-permute-start(bf16[6,256,128]{2,1,0:T(8,128)(2,1)S(1)} %get-tuple-element.49), channel_id=1, source_target_pairs={{0,6},{2,8},{4,10},{6,12},{8,14},{10,0},{12,2},{14,4},{1,7},{3,9},... | collective-permute-start | bytes 1179656 | tf_op jit(solution)/shard_map/ppermute | solution.py:178
  199.1 65.1 %collective-permute-start.26 = (bf16[6,256,128]{2,1,0:T(8,128)(2,1)S(1)}, bf16[6,256,128]{2,1,0:T(8,128)(2,1)S(1)}, u32[]{:S(2)}, u32[]{:S(2)}) collective-permute-start(bf16[6,256,128]{2,1,0:T(8,128)(2,1)S(1)} %get-tuple-element.50), channel_id=1, source_target_pairs={{0,8},{2,10},{4,12},{6,14},{8,0},{10,2},{12,4},{14,6},{1,9},{3,11}... | collective-permute-start | bytes 1179656 | tf_op jit(solution)/shard_map/ppermute | solution.py:178
  200.5 63.7 %collective-permute-start.27 = (bf16[6,256,128]{2,1,0:T(8,128)(2,1)S(1)}, bf16[6,256,128]{2,1,0:T(8,128)(2,1)S(1)}, u32[]{:S(2)}, u32[]{:S(2)}) collective-permute-start(bf16[6,256,128]{2,1,0:T(8,128)(2,1)S(1)} %get-tuple-element.51), channel_id=1, source_target_pairs={{0,10},{2,12},{4,14},{6,0},{8,2},{10,4},{12,6},{14,8},{1,11},{3,13... | collective-permute-start | bytes 1179656 | tf_op jit(solution)/shard_map/ppermute | solution.py:178
  206.4 61.3 %collective-permute-start.28 = (bf16[6,256,128]{2,1,0:T(8,128)(2,1)S(1)}, bf16[6,256,128]{2,1,0:T(8,128)(2,1)S(1)}, u32[]{:S(2)}, u32[]{:S(2)}) collective-permute-start(bf16[6,256,128]{2,1,0:T(8,128)(2,1)S(1)} %get-tuple-element.52), channel_id=1, source_target_pairs={{0,12},{2,14},{4,0},{6,2},{8,4},{10,6},{12,8},{14,10},{1,13},{3,15... | collective-permute-start | bytes 1179656 | tf_op jit(solution)/shard_map/ppermute | solution.py:178
  215.7 52.0 %collective-permute-start.29 = (bf16[6,256,128]{2,1,0:T(8,128)(2,1)S(1)}, bf16[6,256,128]{2,1,0:T(8,128)(2,1)S(1)}, u32[]{:S(2)}, u32[]{:S(2)}) collective-permute-start(bf16[6,256,128]{2,1,0:T(8,128)(2,1)S(1)} %get-tuple-element.53), channel_id=1, source_target_pairs={{0,14},{2,0},{4,2},{6,4},{8,6},{10,8},{12,10},{14,12},{1,15},{3,1}... | collective-permute-start | bytes 1179656 | tf_op jit(solution)/shard_map/ppermute | solution.py:178
  (25 other events, 444.8 us)

commit v2 on v1

--- a/solution.py
+++ b/solution.py
@@ -28,13 +28,12 @@
     return own_target, own_rank, row_source, row_rank
 
 
-def scatter_density_kernel(devices, blocks, width, table, density, *rest):
+def scatter_density_kernel(devices, blocks, table, density, *rest):
     sends, sems = rest[:devices], rest[devices]
-    column = pl.multiple_of(table[2 * blocks] * width, width)
 
     def copy(row, step):
         return pltpu.make_async_copy(
-            density.at[row, :, pl.ds(column, width)],
+            density.at[row],
             sends[step].at[table[blocks + row]],
             sems.at[row],
         )
@@ -119,22 +118,16 @@
         )
         total = term if total is None else total + term
     own[...] = total[:, :half].reshape(own.shape)
-    other[...] = total[:, half:].reshape(other.shape)
-
-
-def scatter_coulomb_kernel(devices, blocks, shell, cap, table, screen, own, other, *rest):
+    other[...] = total[:, half:].reshape(other.shape).astype(other.dtype)
+
+
+def scatter_coulomb_kernel(
+    devices, blocks, some, shell, cap, table, screen, own, other, *rest
+):
     sends = rest[:devices]
     turning, row_buf, col_buf, sems = rest[devices:]
-    block = pl.program_id(0)
+    first = pl.program_id(0) * some
     pairs, half = own.shape[1], own.shape[2]
-    keep = jnp.broadcast_to(screen[0], (half, pairs)).T
-    value = (own[0] + other[0]) * keep
-    turning[...] = value
-    row_buf[block] = value.astype(jnp.bfloat16)
-    for j in range(shell):
-        col_buf[block, pl.ds(j * shell, shell), :] = turning[
-            pl.ds(j, shell, stride=shell), :
-        ].astype(jnp.bfloat16)
 
     def copy(group, b, step):
         buf = (row_buf, col_buf)[group]
@@ -144,14 +137,24 @@
             sems.at[group, b],
         )
 
-    for group in range(2):
-        for step in range(devices):
-
-            @pl.when(table[2 * group * blocks + block] == step)
-            def _():
-                copy(group, block, step).start()
-
-    @pl.when(block == blocks - 1)
+    for b in range(some):
+        block = first + b
+        keep = jnp.broadcast_to(screen[b], (half, pairs)).T
+        value = (own[b] + other[b].astype(jnp.float32)) * keep
+        turning[b] = value
+        row_buf[block] = value.astype(jnp.bfloat16)
+        for j in range(shell):
+            col_buf[block, pl.ds(j * shell, shell), :] = turning[
+                b, pl.ds(j, shell, stride=shell), :
+            ].astype(jnp.bfloat16)
+        for group in range(2):
+            for step in range(devices):
+
+                @pl.when(table[2 * group * blocks + block] == step)
+                def _():
+                    copy(group, block, step).start()
+
+    @pl.when(first == blocks - some)
     def _():
         for group in range(2):
             for b in range(blocks):
@@ -189,15 +192,18 @@
     send_table = ints([(home_source - me) % n, home_row_rank, core[None].astype(jnp.int32)])
     slots = jax.ShapeDtypeStruct((cap, pairs, half), jnp.bfloat16)
     sends = pl.pallas_call(
-        functools.partial(scatter_density_kernel, n, blocks, half),
+        functools.partial(scatter_density_kernel, n, blocks),
         out_shape=[slots] * n,
         grid_spec=pltpu.PrefetchScalarGridSpec(
             num_scalar_prefetch=1,
-            grid=(),
-            in_specs=[any_spec],
+            grid=(1,),
+            in_specs=[
+                pl.BlockSpec((blocks, pairs, half), lambda i, t: (0, 0, t[2 * blocks]))
+            ],
             out_specs=[any_spec] * n,
             scratch_shapes=[pltpu.SemaphoreType.DMA((blocks,))],
         ),
+        compiler_params=params,
         name="scatter_density",
     )(send_table, density)
     received = [sends[0]] + [shift(sends[d], d) for d in range(1, n)]
@@ -207,11 +213,12 @@
         out_shape=[jax.ShapeDtypeStruct((blocks, pairs, half), jnp.bfloat16)],
         grid_spec=pltpu.PrefetchScalarGridSpec(
             num_scalar_prefetch=1,
-            grid=(),
+            grid=(1,),
             in_specs=[any_spec] * n,
-            out_specs=[any_spec],
+            out_specs=[pl.BlockSpec((blocks, pairs, half), lambda i, t: (0, 0, 0))],
             scratch_shapes=[pltpu.SemaphoreType.DMA((1, blocks))],
         ),
+        compiler_params=params,
         name="gather_density",
     )(pick_table, *received)[0]
     other = swap(own)
@@ -248,7 +255,10 @@
 
     mine, theirs = pl.pallas_call(
         functools.partial(apply_kernel, n, some),
-        out_shape=[jax.ShapeDtypeStruct((blocks, pairs, half), jnp.float32)] * 2,
+        out_shape=[
+            jax.ShapeDtypeStruct((blocks, pairs, half), jnp.float32),
+            jax.ShapeDtypeStruct((blocks, pairs, half), jnp.bfloat16),
+        ],
         grid_spec=pltpu.PrefetchScalarGridSpec(
             num_scalar_prefetch=1,
             grid=(steps,),
@@ -266,19 +276,19 @@
     )
     slots = jax.ShapeDtypeStruct((2 * cap, pairs, half), jnp.bfloat16)
     sends = pl.pallas_call(
-        functools.partial(scatter_coulomb_kernel, n, blocks, shell, cap),
+        functools.partial(scatter_coulomb_kernel, n, blocks, some, shell, cap),
         out_shape=[slots] * n,
         grid_spec=pltpu.PrefetchScalarGridSpec(
             num_scalar_prefetch=1,
-            grid=(blocks,),
+            grid=(steps,),
             in_specs=[
-                pl.BlockSpec((1, 1, pairs), block_map),
-                pl.BlockSpec((1, pairs, half), block_map),
-                pl.BlockSpec((1, pairs, half), block_map),
+                pl.BlockSpec((some, 1, pairs), block_map),
+                pl.BlockSpec((some, pairs, half), block_map),
+                pl.BlockSpec((some, pairs, half), block_map),
             ],
             out_specs=[any_spec] * n,
             scratch_shapes=[
-                pltpu.VMEM((pairs, half), jnp.float32),
+                pltpu.VMEM((some, pairs, half), jnp.float32),
                 pltpu.VMEM((blocks, pairs, half), jnp.bfloat16),
                 pltpu.VMEM((blocks, pairs, half), jnp.bfloat16),
                 pltpu.SemaphoreType.DMA((2, blocks)),
@@ -301,11 +311,12 @@
         out_shape=[jax.ShapeDtypeStruct((blocks, pairs, half), jnp.bfloat16)] * 2,
         grid_spec=pltpu.PrefetchScalarGridSpec(
             num_scalar_prefetch=1,
-            grid=(),
+            grid=(1,),
             in_specs=[any_spec] * n,
-            out_specs=[any_spec] * 2,
+            out_specs=[pl.BlockSpec((blocks, pairs, half), lambda i, t: (0, 0, 0))] * 2,
             scratch_shapes=[pltpu.SemaphoreType.DMA((2, blocks))],
         ),
+        compiler_params=params,
         name="gather_coulomb",
     )(in_table, *received)
     return rows, cols

time: 327 us -> 212 us (0.65)
  Pallas kernels: 147 us -> 38.5 us
    pallas_call x1, Pallas kernels: 57.6 us -> 6.3 us  [local(): pl.pallas_call(functools.partial(gather_kernel, n, blocks, 2), out_shape=...]
    pallas_call x2, Pallas kernels: 40.8 us -> 10.1 us  [the longest x1 7.11 us: local(): pl.pallas_call(functools.partial(scatter_coulomb_kernel, n, blocks, some,...]
    pallas_call x1, Pallas kernels: 29.7 us -> 2.81 us  [local(): pl.pallas_call(functools.partial(gather_kernel, n, blocks, 1), out_shape=...]
where the time goes in v2:
time: 212 us
  waiting for transfers between devices  135 us (64%)
  Pallas kernels  38.5 us (18%)
  starting transfers between devices  32 us (15%)
  other arithmetic  3.3 us (2%)
    ppermute x28, waiting for transfers between devices, shift(): return lax.ppermute(x, 'pair', [(s, (s + d) % n) for s in range(n)])  132 us
    ppermute x28, starting transfers between devices, shift(): return lax.ppermute(x, 'pair', [(s, (s + d) % n) for s in range(n)])  30.2 us
    pallas_call x1, Pallas kernels, local(): pl.pallas_call(functools.partial(fit_kernel, n, some, steps), out_shape=[...  9.76 us
    pallas_call x1, Pallas kernels, local(): pl.pallas_call(functools.partial(apply_kernel, n, some), out_shape=[jax.S...  9.52 us
    pallas_call x1, Pallas kernels, local(): pl.pallas_call(functools.partial(scatter_coulomb_kernel, n, blocks, some,...  7.11 us
    pallas_call x1, Pallas kernels, local(): pl.pallas_call(functools.partial(gather_kernel, n, blocks, 2), out_shape=...  6.3 us
  transfers between devices with their start and end apart: 30, of which 24 were waited for; matrix products, arithmetic and copies ran while one was open for 0% of the time, Pallas kernels for 0%

profile of v2, /device:TPU:15, one launch (start us, length us, event | category | flops | bytes accessed | tf_op | source)
XLA Modules:
  0.0 211.7 jit_solution(11219175771012551855)
XLA Ops:
  4.9 3.0 %scatter_density.1 = (bf16[3,256,128]{2,1,0:T(8,128)(2,1)S(1)}, bf16[3,256,128]{2,1,0:T(8,128)(2,1)S(1)}, bf16[3,256,128]{2,1,0:T(8,128)(2,1)S(1)}, bf16[3,256,1...) custom-call(s32[29]{0:T(128)S(1)} %pad_add_fusion.3.table, ...), custom_call_target="tpu_custom_call" | custom-call | tf_op jit(solution)/shard_map/scatter_density/pallas_call | solution.py:194
  15.1 2.8 %collective-permute-done.1.rest_2_ = bf16[3,256,128]{2,1,0:T(8,128)(2,1)S(1)} collective-permute-done((bf16[3,256,128]{2,1,0:T(8,128)(2,1)S(1)}, bf16[3,256,128]{2,1,0:T(8,128)(2,1)S(1)}, u32[]{:S(2)}, u32[]{:S(2)}) %collective-permute-start.1) | collective-permute-done | bytes 196640 | tf_op jit(solution)/shard_map/ppermute | solution.py:181
  18.0 20.0 %collective-permute-done.2.rest_3_ = bf16[3,256,128]{2,1,0:T(8,128)(2,1)S(1)} collective-permute-done((bf16[3,256,128]{2,1,0:T(8,128)(2,1)S(1)}, bf16[3,256,128]{2,1,0:T(8,128)(2,1)S(1)}, u32[]{:S(2)}, u32[]{:S(2)}) %collective-permute-start.2) | collective-permute-done | bytes 196640 | tf_op jit(solution)/shard_map/ppermute | solution.py:181
  38.1 4.2 %collective-permute-done.3.rest_4_ = bf16[3,256,128]{2,1,0:T(8,128)(2,1)S(1)} collective-permute-done((bf16[3,256,128]{2,1,0:T(8,128)(2,1)S(1)}, bf16[3,256,128]{2,1,0:T(8,128)(2,1)S(1)}, u32[]{:S(2)}, u32[]{:S(2)}) %collective-permute-start.3) | collective-permute-done | bytes 196640 | tf_op jit(solution)/shard_map/ppermute | solution.py:181
  42.3 2.9 %collective-permute-done.5.rest_6_ = bf16[3,256,128]{2,1,0:T(8,128)(2,1)S(1)} collective-permute-done((bf16[3,256,128]{2,1,0:T(8,128)(2,1)S(1)}, bf16[3,256,128]{2,1,0:T(8,128)(2,1)S(1)}, u32[]{:S(2)}, u32[]{:S(2)}) %collective-permute-start.5) | collective-permute-done | bytes 196640 | tf_op jit(solution)/shard_map/ppermute | solution.py:181
  46.3 2.8 %gather_density.1.own = bf16[14,256,128]{2,1,0:T(8,128)(2,1)S(1)} custom-call(s32[28]{0:T(128)S(1)} %pad_add_fusion.2.table, bf16[3,256,128]{2,1,0:T(8,128)(2,1)S(1)} %get-tuple-element.28.rest_0_, bf16[3,256,128]{2,1,0:T(8,128)(2,1)S(1)} %collective-permute-done.rest_1_, bf16[3,256,128]{2,1,0:T(8,128)(2,1)S(1)} %collective-permute-done.1.rest_2_, ...), custom_call_target="tpu_custom_call" | custom-call | tf_op jit(solution)/shard_map/gather_density/pallas_call | solution.py:211
  51.8 9.8 %fit.1 = (f32[256,256]{1,0:T(8,128)S(1)}, bf16[256,256]{1,0:T(8,128)(2,1)S(1)}, bf16[256,256]{1,0:T(8,128)(2,1)S(1)}, bf16[256,256]{1,0:T(8,128)(2,1)S(1)}, bf16...) custom-call(s32[1]{0:T(128)} %bitcast.table, ...), custom_call_target="tpu_custom_call" | custom-call | tf_op jit(solution)/shard_map/fit/pallas_call | solution.py:231
  61.7 2.5 %collective-permute-start.10 = (bf16[256,256]{1,0:T(8,128)(2,1)S(1)}, bf16[256,256]{1,0:T(8,128)(2,1)S(1)}, u32[]{:S(2)}, u32[]{:S(2)}) collective-permute-start(bf16[256,256]{1,0:T(8,128)(2,1)S(1)} %get-tuple-element.39), channel_id=1, source_target_pairs={{0,6},{2,8},{4,10},{6,12},{8,14},{10,0},{12,2},{14,4},{1,7},{3,9},... | collective-permute-start | bytes 393224 | tf_op jit(solution)/shard_map/ppermute | solution.py:181
  69.2 12.1 %collective-permute-done.10 = bf16[256,256]{1,0:T(8,128)(2,1)S(1)} collective-permute-done((bf16[256,256]{1,0:T(8,128)(2,1)S(1)}, bf16[256,256]{1,0:T(8,128)(2,1)S(1)}, u32[]{:S(2)}, u32[]{:S(2)}) %collective-permute-start.10) | collective-permute-done | bytes 131104 | tf_op jit(solution)/shard_map/ppermute | solution.py:181
  81.3 2.8 %collective-permute-done.11 = bf16[256,256]{1,0:T(8,128)(2,1)S(1)} collective-permute-done((bf16[256,256]{1,0:T(8,128)(2,1)S(1)}, bf16[256,256]{1,0:T(8,128)(2,1)S(1)}, u32[]{:S(2)}, u32[]{:S(2)}) %collective-permute-start.11) | collective-permute-done | bytes 131104 | tf_op jit(solution)/shard_map/ppermute | solution.py:181
  84.1 2.6 %collective-permute-done.13 = bf16[256,256]{1,0:T(8,128)(2,1)S(1)} collective-permute-done((bf16[256,256]{1,0:T(8,128)(2,1)S(1)}, bf16[256,256]{1,0:T(8,128)(2,1)S(1)}, u32[]{:S(2)}, u32[]{:S(2)}) %collective-permute-start.13) | collective-permute-done | bytes 131104 | tf_op jit(solution)/shard_map/ppermute | solution.py:181
  98.2 5.7 %collective-permute-done.18.rest_4_ = bf16[256,256]{1,0:T(8,128)(2,1)S(1)} collective-permute-done((bf16[256,256]{1,0:T(8,128)(2,1)S(1)}, bf16[256,256]{1,0:T(8,128)(2,1)S(1)}, u32[]{:S(2)}, u32[]{:S(2)}) %collective-permute-start.18) | collective-permute-done | bytes 131104 | tf_op jit(solution)/shard_map/ppermute | solution.py:181
  103.9 2.9 %collective-permute-done.17.rest_3_ = bf16[256,256]{1,0:T(8,128)(2,1)S(1)} collective-permute-done((bf16[256,256]{1,0:T(8,128)(2,1)S(1)}, bf16[256,256]{1,0:T(8,128)(2,1)S(1)}, u32[]{:S(2)}, u32[]{:S(2)}) %collective-permute-start.17) | collective-permute-done | bytes 131104 | tf_op jit(solution)/shard_map/ppermute | solution.py:181
  106.7 2.8 %collective-permute-done.16.rest_2_ = bf16[256,256]{1,0:T(8,128)(2,1)S(1)} collective-permute-done((bf16[256,256]{1,0:T(8,128)(2,1)S(1)}, bf16[256,256]{1,0:T(8,128)(2,1)S(1)}, u32[]{:S(2)}, u32[]{:S(2)}) %collective-permute-start.16) | collective-permute-done | bytes 131104 | tf_op jit(solution)/shard_map/ppermute | solution.py:181
  109.5 2.6 %collective-permute-done.15.rest_1_ = bf16[256,256]{1,0:T(8,128)(2,1)S(1)} collective-permute-done((bf16[256,256]{1,0:T(8,128)(2,1)S(1)}, bf16[256,256]{1,0:T(8,128)(2,1)S(1)}, u32[]{:S(2)}, u32[]{:S(2)}) %collective-permute-start.15) | collective-permute-done | bytes 131104 | tf_op jit(solution)/shard_map/ppermute | solution.py:181
  112.1 9.5 %apply.1 = (f32[14,256,128]{2,1,0:T(8,128)S(1)}, bf16[14,256,128]{2,1,0:T(8,128)(2,1)S(1)}) custom-call(s32[1]{0:T(128)} %bitcast.table, bf16[14,256,2048]{2,1,0:T(8,128)(2,1)} %integrals.3, bf16[256,256]{1,0:T(8,128)(2,1)S(1)} %add_convert_fusion.rest_0_, bf16[256,256]{1,0:T(8,128)(2,1)S(1)} %collective-permute-done.15.rest_1_, ...), custom_call_target="tpu_custom_call" | custom-call | tf_op jit(solution)/shard_map/apply/pallas_call | solution.py:256
  125.0 7.1 %scatter_coulomb.1 = (bf16[6,256,128]{2,1,0:T(8,128)(2,1)S(1)}, bf16[6,256,128]{2,1,0:T(8,128)(2,1)S(1)}, bf16[6,256,128]{2,1,0:T(8,128)(2,1)S(1)}, bf16[6,256,1...) custom-call(s32[56]{0:T(128)S(1)} %pad_add_fusion.1.table, ...), custom_call_target="tpu_custom_call" | custom-call | tf_op jit(solution)/shard_map/scatter_coulomb/pallas_call | solution.py:278
  132.1 2.8 %collective-permute-start.23 = (bf16[6,256,128]{2,1,0:T(8,128)(2,1)S(1)}, bf16[6,256,128]{2,1,0:T(8,128)(2,1)S(1)}, u32[]{:S(2)}, u32[]{:S(2)}) collective-permute-start(bf16[6,256,128]{2,1,0:T(8,128)(2,1)S(1)} %get-tuple-element.47), channel_id=1, source_target_pairs={{0,2},{2,4},{4,6},{6,8},{8,10},{10,12},{12,14},{14,0},{1,3},{3,5},... | collective-permute-start | bytes 1179656 | tf_op jit(solution)/shard_map/ppermute | solution.py:181
  140.4 3.6 %collective-permute-done.23.rest_1_ = bf16[6,256,128]{2,1,0:T(8,128)(2,1)S(1)} collective-permute-done((bf16[6,256,128]{2,1,0:T(8,128)(2,1)S(1)}, bf16[6,256,128]{2,1,0:T(8,128)(2,1)S(1)}, u32[]{:S(2)}, u32[]{:S(2)}) %collective-permute-start.23) | collective-permute-done | bytes 393248 | tf_op jit(solution)/shard_map/ppermute | solution.py:181
  144.1 9.2 %collective-permute-done.24.rest_2_ = bf16[6,256,128]{2,1,0:T(8,128)(2,1)S(1)} collective-permute-done((bf16[6,256,128]{2,1,0:T(8,128)(2,1)S(1)}, bf16[6,256,128]{2,1,0:T(8,128)(2,1)S(1)}, u32[]{:S(2)}, u32[]{:S(2)}) %collective-permute-start.24) | collective-permute-done | bytes 393248 | tf_op jit(solution)/shard_map/ppermute | solution.py:181
  153.4 40.2 %collective-permute-done.25.rest_3_ = bf16[6,256,128]{2,1,0:T(8,128)(2,1)S(1)} collective-permute-done((bf16[6,256,128]{2,1,0:T(8,128)(2,1)S(1)}, bf16[6,256,128]{2,1,0:T(8,128)(2,1)S(1)}, u32[]{:S(2)}, u32[]{:S(2)}) %collective-permute-start.25) | collective-permute-done | bytes 393248 | tf_op jit(solution)/shard_map/ppermute | solution.py:181
  193.6 8.4 %collective-permute-done.26.rest_4_ = bf16[6,256,128]{2,1,0:T(8,128)(2,1)S(1)} collective-permute-done((bf16[6,256,128]{2,1,0:T(8,128)(2,1)S(1)}, bf16[6,256,128]{2,1,0:T(8,128)(2,1)S(1)}, u32[]{:S(2)}, u32[]{:S(2)}) %collective-permute-start.26) | collective-permute-done | bytes 393248 | tf_op jit(solution)/shard_map/ppermute | solution.py:181
  202.0 3.3 %collective-permute-done.28.rest_6_ = bf16[6,256,128]{2,1,0:T(8,128)(2,1)S(1)} collective-permute-done((bf16[6,256,128]{2,1,0:T(8,128)(2,1)S(1)}, bf16[6,256,128]{2,1,0:T(8,128)(2,1)S(1)}, u32[]{:S(2)}, u32[]{:S(2)}) %collective-permute-start.28) | collective-permute-done | bytes 393248 | tf_op jit(solution)/shard_map/ppermute | solution.py:181
  205.4 6.3 %gather_coulomb.1 = (bf16[14,256,128]{2,1,0:T(8,128)(2,1)}, bf16[14,256,128]{2,1,0:T(8,128)(2,1)}) custom-call(s32[56]{0:T(128)S(1)} %pad_add_fusion.table, bf16[6,256,128]{2,1,0:T(8,128)(2,1)S(1)} %get-tuple-element.46.rest_0_, bf16[6,256,128]{2,1,0:T(8,128)(2,1)S(1)} %collective-permute-done.23.rest_1_, ...), custom_call_target="tpu_custom_call" | custom-call | tf_op jit(solution)/shard_map/gather_coulomb/pallas_call | solution.py:309
  (70 shorter events, 41.2 us)
Async XLA Ops:
  9.2 8.7 %collective-permute-start.1 = (bf16[3,256,128]{2,1,0:T(8,128)(2,1)S(1)}, bf16[3,256,128]{2,1,0:T(8,128)(2,1)S(1)}, u32[]{:S(2)}, u32[]{:S(2)}) collective-permute-start(bf16[3,256,128]{2,1,0:T(8,128)(2,1)S(1)} %get-tuple-element.30), channel_id=1, source_target_pairs={{0,4},{2,6},{4,8},{6,10},{8,12},{10,14},{12,0},{14,2},{1,5},{3,7},... | collective-permute-start | bytes 589832 | tf_op jit(solution)/shard_map/ppermute | solution.py:181
  10.5 27.6 %collective-permute-start.2 = (bf16[3,256,128]{2,1,0:T(8,128)(2,1)S(1)}, bf16[3,256,128]{2,1,0:T(8,128)(2,1)S(1)}, u32[]{:S(2)}, u32[]{:S(2)}) collective-permute-start(bf16[3,256,128]{2,1,0:T(8,128)(2,1)S(1)} %get-tuple-element.31), channel_id=1, source_target_pairs={{0,6},{2,8},{4,10},{6,12},{8,14},{10,0},{12,2},{14,4},{1,7},{3,9},... | collective-permute-start | bytes 589832 | tf_op jit(solution)/shard_map/ppermute | solution.py:181
  11.5 30.8 %collective-permute-start.3 = (bf16[3,256,128]{2,1,0:T(8,128)(2,1)S(1)}, bf16[3,256,128]{2,1,0:T(8,128)(2,1)S(1)}, u32[]{:S(2)}, u32[]{:S(2)}) collective-permute-start(bf16[3,256,128]{2,1,0:T(8,128)(2,1)S(1)} %get-tuple-element.32), channel_id=1, source_target_pairs={{0,8},{2,10},{4,12},{6,14},{8,0},{10,2},{12,4},{14,6},{1,9},{3,11}... | collective-permute-start | bytes 589832 | tf_op jit(solution)/shard_map/ppermute | solution.py:181
  12.8 29.5 %collective-permute-start.4 = (bf16[3,256,128]{2,1,0:T(8,128)(2,1)S(1)}, bf16[3,256,128]{2,1,0:T(8,128)(2,1)S(1)}, u32[]{:S(2)}, u32[]{:S(2)}) collective-permute-start(bf16[3,256,128]{2,1,0:T(8,128)(2,1)S(1)} %get-tuple-element.33), channel_id=1, source_target_pairs={{0,10},{2,12},{4,14},{6,0},{8,2},{10,4},{12,6},{14,8},{1,11},{3,13... | collective-permute-start | bytes 589832 | tf_op jit(solution)/shard_map/ppermute | solution.py:181
  13.8 31.4 %collective-permute-start.5 = (bf16[3,256,128]{2,1,0:T(8,128)(2,1)S(1)}, bf16[3,256,128]{2,1,0:T(8,128)(2,1)S(1)}, u32[]{:S(2)}, u32[]{:S(2)}) collective-permute-start(bf16[3,256,128]{2,1,0:T(8,128)(2,1)S(1)} %get-tuple-element.34), channel_id=1, source_target_pairs={{0,12},{2,14},{4,0},{6,2},{8,4},{10,6},{12,8},{14,10},{1,13},{3,15... | collective-permute-start | bytes 589832 | tf_op jit(solution)/shard_map/ppermute | solution.py:181
  17.9 28.4 %collective-permute-start.6 = (bf16[3,256,128]{2,1,0:T(8,128)(2,1)S(1)}, bf16[3,256,128]{2,1,0:T(8,128)(2,1)S(1)}, u32[]{:S(2)}, u32[]{:S(2)}) collective-permute-start(bf16[3,256,128]{2,1,0:T(8,128)(2,1)S(1)} %get-tuple-element.35), channel_id=1, source_target_pairs={{0,14},{2,0},{4,2},{6,4},{8,6},{10,8},{12,10},{14,12},{1,15},{3,1}... | collective-permute-start | bytes 589832 | tf_op jit(solution)/shard_map/ppermute | solution.py:181
  61.6 6.1 %collective-permute-start.9 = (bf16[256,256]{1,0:T(8,128)(2,1)S(1)}, bf16[256,256]{1,0:T(8,128)(2,1)S(1)}, u32[]{:S(2)}, u32[]{:S(2)}) collective-permute-start(bf16[256,256]{1,0:T(8,128)(2,1)S(1)} %get-tuple-element.38), channel_id=1, source_target_pairs={{0,4},{2,6},{4,8},{6,10},{8,12},{10,14},{12,0},{14,2},{1,5},{3,7},... | collective-permute-start | bytes 393224 | tf_op jit(solution)/shard_map/ppermute | solution.py:181
  61.7 19.6 %collective-permute-start.10 = (bf16[256,256]{1,0:T(8,128)(2,1)S(1)}, bf16[256,256]{1,0:T(8,128)(2,1)S(1)}, u32[]{:S(2)}, u32[]{:S(2)}) collective-permute-start(bf16[256,256]{1,0:T(8,128)(2,1)S(1)} %get-tuple-element.39), channel_id=1, source_target_pairs={{0,6},{2,8},{4,10},{6,12},{8,14},{10,0},{12,2},{14,4},{1,7},{3,9},... | collective-permute-start | bytes 393224 | tf_op jit(solution)/shard_map/ppermute | solution.py:181
  64.2 20.0 %collective-permute-start.11 = (bf16[256,256]{1,0:T(8,128)(2,1)S(1)}, bf16[256,256]{1,0:T(8,128)(2,1)S(1)}, u32[]{:S(2)}, u32[]{:S(2)}) collective-permute-start(bf16[256,256]{1,0:T(8,128)(2,1)S(1)} %get-tuple-element.40), channel_id=1, source_target_pairs={{0,8},{2,10},{4,12},{6,14},{8,0},{10,2},{12,4},{14,6},{1,9},{3,11}... | collective-permute-start | bytes 393224 | tf_op jit(solution)/shard_map/ppermute | solution.py:181
  65.2 18.9 %collective-permute-start.12 = (bf16[256,256]{1,0:T(8,128)(2,1)S(1)}, bf16[256,256]{1,0:T(8,128)(2,1)S(1)}, u32[]{:S(2)}, u32[]{:S(2)}) collective-permute-start(bf16[256,256]{1,0:T(8,128)(2,1)S(1)} %get-tuple-element.41), channel_id=1, source_target_pairs={{0,10},{2,12},{4,14},{6,0},{8,2},{10,4},{12,6},{14,8},{1,11},{3,13... | collective-permute-start | bytes 393224 | tf_op jit(solution)/shard_map/ppermute | solution.py:181
  66.3 20.4 %collective-permute-start.13 = (bf16[256,256]{1,0:T(8,128)(2,1)S(1)}, bf16[256,256]{1,0:T(8,128)(2,1)S(1)}, u32[]{:S(2)}, u32[]{:S(2)}) collective-permute-start(bf16[256,256]{1,0:T(8,128)(2,1)S(1)} %get-tuple-element.42), channel_id=1, source_target_pairs={{0,12},{2,14},{4,0},{6,2},{8,4},{10,6},{12,8},{14,10},{1,13},{3,15... | collective-permute-start | bytes 393224 | tf_op jit(solution)/shard_map/ppermute | solution.py:181
  67.8 20.0 %collective-permute-start.14 = (bf16[256,256]{1,0:T(8,128)(2,1)S(1)}, bf16[256,256]{1,0:T(8,128)(2,1)S(1)}, u32[]{:S(2)}, u32[]{:S(2)}) collective-permute-start(bf16[256,256]{1,0:T(8,128)(2,1)S(1)} %get-tuple-element.43), channel_id=1, source_target_pairs={{0,14},{2,0},{4,2},{6,4},{8,6},{10,8},{12,10},{14,12},{1,15},{3,1}... | collective-permute-start | bytes 393224 | tf_op jit(solution)/shard_map/ppermute | solution.py:181
  88.1 10.1 %collective-permute-start.19 = (bf16[256,256]{1,0:T(8,128)(2,1)S(1)}, bf16[256,256]{1,0:T(8,128)(2,1)S(1)}, u32[]{:S(2)}, u32[]{:S(2)}) collective-permute-start(bf16[256,256]{1,0:T(8,128)(2,1)S(1)} %add_convert_fusion.rest_0_), channel_id=1, source_target_pairs={{0,10},{2,12},{4,14},{6,0},{8,2},{10,4},{12,6},{14,8},{1,11},{3,13... | collective-permute-start | bytes 393224 | tf_op jit(solution)/shard_map/ppermute | solution.py:181
  90.3 13.5 %collective-permute-start.18 = (bf16[256,256]{1,0:T(8,128)(2,1)S(1)}, bf16[256,256]{1,0:T(8,128)(2,1)S(1)}, u32[]{:S(2)}, u32[]{:S(2)}) collective-permute-start(bf16[256,256]{1,0:T(8,128)(2,1)S(1)} %add_convert_fusion.rest_0_), channel_id=1, source_target_pairs={{0,8},{2,10},{4,12},{6,14},{8,0},{10,2},{12,4},{14,6},{1,9},{3,11}... | collective-permute-start | bytes 393224 | tf_op jit(solution)/shard_map/ppermute | solution.py:181
  91.5 15.2 %collective-permute-start.17 = (bf16[256,256]{1,0:T(8,128)(2,1)S(1)}, bf16[256,256]{1,0:T(8,128)(2,1)S(1)}, u32[]{:S(2)}, u32[]{:S(2)}) collective-permute-start(bf16[256,256]{1,0:T(8,128)(2,1)S(1)} %add_convert_fusion.rest_0_), channel_id=1, source_target_pairs={{0,6},{2,8},{4,10},{6,12},{8,14},{10,0},{12,2},{14,4},{1,7},{3,9},... | collective-permute-start | bytes 393224 | tf_op jit(solution)/shard_map/ppermute | solution.py:181
  93.5 16.1 %collective-permute-start.16 = (bf16[256,256]{1,0:T(8,128)(2,1)S(1)}, bf16[256,256]{1,0:T(8,128)(2,1)S(1)}, u32[]{:S(2)}, u32[]{:S(2)}) collective-permute-start(bf16[256,256]{1,0:T(8,128)(2,1)S(1)} %add_convert_fusion.rest_0_), channel_id=1, source_target_pairs={{0,4},{2,6},{4,8},{6,10},{8,12},{10,14},{12,0},{14,2},{1,5},{3,7},... | collective-permute-start | bytes 393224 | tf_op jit(solution)/shard_map/ppermute | solution.py:181
  94.0 18.1 %collective-permute-start.15 = (bf16[256,256]{1,0:T(8,128)(2,1)S(1)}, bf16[256,256]{1,0:T(8,128)(2,1)S(1)}, u32[]{:S(2)}, u32[]{:S(2)}) collective-permute-start(bf16[256,256]{1,0:T(8,128)(2,1)S(1)} %add_convert_fusion.rest_0_), channel_id=1, source_target_pairs={{0,2},{2,4},{4,6},{6,8},{8,10},{10,12},{12,14},{14,0},{1,3},{3,5},... | collective-permute-start | bytes 393224 | tf_op jit(solution)/shard_map/ppermute | solution.py:181
  132.1 11.9 %collective-permute-start.23 = (bf16[6,256,128]{2,1,0:T(8,128)(2,1)S(1)}, bf16[6,256,128]{2,1,0:T(8,128)(2,1)S(1)}, u32[]{:S(2)}, u32[]{:S(2)}) collective-permute-start(bf16[6,256,128]{2,1,0:T(8,128)(2,1)S(1)} %get-tuple-element.47), channel_id=1, source_target_pairs={{0,2},{2,4},{4,6},{6,8},{8,10},{10,12},{12,14},{14,0},{1,3},{3,5},... | collective-permute-start | bytes 1179656 | tf_op jit(solution)/shard_map/ppermute | solution.py:181
  134.9 18.4 %collective-permute-start.24 = (bf16[6,256,128]{2,1,0:T(8,128)(2,1)S(1)}, bf16[6,256,128]{2,1,0:T(8,128)(2,1)S(1)}, u32[]{:S(2)}, u32[]{:S(2)}) collective-permute-start(bf16[6,256,128]{2,1,0:T(8,128)(2,1)S(1)} %get-tuple-element.48), channel_id=1, source_target_pairs={{0,4},{2,6},{4,8},{6,10},{8,12},{10,14},{12,0},{14,2},{1,5},{3,7},... | collective-permute-start | bytes 1179656 | tf_op jit(solution)/shard_map/ppermute | solution.py:181
  134.9 58.7 %collective-permute-start.25 = (bf16[6,256,128]{2,1,0:T(8,128)(2,1)S(1)}, bf16[6,256,128]{2,1,0:T(8,128)(2,1)S(1)}, u32[]{:S(2)}, u32[]{:S(2)}) collective-permute-start(bf16[6,256,128]{2,1,0:T(8,128)(2,1)S(1)} %get-tuple-element.49), channel_id=1, source_target_pairs={{0,6},{2,8},{4,10},{6,12},{8,14},{10,0},{12,2},{14,4},{1,7},{3,9},... | collective-permute-start | bytes 1179656 | tf_op jit(solution)/shard_map/ppermute | solution.py:181
  136.8 65.2 %collective-permute-start.26 = (bf16[6,256,128]{2,1,0:T(8,128)(2,1)S(1)}, bf16[6,256,128]{2,1,0:T(8,128)(2,1)S(1)}, u32[]{:S(2)}, u32[]{:S(2)}) collective-permute-start(bf16[6,256,128]{2,1,0:T(8,128)(2,1)S(1)} %get-tuple-element.50), channel_id=1, source_target_pairs={{0,8},{2,10},{4,12},{6,14},{8,0},{10,2},{12,4},{14,6},{1,9},{3,11}... | collective-permute-start | bytes 1179656 | tf_op jit(solution)/shard_map/ppermute | solution.py:181
  138.1 63.9 %collective-permute-start.27 = (bf16[6,256,128]{2,1,0:T(8,128)(2,1)S(1)}, bf16[6,256,128]{2,1,0:T(8,128)(2,1)S(1)}, u32[]{:S(2)}, u32[]{:S(2)}) collective-permute-start(bf16[6,256,128]{2,1,0:T(8,128)(2,1)S(1)} %get-tuple-element.51), channel_id=1, source_target_pairs={{0,10},{2,12},{4,14},{6,0},{8,2},{10,4},{12,6},{14,8},{1,11},{3,13... | collective-permute-start | bytes 1179656 | tf_op jit(solution)/shard_map/ppermute | solution.py:181
  144.0 61.3 %collective-permute-start.28 = (bf16[6,256,128]{2,1,0:T(8,128)(2,1)S(1)}, bf16[6,256,128]{2,1,0:T(8,128)(2,1)S(1)}, u32[]{:S(2)}, u32[]{:S(2)}) collective-permute-start(bf16[6,256,128]{2,1,0:T(8,128)(2,1)S(1)} %get-tuple-element.52), channel_id=1, source_target_pairs={{0,12},{2,14},{4,0},{6,2},{8,4},{10,6},{12,8},{14,10},{1,13},{3,15... | collective-permute-start | bytes 1179656 | tf_op jit(solution)/shard_map/ppermute | solution.py:181
  153.3 52.1 %collective-permute-start.29 = (bf16[6,256,128]{2,1,0:T(8,128)(2,1)S(1)}, bf16[6,256,128]{2,1,0:T(8,128)(2,1)S(1)}, u32[]{:S(2)}, u32[]{:S(2)}) collective-permute-start(bf16[6,256,128]{2,1,0:T(8,128)(2,1)S(1)} %get-tuple-element.53), channel_id=1, source_target_pairs={{0,14},{2,0},{4,2},{6,4},{8,6},{10,8},{12,10},{14,12},{1,15},{3,1}... | collective-permute-start | bytes 1179656 | tf_op jit(solution)/shard_map/ppermute | solution.py:181
  (9 other events, 119.2 us)

commit v3 on v0

v3 whole, which is shorter than its diff:
```python
import functools
import math

import jax
import jax.numpy as jnp
from jax import lax
from jax.experimental import pallas as pl
from jax.experimental.pallas import tpu as pltpu
from jax.sharding import PartitionSpec as P

VMEM_BYTES = 48 * 1024 * 1024
CHAINS = 2


def tables(slots, devices, blocks_dev, me):
    total = slots.shape[0]
    numbers = jnp.arange(total, dtype=jnp.int32)
    source = numbers // blocks_dev
    target = slots // blocks_dev
    joined = source * devices + target
    earlier = (joined[:, None] == joined[None, :]) & (numbers[None, :] < numbers[:, None])
    rank = jnp.sum(earlier.astype(jnp.int32), axis=1)
    own_target = lax.dynamic_slice_in_dim(target, me * blocks_dev, blocks_dev, 0)
    own_rank = lax.dynamic_slice_in_dim(rank, me * blocks_dev, blocks_dev, 0)
    rows = me * blocks_dev + jnp.arange(blocks_dev, dtype=jnp.int32)
    hot = slots[None, :] == rows[:, None]
    row_source = jnp.sum(jnp.where(hot, source[None, :], 0), axis=1)
    row_rank = jnp.sum(jnp.where(hot, rank[None, :], 0), axis=1)
    return own_target, own_rank, row_source, row_rank


def scatter_density_kernel(devices, blocks, table, density, *rest):
    sends, turned, sems = rest[: CHAINS * devices], rest[-2], rest[-1]
    part = turned.shape[2]

    def copy(chain, row, step):
        return pltpu.make_async_copy(
            turned.at[chain, row],
            sends[chain * devices + step].at[table[blocks + row]],
            sems.at[chain, row],
        )

    for row in range(blocks):
        value = density[row].T
        for chain in range(CHAINS):
            turned[chain, row] = value[chain * part : (chain + 1) * part]
        for chain in range(CHAINS):
            for step in range(devices):

                @pl.when(table[row] == step)
                def _():
                    copy(chain, row, step).start()

    for chain in range(CHAINS):
        for row in range(blocks):
            copy(chain, row, 0).wait()


def gather_density_kernel(devices, blocks, table, *rest):
    received, out, sems = rest[:devices], rest[devices], rest[devices + 1]

    def copy(row, step):
        return pltpu.make_async_copy(
            received[step].at[table[blocks + row]], out.at[row], sems.at[row]
        )

    for row in range(blocks):
        for step in range(devices):

            @pl.when(table[row] == step)
            def _():
                copy(row, step).start()

    for row in range(blocks):
        copy(row, 0).wait()


def fit_kernel(devices, some, steps, table, factor, own, other, integrals, keep, send, total):
    step = pl.program_id(0)
    width = keep.shape[2]

    @pl.when(step == 0)
    def _():
        total[...] = jnp.zeros_like(total)

    fitted = jnp.concatenate(
        [jnp.concatenate([own[b], other[b]], axis=0) * factor[b] for b in range(some)], axis=1
    )
    flat = integrals.reshape(some * integrals.shape[1], integrals.shape[2])
    for chunk in range(devices):
        at = pl.ds(chunk * width, width)
        total[:, at] += jnp.dot(fitted, flat[:, at], preferred_element_type=jnp.float32)

    @pl.when(step == steps - 1)
    def _():
        for e in range(devices):
            value = total[:, pl.ds(pl.multiple_of(table[e] * width, width), width)]
            if e % 2:
                send[e // 2] = value.astype(send.dtype)
            else:
                keep[e // 2] = value


def apply_kernel(devices, some, order, table, integrals, near, far, own, other):
    width = near.shape[2]
    part = own.shape[1]
    pairs = integrals.shape[1]
    flat = integrals.reshape(some * pairs, integrals.shape[2])
    total = None
    for i, e in enumerate(order):
        chunk = near[i] if i < devices // 2 else far[i - devices // 2]
        term = lax.dot_general(
            flat[:, pl.ds(pl.multiple_of(table[e] * width, width), width)],
            chunk,
            (((1,), (1,)), ((), ())),
            preferred_element_type=jnp.float32,
        )
        total = term if total is None else total + term
    for b in range(some):
        value = total[b * pairs : (b + 1) * pairs].T
        own[b] = value[:part]
        other[b] = value[part:].astype(other.dtype)


def scatter_coulomb_kernel(devices, blocks, some, cap, table, screen, own, other, *rest):
    sends, ready, sems = rest[:devices], rest[devices], rest[devices + 1]
    first = pl.program_id(0) * some

    def copy(group, b, step):
        return pltpu.make_async_copy(
            ready.at[b],
            sends[step].at[group * cap + table[(2 * group + 1) * blocks + b]],
            sems.at[group, b],
        )

    for b in range(some):
        block = first + b
        value = (own[b] + other[b].astype(jnp.float32)) * screen[b]
        ready[block] = value.astype(jnp.bfloat16)
        for group in range(2):
            for step in range(devices):

                @pl.when(table[2 * group * blocks + block] == step)
                def _():
                    copy(group, block, step).start()

    @pl.when(first == blocks - some)
    def _():
        for group in range(2):
            for b in range(blocks):
                copy(group, b, 0).wait()


def gather_coulomb_kernel(devices, blocks, shell, table, *rest):
    received = rest[: CHAINS * devices]
    rows, cols, landed, turning, sems = rest[CHAINS * devices :]
    block = pl.program_id(0)
    part = landed.shape[2] // CHAINS

    def copy(chain, group, row, step):
        return pltpu.make_async_copy(
            received[chain * devices + step].at[table[(2 * group + 1) * blocks + row]],
            landed.at[group, row, pl.ds(chain * part, part)],
            sems.at[chain, group, row],
        )

    @pl.when(block == 0)
    def _():
        for row in range(blocks):
            for group in range(2):
                for chain in range(CHAINS):
                    for step in range(devices):

                        @pl.when(table[2 * group * blocks + row] == step)
                        def _():
                            copy(chain, group, row, step).start()

    for group in range(2):
        for chain in range(CHAINS):
            copy(chain, group, block, 0).wait()
    rows[0] = landed[0, block].T
    turning[...] = landed[1, block].astype(jnp.float32).T
    for j in range(shell):
        cols[0, pl.ds(j * shell, shell), :] = turning[
            pl.ds(j, shell, stride=shell), :
        ].astype(jnp.bfloat16)


def local(three_index, density, screen, pair_shells, home_slot, mirror_slot):
    blocks, pairs, aux_dev = three_index.shape
    ndens = density.shape[2]
    shell = math.isqrt(pairs)
    n = lax.axis_size("pair")
    cores = lax.axis_size("aux")
    me = lax.axis_index("pair")
    core = lax.axis_index("aux")
    half = ndens // cores
    part = half // CHAINS
    both = cores * part
    width = aux_dev // n
    cap = 2 + (blocks - 1) // n
    some = 2 if blocks % 2 == 0 else 1
    steps = blocks // some
    any_spec = pl.BlockSpec(memory_space=pl.ANY)
    params = pltpu.CompilerParams(vmem_limit_bytes=VMEM_BYTES)
    bf16, f32 = jnp.bfloat16, jnp.float32
    block_map = lambda i, t: (i, 0, 0)
    whole_map = lambda i, t: (0, 0, 0)
    ints = functools.partial(jnp.concatenate, axis=0)

    def shift(x, d):
        return lax.ppermute(x, "pair", [(s, (s + d) % n) for s in range(n)])

    def flip(x, bit):
        return lax.ppermute(x, "pair", [(s, s ^ bit) for s in range(n)])

    def swap(x):
        return lax.ppermute(x, "aux", [(s, (s + 1) % cores) for s in range(cores)])

    home_target, home_rank, home_source, home_row_rank = tables(home_slot, n, blocks, me)
    mirror_target, mirror_rank, mirror_source, mirror_row_rank = tables(
        mirror_slot, n, blocks, me
    )
    send_table = ints([(home_source - me) % n, home_row_rank, core[None].astype(jnp.int32)])
    pick_table = ints([(me - home_target) % n, home_rank])
    chunk_table = me ^ jnp.arange(n, dtype=jnp.int32)
    out_table = ints([(home_target - me) % n, home_rank, (mirror_target - me) % n, mirror_rank])
    in_table = ints(
        [(me - home_source) % n, home_row_rank, (me - mirror_source) % n, cap + mirror_row_rank]
    )
    weight = jnp.where(pair_shells[:, 0] != pair_shells[:, 1], 2.0, 1.0)
    factor = (screen.astype(f32) * weight[:, None]).astype(bf16)[:, None, :]
    keeping = screen.astype(f32)[:, None, :]

    sends = pl.pallas_call(
        functools.partial(scatter_density_kernel, n, blocks),
        out_shape=[jax.ShapeDtypeStruct((cap, part, pairs), bf16)] * (CHAINS * n),
        grid_spec=pltpu.PrefetchScalarGridSpec(
            num_scalar_prefetch=1,
            grid=(1,),
            in_specs=[pl.BlockSpec((blocks, pairs, half), lambda i, t: (0, 0, t[2 * blocks]))],
            out_specs=[any_spec] * (CHAINS * n),
            scratch_shapes=[
                pltpu.VMEM((CHAINS, blocks, part, pairs), bf16),
                pltpu.SemaphoreType.DMA((CHAINS, blocks)),
            ],
        ),
        compiler_params=params,
        name="scatter_density",
    )(send_table, density)

    def fetch(chain):
        mine = sends[chain * n : (chain + 1) * n]
        received = [mine[0]] + [shift(mine[d], d) for d in range(1, n)]
        own = pl.pallas_call(
            functools.partial(gather_density_kernel, n, blocks),
            out_shape=jax.ShapeDtypeStruct((blocks, part, pairs), bf16),
            grid_spec=pltpu.PrefetchScalarGridSpec(
                num_scalar_prefetch=1,
                grid=(1,),
                in_specs=[any_spec] * n,
                out_specs=pl.BlockSpec((blocks, part, pairs), whole_map),
                scratch_shapes=[pltpu.SemaphoreType.DMA((blocks,))],
            ),
            compiler_params=params,
            name="gather_density",
        )(pick_table, *received)
        return own, swap(own)

    def fit(own, other):
        keep, send = pl.pallas_call(
            functools.partial(fit_kernel, n, some, steps),
            out_shape=[
                jax.ShapeDtypeStruct((n // 2, both, width), f32),
                jax.ShapeDtypeStruct((n // 2, both, width), bf16),
            ],
            grid_spec=pltpu.PrefetchScalarGridSpec(
                num_scalar_prefetch=1,
                grid=(steps,),
                in_specs=[
                    pl.BlockSpec((some, 1, pairs), block_map),
                    pl.BlockSpec((some, part, pairs), block_map),
                    pl.BlockSpec((some, part, pairs), block_map),
                    pl.BlockSpec((some, pairs, aux_dev), block_map),
                ],
                out_specs=[pl.BlockSpec((n // 2, both, width), whole_map)] * 2,
                scratch_shapes=[pltpu.VMEM((both, aux_dev), f32)],
            ),
            compiler_params=params,
            cost_estimate=pl.CostEstimate(
                flops=2 * blocks * pairs * aux_dev * both,
                bytes_accessed=2 * blocks * pairs * aux_dev,
                transcendentals=0,
            ),
            name="fit",
        )(chunk_table, factor, own, other, three_index)
        bit = 1
        while True:
            value = keep + flip(send, bit).astype(f32)
            bit *= 2
            if bit == n:
                break
            keep, send = value[0::2], value[1::2].astype(bf16)
        near, order = value.astype(bf16), [0]
        while True:
            bit //= 2
            far = flip(near, bit)
            order = order + [e ^ bit for e in order]
            if bit == 1:
                return near, far, order
            near = jnp.concatenate([near, far], axis=0)

    def apply(near, far, order):
        mine, theirs = pl.pallas_call(
            functools.partial(apply_kernel, n, some, order),
            out_shape=[
                jax.ShapeDtypeStruct((blocks, part, pairs), f32),
                jax.ShapeDtypeStruct((blocks, part, pairs), bf16),
            ],
            grid_spec=pltpu.PrefetchScalarGridSpec(
                num_scalar_prefetch=1,
                grid=(steps,),
                in_specs=[
                    pl.BlockSpec((some, pairs, aux_dev), block_map),
                    pl.BlockSpec((n // 2, both, width), whole_map),
                    pl.BlockSpec((n // 2, both, width), whole_map),
                ],
                out_specs=[pl.BlockSpec((some, part, pairs), block_map)] * 2,
            ),
            compiler_params=params,
            cost_estimate=pl.CostEstimate(
                flops=2 * blocks * pairs * aux_dev * both,
                bytes_accessed=2 * blocks * pairs * aux_dev,
                transcendentals=0,
            ),
            name="apply",
        )(chunk_table, three_index, near, far)
        return mine, swap(theirs)

    def deliver(mine, added):
        out = pl.pallas_call(
            functools.partial(scatter_coulomb_kernel, n, blocks, some, cap),
            out_shape=[jax.ShapeDtypeStruct((2 * cap, part, pairs), bf16)] * n,
            grid_spec=pltpu.PrefetchScalarGridSpec(
                num_scalar_prefetch=1,
                grid=(steps,),
                in_specs=[
                    pl.BlockSpec((some, 1, pairs), block_map),
                    pl.BlockSpec((some, part, pairs), block_map),
                    pl.BlockSpec((some, part, pairs), block_map),
                ],
                out_specs=[any_spec] * n,
                scratch_shapes=[
                    pltpu.VMEM((blocks, part, pairs), bf16),
                    pltpu.SemaphoreType.DMA((2, blocks)),
                ],
            ),
            compiler_params=params,
            name="scatter_coulomb",
        )(out_table, keeping, mine, added)
        return [out[0]] + [shift(out[d], d) for d in range(1, n)]

    fetched = [fetch(chain) for chain in range(CHAINS)]
    fits = [fit(*pair) for pair in fetched]
    sums = [apply(*found) for found in fits]
    received = [piece for pair in sums for piece in deliver(*pair)]
    rows, cols = pl.pallas_call(
        functools.partial(gather_coulomb_kernel, n, blocks, shell),
        out_shape=[jax.ShapeDtypeStruct((blocks, pairs, half), bf16)] * 2,
        grid_spec=pltpu.PrefetchScalarGridSpec(
            num_scalar_prefetch=1,
            grid=(blocks,),
            in_specs=[any_spec] * (CHAINS * n),
            out_specs=[pl.BlockSpec((1, pairs, half), block_map)] * 2,
            scratch_shapes=[
                pltpu.VMEM((2, blocks, half, pairs), bf16),
                pltpu.VMEM((pairs, half), f32),
                pltpu.SemaphoreType.DMA((CHAINS, 2, blocks)),
            ],
        ),
        compiler_params=params,
        name="gather_coulomb",
    )(in_table, *received)
    return rows, cols


def solution(mesh):
    in_specs = (
        P(("mol", "pair"), None, "aux"),
        P(("mol", "pair"), None, None),
        P(("mol", "pair"), None),
        P(("mol", "pair"), None),
        P("mol"),
        P("mol"),
    )
    out_specs = (P(("mol", "pair"), None, "aux"), P(("mol", "pair"), None, "aux"))
    return jax.shard_map(local, mesh=mesh, in_specs=in_specs, out_specs=out_specs, check_vma=False)
```

time: 500 us -> 220 us (0.44)
  the two profiles are of different devices: /device:TPU:0 before, /device:TPU:13 now
where the time goes in v3:
time: 220 us; the launch traced here: 219 us
  waiting for transfers between devices  88 us (40%)
  Pallas kernels  69 us (31%)
  starting transfers between devices  54.3 us (25%)
  other arithmetic  4.96 us (2%)
    ppermute x28, waiting for transfers between devices, shift(): return lax.ppermute(x, 'pair', [(s, (s + d) % n) for s in range(n)])  73.5 us
    ppermute x28, starting transfers between devices, shift(): return lax.ppermute(x, 'pair', [(s, (s + d) % n) for s in range(n)])  28 us
    pallas_call x2, Pallas kernels, apply(): pl.pallas_call(functools.partial(apply_kernel, n, some, order), out_shape...  20.3 us
    pallas_call x2, Pallas kernels, fit(): pl.pallas_call(functools.partial(fit_kernel, n, some, steps), out_shape=[...  18.2 us
    ppermute x12, waiting for transfers between devices, flip(): return lax.ppermute(x, 'pair', [(s, s ^ bit) for s in range(n)])  14.4 us
    ppermute x12, starting transfers between devices, flip(): return lax.ppermute(x, 'pair', [(s, s ^ bit) for s in range(n)])  14.4 us
    pallas_call x1, Pallas kernels, local(): pl.pallas_call(functools.partial(gather_coulomb_kernel, n, blocks, shell)...  12.8 us
    ppermute x4, starting transfers between devices, swap(): return lax.ppermute(x, 'aux', [(s, (s + 1) % cores) for s in range(cores)])  11.9 us
  transfers between devices with their start and end apart: 44, of which 19 were waited for; matrix products, arithmetic and copies ran while one was open for 1% of the time, Pallas kernels for 23%

profile of v3, /device:TPU:13, one launch (start us, length us, event | category | flops | bytes accessed | tf_op | source)
XLA Modules:
  0.0 219.1 jit_solution(10487851392082181307)
XLA Ops:
  4.9 4.8 %scatter_density.1 = (bf16[3,64,256]{2,1,0:T(8,128)(2,1)S(1)}, bf16[3,64,256]{2,1,0:T(8,128)(2,1)S(1)}, bf16[3,64,256]{2,1,0:T(8,128)(2,1)S(1)}, bf16[3,64,256]{...) custom-call(s32[29]{0:T(128)S(1)} %pad_add_fusion.3.table, ...), custom_call_target="tpu_custom_call" | custom-call | tf_op jit(solution)/shard_map/scatter_density/pallas_call | solution.py:235
  18.4 6.9 %collective-permute-done.2.rest_3_ = bf16[3,64,256]{2,1,0:T(8,128)(2,1)S(1)} collective-permute-done((bf16[3,64,256]{2,1,0:T(8,128)(2,1)S(1)}, bf16[3,64,256]{2,1,0:T(8,128)(2,1)S(1)}, u32[]{:S(2)}, u32[]{:S(2)}) %collective-permute-start.2) | collective-permute-done | bytes 98336 | tf_op jit(solution)/shard_map/ppermute | solution.py:212
  29.8 5.7 %collective-permute-done.5.rest_6_ = bf16[3,64,256]{2,1,0:T(8,128)(2,1)S(1)} collective-permute-done((bf16[3,64,256]{2,1,0:T(8,128)(2,1)S(1)}, bf16[3,64,256]{2,1,0:T(8,128)(2,1)S(1)}, u32[]{:S(2)}, u32[]{:S(2)}) %collective-permute-start.5) | collective-permute-done | bytes 98336 | tf_op jit(solution)/shard_map/ppermute | solution.py:212
  37.8 3.6 %collective-permute-start.28 = (bf16[3,64,256]{2,1,0:T(8,128)(2,1)S(1)}, bf16[3,64,256]{2,1,0:T(8,128)(2,1)S(1)}, u32[]{:S(2)}, u32[]{:S(2)}) collective-permute-start(bf16[3,64,256]{2,1,0:T(8,128)(2,1)S(1)} %get-tuple-element.69), channel_id=1, source_target_pairs={{0,14},{2,0},{4,2},{6,4},{8,6},{10,8},{12,10},{14,12},{1,15},{3,1}... | collective-permute-start | bytes 294920 | tf_op jit(solution)/shard_map/ppermute | solution.py:212
  41.4 2.5 %collective-permute-start.7 = (bf16[14,64,256]{2,1,0:T(8,128)(2,1)S(1)}, bf16[14,64,256]{2,1,0:T(8,128)(2,1)S(1)}, u32[]{:S(2)}, u32[]{:S(2)}) collective-permute-start(bf16[14,64,256]{2,1,0:T(8,128)(2,1)S(1)} %gather_density.2.own), channel_id=1, source_target_pairs={{0,1},{1,0},{2,3},{3,2},{4,5},{5,4},{6,7},{7,6},{8,9},{9,8},{10,11... | collective-permute-start | bytes 1376264 | tf_op jit(solution)/shard_map/ppermute | solution.py:218
  44.7 2.5 %collective-permute-done.27.rest_6_ = bf16[3,64,256]{2,1,0:T(8,128)(2,1)S(1)} collective-permute-done((bf16[3,64,256]{2,1,0:T(8,128)(2,1)S(1)}, bf16[3,64,256]{2,1,0:T(8,128)(2,1)S(1)}, u32[]{:S(2)}, u32[]{:S(2)}) %collective-permute-start.27) | collective-permute-done | bytes 98336 | tf_op jit(solution)/shard_map/ppermute | solution.py:212
  52.6 9.1 %fit.2 = (f32[4,128,256]{2,1,0:T(8,128)S(1)}, bf16[4,128,256]{2,1,0:T(8,128)(2,1)S(1)}) custom-call(s32[8]{0:T(128)S(1)} %iota_xor_fusion.table, bf16[14,1,256]{2,1,0:T(2,128)(2,1)S(1)} %copy.10.factor, bf16[14,64,256]{2,1,0:T(8,128)(2,1)S(1)} %gather_density.2.own, bf16[14,64,256]{2,1,0:T(8,128)(2,1)S(1)} %collective-permute-done.7.other, ...), custom_call_target="tpu_custom_call" | custom-call | flops 1879048192 | bytes 14680064 | tf_op jit(solution)/shard_map/fit/pallas_call | solution.py:271
  61.8 9.1 %fit.3 = (f32[4,128,256]{2,1,0:T(8,128)S(1)}, bf16[4,128,256]{2,1,0:T(8,128)(2,1)S(1)}) custom-call(s32[8]{0:T(128)S(1)} %iota_xor_fusion.table, bf16[14,1,256]{2,1,0:T(2,128)(2,1)S(1)} %copy.10.factor, bf16[14,64,256]{2,1,0:T(8,128)(2,1)S(1)} %gather_density.3.own, bf16[14,64,256]{2,1,0:T(8,128)(2,1)S(1)} %collective-permute-done.29.other, ...), custom_call_target="tpu_custom_call" | custom-call | flops 1879048192 | bytes 14680064 | tf_op jit(solution)/shard_map/fit/pallas_call | solution.py:271
  73.0 5.9 %collective-permute-done.30 = bf16[4,128,256]{2,1,0:T(8,128)(2,1)S(1)} collective-permute-done((bf16[4,128,256]{2,1,0:T(8,128)(2,1)S(1)}, bf16[4,128,256]{2,1,0:T(8,128)(2,1)S(1)}, u32[]{:S(2)}, u32[]{:S(2)}) %collective-permute-start.30) | collective-permute-done | bytes 262176 | tf_op jit(solution)/shard_map/ppermute | solution.py:215
  80.4 2.8 %collective-permute-done.31 = bf16[2,128,256]{2,1,0:T(8,128)(2,1)S(1)} collective-permute-done((bf16[2,128,256]{2,1,0:T(8,128)(2,1)S(1)}, bf16[2,128,256]{2,1,0:T(8,128)(2,1)S(1)}, u32[]{:S(2)}, u32[]{:S(2)}) %collective-permute-start.31) | collective-permute-done | bytes 131104 | tf_op jit(solution)/shard_map/ppermute | solution.py:215
  91.8 2.9 %collective-permute-start.34 = (bf16[2,128,256]{2,1,0:T(8,128)(2,1)S(1)}, bf16[2,128,256]{2,1,0:T(8,128)(2,1)S(1)}, u32[]{:S(2)}, u32[]{:S(2)}) collective-permute-start(bf16[2,128,256]{2,1,0:T(8,128)(2,1)S(1)} %pad_maximum_fusion.3), channel_id=1, source_target_pairs={{0,4},{2,6},{4,0},{6,2},{8,12},{10,14},{12,8},{14,10},{1,5},{3,7},... | collective-permute-start | bytes 393224 | tf_op jit(solution)/shard_map/ppermute | solution.py:215
  100.0 10.2 %apply.2 = (f32[14,64,256]{2,1,0:T(8,128)S(1)}, bf16[14,64,256]{2,1,0:T(8,128)(2,1)S(1)}) custom-call(s32[8]{0:T(128)S(1)} %iota_xor_fusion.table, bf16[14,256,2048]{2,1,0:T(8,128)(2,1)} %integrals.7, bf16[4,128,256]{2,1,0:T(8,128)(2,1)S(1)} %pad_maximum_fusion.near, bf16[4,128,256]{2,1,0:T(8,128)(2,1)S(1)} %collective-permute-done.13.far), custom_call_target="tpu_custom_call" | custom-call | flops 1879048192 | bytes 14680064 | tf_op jit(solution)/shard_map/apply/pallas_call | solution.py:314
  110.2 7.0 %collective-permute-start.14 = (bf16[14,64,256]{2,1,0:T(8,128)(2,1)S(1)}, bf16[14,64,256]{2,1,0:T(8,128)(2,1)S(1)}, u32[]{:S(2)}, u32[]{:S(2)}) collective-permute-start(bf16[14,64,256]{2,1,0:T(8,128)(2,1)S(1)} %get-tuple-element.53), channel_id=1, source_target_pairs={{0,1},{1,0},{2,3},{3,2},{4,5},{5,4},{6,7},{7,6},{8,9},{9,8},{10,11... | collective-permute-start | bytes 1376264 | tf_op jit(solution)/shard_map/ppermute | solution.py:218
  117.3 10.2 %apply.3 = (f32[14,64,256]{2,1,0:T(8,128)S(1)}, bf16[14,64,256]{2,1,0:T(8,128)(2,1)S(1)}) custom-call(s32[8]{0:T(128)S(1)} %iota_xor_fusion.table, bf16[14,256,2048]{2,1,0:T(8,128)(2,1)} %integrals.7, bf16[4,128,256]{2,1,0:T(8,128)(2,1)S(1)} %pad_maximum_fusion.1.near, bf16[4,128,256]{2,1,0:T(8,128)(2,1)S(1)} %collective-permute-done.35.far), custom_call_target="tpu_custom_call" | custom-call | flops 1879048192 | bytes 14680064 | tf_op jit(solution)/shard_map/apply/pallas_call | solution.py:314
  127.8 4.2 %scatter_coulomb.2 = (bf16[6,64,256]{2,1,0:T(8,128)(2,1)S(1)}, bf16[6,64,256]{2,1,0:T(8,128)(2,1)S(1)}, bf16[6,64,256]{2,1,0:T(8,128)(2,1)S(1)}, bf16[6,64,256]{...) custom-call(s32[56]{0:T(128)S(1)} %pad_add_fusion.1.table, ...), custom_call_target="tpu_custom_call" | custom-call | tf_op jit(solution)/shard_map/scatter_coulomb/pallas_call | solution.py:341
  139.7 4.2 %scatter_coulomb.3 = (bf16[6,64,256]{2,1,0:T(8,128)(2,1)S(1)}, bf16[6,64,256]{2,1,0:T(8,128)(2,1)S(1)}, bf16[6,64,256]{2,1,0:T(8,128)(2,1)S(1)}, bf16[6,64,256]{...) custom-call(s32[56]{0:T(128)S(1)} %pad_add_fusion.1.table, ...), custom_call_target="tpu_custom_call" | custom-call | tf_op jit(solution)/shard_map/scatter_coulomb/pallas_call | solution.py:341
  146.4 15.7 %collective-permute-done.17.rest_3_ = bf16[6,64,256]{2,1,0:T(8,128)(2,1)S(1)} collective-permute-done((bf16[6,64,256]{2,1,0:T(8,128)(2,1)S(1)}, bf16[6,64,256]{2,1,0:T(8,128)(2,1)S(1)}, u32[]{:S(2)}, u32[]{:S(2)}) %collective-permute-start.17) | collective-permute-done | bytes 196640 | tf_op jit(solution)/shard_map/ppermute | solution.py:212
  162.1 4.2 %collective-permute-done.18.rest_4_ = bf16[6,64,256]{2,1,0:T(8,128)(2,1)S(1)} collective-permute-done((bf16[6,64,256]{2,1,0:T(8,128)(2,1)S(1)}, bf16[6,64,256]{2,1,0:T(8,128)(2,1)S(1)}, u32[]{:S(2)}, u32[]{:S(2)}) %collective-permute-start.18) | collective-permute-done | bytes 196640 | tf_op jit(solution)/shard_map/ppermute | solution.py:212
  166.4 14.3 %collective-permute-done.20.rest_6_ = bf16[6,64,256]{2,1,0:T(8,128)(2,1)S(1)} collective-permute-done((bf16[6,64,256]{2,1,0:T(8,128)(2,1)S(1)}, bf16[6,64,256]{2,1,0:T(8,128)(2,1)S(1)}, u32[]{:S(2)}, u32[]{:S(2)}) %collective-permute-start.20) | collective-permute-done | bytes 196640 | tf_op jit(solution)/shard_map/ppermute | solution.py:212
  181.2 3.1 %collective-permute-start.43 = (bf16[6,64,256]{2,1,0:T(8,128)(2,1)S(1)}, bf16[6,64,256]{2,1,0:T(8,128)(2,1)S(1)}, u32[]{:S(2)}, u32[]{:S(2)}) collective-permute-start(bf16[6,64,256]{2,1,0:T(8,128)(2,1)S(1)} %get-tuple-element.81), channel_id=1, source_target_pairs={{0,14},{2,0},{4,2},{6,4},{8,6},{10,8},{12,10},{14,12},{1,15},{3,1}... | collective-permute-start | bytes 589832 | tf_op jit(solution)/shard_map/ppermute | solution.py:212
  184.4 11.4 %collective-permute-done.39.rest_11_ = bf16[6,64,256]{2,1,0:T(8,128)(2,1)S(1)} collective-permute-done((bf16[6,64,256]{2,1,0:T(8,128)(2,1)S(1)}, bf16[6,64,256]{2,1,0:T(8,128)(2,1)S(1)}, u32[]{:S(2)}, u32[]{:S(2)}) %collective-permute-start.39) | collective-permute-done | bytes 196640 | tf_op jit(solution)/shard_map/ppermute | solution.py:212
  195.8 4.2 %collective-permute-done.40.rest_12_ = bf16[6,64,256]{2,1,0:T(8,128)(2,1)S(1)} collective-permute-done((bf16[6,64,256]{2,1,0:T(8,128)(2,1)S(1)}, bf16[6,64,256]{2,1,0:T(8,128)(2,1)S(1)}, u32[]{:S(2)}, u32[]{:S(2)}) %collective-permute-start.40) | collective-permute-done | bytes 196640 | tf_op jit(solution)/shard_map/ppermute | solution.py:212
  200.0 6.0 %collective-permute-done.42.rest_14_ = bf16[6,64,256]{2,1,0:T(8,128)(2,1)S(1)} collective-permute-done((bf16[6,64,256]{2,1,0:T(8,128)(2,1)S(1)}, bf16[6,64,256]{2,1,0:T(8,128)(2,1)S(1)}, u32[]{:S(2)}, u32[]{:S(2)}) %collective-permute-start.42) | collective-permute-done | bytes 196640 | tf_op jit(solution)/shard_map/ppermute | solution.py:212
  206.1 12.8 %gather_coulomb.1 = (bf16[14,256,128]{2,1,0:T(8,128)(2,1)}, bf16[14,256,128]{2,1,0:T(8,128)(2,1)}) custom-call(s32[56]{0:T(128)S(1)} %pad_add_fusion.table, bf16[6,64,256]{2,1,0:T(8,128)(2,1)S(1)} %get-tuple-element.54.rest_0_, bf16[6,64,256]{2,1,0:T(8,128)(2,1)S(1)} %collective-permute-done.15.rest_1_, ...), custom_call_target="tpu_custom_call" | custom-call | tf_op jit(solution)/shard_map/gather_coulomb/pallas_call | solution.py:367
  (114 shorter events, 54.8 us)
Async XLA Ops:
  12.3 12.9 %collective-permute-start.2 = (bf16[3,64,256]{2,1,0:T(8,128)(2,1)S(1)}, bf16[3,64,256]{2,1,0:T(8,128)(2,1)S(1)}, u32[]{:S(2)}, u32[]{:S(2)}) collective-permute-start(bf16[3,64,256]{2,1,0:T(8,128)(2,1)S(1)} %get-tuple-element.45), channel_id=1, source_target_pairs={{0,6},{2,8},{4,10},{6,12},{8,14},{10,0},{12,2},{14,4},{1,7},{3,9},... | collective-permute-start | bytes 294920 | tf_op jit(solution)/shard_map/ppermute | solution.py:212
  13.3 14.3 %collective-permute-start.3 = (bf16[3,64,256]{2,1,0:T(8,128)(2,1)S(1)}, bf16[3,64,256]{2,1,0:T(8,128)(2,1)S(1)}, u32[]{:S(2)}, u32[]{:S(2)}) collective-permute-start(bf16[3,64,256]{2,1,0:T(8,128)(2,1)S(1)} %get-tuple-element.46), channel_id=1, source_target_pairs={{0,8},{2,10},{4,12},{6,14},{8,0},{10,2},{12,4},{14,6},{1,9},{3,11}... | collective-permute-start | bytes 294920 | tf_op jit(solution)/shard_map/ppermute | solution.py:212
  14.6 15.1 %collective-permute-start.4 = (bf16[3,64,256]{2,1,0:T(8,128)(2,1)S(1)}, bf16[3,64,256]{2,1,0:T(8,128)(2,1)S(1)}, u32[]{:S(2)}, u32[]{:S(2)}) collective-permute-start(bf16[3,64,256]{2,1,0:T(8,128)(2,1)S(1)} %get-tuple-element.47), channel_id=1, source_target_pairs={{0,10},{2,12},{4,14},{6,0},{8,2},{10,4},{12,6},{14,8},{1,11},{3,13... | collective-permute-start | bytes 294920 | tf_op jit(solution)/shard_map/ppermute | solution.py:212
  15.7 19.8 %collective-permute-start.5 = (bf16[3,64,256]{2,1,0:T(8,128)(2,1)S(1)}, bf16[3,64,256]{2,1,0:T(8,128)(2,1)S(1)}, u32[]{:S(2)}, u32[]{:S(2)}) collective-permute-start(bf16[3,64,256]{2,1,0:T(8,128)(2,1)S(1)} %get-tuple-element.48), channel_id=1, source_target_pairs={{0,12},{2,14},{4,0},{6,2},{8,4},{10,6},{12,8},{14,10},{1,13},{3,15... | collective-permute-start | bytes 294920 | tf_op jit(solution)/shard_map/ppermute | solution.py:212
  17.0 18.5 %collective-permute-start.6 = (bf16[3,64,256]{2,1,0:T(8,128)(2,1)S(1)}, bf16[3,64,256]{2,1,0:T(8,128)(2,1)S(1)}, u32[]{:S(2)}, u32[]{:S(2)}) collective-permute-start(bf16[3,64,256]{2,1,0:T(8,128)(2,1)S(1)} %get-tuple-element.49), channel_id=1, source_target_pairs={{0,14},{2,0},{4,2},{6,4},{8,6},{10,8},{12,10},{14,12},{1,15},{3,1}... | collective-permute-start | bytes 294920 | tf_op jit(solution)/shard_map/ppermute | solution.py:212
  25.2 12.5 %collective-permute-start.22 = (bf16[3,64,256]{2,1,0:T(8,128)(2,1)S(1)}, bf16[3,64,256]{2,1,0:T(8,128)(2,1)S(1)}, u32[]{:S(2)}, u32[]{:S(2)}) collective-permute-start(bf16[3,64,256]{2,1,0:T(8,128)(2,1)S(1)} %get-tuple-element.63), channel_id=1, source_target_pairs={{0,2},{2,4},{4,6},{6,8},{8,10},{10,12},{12,14},{14,0},{1,3},{3,5},... | collective-permute-start | bytes 294920 | tf_op jit(solution)/shard_map/ppermute | solution.py:212
  29.8 11.7 %collective-permute-start.24 = (bf16[3,64,256]{2,1,0:T(8,128)(2,1)S(1)}, bf16[3,64,256]{2,1,0:T(8,128)(2,1)S(1)}, u32[]{:S(2)}, u32[]{:S(2)}) collective-permute-start(bf16[3,64,256]{2,1,0:T(8,128)(2,1)S(1)} %get-tuple-element.65), channel_id=1, source_target_pairs={{0,6},{2,8},{4,10},{6,12},{8,14},{10,0},{12,2},{14,4},{1,7},{3,9},... | collective-permute-start | bytes 294920 | tf_op jit(solution)/shard_map/ppermute | solution.py:212
  49.4 12.3 %collective-permute-start.29 = (bf16[14,64,256]{2,1,0:T(8,128)(2,1)S(1)}, bf16[14,64,256]{2,1,0:T(8,128)(2,1)S(1)}, u32[]{:S(2)}, u32[]{:S(2)}) collective-permute-start(bf16[14,64,256]{2,1,0:T(8,128)(2,1)S(1)} %gather_density.3.own), channel_id=1, source_target_pairs={{0,1},{1,0},{2,3},{3,2},{4,5},{5,4},{6,7},{7,6},{8,9},{9,8},{10,11... | collective-permute-start | bytes 1376264 | tf_op jit(solution)/shard_map/ppermute | solution.py:218
  97.8 19.4 %collective-permute-start.35 = (bf16[4,128,256]{2,1,0:T(8,128)(2,1)S(1)}, bf16[4,128,256]{2,1,0:T(8,128)(2,1)S(1)}, u32[]{:S(2)}, u32[]{:S(2)}) collective-permute-start(bf16[4,128,256]{2,1,0:T(8,128)(2,1)S(1)} %pad_maximum_fusion.1.near), channel_id=1, source_target_pairs={{0,2},{2,0},{4,6},{6,4},{8,10},{10,8},{12,14},{14,12},{1,3},{3,1},... | collective-permute-start | bytes 786440 | tf_op jit(solution)/shard_map/ppermute | solution.py:215
  110.2 17.6 %collective-permute-start.14 = (bf16[14,64,256]{2,1,0:T(8,128)(2,1)S(1)}, bf16[14,64,256]{2,1,0:T(8,128)(2,1)S(1)}, u32[]{:S(2)}, u32[]{:S(2)}) collective-permute-start(bf16[14,64,256]{2,1,0:T(8,128)(2,1)S(1)} %get-tuple-element.53), channel_id=1, source_target_pairs={{0,1},{1,0},{2,3},{3,2},{4,5},{5,4},{6,7},{7,6},{8,9},{9,8},{10,11... | collective-permute-start | bytes 1376264 | tf_op jit(solution)/shard_map/ppermute | solution.py:218
  132.0 12.0 %collective-permute-start.15 = (bf16[6,64,256]{2,1,0:T(8,128)(2,1)S(1)}, bf16[6,64,256]{2,1,0:T(8,128)(2,1)S(1)}, u32[]{:S(2)}, u32[]{:S(2)}) collective-permute-start(bf16[6,64,256]{2,1,0:T(8,128)(2,1)S(1)} %get-tuple-element.55), channel_id=1, source_target_pairs={{0,2},{2,4},{4,6},{6,8},{8,10},{10,12},{12,14},{14,0},{1,3},{3,5},... | collective-permute-start | bytes 589832 | tf_op jit(solution)/shard_map/ppermute | solution.py:212
  133.0 13.4 %collective-permute-start.16 = (bf16[6,64,256]{2,1,0:T(8,128)(2,1)S(1)}, bf16[6,64,256]{2,1,0:T(8,128)(2,1)S(1)}, u32[]{:S(2)}, u32[]{:S(2)}) collective-permute-start(bf16[6,64,256]{2,1,0:T(8,128)(2,1)S(1)} %get-tuple-element.56), channel_id=1, source_target_pairs={{0,4},{2,6},{4,8},{6,10},{8,12},{10,14},{12,0},{14,2},{1,5},{3,7},... | collective-permute-start | bytes 589832 | tf_op jit(solution)/shard_map/ppermute | solution.py:212
  135.3 26.8 %collective-permute-start.17 = (bf16[6,64,256]{2,1,0:T(8,128)(2,1)S(1)}, bf16[6,64,256]{2,1,0:T(8,128)(2,1)S(1)}, u32[]{:S(2)}, u32[]{:S(2)}) collective-permute-start(bf16[6,64,256]{2,1,0:T(8,128)(2,1)S(1)} %get-tuple-element.57), channel_id=1, source_target_pairs={{0,6},{2,8},{4,10},{6,12},{8,14},{10,0},{12,2},{14,4},{1,7},{3,9},... | collective-permute-start | bytes 589832 | tf_op jit(solution)/shard_map/ppermute | solution.py:212
  137.4 28.9 %collective-permute-start.18 = (bf16[6,64,256]{2,1,0:T(8,128)(2,1)S(1)}, bf16[6,64,256]{2,1,0:T(8,128)(2,1)S(1)}, u32[]{:S(2)}, u32[]{:S(2)}) collective-permute-start(bf16[6,64,256]{2,1,0:T(8,128)(2,1)S(1)} %get-tuple-element.58), channel_id=1, source_target_pairs={{0,8},{2,10},{4,12},{6,14},{8,0},{10,2},{12,4},{14,6},{1,9},{3,11}... | collective-permute-start | bytes 589832 | tf_op jit(solution)/shard_map/ppermute | solution.py:212
  137.4 28.9 %collective-permute-start.19 = (bf16[6,64,256]{2,1,0:T(8,128)(2,1)S(1)}, bf16[6,64,256]{2,1,0:T(8,128)(2,1)S(1)}, u32[]{:S(2)}, u32[]{:S(2)}) collective-permute-start(bf16[6,64,256]{2,1,0:T(8,128)(2,1)S(1)} %get-tuple-element.59), channel_id=1, source_target_pairs={{0,10},{2,12},{4,14},{6,0},{8,2},{10,4},{12,6},{14,8},{1,11},{3,13... | collective-permute-start | bytes 589832 | tf_op jit(solution)/shard_map/ppermute | solution.py:212
  144.0 36.7 %collective-permute-start.20 = (bf16[6,64,256]{2,1,0:T(8,128)(2,1)S(1)}, bf16[6,64,256]{2,1,0:T(8,128)(2,1)S(1)}, u32[]{:S(2)}, u32[]{:S(2)}) collective-permute-start(bf16[6,64,256]{2,1,0:T(8,128)(2,1)S(1)} %get-tuple-element.60), channel_id=1, source_target_pairs={{0,12},{2,14},{4,0},{6,2},{8,4},{10,6},{12,8},{14,10},{1,13},{3,15... | collective-permute-start | bytes 589832 | tf_op jit(solution)/shard_map/ppermute | solution.py:212
  146.4 34.4 %collective-permute-start.21 = (bf16[6,64,256]{2,1,0:T(8,128)(2,1)S(1)}, bf16[6,64,256]{2,1,0:T(8,128)(2,1)S(1)}, u32[]{:S(2)}, u32[]{:S(2)}) collective-permute-start(bf16[6,64,256]{2,1,0:T(8,128)(2,1)S(1)} %get-tuple-element.61), channel_id=1, source_target_pairs={{0,14},{2,0},{4,2},{6,4},{8,6},{10,8},{12,10},{14,12},{1,15},{3,1}... | collective-permute-start | bytes 589832 | tf_op jit(solution)/shard_map/ppermute | solution.py:212
  162.1 18.8 %collective-permute-start.37 = (bf16[6,64,256]{2,1,0:T(8,128)(2,1)S(1)}, bf16[6,64,256]{2,1,0:T(8,128)(2,1)S(1)}, u32[]{:S(2)}, u32[]{:S(2)}) collective-permute-start(bf16[6,64,256]{2,1,0:T(8,128)(2,1)S(1)} %get-tuple-element.75), channel_id=1, source_target_pairs={{0,2},{2,4},{4,6},{6,8},{8,10},{10,12},{12,14},{14,0},{1,3},{3,5},... | collective-permute-start | bytes 589832 | tf_op jit(solution)/shard_map/ppermute | solution.py:212
  166.3 14.9 %collective-permute-start.38 = (bf16[6,64,256]{2,1,0:T(8,128)(2,1)S(1)}, bf16[6,64,256]{2,1,0:T(8,128)(2,1)S(1)}, u32[]{:S(2)}, u32[]{:S(2)}) collective-permute-start(bf16[6,64,256]{2,1,0:T(8,128)(2,1)S(1)} %get-tuple-element.76), channel_id=1, source_target_pairs={{0,4},{2,6},{4,8},{6,10},{8,12},{10,14},{12,0},{14,2},{1,5},{3,7},... | collective-permute-start | bytes 589832 | tf_op jit(solution)/shard_map/ppermute | solution.py:212
  166.4 29.4 %collective-permute-start.39 = (bf16[6,64,256]{2,1,0:T(8,128)(2,1)S(1)}, bf16[6,64,256]{2,1,0:T(8,128)(2,1)S(1)}, u32[]{:S(2)}, u32[]{:S(2)}) collective-permute-start(bf16[6,64,256]{2,1,0:T(8,128)(2,1)S(1)} %get-tuple-element.77), channel_id=1, source_target_pairs={{0,6},{2,8},{4,10},{6,12},{8,14},{10,0},{12,2},{14,4},{1,7},{3,9},... | collective-permute-start | bytes 589832 | tf_op jit(solution)/shard_map/ppermute | solution.py:212
  180.7 19.3 %collective-permute-start.40 = (bf16[6,64,256]{2,1,0:T(8,128)(2,1)S(1)}, bf16[6,64,256]{2,1,0:T(8,128)(2,1)S(1)}, u32[]{:S(2)}, u32[]{:S(2)}) collective-permute-start(bf16[6,64,256]{2,1,0:T(8,128)(2,1)S(1)} %get-tuple-element.78), channel_id=1, source_target_pairs={{0,8},{2,10},{4,12},{6,14},{8,0},{10,2},{12,4},{14,6},{1,9},{3,11}... | collective-permute-start | bytes 589832 | tf_op jit(solution)/shard_map/ppermute | solution.py:212
  180.8 19.2 %collective-permute-start.41 = (bf16[6,64,256]{2,1,0:T(8,128)(2,1)S(1)}, bf16[6,64,256]{2,1,0:T(8,128)(2,1)S(1)}, u32[]{:S(2)}, u32[]{:S(2)}) collective-permute-start(bf16[6,64,256]{2,1,0:T(8,128)(2,1)S(1)} %get-tuple-element.79), channel_id=1, source_target_pairs={{0,10},{2,12},{4,14},{6,0},{8,2},{10,4},{12,6},{14,8},{1,11},{3,13... | collective-permute-start | bytes 589832 | tf_op jit(solution)/shard_map/ppermute | solution.py:212
  180.8 25.2 %collective-permute-start.42 = (bf16[6,64,256]{2,1,0:T(8,128)(2,1)S(1)}, bf16[6,64,256]{2,1,0:T(8,128)(2,1)S(1)}, u32[]{:S(2)}, u32[]{:S(2)}) collective-permute-start(bf16[6,64,256]{2,1,0:T(8,128)(2,1)S(1)} %get-tuple-element.80), channel_id=1, source_target_pairs={{0,12},{2,14},{4,0},{6,2},{8,4},{10,6},{12,8},{14,10},{1,13},{3,15... | collective-permute-start | bytes 589832 | tf_op jit(solution)/shard_map/ppermute | solution.py:212
  181.2 25.0 %collective-permute-start.43 = (bf16[6,64,256]{2,1,0:T(8,128)(2,1)S(1)}, bf16[6,64,256]{2,1,0:T(8,128)(2,1)S(1)}, u32[]{:S(2)}, u32[]{:S(2)}) collective-permute-start(bf16[6,64,256]{2,1,0:T(8,128)(2,1)S(1)} %get-tuple-element.81), channel_id=1, source_target_pairs={{0,14},{2,0},{4,2},{6,4},{8,6},{10,8},{12,10},{14,12},{1,15},{3,1}... | collective-permute-start | bytes 589832 | tf_op jit(solution)/shard_map/ppermute | solution.py:212
  (22 other events, 176.7 us)

commit v4 on v0

v4 whole, which is shorter than its diff:
```python
import functools
import math

import jax
import jax.numpy as jnp
from jax import lax
from jax.experimental import pallas as pl
from jax.experimental.pallas import tpu as pltpu
from jax.sharding import PartitionSpec as P

VMEM_BYTES = 24 * 1024 * 1024
CHAINS = 2


def tables(slots, devices, blocks_dev, me):
    total = slots.shape[0]
    numbers = jnp.arange(total, dtype=jnp.int32)
    source = numbers // blocks_dev
    target = slots // blocks_dev
    joined = source * devices + target
    earlier = (joined[:, None] == joined[None, :]) & (numbers[None, :] < numbers[:, None])
    rank = jnp.sum(earlier.astype(jnp.int32), axis=1)
    own_target = lax.dynamic_slice_in_dim(target, me * blocks_dev, blocks_dev, 0)
    own_rank = lax.dynamic_slice_in_dim(rank, me * blocks_dev, blocks_dev, 0)
    rows = me * blocks_dev + jnp.arange(blocks_dev, dtype=jnp.int32)
    hot = slots[None, :] == rows[:, None]
    row_source = jnp.sum(jnp.where(hot, source[None, :], 0), axis=1)
    row_rank = jnp.sum(jnp.where(hot, rank[None, :], 0), axis=1)
    return own_target, own_rank, row_source, row_rank


def slots_of(steps, ranks, devices, cap):
    held = (steps * cap + ranks)[None, :] == jnp.arange(devices * cap, dtype=jnp.int32)[:, None]
    numbers = jnp.arange(steps.shape[0], dtype=jnp.int32)
    return jnp.max(jnp.where(held, numbers[None, :], -1), axis=1)


def load_kernel(source, target, sem):
    copy = pltpu.make_async_copy(source, target, sem)
    copy.start()
    copy.wait()


def scatter_density_kernel(devices, blocks, cap, table, density, *rest):
    sends, turned = rest[: CHAINS * devices], rest[-1]
    part = sends[0].shape[1]
    for row in range(blocks):
        turned[row] = density[row].T
    for step in range(devices):
        for rank in range(cap):
            row = jnp.maximum(table[step * cap + rank], 0)
            for chain in range(CHAINS):
                sends[chain * devices + step][rank] = turned[row, pl.ds(chain * part, part)]


def gather_density_kernel(devices, cap, table, *rest):
    received, out = rest[:devices], rest[-1]
    for step in range(devices):
        for rank in range(cap):
            row = table[step * cap + rank]

            @pl.when(row >= 0)
            def _():
                out[row] = received[step][rank]


def fit_kernel(devices, blocks, table, factor, own, other, integrals, keep, send):
    width = keep.shape[2]
    pairs = integrals.shape[1]
    fitted = jnp.concatenate(
        [jnp.concatenate([own[b], other[b]], axis=0) * factor[b] for b in range(blocks)], axis=1
    )
    for e in range(devices):
        at = pl.ds(pl.multiple_of(table[e] * width, width), width)
        value = jnp.dot(
            fitted,
            integrals[:, :, at].reshape(blocks * pairs, width),
            preferred_element_type=jnp.float32,
        )
        if e % 2:
            send[e // 2] = value.astype(send.dtype)
        else:
            keep[e // 2] = value


def apply_kernel(devices, blocks, order, table, integrals, near, far, *rest):
    own, other = rest[-2:]
    width = near.shape[2]
    part = own.shape[1]
    pairs = integrals.shape[1]
    total = None
    for i, e in enumerate(order):
        chunk = near[i] if i < devices // 2 else far[i - devices // 2]
        at = pl.ds(pl.multiple_of(table[e] * width, width), width)
        term = lax.dot_general(
            integrals[:, :, at].reshape(blocks * pairs, width),
            chunk,
            (((1,), (1,)), ((), ())),
            preferred_element_type=jnp.float32,
        )
        total = term if total is None else total + term
    for b in range(blocks):
        value = total[b * pairs : (b + 1) * pairs].T
        own[b] = value[:part]
        other[b] = value[part:].astype(other.dtype)


def scatter_coulomb_kernel(devices, blocks, cap, table, screen, own, other, *rest):
    sends, ready = rest[:devices], rest[devices]
    for b in range(blocks):
        value = (own[b] + other[b].astype(jnp.float32)) * screen[b]
        ready[b] = value.astype(jnp.bfloat16)
    for group in range(2):
        for step in range(devices):
            for rank in range(cap):
                b = jnp.maximum(table[(group * devices + step) * cap + rank], 0)
                sends[step][group * cap + rank] = ready[b]


def gather_coulomb_kernel(devices, blocks, shell, cap, table, *rest):
    received = rest[: CHAINS * devices]
    rows, cols, landed, done, sems = rest[CHAINS * devices :]
    part = received[0].shape[1]
    pairs = landed.shape[3]
    for group in range(2):
        for step in range(devices):
            for rank in range(cap):
                row = table[(group * devices + step) * cap + rank]

                @pl.when(row >= 0)
                def _():
                    for chain in range(CHAINS):
                        landed[group, row, pl.ds(chain * part, part)] = received[
                            chain * devices + step
                        ][group * cap + rank]

    to = lax.broadcasted_iota(jnp.int32, (pairs, pairs), 0)
    source = lax.broadcasted_iota(jnp.int32, (pairs, pairs), 1)
    turns = (to, (to % shell) * shell + to // shell)
    copies = []
    for group in range(2):
        turn = (source == turns[group]).astype(jnp.bfloat16)
        for row in range(blocks):
            done[group, row] = lax.dot_general(
                turn,
                landed[group, row],
                (((1,), (1,)), ((), ())),
                preferred_element_type=jnp.float32,
            ).astype(jnp.bfloat16)
            copy = pltpu.make_async_copy(
                done.at[group, row], (rows, cols)[group].at[row], sems.at[group, row]
            )
            copy.start()
            copies.append(copy)
    for copy in copies:
        copy.wait()


def local(three_index, density, screen, pair_shells, home_slot, mirror_slot):
    blocks, pairs, aux_dev = three_index.shape
    ndens = density.shape[2]
    shell = math.isqrt(pairs)
    n = lax.axis_size("pair")
    cores = lax.axis_size("aux")
    me = lax.axis_index("pair")
    core = lax.axis_index("aux")
    half = ndens // cores
    part = half // CHAINS
    both = cores * part
    width = aux_dev // n
    cap = 2 + (blocks - 1) // n
    bf16, f32 = jnp.bfloat16, jnp.float32
    in_vmem = pl.BlockSpec(memory_space=pltpu.VMEM)
    anywhere = pl.BlockSpec(memory_space=pl.ANY)
    ints = functools.partial(jnp.concatenate, axis=0)

    def call(kernel, name, table, args, out_shape, out_specs, after=(), scratch=(), flops=0):
        return pl.pallas_call(
            kernel,
            out_shape=out_shape,
            grid_spec=pltpu.PrefetchScalarGridSpec(
                num_scalar_prefetch=1,
                grid=(),
                in_specs=[in_vmem] * len(args) + [anywhere] * len(after),
                out_specs=out_specs,
                scratch_shapes=list(scratch),
            ),
            compiler_params=pltpu.CompilerParams(vmem_limit_bytes=VMEM_BYTES),
            cost_estimate=pl.CostEstimate(flops=flops, bytes_accessed=0, transcendentals=0),
            name=name,
        )(table, *args, *after)

    def shift(x, d):
        return lax.ppermute(x, "pair", [(s, (s + d) % n) for s in range(n)])

    def flip(x, bit):
        return lax.ppermute(x, "pair", [(s, s ^ bit) for s in range(n)])

    def swap(x):
        return lax.ppermute(x, "aux", [(s, (s + 1) % cores) for s in range(cores)])

    home_target, home_rank, home_source, home_row_rank = tables(home_slot, n, blocks, me)
    mirror_target, mirror_rank, mirror_source, mirror_row_rank = tables(
        mirror_slot, n, blocks, me
    )
    send_table = ints(
        [slots_of((home_source - me) % n, home_row_rank, n, cap), core[None].astype(jnp.int32)]
    )
    pick_table = slots_of((me - home_target) % n, home_rank, n, cap)
    chunk_table = me ^ jnp.arange(n, dtype=jnp.int32)
    out_table = ints(
        [
            slots_of((home_target - me) % n, home_rank, n, cap),
            slots_of((mirror_target - me) % n, mirror_rank, n, cap),
        ]
    )
    in_table = ints(
        [
            slots_of((me - home_source) % n, home_row_rank, n, cap),
            slots_of((me - mirror_source) % n, mirror_row_rank, n, cap),
        ]
    )
    weight = jnp.where(pair_shells[:, 0] != pair_shells[:, 1], 2.0, 1.0)
    factor = (screen.astype(f32) * weight[:, None]).astype(bf16)[:, None, :]
    keeping = screen.astype(f32)[:, None, :]

    integrals = pl.pallas_call(
        load_kernel,
        out_shape=pltpu.VMEM((blocks, pairs, aux_dev), bf16),
        in_specs=[anywhere],
        out_specs=in_vmem,
        scratch_shapes=[pltpu.SemaphoreType.DMA],
        compiler_params=pltpu.CompilerParams(vmem_limit_bytes=2 * 1024 * 1024),
        name="load_integrals",
    )(three_index)

    sends = pl.pallas_call(
        functools.partial(scatter_density_kernel, n, blocks, cap),
        out_shape=[jax.ShapeDtypeStruct((cap, part, pairs), bf16)] * (CHAINS * n),
        grid_spec=pltpu.PrefetchScalarGridSpec(
            num_scalar_prefetch=1,
            grid=(1,),
            in_specs=[pl.BlockSpec((blocks, pairs, half), lambda i, t: (0, 0, t[n * cap]))],
            out_specs=[pl.BlockSpec((cap, part, pairs), lambda i, t: (0, 0, 0))] * (CHAINS * n),
            scratch_shapes=[pltpu.VMEM((blocks, half, pairs), bf16)],
        ),
        compiler_params=pltpu.CompilerParams(vmem_limit_bytes=VMEM_BYTES),
        name="scatter_density",
    )(send_table, density)

    def fetch(chain, after):
        mine = sends[chain * n : (chain + 1) * n]
        received = [mine[0]] + [shift(mine[d], d) for d in range(1, n)]
        own = call(
            functools.partial(gather_density_kernel, n, cap),
            "gather_density",
            pick_table,
            received,
            jax.ShapeDtypeStruct((blocks, part, pairs), bf16),
            in_vmem,
            after,
        )
        return own, swap(own)

    def fit(own, other):
        return call(
            functools.partial(fit_kernel, n, blocks),
            "fit",
            chunk_table,
            [factor, own, other, integrals],
            [
                jax.ShapeDtypeStruct((n // 2, both, width), f32),
                jax.ShapeDtypeStruct((n // 2, both, width), bf16),
            ],
            [in_vmem] * 2,
            flops=2 * blocks * pairs * aux_dev * both,
        )

    def total(keep, send):
        bit = 1
        while True:
            value = keep + flip(send, bit).astype(f32)
            bit *= 2
            if bit == n:
                break
            keep, send = value[0::2], value[1::2].astype(bf16)
        near, order = value.astype(bf16), [0]
        while True:
            bit //= 2
            far = flip(near, bit)
            order = order + [e ^ bit for e in order]
            if bit == 1:
                return near, far, order
            near = jnp.concatenate([near, far], axis=0)

    def apply(near, far, order, after):
        mine, theirs = call(
            functools.partial(apply_kernel, n, blocks, order),
            "apply",
            chunk_table,
            [integrals, near, far],
            [
                jax.ShapeDtypeStruct((blocks, part, pairs), f32),
                jax.ShapeDtypeStruct((blocks, part, pairs), bf16),
            ],
            [in_vmem] * 2,
            after,
            flops=2 * blocks * pairs * aux_dev * both,
        )
        return mine, swap(theirs)

    def pack(mine, added):
        return call(
            functools.partial(scatter_coulomb_kernel, n, blocks, cap),
            "scatter_coulomb",
            out_table,
            [keeping, mine, added],
            [jax.ShapeDtypeStruct((2 * cap, part, pairs), bf16)] * n,
            [in_vmem] * n,
            scratch=[pltpu.VMEM((blocks, part, pairs), bf16)],
        )

    fits = []
    for chain in range(CHAINS):
        fits.append(fit(*fetch(chain, fits[-1][:1] if fits else ())))
    packed = []
    for pieces in fits:
        packed.append(pack(*apply(*total(*pieces), packed[-1][:1] if packed else ())))
    received = [
        out[d] if d == 0 else shift(out[d], d) for out in packed for d in range(n)
    ]
    return call(
        functools.partial(gather_coulomb_kernel, n, blocks, shell, cap),
        "gather_coulomb",
        in_table,
        received,
        [jax.ShapeDtypeStruct((blocks, pairs, half), bf16)] * 2,
        [anywhere] * 2,
        scratch=[
            pltpu.VMEM((2, blocks, half, pairs), bf16),
            pltpu.VMEM((2, blocks, pairs, half), bf16),
            pltpu.SemaphoreType.DMA((2, blocks)),
        ],
    )


def solution(mesh):
    in_specs = (
        P(("mol", "pair"), None, "aux"),
        P(("mol", "pair"), None, None),
        P(("mol", "pair"), None),
        P(("mol", "pair"), None),
        P("mol"),
        P("mol"),
    )
    out_specs = (P(("mol", "pair"), None, "aux"), P(("mol", "pair"), None, "aux"))
    return jax.shard_map(local, mesh=mesh, in_specs=in_specs, out_specs=out_specs, check_vma=False)
```

time: 500 us -> 197 us (0.39)
  the two profiles are of different devices: /device:TPU:0 before, /device:TPU:14 now
where the time goes in v4:
time: 197 us
  waiting for transfers between devices  114 us (58%)
  starting transfers between devices  47.3 us (24%)
  Pallas kernels  23 us (12%)
  local copies, waits for them, and re-layouts  6.74 us (3%)
  other arithmetic  5.41 us (3%)
    ppermute x28, waiting for transfers between devices, shift(): return lax.ppermute(x, 'pair', [(s, (s + d) % n) for s in range(n)])  84.1 us
    ppermute x28, starting transfers between devices, shift(): return lax.ppermute(x, 'pair', [(s, (s + d) % n) for s in range(n)])  32.6 us
    ppermute x12, waiting for transfers between devices, flip(): return lax.ppermute(x, 'pair', [(s, s ^ bit) for s in range(n)])  29.4 us
    pallas_call x9, Pallas kernels, call(): pl.pallas_call(kernel, out_shape=out_shape, grid_spec=pltpu.PrefetchScala...  21.1 us
    ppermute x12, starting transfers between devices, flip(): return lax.ppermute(x, 'pair', [(s, s ^ bit) for s in range(n)])  14.4 us
    unnamed x6, local copies, waits for them, and re-layouts  6.68 us
  transfers between devices with their start and end apart: 44, of which 27 were waited for; matrix products, arithmetic and copies ran while one was open for 1% of the time, Pallas kernels for 6%

profile of v4, /device:TPU:14, one launch (start us, length us, event | category | flops | bytes accessed | tf_op | source)
XLA Modules:
  0.0 197.1 jit_solution(7748364084461298785)
XLA Ops:
  14.7 6.5 %collective-permute-done.1.rest_2_ = bf16[3,64,256]{2,1,0:T(8,128)(2,1)S(1)} collective-permute-done((bf16[3,64,256]{2,1,0:T(8,128)(2,1)S(1)}, bf16[3,64,256]{2,1,0:T(8,128)(2,1)S(1)}, u32[]{:S(2)}, u32[]{:S(2)}) %collective-permute-start.1) | collective-permute-done | bytes 98336 | tf_op jit(solution)/shard_map/ppermute | solution.py:194
  30.1 5.2 %copy-done = bf16[14,256,2048]{2,1,0:T(8,128)(2,1)S(1)} copy-done((bf16[14,256,2048]{2,1,0:T(8,128)(2,1)S(1)}, bf16[14,256,2048]{2,1,0:T(8,128)(2,1)}, u32[]{:S(2)}) %copy-start) | copy-done | bytes 14680088
  39.1 2.8 %collective-permute-start.22 = (bf16[3,64,256]{2,1,0:T(8,128)(2,1)S(1)}, bf16[3,64,256]{2,1,0:T(8,128)(2,1)S(1)}, u32[]{:S(2)}, u32[]{:S(2)}) collective-permute-start(bf16[3,64,256]{2,1,0:T(8,128)(2,1)S(1)} %get-tuple-element.63), channel_id=1, source_target_pairs={{0,2},{2,4},{4,6},{6,8},{8,10},{10,12},{12,14},{14,0},{1,3},{3,5},... | collective-permute-start | bytes 294920 | tf_op jit(solution)/shard_map/ppermute | solution.py:194
  45.0 7.1 %collective-permute-done.22.rest_1_ = bf16[3,64,256]{2,1,0:T(8,128)(2,1)S(1)} collective-permute-done((bf16[3,64,256]{2,1,0:T(8,128)(2,1)S(1)}, bf16[3,64,256]{2,1,0:T(8,128)(2,1)S(1)}, u32[]{:S(2)}, u32[]{:S(2)}) %collective-permute-start.22) | collective-permute-done | bytes 98336 | tf_op jit(solution)/shard_map/ppermute | solution.py:194
  56.4 2.8 %collective-permute-done.25.rest_4_ = bf16[3,64,256]{2,1,0:T(8,128)(2,1)S(1)} collective-permute-done((bf16[3,64,256]{2,1,0:T(8,128)(2,1)S(1)}, bf16[3,64,256]{2,1,0:T(8,128)(2,1)S(1)}, u32[]{:S(2)}, u32[]{:S(2)}) %collective-permute-start.25) | collective-permute-done | bytes 98336 | tf_op jit(solution)/shard_map/ppermute | solution.py:194
  59.5 2.9 %collective-permute-done.28.rest_7_ = bf16[3,64,256]{2,1,0:T(8,128)(2,1)S(1)} collective-permute-done((bf16[3,64,256]{2,1,0:T(8,128)(2,1)S(1)}, bf16[3,64,256]{2,1,0:T(8,128)(2,1)S(1)}, u32[]{:S(2)}, u32[]{:S(2)}) %collective-permute-start.28) | collective-permute-done | bytes 98336 | tf_op jit(solution)/shard_map/ppermute | solution.py:194
  63.7 5.9 %collective-permute-done.9 = bf16[2,128,256]{2,1,0:T(8,128)(2,1)S(1)} collective-permute-done((bf16[2,128,256]{2,1,0:T(8,128)(2,1)S(1)}, bf16[2,128,256]{2,1,0:T(8,128)(2,1)S(1)}, u32[]{:S(2)}, u32[]{:S(2)}) %collective-permute-start.9) | collective-permute-done | bytes 131104 | tf_op jit(solution)/shard_map/ppermute | solution.py:197
  69.6 3.5 %collective-permute-start.10 = (bf16[1,128,256]{2,1,0:T(8,128)(2,1)S(1)}, bf16[1,128,256]{2,1,0:T(8,128)(2,1)S(1)}, u32[]{:S(2)}, u32[]{:S(2)}) collective-permute-start(bf16[1,128,256]{2,1,0:T(8,128)(2,1)S(1)} %slice.65), channel_id=1, source_target_pairs={{0,8},{2,10},{4,12},{6,14},{8,0},{10,2},{12,4},{14,6},{1,9},{3,11}... | collective-permute-start | bytes 196616 | tf_op jit(solution)/shard_map/ppermute | solution.py:197
  79.2 4.4 %collective-permute-done.30 = bf16[4,128,256]{2,1,0:T(8,128)(2,1)S(1)} collective-permute-done((bf16[4,128,256]{2,1,0:T(8,128)(2,1)S(1)}, bf16[4,128,256]{2,1,0:T(8,128)(2,1)S(1)}, u32[]{:S(2)}, u32[]{:S(2)}) %collective-permute-start.30) | collective-permute-done | bytes 262176 | tf_op jit(solution)/shard_map/ppermute | solution.py:197
  85.9 3.9 %collective-permute-done.31 = bf16[2,128,256]{2,1,0:T(8,128)(2,1)S(1)} collective-permute-done((bf16[2,128,256]{2,1,0:T(8,128)(2,1)S(1)}, bf16[2,128,256]{2,1,0:T(8,128)(2,1)S(1)}, u32[]{:S(2)}, u32[]{:S(2)}) %collective-permute-start.31) | collective-permute-done | bytes 131104 | tf_op jit(solution)/shard_map/ppermute | solution.py:197
  92.7 2.8 %collective-permute-done.32 = bf16[1,128,256]{2,1,0:T(8,128)(2,1)S(1)} collective-permute-done((bf16[1,128,256]{2,1,0:T(8,128)(2,1)S(1)}, bf16[1,128,256]{2,1,0:T(8,128)(2,1)S(1)}, u32[]{:S(2)}, u32[]{:S(2)}) %collective-permute-start.32) | collective-permute-done | bytes 65568 | tf_op jit(solution)/shard_map/ppermute | solution.py:197
  97.6 4.7 %apply.2 = (f32[14,64,256]{2,1,0:T(8,128)S(1)}, bf16[14,64,256]{2,1,0:T(8,128)(2,1)S(1)}) custom-call(s32[8]{0:T(128)S(1)} %iota_xor_fusion.table, bf16[14,256,2048]{2,1,0:T(8,128)(2,1)S(1)} %load_integrals.1.integrals, bf16[4,128,256]{2,1,0:T(8,128)(2,1)S(1)} %pad_maximum_fusion.near, bf16[4,128,256]{2,1,0:T(8,128)(2,1)S(1)} %collective-permute-done.13.far), custom_call_target="tpu_custom_call" | custom-call | flops 1879048192 | tf_op jit(solution)/shard_map/apply/pallas_call | solution.py:178
  103.3 5.1 %collective-permute-done.34 = bf16[2,128,256]{2,1,0:T(8,128)(2,1)S(1)} collective-permute-done((bf16[2,128,256]{2,1,0:T(8,128)(2,1)S(1)}, bf16[2,128,256]{2,1,0:T(8,128)(2,1)S(1)}, u32[]{:S(2)}, u32[]{:S(2)}) %collective-permute-start.34) | collective-permute-done | bytes 131104 | tf_op jit(solution)/shard_map/ppermute | solution.py:197
  110.9 5.5 %collective-permute-done.35.far = bf16[4,128,256]{2,1,0:T(8,128)(2,1)S(1)} collective-permute-done((bf16[4,128,256]{2,1,0:T(8,128)(2,1)S(1)}, bf16[4,128,256]{2,1,0:T(8,128)(2,1)S(1)}, u32[]{:S(2)}, u32[]{:S(2)}) %collective-permute-start.35) | collective-permute-done | bytes 262176 | tf_op jit(solution)/shard_map/ppermute | solution.py:197
  116.4 4.7 %apply.3 = (f32[14,64,256]{2,1,0:T(8,128)S(1)}, bf16[14,64,256]{2,1,0:T(8,128)(2,1)S(1)}) custom-call(s32[8]{0:T(128)S(1)} %iota_xor_fusion.table, bf16[14,256,2048]{2,1,0:T(8,128)(2,1)S(1)} %load_integrals.1.integrals, bf16[4,128,256]{2,1,0:T(8,128)(2,1)S(1)} %pad_maximum_fusion.1.near, bf16[4,128,256]{2,1,0:T(8,128)(2,1)S(1)} %collective-permute-done.35.far, ...), custom_call_target="tpu_custom_call" | custom-call | flops 1879048192 | tf_op jit(solution)/shard_map/apply/pallas_call | solution.py:178
  126.4 2.9 %collective-permute-start.19 = (bf16[6,64,256]{2,1,0:T(8,128)(2,1)S(1)}, bf16[6,64,256]{2,1,0:T(8,128)(2,1)S(1)}, u32[]{:S(2)}, u32[]{:S(2)}) collective-permute-start(bf16[6,64,256]{2,1,0:T(8,128)(2,1)S(1)} %get-tuple-element.59), channel_id=1, source_target_pairs={{0,10},{2,12},{4,14},{6,0},{8,2},{10,4},{12,6},{14,8},{1,11},{3,13... | collective-permute-start | bytes 589832 | tf_op jit(solution)/shard_map/ppermute | solution.py:194
  133.9 19.3 %collective-permute-done.17.rest_3_ = bf16[6,64,256]{2,1,0:T(8,128)(2,1)S(1)} collective-permute-done((bf16[6,64,256]{2,1,0:T(8,128)(2,1)S(1)}, bf16[6,64,256]{2,1,0:T(8,128)(2,1)S(1)}, u32[]{:S(2)}, u32[]{:S(2)}) %collective-permute-start.17) | collective-permute-done | bytes 196640 | tf_op jit(solution)/shard_map/ppermute | solution.py:194
  153.2 4.2 %collective-permute-done.18.rest_4_ = bf16[6,64,256]{2,1,0:T(8,128)(2,1)S(1)} collective-permute-done((bf16[6,64,256]{2,1,0:T(8,128)(2,1)S(1)}, bf16[6,64,256]{2,1,0:T(8,128)(2,1)S(1)}, u32[]{:S(2)}, u32[]{:S(2)}) %collective-permute-start.18) | collective-permute-done | bytes 196640 | tf_op jit(solution)/shard_map/ppermute | solution.py:194
  158.2 14.3 %collective-permute-done.20.rest_6_ = bf16[6,64,256]{2,1,0:T(8,128)(2,1)S(1)} collective-permute-done((bf16[6,64,256]{2,1,0:T(8,128)(2,1)S(1)}, bf16[6,64,256]{2,1,0:T(8,128)(2,1)S(1)}, u32[]{:S(2)}, u32[]{:S(2)}) %collective-permute-start.20) | collective-permute-done | bytes 196640 | tf_op jit(solution)/shard_map/ppermute | solution.py:194
  173.6 3.4 %collective-permute-start.43 = (bf16[6,64,256]{2,1,0:T(8,128)(2,1)S(1)}, bf16[6,64,256]{2,1,0:T(8,128)(2,1)S(1)}, u32[]{:S(2)}, u32[]{:S(2)}) collective-permute-start(bf16[6,64,256]{2,1,0:T(8,128)(2,1)S(1)} %get-tuple-element.81), channel_id=1, source_target_pairs={{0,14},{2,0},{4,2},{6,4},{8,6},{10,8},{12,10},{14,12},{1,15},{3,1}... | collective-permute-start | bytes 589832 | tf_op jit(solution)/shard_map/ppermute | solution.py:194
  177.1 9.8 %collective-permute-done.39.rest_11_ = bf16[6,64,256]{2,1,0:T(8,128)(2,1)S(1)} collective-permute-done((bf16[6,64,256]{2,1,0:T(8,128)(2,1)S(1)}, bf16[6,64,256]{2,1,0:T(8,128)(2,1)S(1)}, u32[]{:S(2)}, u32[]{:S(2)}) %collective-permute-start.39) | collective-permute-done | bytes 196640 | tf_op jit(solution)/shard_map/ppermute | solution.py:194
  186.9 3.8 %collective-permute-done.40.rest_12_ = bf16[6,64,256]{2,1,0:T(8,128)(2,1)S(1)} collective-permute-done((bf16[6,64,256]{2,1,0:T(8,128)(2,1)S(1)}, bf16[6,64,256]{2,1,0:T(8,128)(2,1)S(1)}, u32[]{:S(2)}, u32[]{:S(2)}) %collective-permute-start.40) | collective-permute-done | bytes 196640 | tf_op jit(solution)/shard_map/ppermute | solution.py:194
  190.7 2.8 %collective-permute-done.42.rest_14_ = bf16[6,64,256]{2,1,0:T(8,128)(2,1)S(1)} collective-permute-done((bf16[6,64,256]{2,1,0:T(8,128)(2,1)S(1)}, bf16[6,64,256]{2,1,0:T(8,128)(2,1)S(1)}, u32[]{:S(2)}, u32[]{:S(2)}) %collective-permute-start.42) | collective-permute-done | bytes 196640 | tf_op jit(solution)/shard_map/ppermute | solution.py:194
  193.9 3.0 %gather_coulomb.1 = (bf16[14,256,128]{2,1,0:T(8,128)(2,1)}, bf16[14,256,128]{2,1,0:T(8,128)(2,1)}) custom-call(s32[48]{0:T(128)S(1)} %pad_add_fusion.table, bf16[6,64,256]{2,1,0:T(8,128)(2,1)S(1)} %get-tuple-element.54.rest_0_, bf16[6,64,256]{2,1,0:T(8,128)(2,1)S(1)} %collective-permute-done.15.rest_1_, ...), custom_call_target="tpu_custom_call" | custom-call | tf_op jit(solution)/shard_map/gather_coulomb/pallas_call | solution.py:178
  (119 shorter events, 64.7 us)
Async XLA Ops:
  7.6 13.6 %collective-permute-start.1 = (bf16[3,64,256]{2,1,0:T(8,128)(2,1)S(1)}, bf16[3,64,256]{2,1,0:T(8,128)(2,1)S(1)}, u32[]{:S(2)}, u32[]{:S(2)}) collective-permute-start(bf16[3,64,256]{2,1,0:T(8,128)(2,1)S(1)} %get-tuple-element.44), channel_id=1, source_target_pairs={{0,4},{2,6},{4,8},{6,10},{8,12},{10,14},{12,0},{14,2},{1,5},{3,7},... | collective-permute-start | bytes 294920 | tf_op jit(solution)/shard_map/ppermute | solution.py:194
  9.1 14.1 %collective-permute-start.2 = (bf16[3,64,256]{2,1,0:T(8,128)(2,1)S(1)}, bf16[3,64,256]{2,1,0:T(8,128)(2,1)S(1)}, u32[]{:S(2)}, u32[]{:S(2)}) collective-permute-start(bf16[3,64,256]{2,1,0:T(8,128)(2,1)S(1)} %get-tuple-element.45), channel_id=1, source_target_pairs={{0,6},{2,8},{4,10},{6,12},{8,14},{10,0},{12,2},{14,4},{1,7},{3,9},... | collective-permute-start | bytes 294920 | tf_op jit(solution)/shard_map/ppermute | solution.py:194
  10.3 14.1 %collective-permute-start.3 = (bf16[3,64,256]{2,1,0:T(8,128)(2,1)S(1)}, bf16[3,64,256]{2,1,0:T(8,128)(2,1)S(1)}, u32[]{:S(2)}, u32[]{:S(2)}) collective-permute-start(bf16[3,64,256]{2,1,0:T(8,128)(2,1)S(1)} %get-tuple-element.46), channel_id=1, source_target_pairs={{0,8},{2,10},{4,12},{6,14},{8,0},{10,2},{12,4},{14,6},{1,9},{3,11}... | collective-permute-start | bytes 294920 | tf_op jit(solution)/shard_map/ppermute | solution.py:194
  12.0 12.4 %collective-permute-start.4 = (bf16[3,64,256]{2,1,0:T(8,128)(2,1)S(1)}, bf16[3,64,256]{2,1,0:T(8,128)(2,1)S(1)}, u32[]{:S(2)}, u32[]{:S(2)}) collective-permute-start(bf16[3,64,256]{2,1,0:T(8,128)(2,1)S(1)} %get-tuple-element.47), channel_id=1, source_target_pairs={{0,10},{2,12},{4,14},{6,0},{8,2},{10,4},{12,6},{14,8},{1,11},{3,13... | collective-permute-start | bytes 294920 | tf_op jit(solution)/shard_map/ppermute | solution.py:194
  13.3 12.9 %collective-permute-start.5 = (bf16[3,64,256]{2,1,0:T(8,128)(2,1)S(1)}, bf16[3,64,256]{2,1,0:T(8,128)(2,1)S(1)}, u32[]{:S(2)}, u32[]{:S(2)}) collective-permute-start(bf16[3,64,256]{2,1,0:T(8,128)(2,1)S(1)} %get-tuple-element.48), channel_id=1, source_target_pairs={{0,12},{2,14},{4,0},{6,2},{8,4},{10,6},{12,8},{14,10},{1,13},{3,15... | collective-permute-start | bytes 294920 | tf_op jit(solution)/shard_map/ppermute | solution.py:194
  39.0 24.4 %collective-permute-start.8 = (bf16[4,128,256]{2,1,0:T(8,128)(2,1)S(1)}, bf16[4,128,256]{2,1,0:T(8,128)(2,1)S(1)}, u32[]{:S(2)}, u32[]{:S(2)}) collective-permute-start(bf16[4,128,256]{2,1,0:T(8,128)(2,1)S(1)} %get-tuple-element.51), channel_id=1, source_target_pairs={{0,2},{2,0},{4,6},{6,4},{8,10},{10,8},{12,14},{14,12},{1,3},{3,1},... | collective-permute-start | bytes 786440 | tf_op jit(solution)/shard_map/ppermute | solution.py:197
  39.1 12.9 %collective-permute-start.22 = (bf16[3,64,256]{2,1,0:T(8,128)(2,1)S(1)}, bf16[3,64,256]{2,1,0:T(8,128)(2,1)S(1)}, u32[]{:S(2)}, u32[]{:S(2)}) collective-permute-start(bf16[3,64,256]{2,1,0:T(8,128)(2,1)S(1)} %get-tuple-element.63), channel_id=1, source_target_pairs={{0,2},{2,4},{4,6},{6,8},{8,10},{10,12},{12,14},{14,0},{1,3},{3,5},... | collective-permute-start | bytes 294920 | tf_op jit(solution)/shard_map/ppermute | solution.py:194
  42.0 10.1 %collective-permute-start.23 = (bf16[3,64,256]{2,1,0:T(8,128)(2,1)S(1)}, bf16[3,64,256]{2,1,0:T(8,128)(2,1)S(1)}, u32[]{:S(2)}, u32[]{:S(2)}) collective-permute-start(bf16[3,64,256]{2,1,0:T(8,128)(2,1)S(1)} %get-tuple-element.64), channel_id=1, source_target_pairs={{0,4},{2,6},{4,8},{6,10},{8,12},{10,14},{12,0},{14,2},{1,5},{3,7},... | collective-permute-start | bytes 294920 | tf_op jit(solution)/shard_map/ppermute | solution.py:194
  42.5 12.0 %collective-permute-start.24 = (bf16[3,64,256]{2,1,0:T(8,128)(2,1)S(1)}, bf16[3,64,256]{2,1,0:T(8,128)(2,1)S(1)}, u32[]{:S(2)}, u32[]{:S(2)}) collective-permute-start(bf16[3,64,256]{2,1,0:T(8,128)(2,1)S(1)} %get-tuple-element.65), channel_id=1, source_target_pairs={{0,6},{2,8},{4,10},{6,12},{8,14},{10,0},{12,2},{14,4},{1,7},{3,9},... | collective-permute-start | bytes 294920 | tf_op jit(solution)/shard_map/ppermute | solution.py:194
  42.5 16.7 %collective-permute-start.25 = (bf16[3,64,256]{2,1,0:T(8,128)(2,1)S(1)}, bf16[3,64,256]{2,1,0:T(8,128)(2,1)S(1)}, u32[]{:S(2)}, u32[]{:S(2)}) collective-permute-start(bf16[3,64,256]{2,1,0:T(8,128)(2,1)S(1)} %get-tuple-element.66), channel_id=1, source_target_pairs={{0,8},{2,10},{4,12},{6,14},{8,0},{10,2},{12,4},{14,6},{1,9},{3,11}... | collective-permute-start | bytes 294920 | tf_op jit(solution)/shard_map/ppermute | solution.py:194
  63.4 9.7 %collective-permute-start.29 = (bf16[14,64,256]{2,1,0:T(8,128)(2,1)S(1)}, bf16[14,64,256]{2,1,0:T(8,128)(2,1)S(1)}, u32[]{:S(2)}, u32[]{:S(2)}) collective-permute-start(bf16[14,64,256]{2,1,0:T(8,128)(2,1)S(1)} %gather_density.3.own), channel_id=1, source_target_pairs={{0,1},{1,0},{2,3},{3,2},{4,5},{5,4},{6,7},{7,6},{8,9},{9,8},{10,11... | collective-permute-start | bytes 1376264 | tf_op jit(solution)/shard_map/ppermute | solution.py:200
  122.7 11.2 %collective-permute-start.16 = (bf16[6,64,256]{2,1,0:T(8,128)(2,1)S(1)}, bf16[6,64,256]{2,1,0:T(8,128)(2,1)S(1)}, u32[]{:S(2)}, u32[]{:S(2)}) collective-permute-start(bf16[6,64,256]{2,1,0:T(8,128)(2,1)S(1)} %get-tuple-element.56), channel_id=1, source_target_pairs={{0,4},{2,6},{4,8},{6,10},{8,12},{10,14},{12,0},{14,2},{1,5},{3,7},... | collective-permute-start | bytes 589832 | tf_op jit(solution)/shard_map/ppermute | solution.py:194
  124.2 29.0 %collective-permute-start.17 = (bf16[6,64,256]{2,1,0:T(8,128)(2,1)S(1)}, bf16[6,64,256]{2,1,0:T(8,128)(2,1)S(1)}, u32[]{:S(2)}, u32[]{:S(2)}) collective-permute-start(bf16[6,64,256]{2,1,0:T(8,128)(2,1)S(1)} %get-tuple-element.57), channel_id=1, source_target_pairs={{0,6},{2,8},{4,10},{6,12},{8,14},{10,0},{12,2},{14,4},{1,7},{3,9},... | collective-permute-start | bytes 589832 | tf_op jit(solution)/shard_map/ppermute | solution.py:194
  125.7 31.8 %collective-permute-start.18 = (bf16[6,64,256]{2,1,0:T(8,128)(2,1)S(1)}, bf16[6,64,256]{2,1,0:T(8,128)(2,1)S(1)}, u32[]{:S(2)}, u32[]{:S(2)}) collective-permute-start(bf16[6,64,256]{2,1,0:T(8,128)(2,1)S(1)} %get-tuple-element.58), channel_id=1, source_target_pairs={{0,8},{2,10},{4,12},{6,14},{8,0},{10,2},{12,4},{14,6},{1,9},{3,11}... | collective-permute-start | bytes 589832 | tf_op jit(solution)/shard_map/ppermute | solution.py:194
  126.4 31.8 %collective-permute-start.19 = (bf16[6,64,256]{2,1,0:T(8,128)(2,1)S(1)}, bf16[6,64,256]{2,1,0:T(8,128)(2,1)S(1)}, u32[]{:S(2)}, u32[]{:S(2)}) collective-permute-start(bf16[6,64,256]{2,1,0:T(8,128)(2,1)S(1)} %get-tuple-element.59), channel_id=1, source_target_pairs={{0,10},{2,12},{4,14},{6,0},{8,2},{10,4},{12,6},{14,8},{1,11},{3,13... | collective-permute-start | bytes 589832 | tf_op jit(solution)/shard_map/ppermute | solution.py:194
  130.1 42.4 %collective-permute-start.20 = (bf16[6,64,256]{2,1,0:T(8,128)(2,1)S(1)}, bf16[6,64,256]{2,1,0:T(8,128)(2,1)S(1)}, u32[]{:S(2)}, u32[]{:S(2)}) collective-permute-start(bf16[6,64,256]{2,1,0:T(8,128)(2,1)S(1)} %get-tuple-element.60), channel_id=1, source_target_pairs={{0,12},{2,14},{4,0},{6,2},{8,4},{10,6},{12,8},{14,10},{1,13},{3,15... | collective-permute-start | bytes 589832 | tf_op jit(solution)/shard_map/ppermute | solution.py:194
  133.9 39.0 %collective-permute-start.21 = (bf16[6,64,256]{2,1,0:T(8,128)(2,1)S(1)}, bf16[6,64,256]{2,1,0:T(8,128)(2,1)S(1)}, u32[]{:S(2)}, u32[]{:S(2)}) collective-permute-start(bf16[6,64,256]{2,1,0:T(8,128)(2,1)S(1)} %get-tuple-element.61), channel_id=1, source_target_pairs={{0,14},{2,0},{4,2},{6,4},{8,6},{10,8},{12,10},{14,12},{1,15},{3,1}... | collective-permute-start | bytes 589832 | tf_op jit(solution)/shard_map/ppermute | solution.py:194
  153.2 19.7 %collective-permute-start.37 = (bf16[6,64,256]{2,1,0:T(8,128)(2,1)S(1)}, bf16[6,64,256]{2,1,0:T(8,128)(2,1)S(1)}, u32[]{:S(2)}, u32[]{:S(2)}) collective-permute-start(bf16[6,64,256]{2,1,0:T(8,128)(2,1)S(1)} %get-tuple-element.75), channel_id=1, source_target_pairs={{0,2},{2,4},{4,6},{6,8},{8,10},{10,12},{12,14},{14,0},{1,3},{3,5},... | collective-permute-start | bytes 589832 | tf_op jit(solution)/shard_map/ppermute | solution.py:194
  157.5 16.1 %collective-permute-start.38 = (bf16[6,64,256]{2,1,0:T(8,128)(2,1)S(1)}, bf16[6,64,256]{2,1,0:T(8,128)(2,1)S(1)}, u32[]{:S(2)}, u32[]{:S(2)}) collective-permute-start(bf16[6,64,256]{2,1,0:T(8,128)(2,1)S(1)} %get-tuple-element.76), channel_id=1, source_target_pairs={{0,4},{2,6},{4,8},{6,10},{8,12},{10,14},{12,0},{14,2},{1,5},{3,7},... | collective-permute-start | bytes 589832 | tf_op jit(solution)/shard_map/ppermute | solution.py:194
  158.2 28.8 %collective-permute-start.39 = (bf16[6,64,256]{2,1,0:T(8,128)(2,1)S(1)}, bf16[6,64,256]{2,1,0:T(8,128)(2,1)S(1)}, u32[]{:S(2)}, u32[]{:S(2)}) collective-permute-start(bf16[6,64,256]{2,1,0:T(8,128)(2,1)S(1)} %get-tuple-element.77), channel_id=1, source_target_pairs={{0,6},{2,8},{4,10},{6,12},{8,14},{10,0},{12,2},{14,4},{1,7},{3,9},... | collective-permute-start | bytes 589832 | tf_op jit(solution)/shard_map/ppermute | solution.py:194
  172.5 18.2 %collective-permute-start.40 = (bf16[6,64,256]{2,1,0:T(8,128)(2,1)S(1)}, bf16[6,64,256]{2,1,0:T(8,128)(2,1)S(1)}, u32[]{:S(2)}, u32[]{:S(2)}) collective-permute-start(bf16[6,64,256]{2,1,0:T(8,128)(2,1)S(1)} %get-tuple-element.78), channel_id=1, source_target_pairs={{0,8},{2,10},{4,12},{6,14},{8,0},{10,2},{12,4},{14,6},{1,9},{3,11}... | collective-permute-start | bytes 589832 | tf_op jit(solution)/shard_map/ppermute | solution.py:194
  172.9 17.8 %collective-permute-start.41 = (bf16[6,64,256]{2,1,0:T(8,128)(2,1)S(1)}, bf16[6,64,256]{2,1,0:T(8,128)(2,1)S(1)}, u32[]{:S(2)}, u32[]{:S(2)}) collective-permute-start(bf16[6,64,256]{2,1,0:T(8,128)(2,1)S(1)} %get-tuple-element.79), channel_id=1, source_target_pairs={{0,10},{2,12},{4,14},{6,0},{8,2},{10,4},{12,6},{14,8},{1,11},{3,13... | collective-permute-start | bytes 589832 | tf_op jit(solution)/shard_map/ppermute | solution.py:194
  172.9 20.6 %collective-permute-start.42 = (bf16[6,64,256]{2,1,0:T(8,128)(2,1)S(1)}, bf16[6,64,256]{2,1,0:T(8,128)(2,1)S(1)}, u32[]{:S(2)}, u32[]{:S(2)}) collective-permute-start(bf16[6,64,256]{2,1,0:T(8,128)(2,1)S(1)} %get-tuple-element.80), channel_id=1, source_target_pairs={{0,12},{2,14},{4,0},{6,2},{8,4},{10,6},{12,8},{14,10},{1,13},{3,15... | collective-permute-start | bytes 589832 | tf_op jit(solution)/shard_map/ppermute | solution.py:194
  173.6 20.3 %collective-permute-start.43 = (bf16[6,64,256]{2,1,0:T(8,128)(2,1)S(1)}, bf16[6,64,256]{2,1,0:T(8,128)(2,1)S(1)}, u32[]{:S(2)}, u32[]{:S(2)}) collective-permute-start(bf16[6,64,256]{2,1,0:T(8,128)(2,1)S(1)} %get-tuple-element.81), channel_id=1, source_target_pairs={{0,14},{2,0},{4,2},{6,4},{8,6},{10,8},{12,10},{14,12},{1,15},{3,1}... | collective-permute-start | bytes 589832 | tf_op jit(solution)/shard_map/ppermute | solution.py:194
  (23 other events, 187.9 us)

commit v5 on v4

--- a/solution.py
+++ b/solution.py
@@ -42,26 +42,31 @@
 
 
 def scatter_density_kernel(devices, blocks, cap, table, density, *rest):
-    sends, turned = rest[: CHAINS * devices], rest[-1]
-    part = sends[0].shape[1]
+    sends, whole, turned = rest[:devices], rest[devices], rest[-1]
+    part = whole.shape[2]
     for row in range(blocks):
         turned[row] = density[row].T
     for step in range(devices):
         for rank in range(cap):
             row = jnp.maximum(table[step * cap + rank], 0)
-            for chain in range(CHAINS):
-                sends[chain * devices + step][rank] = turned[row, pl.ds(chain * part, part)]
-
-
-def gather_density_kernel(devices, cap, table, *rest):
-    received, out = rest[:devices], rest[-1]
+            sends[step][rank] = turned[row, pl.ds(0, part)]
+            row = jnp.maximum(table[(devices + step) * cap + rank], 0)
+            whole[step, rank] = turned[row, pl.ds(part, part)]
+
+
+def slot(received, devices, step, rank):
+    return received[0][step, rank] if len(received) == 1 else received[step][rank]
+
+
+def gather_density_kernel(devices, cap, count, table, *rest):
+    received, out = rest[:count], rest[-1]
     for step in range(devices):
         for rank in range(cap):
             row = table[step * cap + rank]
 
             @pl.when(row >= 0)
             def _():
-                out[row] = received[step][rank]
+                out[row] = slot(received, devices, step, rank)
 
 
 def fit_kernel(devices, blocks, table, factor, own, other, integrals, keep, send):
@@ -106,7 +111,7 @@
 
 
 def scatter_coulomb_kernel(devices, blocks, cap, table, screen, own, other, *rest):
-    sends, ready = rest[:devices], rest[devices]
+    sends, ready = rest[:-1], rest[-1]
     for b in range(blocks):
         value = (own[b] + other[b].astype(jnp.float32)) * screen[b]
         ready[b] = value.astype(jnp.bfloat16)
@@ -114,25 +119,31 @@
         for step in range(devices):
             for rank in range(cap):
                 b = jnp.maximum(table[(group * devices + step) * cap + rank], 0)
-                sends[step][group * cap + rank] = ready[b]
-
-
-def gather_coulomb_kernel(devices, blocks, shell, cap, table, *rest):
-    received = rest[: CHAINS * devices]
-    rows, cols, landed, done, sems = rest[CHAINS * devices :]
-    part = received[0].shape[1]
+                if len(sends) == 1:
+                    sends[0][step, group * cap + rank] = ready[b]
+                else:
+                    sends[step][group * cap + rank] = ready[b]
+
+
+def gather_coulomb_kernel(devices, blocks, shell, cap, counts, table, *rest):
+    received, start = [], 0
+    for count in counts:
+        received.append(rest[start : start + count])
+        start += count
+    rows, cols, landed, done, sems = rest[start:]
+    part = landed.shape[2] // len(counts)
     pairs = landed.shape[3]
-    for group in range(2):
-        for step in range(devices):
-            for rank in range(cap):
-                row = table[(group * devices + step) * cap + rank]
-
-                @pl.when(row >= 0)
-                def _():
-                    for chain in range(CHAINS):
-                        landed[group, row, pl.ds(chain * part, part)] = received[
-                            chain * devices + step
-                        ][group * cap + rank]
+    for chain, pieces in enumerate(received):
+        for group in range(2):
+            for step in range(devices):
+                for rank in range(cap):
+                    row = table[((chain * 2 + group) * devices + step) * cap + rank]
+
+                    @pl.when(row >= 0)
+                    def _():
+                        landed[group, row, pl.ds(chain * part, part)] = slot(
+                            pieces, devices, step, group * cap + rank
+                        )
 
     to = lax.broadcasted_iota(jnp.int32, (pairs, pairs), 0)
     source = lax.broadcasted_iota(jnp.int32, (pairs, pairs), 1)
@@ -174,27 +185,30 @@
     anywhere = pl.BlockSpec(memory_space=pl.ANY)
     ints = functools.partial(jnp.concatenate, axis=0)
 
-    def call(kernel, name, table, args, out_shape, out_specs, after=(), scratch=(), flops=0):
+    def call(kernel, name, table, args, out_shape, out_specs, ready=(), scratch=(), flops=0):
         return pl.pallas_call(
             kernel,
             out_shape=out_shape,
             grid_spec=pltpu.PrefetchScalarGridSpec(
                 num_scalar_prefetch=1,
                 grid=(),
-                in_specs=[in_vmem] * len(args) + [anywhere] * len(after),
+                in_specs=[in_vmem] * len(args) + [anywhere] * len(ready),
                 out_specs=out_specs,
                 scratch_shapes=list(scratch),
             ),
             compiler_params=pltpu.CompilerParams(vmem_limit_bytes=VMEM_BYTES),
             cost_estimate=pl.CostEstimate(flops=flops, bytes_accessed=0, transcendentals=0),
             name=name,
-        )(table, *args, *after)
+        )(table, *args, *ready)
 
     def shift(x, d):
         return lax.ppermute(x, "pair", [(s, (s + d) % n) for s in range(n)])
 
     def flip(x, bit):
         return lax.ppermute(x, "pair", [(s, s ^ bit) for s in range(n)])
+
+    def after(x, *others):
+        return lax.optimization_barrier((x, *others))[0]
 
     def swap(x):
         return lax.ppermute(x, "aux", [(s, (s + 1) % cores) for s in range(cores)])
@@ -203,21 +217,31 @@
     mirror_target, mirror_rank, mirror_source, mirror_row_rank = tables(
         mirror_slot, n, blocks, me
     )
+    held = functools.partial(slots_of, devices=n, cap=cap)
     send_table = ints(
-        [slots_of((home_source - me) % n, home_row_rank, n, cap), core[None].astype(jnp.int32)]
-    )
-    pick_table = slots_of((me - home_target) % n, home_rank, n, cap)
+        [
+            held((home_source - me) % n, home_row_rank),
+            held(home_source, home_row_rank),
+            core[None].astype(jnp.int32),
+        ]
+    )
+    pick_tables = (held((me - home_target) % n, home_rank), held(home_target, home_rank))
     chunk_table = me ^ jnp.arange(n, dtype=jnp.int32)
-    out_table = ints(
-        [
-            slots_of((home_target - me) % n, home_rank, n, cap),
-            slots_of((mirror_target - me) % n, mirror_rank, n, cap),
-        ]
+    out_tables = (
+        ints([held(home_target, home_rank), held(mirror_target, mirror_rank)]),
+        ints(
+            [
+                held((home_target - me) % n, home_rank),
+                held((mirror_target - me) % n, mirror_rank),
+            ]
+        ),
     )
     in_table = ints(
         [
-            slots_of((me - home_source) % n, home_row_rank, n, cap),
-            slots_of((me - mirror_source) % n, mirror_row_rank, n, cap),
+            held(home_source, home_row_rank),
+            held(mirror_source, mirror_row_rank),
+            held((me - home_source) % n, home_row_rank),
+            held((me - mirror_source) % n, mirror_row_rank),
         ]
     )
     weight = jnp.where(pair_shells[:, 0] != pair_shells[:, 1], 2.0, 1.0)
@@ -236,29 +260,29 @@
 
     sends = pl.pallas_call(
         functools.partial(scatter_density_kernel, n, blocks, cap),
-        out_shape=[jax.ShapeDtypeStruct((cap, part, pairs), bf16)] * (CHAINS * n),
+        out_shape=[jax.ShapeDtypeStruct((cap, part, pairs), bf16)] * n
+        + [jax.ShapeDtypeStruct((n, cap, part, pairs), bf16)],
         grid_spec=pltpu.PrefetchScalarGridSpec(
             num_scalar_prefetch=1,
             grid=(1,),
-            in_specs=[pl.BlockSpec((blocks, pairs, half), lambda i, t: (0, 0, t[n * cap]))],
-            out_specs=[pl.BlockSpec((cap, part, pairs), lambda i, t: (0, 0, 0))] * (CHAINS * n),
+            in_specs=[pl.BlockSpec((blocks, pairs, half), lambda i, t: (0, 0, t[2 * n * cap]))],
+            out_specs=[pl.BlockSpec((cap, part, pairs), lambda i, t: (0, 0, 0))] * n
+            + [pl.BlockSpec((n, cap, part, pairs), lambda i, t: (0, 0, 0, 0))],
             scratch_shapes=[pltpu.VMEM((blocks, half, pairs), bf16)],
         ),
         compiler_params=pltpu.CompilerParams(vmem_limit_bytes=VMEM_BYTES),
         name="scatter_density",
     )(send_table, density)
 
-    def fetch(chain, after):
-        mine = sends[chain * n : (chain + 1) * n]
-        received = [mine[0]] + [shift(mine[d], d) for d in range(1, n)]
+    def fetch(received, pick_table, ready):
         own = call(
-            functools.partial(gather_density_kernel, n, cap),
+            functools.partial(gather_density_kernel, n, cap, len(received)),
             "gather_density",
             pick_table,
             received,
             jax.ShapeDtypeStruct((blocks, part, pairs), bf16),
             in_vmem,
-            after,
+            ready,
         )
         return own, swap(own)
 
@@ -276,7 +300,7 @@
             flops=2 * blocks * pairs * aux_dev * both,
         )
 
-    def total(keep, send):
+    def total(keep, send, marks):
         bit = 1
         while True:
             value = keep + flip(send, bit).astype(f32)
@@ -284,6 +308,7 @@
             if bit == n:
                 break
             keep, send = value[0::2], value[1::2].astype(bf16)
+            marks.append(send)
         near, order = value.astype(bf16), [0]
         while True:
             bit //= 2
@@ -293,7 +318,7 @@
                 return near, far, order
             near = jnp.concatenate([near, far], axis=0)
 
-    def apply(near, far, order, after):
+    def apply(near, far, order, ready):
         mine, theirs = call(
             functools.partial(apply_kernel, n, blocks, order),
             "apply",
@@ -304,33 +329,41 @@
                 jax.ShapeDtypeStruct((blocks, part, pairs), bf16),
             ],
             [in_vmem] * 2,
-            after,
+            ready,
             flops=2 * blocks * pairs * aux_dev * both,
         )
         return mine, swap(theirs)
 
-    def pack(mine, added):
+    def pack(mine, added, out_table, shapes):
         return call(
             functools.partial(scatter_coulomb_kernel, n, blocks, cap),
             "scatter_coulomb",
             out_table,
             [keeping, mine, added],
-            [jax.ShapeDtypeStruct((2 * cap, part, pairs), bf16)] * n,
-            [in_vmem] * n,
+            shapes,
+            [in_vmem] * len(shapes),
             scratch=[pltpu.VMEM((blocks, part, pairs), bf16)],
         )
 
-    fits = []
-    for chain in range(CHAINS):
-        fits.append(fit(*fetch(chain, fits[-1][:1] if fits else ())))
-    packed = []
-    for pieces in fits:
-        packed.append(pack(*apply(*total(*pieces), packed[-1][:1] if packed else ())))
-    received = [
-        out[d] if d == 0 else shift(out[d], d) for out in packed for d in range(n)
-    ]
+    def spread(x):
+        return lax.all_to_all(x, "pair", 0, 0, tiled=True)
+
+    first = [sends[0]]
+    for d in range(1, n):
+        first.append(shift(after(sends[d], integrals) if d > n - 3 else sends[d], d))
+    second = [spread(sends[n])]
+    marks = []
+    begun = fit(*fetch(first, pick_tables[0], ()))
+    found = total(*begun, marks)
+    begun = fit(*fetch(second, pick_tables[1], marks[:1]))
+    whole = [jax.ShapeDtypeStruct((n, 2 * cap, part, pairs), bf16)]
+    pieces = [jax.ShapeDtypeStruct((2 * cap, part, pairs), bf16)] * n
+    out = pack(*apply(*found, ()), out_tables[0], whole)
+    received = [spread(out[0])]
+    out = pack(*apply(*total(*begun, marks), out), out_tables[1], pieces)
+    received += [out[0]] + [shift(out[d], d) for d in range(1, n)]
     return call(
-        functools.partial(gather_coulomb_kernel, n, blocks, shell, cap),
+        functools.partial(gather_coulomb_kernel, n, blocks, shell, cap, (1, n)),
         "gather_coulomb",
         in_table,
         received,

time: 197 us -> 213 us (1.081)
  the two profiles are of different devices: /device:TPU:14 before, /device:TPU:13 now
where the time goes in v5:
time: 213 us
  waiting for transfers between devices  107 us (50%)
  starting transfers between devices  58.5 us (27%)
  Pallas kernels  25.1 us (12%)
  local copies, waits for them, and re-layouts  17.1 us (8%)
  other arithmetic  4.37 us (2%)
    ppermute x12, waiting for transfers between devices, flip(): return lax.ppermute(x, 'pair', [(s, s ^ bit) for s in range(n)])  68 us
    ppermute x14, waiting for transfers between devices, shift(): return lax.ppermute(x, 'pair', [(s, (s + d) % n) for s in range(n)])  36.3 us
    pallas_call x9, Pallas kernels, call(): pl.pallas_call(kernel, out_shape=out_shape, grid_spec=pltpu.PrefetchScala...  22.3 us
    ppermute x14, starting transfers between devices, shift(): return lax.ppermute(x, 'pair', [(s, (s + d) % n) for s in range(n)])  17.9 us
    unnamed x14, local copies, waits for them, and re-layouts  17 us
    ppermute x12, starting transfers between devices, flip(): return lax.ppermute(x, 'pair', [(s, s ^ bit) for s in range(n)])  15.3 us
    ppermute x4, starting transfers between devices, swap(): return lax.ppermute(x, 'aux', [(s, (s + 1) % cores) for s in range(cores)])  13.2 us
    all_to_all x2, starting transfers between devices, spread(): return lax.all_to_all(x, 'pair', 0, 0, tiled=True)  12.2 us
  transfers between devices with their start and end apart: 32, of which 19 were waited for; matrix products, arithmetic and copies ran while one was open for 1% of the time, Pallas kernels for 8%

profile of v5, /device:TPU:13, one launch (start us, length us, event | category | flops | bytes accessed | tf_op | source)
XLA Modules:
  0.0 212.9 jit_solution(5062219963951353590)
XLA Ops:
  12.8 5.2 %copy-done.3 = bf16[14,256,2048]{2,1,0:T(8,128)(2,1)S(1)} copy-done((bf16[14,256,2048]{2,1,0:T(8,128)(2,1)S(1)}, bf16[14,256,2048]{2,1,0:T(8,128)(2,1)}, u32[]{:S(2)}) %copy-start.3) | copy-done | bytes 14680088
  23.6 3.8 %collective-permute-done.5.rest_6_ = bf16[3,64,256]{2,1,0:T(8,128)(2,1)S(1)} collective-permute-done((bf16[3,64,256]{2,1,0:T(8,128)(2,1)S(1)}, bf16[3,64,256]{2,1,0:T(8,128)(2,1)S(1)}, u32[]{:S(2)}, u32[]{:S(2)}) %collective-permute-start.5) | collective-permute-done | bytes 98336 | tf_op jit(solution)/shard_map/ppermute | solution.py:205
  31.5 2.8 %fit.2 = (f32[4,128,256]{2,1,0:T(8,128)S(1)}, bf16[4,128,256]{2,1,0:T(8,128)(2,1)S(1)}) custom-call(s32[8]{0:T(128)S(1)} %iota_xor_fusion.table, bf16[14,1,256]{2,1,0:T(2,128)(2,1)S(1)} %copy.10.factor, bf16[14,64,256]{2,1,0:T(8,128)(2,1)S(1)} %gather_density.2.own, bf16[14,64,256]{2,1,0:T(8,128)(2,1)S(1)} %collective-permute-done.7.other, ...), custom_call_target="tpu_custom_call" | custom-call | flops 1879048192 | tf_op jit(solution)/shard_map/fit/pallas_call | solution.py:189
  34.4 5.8 %all-to-all-start.1 = ((bf16[8,3,64,256]{3,2,1,0:T(8,128)(2,1)}), bf16[8,3,64,256]{3,2,1,0:T(8,128)(2,1)S(1)}, u32[]{:S(2)}, u32[]{:S(2)}) async-start(bf16[8,3,64,256]{3,2,1,0:T(8,128)(2,1)} %get-tuple-element.43), calls=%async_computation.1 | async-start | bytes 1572864 | tf_op jit(solution)/shard_map/all_to_all | solution.py:349
  43.2 12.9 %collective-permute-done.9 = bf16[2,128,256]{2,1,0:T(8,128)(2,1)S(1)} collective-permute-done((bf16[2,128,256]{2,1,0:T(8,128)(2,1)S(1)}, bf16[2,128,256]{2,1,0:T(8,128)(2,1)S(1)}, u32[]{:S(2)}, u32[]{:S(2)}) %collective-permute-start.9) | collective-permute-done | bytes 131104 | tf_op jit(solution)/shard_map/ppermute | solution.py:208
  57.4 2.9 %collective-permute-done.10 = bf16[1,128,256]{2,1,0:T(8,128)(2,1)S(1)} collective-permute-done((bf16[1,128,256]{2,1,0:T(8,128)(2,1)S(1)}, bf16[1,128,256]{2,1,0:T(8,128)(2,1)S(1)}, u32[]{:S(2)}, u32[]{:S(2)}) %collective-permute-start.10) | collective-permute-done | bytes 65568 | tf_op jit(solution)/shard_map/ppermute | solution.py:208
  61.5 2.9 %collective-permute-done.11 = bf16[1,128,256]{2,1,0:T(8,128)(2,1)S(1)} collective-permute-done((bf16[1,128,256]{2,1,0:T(8,128)(2,1)S(1)}, bf16[1,128,256]{2,1,0:T(8,128)(2,1)S(1)}, u32[]{:S(2)}, u32[]{:S(2)}) %collective-permute-start.11) | collective-permute-done | bytes 65568 | tf_op jit(solution)/shard_map/ppermute | solution.py:208
  66.4 3.1 %collective-permute-done.12 = bf16[2,128,256]{2,1,0:T(8,128)(2,1)S(1)} collective-permute-done((bf16[2,128,256]{2,1,0:T(8,128)(2,1)S(1)}, bf16[2,128,256]{2,1,0:T(8,128)(2,1)S(1)}, u32[]{:S(2)}, u32[]{:S(2)}) %collective-permute-start.12) | collective-permute-done | bytes 131104 | tf_op jit(solution)/shard_map/ppermute | solution.py:208
  70.8 4.1 %collective-permute-start.15 = (bf16[14,64,256]{2,1,0:T(8,128)(2,1)S(1)}, bf16[14,64,256]{2,1,0:T(8,128)(2,1)S(1)}, u32[]{:S(2)}, u32[]{:S(2)}) collective-permute-start(bf16[14,64,256]{2,1,0:T(8,128)(2,1)S(1)} %gather_density.3.own), channel_id=1, source_target_pairs={{0,1},{1,0},{2,3},{3,2},{4,5},{5,4},{6,7},{7,6},{8,9},{9,8},{10,11... | collective-permute-start | bytes 1376264 | tf_op jit(solution)/shard_map/ppermute | solution.py:214
  74.9 5.2 %copy-done.1 = bf16[14,256,2048]{2,1,0:T(8,128)(2,1)S(1)} copy-done((bf16[14,256,2048]{2,1,0:T(8,128)(2,1)S(1)}, bf16[14,256,2048]{2,1,0:T(8,128)(2,1)}, u32[]{:S(2)}) %copy-start.1) | copy-done | bytes 14680088
  80.1 4.6 %apply.2 = (f32[14,64,256]{2,1,0:T(8,128)S(1)}, bf16[14,64,256]{2,1,0:T(8,128)(2,1)S(1)}) custom-call(s32[8]{0:T(128)S(1)} %iota_xor_fusion.table, bf16[14,256,2048]{2,1,0:T(8,128)(2,1)S(1)} %copy-done.1, bf16[4,128,256]{2,1,0:T(8,128)(2,1)S(1)} %pad_maximum_fusion.near, bf16[4,128,256]{2,1,0:T(8,128)(2,1)S(1)} %collective-permute-done.13.far), custom_call_target="tpu_custom_call" | custom-call | flops 1879048192 | tf_op jit(solution)/shard_map/apply/pallas_call | solution.py:189
  84.7 5.3 %collective-permute-start.14 = (bf16[14,64,256]{2,1,0:T(8,128)(2,1)S(1)}, bf16[14,64,256]{2,1,0:T(8,128)(2,1)S(1)}, u32[]{:S(2)}, u32[]{:S(2)}) collective-permute-start(bf16[14,64,256]{2,1,0:T(8,128)(2,1)S(1)} %get-tuple-element.42), channel_id=1, source_target_pairs={{0,1},{1,0},{2,3},{3,2},{4,5},{5,4},{6,7},{7,6},{8,9},{9,8},{10,11... | collective-permute-start | bytes 1376264 | tf_op jit(solution)/shard_map/ppermute | solution.py:214
  90.1 2.8 %fit.3 = (f32[4,128,256]{2,1,0:T(8,128)S(1)}, bf16[4,128,256]{2,1,0:T(8,128)(2,1)S(1)}) custom-call(s32[8]{0:T(128)S(1)} %iota_xor_fusion.table, bf16[14,1,256]{2,1,0:T(2,128)(2,1)S(1)} %copy.10.factor, bf16[14,64,256]{2,1,0:T(8,128)(2,1)S(1)} %gather_density.3.own, bf16[14,64,256]{2,1,0:T(8,128)(2,1)S(1)} %collective-permute-done.15.other, ...), custom_call_target="tpu_custom_call" | custom-call | flops 1879048192 | tf_op jit(solution)/shard_map/fit/pallas_call | solution.py:189
  95.1 6.4 %all-to-all-start = ((bf16[8,6,64,256]{3,2,1,0:T(8,128)(2,1)}), bf16[8,6,64,256]{3,2,1,0:T(8,128)(2,1)S(1)}, u32[]{:S(2)}, u32[]{:S(2)}) async-start(bf16[8,6,64,256]{3,2,1,0:T(8,128)(2,1)} %scatter_coulomb.2.rest_0_), calls=%async_computation | async-start | bytes 3145728 | tf_op jit(solution)/shard_map/all_to_all | solution.py:349
  102.9 28.6 %collective-permute-done.17 = bf16[2,128,256]{2,1,0:T(8,128)(2,1)S(1)} collective-permute-done((bf16[2,128,256]{2,1,0:T(8,128)(2,1)S(1)}, bf16[2,128,256]{2,1,0:T(8,128)(2,1)S(1)}, u32[]{:S(2)}, u32[]{:S(2)}) %collective-permute-start.17) | collective-permute-done | bytes 131104 | tf_op jit(solution)/shard_map/ppermute | solution.py:208
  132.0 6.7 %collective-permute-done.18 = bf16[1,128,256]{2,1,0:T(8,128)(2,1)S(1)} collective-permute-done((bf16[1,128,256]{2,1,0:T(8,128)(2,1)S(1)}, bf16[1,128,256]{2,1,0:T(8,128)(2,1)S(1)}, u32[]{:S(2)}, u32[]{:S(2)}) %collective-permute-start.18) | collective-permute-done | bytes 65568 | tf_op jit(solution)/shard_map/ppermute | solution.py:208
  138.7 3.2 %collective-permute-start.19 = (bf16[1,128,256]{2,1,0:T(8,128)(2,1)S(1)}, bf16[1,128,256]{2,1,0:T(8,128)(2,1)S(1)}, u32[]{:S(2)}, u32[]{:S(2)}) collective-permute-start(bf16[1,128,256]{2,1,0:T(8,128)(2,1)S(1)} %fusion), channel_id=1, source_target_pairs={{0,8},{2,10},{4,12},{6,14},{8,0},{10,2},{12,4},{14,6},{1,9},{3,11}... | collective-permute-start | bytes 196616 | tf_op jit(solution)/shard_map/ppermute | solution.py:208
  150.7 4.6 %collective-permute-done.21.far = bf16[4,128,256]{2,1,0:T(8,128)(2,1)S(1)} collective-permute-done((bf16[4,128,256]{2,1,0:T(8,128)(2,1)S(1)}, bf16[4,128,256]{2,1,0:T(8,128)(2,1)S(1)}, u32[]{:S(2)}, u32[]{:S(2)}) %collective-permute-start.21) | collective-permute-done | bytes 262176 | tf_op jit(solution)/shard_map/ppermute | solution.py:208
  155.3 5.2 %copy-done.2 = bf16[14,256,2048]{2,1,0:T(8,128)(2,1)S(1)} copy-done((bf16[14,256,2048]{2,1,0:T(8,128)(2,1)S(1)}, bf16[14,256,2048]{2,1,0:T(8,128)(2,1)}, u32[]{:S(2)}) %copy-start.2) | copy-done | bytes 14680088
  160.5 4.6 %apply.3 = (f32[14,64,256]{2,1,0:T(8,128)S(1)}, bf16[14,64,256]{2,1,0:T(8,128)(2,1)S(1)}) custom-call(s32[8]{0:T(128)S(1)} %iota_xor_fusion.table, bf16[14,256,2048]{2,1,0:T(8,128)(2,1)S(1)} %copy-done.2, bf16[4,128,256]{2,1,0:T(8,128)(2,1)S(1)} %pad_maximum_fusion.1.near, bf16[4,128,256]{2,1,0:T(8,128)(2,1)S(1)} %collective-permute-done.21.far, ...), custom_call_target="tpu_custom_call" | custom-call | flops 1879048192 | tf_op jit(solution)/shard_map/apply/pallas_call | solution.py:189
  181.8 18.9 %collective-permute-done.25.rest_4_ = bf16[6,64,256]{2,1,0:T(8,128)(2,1)S(1)} collective-permute-done((bf16[6,64,256]{2,1,0:T(8,128)(2,1)S(1)}, bf16[6,64,256]{2,1,0:T(8,128)(2,1)S(1)}, u32[]{:S(2)}, u32[]{:S(2)}) %collective-permute-start.25) | collective-permute-done | bytes 196640 | tf_op jit(solution)/shard_map/ppermute | solution.py:205
  200.7 4.2 %collective-permute-done.26.rest_5_ = bf16[6,64,256]{2,1,0:T(8,128)(2,1)S(1)} collective-permute-done((bf16[6,64,256]{2,1,0:T(8,128)(2,1)S(1)}, bf16[6,64,256]{2,1,0:T(8,128)(2,1)S(1)}, u32[]{:S(2)}, u32[]{:S(2)}) %collective-permute-start.26) | collective-permute-done | bytes 196640 | tf_op jit(solution)/shard_map/ppermute | solution.py:205
  204.9 4.5 %collective-permute-done.28.rest_7_ = bf16[6,64,256]{2,1,0:T(8,128)(2,1)S(1)} collective-permute-done((bf16[6,64,256]{2,1,0:T(8,128)(2,1)S(1)}, bf16[6,64,256]{2,1,0:T(8,128)(2,1)S(1)}, u32[]{:S(2)}, u32[]{:S(2)}) %collective-permute-start.28) | collective-permute-done | bytes 196640 | tf_op jit(solution)/shard_map/ppermute | solution.py:205
  209.4 3.3 %gather_coulomb.1 = (bf16[14,256,128]{2,1,0:T(8,128)(2,1)}, bf16[14,256,128]{2,1,0:T(8,128)(2,1)}) custom-call(s32[96]{0:T(128)S(1)} %pad_add_fusion.table, bf16[8,6,64,256]{3,2,1,0:T(8,128)(2,1)S(1)} %all-to-all-done.rest_0_, bf16[6,64,256]{2,1,0:T(8,128)(2,1)S(1)} %get-tuple-element.48.rest_1_, bf16[6,64,256]{2,1,0:T(8,128)(2,1)S(1)} %collective-permute-done.23.rest_2_, ...), custom_call_target="tpu_custom_call" | custom-call | tf_op jit(solution)/shard_map/gather_coulomb/pallas_call | solution.py:189
  (108 shorter events, 60.2 us)
Async XLA Ops:
  7.0 12.0 %collective-permute-start = (bf16[3,64,256]{2,1,0:T(8,128)(2,1)S(1)}, bf16[3,64,256]{2,1,0:T(8,128)(2,1)S(1)}, u32[]{:S(2)}, u32[]{:S(2)}) collective-permute-start(bf16[3,64,256]{2,1,0:T(8,128)(2,1)S(1)} %get-tuple-element.30), channel_id=1, source_target_pairs={{0,2},{2,4},{4,6},{6,8},{8,10},{10,12},{12,14},{14,0},{1,3},{3,5},... | collective-permute-start | bytes 294920 | tf_op jit(solution)/shard_map/ppermute | solution.py:205
  8.2 12.0 %collective-permute-start.1 = (bf16[3,64,256]{2,1,0:T(8,128)(2,1)S(1)}, bf16[3,64,256]{2,1,0:T(8,128)(2,1)S(1)}, u32[]{:S(2)}, u32[]{:S(2)}) collective-permute-start(bf16[3,64,256]{2,1,0:T(8,128)(2,1)S(1)} %get-tuple-element.31), channel_id=1, source_target_pairs={{0,4},{2,6},{4,8},{6,10},{8,12},{10,14},{12,0},{14,2},{1,5},{3,7},... | collective-permute-start | bytes 294920 | tf_op jit(solution)/shard_map/ppermute | solution.py:205
  9.5 12.3 %collective-permute-start.2 = (bf16[3,64,256]{2,1,0:T(8,128)(2,1)S(1)}, bf16[3,64,256]{2,1,0:T(8,128)(2,1)S(1)}, u32[]{:S(2)}, u32[]{:S(2)}) collective-permute-start(bf16[3,64,256]{2,1,0:T(8,128)(2,1)S(1)} %get-tuple-element.32), channel_id=1, source_target_pairs={{0,6},{2,8},{4,10},{6,12},{8,14},{10,0},{12,2},{14,4},{1,7},{3,9},... | collective-permute-start | bytes 294920 | tf_op jit(solution)/shard_map/ppermute | solution.py:205
  10.5 13.1 %collective-permute-start.3 = (bf16[3,64,256]{2,1,0:T(8,128)(2,1)S(1)}, bf16[3,64,256]{2,1,0:T(8,128)(2,1)S(1)}, u32[]{:S(2)}, u32[]{:S(2)}) collective-permute-start(bf16[3,64,256]{2,1,0:T(8,128)(2,1)S(1)} %get-tuple-element.33), channel_id=1, source_target_pairs={{0,8},{2,10},{4,12},{6,14},{8,0},{10,2},{12,4},{14,6},{1,9},{3,11}... | collective-permute-start | bytes 294920 | tf_op jit(solution)/shard_map/ppermute | solution.py:205
  11.8 11.8 %collective-permute-start.4 = (bf16[3,64,256]{2,1,0:T(8,128)(2,1)S(1)}, bf16[3,64,256]{2,1,0:T(8,128)(2,1)S(1)}, u32[]{:S(2)}, u32[]{:S(2)}) collective-permute-start(bf16[3,64,256]{2,1,0:T(8,128)(2,1)S(1)} %get-tuple-element.34), channel_id=1, source_target_pairs={{0,10},{2,12},{4,14},{6,0},{8,2},{10,4},{12,6},{14,8},{1,11},{3,13... | collective-permute-start | bytes 294920 | tf_op jit(solution)/shard_map/ppermute | solution.py:205
  19.0 8.3 %collective-permute-start.5 = (bf16[3,64,256]{2,1,0:T(8,128)(2,1)S(1)}, bf16[3,64,256]{2,1,0:T(8,128)(2,1)S(1)}, u32[]{:S(2)}, u32[]{:S(2)}) collective-permute-start(bf16[3,64,256]{2,1,0:T(8,128)(2,1)S(1)} %get-tuple-element.36), channel_id=1, source_target_pairs={{0,12},{2,14},{4,0},{6,2},{8,4},{10,6},{12,8},{14,10},{1,13},{3,15... | collective-permute-start | bytes 294920 | tf_op jit(solution)/shard_map/ppermute | solution.py:205
  20.2 8.0 %collective-permute-start.6 = (bf16[3,64,256]{2,1,0:T(8,128)(2,1)S(1)}, bf16[3,64,256]{2,1,0:T(8,128)(2,1)S(1)}, u32[]{:S(2)}, u32[]{:S(2)}) collective-permute-start(bf16[3,64,256]{2,1,0:T(8,128)(2,1)S(1)} %get-tuple-element.38), channel_id=1, source_target_pairs={{0,14},{2,0},{4,2},{6,4},{8,6},{10,8},{12,10},{14,12},{1,15},{3,1}... | collective-permute-start | bytes 294920 | tf_op jit(solution)/shard_map/ppermute | solution.py:205
  34.3 7.6 %collective-permute-start.8 = (bf16[4,128,256]{2,1,0:T(8,128)(2,1)S(1)}, bf16[4,128,256]{2,1,0:T(8,128)(2,1)S(1)}, u32[]{:S(2)}, u32[]{:S(2)}) collective-permute-start(bf16[4,128,256]{2,1,0:T(8,128)(2,1)S(1)} %get-tuple-element.40), channel_id=1, source_target_pairs={{0,2},{2,0},{4,6},{6,4},{8,10},{10,8},{12,14},{14,12},{1,3},{3,1},... | collective-permute-start | bytes 786440 | tf_op jit(solution)/shard_map/ppermute | solution.py:208
  34.4 35.7 %all-to-all-start.1 = ((bf16[8,3,64,256]{3,2,1,0:T(8,128)(2,1)}), bf16[8,3,64,256]{3,2,1,0:T(8,128)(2,1)S(1)}, u32[]{:S(2)}, u32[]{:S(2)}) async-start(bf16[8,3,64,256]{3,2,1,0:T(8,128)(2,1)} %get-tuple-element.43), calls=%async_computation.1 | async-start | bytes 1572864 | tf_op jit(solution)/shard_map/all_to_all | solution.py:349
  42.0 14.2 %collective-permute-start.9 = (bf16[2,128,256]{2,1,0:T(8,128)(2,1)S(1)}, bf16[2,128,256]{2,1,0:T(8,128)(2,1)S(1)}, u32[]{:S(2)}, u32[]{:S(2)}) collective-permute-start(bf16[2,128,256]{2,1,0:T(8,128)(2,1)S(1)} %slice.41.rest_1_), channel_id=1, source_target_pairs={{0,4},{2,6},{4,0},{6,2},{8,12},{10,14},{12,8},{14,10},{1,5},{3,7},... | collective-permute-start | bytes 393224 | tf_op jit(solution)/shard_map/ppermute | solution.py:208
  70.8 19.3 %collective-permute-start.15 = (bf16[14,64,256]{2,1,0:T(8,128)(2,1)S(1)}, bf16[14,64,256]{2,1,0:T(8,128)(2,1)S(1)}, u32[]{:S(2)}, u32[]{:S(2)}) collective-permute-start(bf16[14,64,256]{2,1,0:T(8,128)(2,1)S(1)} %gather_density.3.own), channel_id=1, source_target_pairs={{0,1},{1,0},{2,3},{3,2},{4,5},{5,4},{6,7},{7,6},{8,9},{9,8},{10,11... | collective-permute-start | bytes 1376264 | tf_op jit(solution)/shard_map/ppermute | solution.py:214
  84.7 8.5 %collective-permute-start.14 = (bf16[14,64,256]{2,1,0:T(8,128)(2,1)S(1)}, bf16[14,64,256]{2,1,0:T(8,128)(2,1)S(1)}, u32[]{:S(2)}, u32[]{:S(2)}) collective-permute-start(bf16[14,64,256]{2,1,0:T(8,128)(2,1)S(1)} %get-tuple-element.42), channel_id=1, source_target_pairs={{0,1},{1,0},{2,3},{3,2},{4,5},{5,4},{6,7},{7,6},{8,9},{9,8},{10,11... | collective-permute-start | bytes 1376264 | tf_op jit(solution)/shard_map/ppermute | solution.py:214
  92.9 8.6 %collective-permute-start.16 = (bf16[4,128,256]{2,1,0:T(8,128)(2,1)S(1)}, bf16[4,128,256]{2,1,0:T(8,128)(2,1)S(1)}, u32[]{:S(2)}, u32[]{:S(2)}) collective-permute-start(bf16[4,128,256]{2,1,0:T(8,128)(2,1)S(1)} %get-tuple-element.45), channel_id=1, source_target_pairs={{0,2},{2,0},{4,6},{6,4},{8,10},{10,8},{12,14},{14,12},{1,3},{3,1},... | collective-permute-start | bytes 786440 | tf_op jit(solution)/shard_map/ppermute | solution.py:208
  95.1 114.4 %all-to-all-start = ((bf16[8,6,64,256]{3,2,1,0:T(8,128)(2,1)}), bf16[8,6,64,256]{3,2,1,0:T(8,128)(2,1)S(1)}, u32[]{:S(2)}, u32[]{:S(2)}) async-start(bf16[8,6,64,256]{3,2,1,0:T(8,128)(2,1)} %scatter_coulomb.2.rest_0_), calls=%async_computation | async-start | bytes 3145728 | tf_op jit(solution)/shard_map/all_to_all | solution.py:349
  101.6 29.9 %collective-permute-start.17 = (bf16[2,128,256]{2,1,0:T(8,128)(2,1)S(1)}, bf16[2,128,256]{2,1,0:T(8,128)(2,1)S(1)}, u32[]{:S(2)}, u32[]{:S(2)}) collective-permute-start(bf16[2,128,256]{2,1,0:T(8,128)(2,1)S(1)} %slice.45), channel_id=1, source_target_pairs={{0,4},{2,6},{4,0},{6,2},{8,12},{10,14},{12,8},{14,10},{1,5},{3,7},... | collective-permute-start | bytes 393224 | tf_op jit(solution)/shard_map/ppermute | solution.py:208
  131.6 7.2 %collective-permute-start.18 = (bf16[1,128,256]{2,1,0:T(8,128)(2,1)S(1)}, bf16[1,128,256]{2,1,0:T(8,128)(2,1)S(1)}, u32[]{:S(2)}, u32[]{:S(2)}) collective-permute-start(bf16[1,128,256]{2,1,0:T(8,128)(2,1)S(1)} %slice.64), channel_id=1, source_target_pairs={{0,8},{2,10},{4,12},{6,14},{8,0},{10,2},{12,4},{14,6},{1,9},{3,11}... | collective-permute-start | bytes 196616 | tf_op jit(solution)/shard_map/ppermute | solution.py:208
  148.6 6.7 %collective-permute-start.21 = (bf16[4,128,256]{2,1,0:T(8,128)(2,1)S(1)}, bf16[4,128,256]{2,1,0:T(8,128)(2,1)S(1)}, u32[]{:S(2)}, u32[]{:S(2)}) collective-permute-start(bf16[4,128,256]{2,1,0:T(8,128)(2,1)S(1)} %pad_maximum_fusion.1.near), channel_id=1, source_target_pairs={{0,2},{2,0},{4,6},{6,4},{8,10},{10,8},{12,14},{14,12},{1,3},{3,1},... | collective-permute-start | bytes 786440 | tf_op jit(solution)/shard_map/ppermute | solution.py:208
  170.0 7.4 %collective-permute-start.23 = (bf16[6,64,256]{2,1,0:T(8,128)(2,1)S(1)}, bf16[6,64,256]{2,1,0:T(8,128)(2,1)S(1)}, u32[]{:S(2)}, u32[]{:S(2)}) collective-permute-start(bf16[6,64,256]{2,1,0:T(8,128)(2,1)S(1)} %get-tuple-element.49), channel_id=1, source_target_pairs={{0,2},{2,4},{4,6},{6,8},{8,10},{10,12},{12,14},{14,0},{1,3},{3,5},... | collective-permute-start | bytes 589832 | tf_op jit(solution)/shard_map/ppermute | solution.py:205
  171.5 10.1 %collective-permute-start.24 = (bf16[6,64,256]{2,1,0:T(8,128)(2,1)S(1)}, bf16[6,64,256]{2,1,0:T(8,128)(2,1)S(1)}, u32[]{:S(2)}, u32[]{:S(2)}) collective-permute-start(bf16[6,64,256]{2,1,0:T(8,128)(2,1)S(1)} %get-tuple-element.50), channel_id=1, source_target_pairs={{0,4},{2,6},{4,8},{6,10},{8,12},{10,14},{12,0},{14,2},{1,5},{3,7},... | collective-permute-start | bytes 589832 | tf_op jit(solution)/shard_map/ppermute | solution.py:205
  172.7 28.0 %collective-permute-start.25 = (bf16[6,64,256]{2,1,0:T(8,128)(2,1)S(1)}, bf16[6,64,256]{2,1,0:T(8,128)(2,1)S(1)}, u32[]{:S(2)}, u32[]{:S(2)}) collective-permute-start(bf16[6,64,256]{2,1,0:T(8,128)(2,1)S(1)} %get-tuple-element.51), channel_id=1, source_target_pairs={{0,6},{2,8},{4,10},{6,12},{8,14},{10,0},{12,2},{14,4},{1,7},{3,9},... | collective-permute-start | bytes 589832 | tf_op jit(solution)/shard_map/ppermute | solution.py:205
  174.8 30.1 %collective-permute-start.26 = (bf16[6,64,256]{2,1,0:T(8,128)(2,1)S(1)}, bf16[6,64,256]{2,1,0:T(8,128)(2,1)S(1)}, u32[]{:S(2)}, u32[]{:S(2)}) collective-permute-start(bf16[6,64,256]{2,1,0:T(8,128)(2,1)S(1)} %get-tuple-element.52), channel_id=1, source_target_pairs={{0,8},{2,10},{4,12},{6,14},{8,0},{10,2},{12,4},{14,6},{1,9},{3,11}... | collective-permute-start | bytes 589832 | tf_op jit(solution)/shard_map/ppermute | solution.py:205
  175.2 29.6 %collective-permute-start.27 = (bf16[6,64,256]{2,1,0:T(8,128)(2,1)S(1)}, bf16[6,64,256]{2,1,0:T(8,128)(2,1)S(1)}, u32[]{:S(2)}, u32[]{:S(2)}) collective-permute-start(bf16[6,64,256]{2,1,0:T(8,128)(2,1)S(1)} %get-tuple-element.53), channel_id=1, source_target_pairs={{0,10},{2,12},{4,14},{6,0},{8,2},{10,4},{12,6},{14,8},{1,11},{3,13... | collective-permute-start | bytes 589832 | tf_op jit(solution)/shard_map/ppermute | solution.py:205
  177.4 32.0 %collective-permute-start.28 = (bf16[6,64,256]{2,1,0:T(8,128)(2,1)S(1)}, bf16[6,64,256]{2,1,0:T(8,128)(2,1)S(1)}, u32[]{:S(2)}, u32[]{:S(2)}) collective-permute-start(bf16[6,64,256]{2,1,0:T(8,128)(2,1)S(1)} %get-tuple-element.54), channel_id=1, source_target_pairs={{0,12},{2,14},{4,0},{6,2},{8,4},{10,6},{12,8},{14,10},{1,13},{3,15... | collective-permute-start | bytes 589832 | tf_op jit(solution)/shard_map/ppermute | solution.py:205
  181.6 27.8 %collective-permute-start.29 = (bf16[6,64,256]{2,1,0:T(8,128)(2,1)S(1)}, bf16[6,64,256]{2,1,0:T(8,128)(2,1)S(1)}, u32[]{:S(2)}, u32[]{:S(2)}) collective-permute-start(bf16[6,64,256]{2,1,0:T(8,128)(2,1)S(1)} %get-tuple-element.55), channel_id=1, source_target_pairs={{0,14},{2,0},{4,2},{6,4},{8,6},{10,8},{12,10},{14,12},{1,15},{3,1}... | collective-permute-start | bytes 589832 | tf_op jit(solution)/shard_map/ppermute | solution.py:205
  (15 other events, 91.6 us)

commit v6 on v4

v6 whole, which is shorter than its diff:
```python
import functools
import math

import jax
import jax.numpy as jnp
from jax import lax
from jax.experimental import pallas as pl
from jax.experimental.pallas import tpu as pltpu
from jax.sharding import PartitionSpec as P

VMEM_BYTES = 20 * 1024 * 1024


def tables(slots, devices, blocks_dev, me):
    total = slots.shape[0]
    numbers = jnp.arange(total, dtype=jnp.int32)
    source = numbers // blocks_dev
    target = slots // blocks_dev
    joined = source * devices + target
    earlier = (joined[:, None] == joined[None, :]) & (numbers[None, :] < numbers[:, None])
    rank = jnp.sum(earlier.astype(jnp.int32), axis=1)
    own_target = lax.dynamic_slice_in_dim(target, me * blocks_dev, blocks_dev, 0)
    own_rank = lax.dynamic_slice_in_dim(rank, me * blocks_dev, blocks_dev, 0)
    rows = me * blocks_dev + jnp.arange(blocks_dev, dtype=jnp.int32)
    hot = slots[None, :] == rows[:, None]
    row_source = jnp.sum(jnp.where(hot, source[None, :], 0), axis=1)
    row_rank = jnp.sum(jnp.where(hot, rank[None, :], 0), axis=1)
    return own_target, own_rank, row_source, row_rank


def slots_of(steps, ranks, devices, cap):
    held = (steps * cap + ranks)[None, :] == jnp.arange(devices * cap, dtype=jnp.int32)[:, None]
    numbers = jnp.arange(steps.shape[0], dtype=jnp.int32)
    return jnp.max(jnp.where(held, numbers[None, :], -1), axis=1)


def load_kernel(source, target, sem):
    copy = pltpu.make_async_copy(source, target, sem)
    copy.start()
    copy.wait()


def scatter_density_kernel(devices, blocks, cap, table, density, *rest):
    sends, turned = rest[:devices], rest[-1]
    for row in range(blocks):
        turned[row] = density[row].T
    for step in range(devices):
        for rank in range(cap):
            row = jnp.maximum(table[step * cap + rank], 0)
            sends[step][rank] = turned[row]


def gather_density_kernel(devices, cap, table, *rest):
    received, out = rest[:devices], rest[-1]
    for step in range(devices):
        for rank in range(cap):
            row = table[step * cap + rank]

            @pl.when(row >= 0)
            def _():
                out[row] = received[step][rank]


def fit_kernel(bits, blocks, table, factor, density, integrals, *rest):
    keep, send = rest[-2:]
    width = keep.shape[2]
    pairs = integrals.shape[1]
    fitted = jnp.concatenate([density[b] * factor[b] for b in range(blocks)], axis=1)
    for i in range(keep.shape[0]):
        e = sum(bit for j, bit in enumerate(bits[1:]) if i >> j & 1)
        for relative, out in ((e ^ bits[0], send), (e, keep)):
            at = pl.ds(pl.multiple_of(table[relative] * width, width), width)
            out[i] = jnp.dot(
                fitted,
                integrals[:, :, at].reshape(blocks * pairs, width),
                preferred_element_type=jnp.float32,
            ).astype(out.dtype)


def apply_kernel(orders, some, table, integrals, near, far, near_other, far_other, own, other):
    blocks, pairs, half = integrals.shape[0], integrals.shape[1], own.shape[1]
    count, _, width = near.shape
    chunks = []
    for order, low, high in ((orders[0], near, far), (orders[1], near_other, far_other)):
        chunks.append({e: (low, i) if i < count else (high, i - count) for i, e in enumerate(order)})
    for first in range(0, blocks, some):
        total = None
        for e in range(2 * count):
            at = pl.ds(pl.multiple_of(table[e] * width, width), width)
            term = lax.dot_general(
                integrals[first : first + some, :, at].reshape(some * pairs, width),
                jnp.concatenate([piece[e][0][piece[e][1]] for piece in chunks], axis=0),
                (((1,), (1,)), ((), ())),
                preferred_element_type=jnp.float32,
            )
            total = term if total is None else total + term
        for b in range(some):
            value = total[b * pairs : (b + 1) * pairs].T
            own[first + b] = value[:half]
            other[first + b] = value[half:].astype(other.dtype)


def scatter_coulomb_kernel(devices, blocks, cap, table, screen, own, other, *rest):
    sends, ready = rest[:devices], rest[devices]
    for b in range(blocks):
        value = (own[b] + other[b].astype(jnp.float32)) * screen[b]
        ready[b] = value.astype(jnp.bfloat16)
    for group in range(2):
        for step in range(devices):
            for rank in range(cap):
                b = jnp.maximum(table[(group * devices + step) * cap + rank], 0)
                sends[step][group * cap + rank] = ready[b]


def gather_coulomb_kernel(devices, blocks, shell, cap, table, *rest):
    received = rest[:devices]
    rows, cols, landed, done, sems = rest[devices:]
    pairs = landed.shape[3]
    for group in range(2):
        for step in range(devices):
            for rank in range(cap):
                row = table[(group * devices + step) * cap + rank]

                @pl.when(row >= 0)
                def _():
                    landed[group, row] = received[step][group * cap + rank]

    to = lax.broadcasted_iota(jnp.int32, (pairs, pairs), 0)
    source = lax.broadcasted_iota(jnp.int32, (pairs, pairs), 1)
    turns = (to, (to % shell) * shell + to // shell)
    copies = []
    for group in range(2):
        turn = (source == turns[group]).astype(jnp.bfloat16)
        for row in range(blocks):
            done[group, row] = lax.dot_general(
                turn,
                landed[group, row],
                (((1,), (1,)), ((), ())),
                preferred_element_type=jnp.float32,
            ).astype(jnp.bfloat16)
            copy = pltpu.make_async_copy(
                done.at[group, row], (rows, cols)[group].at[row], sems.at[group, row]
            )
            copy.start()
            copies.append(copy)
    for copy in copies:
        copy.wait()


def local(three_index, density, screen, pair_shells, home_slot, mirror_slot):
    blocks, pairs, aux_dev = three_index.shape
    ndens = density.shape[2]
    shell = math.isqrt(pairs)
    n = lax.axis_size("pair")
    cores = lax.axis_size("aux")
    me = lax.axis_index("pair")
    core = lax.axis_index("aux")
    half = ndens // cores
    width = aux_dev // n
    cap = 2 + (blocks - 1) // n
    bf16, f32 = jnp.bfloat16, jnp.float32
    in_vmem = pl.BlockSpec(memory_space=pltpu.VMEM)
    anywhere = pl.BlockSpec(memory_space=pl.ANY)
    ints = functools.partial(jnp.concatenate, axis=0)

    def call(kernel, name, table, args, out_shape, out_specs, ready=(), scratch=()):
        return pl.pallas_call(
            kernel,
            out_shape=out_shape,
            grid_spec=pltpu.PrefetchScalarGridSpec(
                num_scalar_prefetch=1,
                grid=(),
                in_specs=[in_vmem] * len(args) + [anywhere] * len(ready),
                out_specs=out_specs,
                scratch_shapes=list(scratch),
            ),
            compiler_params=pltpu.CompilerParams(vmem_limit_bytes=VMEM_BYTES),
            name=name,
        )(table, *args, *ready)

    def shift(x, d):
        return lax.ppermute(x, "pair", [(s, (s + d) % n) for s in range(n)])

    def flip(x, bit):
        return lax.ppermute(x, "pair", [(s, s ^ bit) for s in range(n)])

    def swap(x):
        return lax.ppermute(x, "aux", [(s, (s + 1) % cores) for s in range(cores)])

    def after(x, *others):
        return lax.optimization_barrier((x, *others))[0]

    home_target, home_rank, home_source, home_row_rank = tables(home_slot, n, blocks, me)
    mirror_target, mirror_rank, mirror_source, mirror_row_rank = tables(
        mirror_slot, n, blocks, me
    )
    held = functools.partial(slots_of, devices=n, cap=cap)
    send_table = ints([held((home_source - me) % n, home_row_rank), core[None].astype(jnp.int32)])
    pick_table = held((me - home_target) % n, home_rank)
    chunk_table = me ^ jnp.arange(n, dtype=jnp.int32)
    out_table = ints(
        [
            held((home_target - me) % n, home_rank),
            held((mirror_target - me) % n, mirror_rank),
        ]
    )
    in_table = ints(
        [held((me - home_source) % n, home_row_rank), held((me - mirror_source) % n, mirror_row_rank)]
    )
    weight = jnp.where(pair_shells[:, 0] != pair_shells[:, 1], 2.0, 1.0)
    factor = (screen.astype(f32) * weight[:, None]).astype(bf16)[:, None, :]
    keeping = screen.astype(f32)[:, None, :]

    integrals = pl.pallas_call(
        load_kernel,
        out_shape=pltpu.VMEM((blocks, pairs, aux_dev), bf16),
        in_specs=[anywhere],
        out_specs=in_vmem,
        scratch_shapes=[pltpu.SemaphoreType.DMA],
        compiler_params=pltpu.CompilerParams(vmem_limit_bytes=2 * 1024 * 1024),
        name="load_integrals",
    )(three_index)

    sends = pl.pallas_call(
        functools.partial(scatter_density_kernel, n, blocks, cap),
        out_shape=[jax.ShapeDtypeStruct((cap, half, pairs), bf16)] * n,
        grid_spec=pltpu.PrefetchScalarGridSpec(
            num_scalar_prefetch=1,
            grid=(1,),
            in_specs=[pl.BlockSpec((blocks, pairs, half), lambda i, t: (0, 0, t[n * cap]))],
            out_specs=[pl.BlockSpec((cap, half, pairs), lambda i, t: (0, 0, 0))] * n,
            scratch_shapes=[pltpu.VMEM((blocks, half, pairs), bf16)],
        ),
        compiler_params=pltpu.CompilerParams(vmem_limit_bytes=VMEM_BYTES),
        name="scatter_density",
    )(send_table, density)
    received = [sends[0]] + [
        shift(after(sends[d], integrals) if d > n - 3 else sends[d], d) for d in range(1, n)
    ]
    own = call(
        functools.partial(gather_density_kernel, n, cap),
        "gather_density",
        pick_table,
        received,
        jax.ShapeDtypeStruct((blocks, half, pairs), bf16),
        in_vmem,
    )
    other = swap(own)

    bits = [1 << j for j in range(n.bit_length() - 1)]
    orders = (bits, bits[1::-1] + bits[2:])

    def fit(value, bits, ready=()):
        return call(
            functools.partial(fit_kernel, bits, blocks),
            "fit",
            chunk_table,
            [factor, value, integrals],
            [
                jax.ShapeDtypeStruct((n // 2, half, width), f32),
                jax.ShapeDtypeStruct((n // 2, half, width), bf16),
            ],
            [in_vmem] * 2,
            ready,
        )

    def step_together(states):
        flat, tree = jax.tree.flatten(states)
        return jax.tree.unflatten(tree, lax.optimization_barrier(flat))

    def totals(states):
        for j in range(len(bits)):
            states = step_together(states)
            found = []
            for (keep, send), order in zip(states, orders):
                value = keep + flip(send, order[j]).astype(f32)
                if j < len(bits) - 1:
                    found.append((value[0::2], value[1::2].astype(bf16)))
                else:
                    found.append(value.astype(bf16))
            states = found
        relative = [[0] for _ in orders]
        for j in reversed(range(len(bits))):
            states = step_together(states)
            fars = [flip(near, order[j]) for near, order in zip(states, orders)]
            relative = [r + [e ^ order[j] for e in r] for r, order in zip(relative, orders)]
            if j == 0:
                return [(*pair, r) for pair, r in zip(zip(states, fars), relative)]
            states = [jnp.concatenate(pair, axis=0) for pair in zip(states, fars)]

    fit_own = fit(own, orders[0])
    fit_other = fit(other, orders[1], fit_own[:1])
    (near_own, far_own, order_own), (near_other, far_other, order_other) = totals(
        [tuple(fit_own), tuple(fit_other)]
    )

    mine, theirs = call(
        functools.partial(apply_kernel, (order_own, order_other), blocks // 2),
        "apply",
        chunk_table,
        [integrals, near_own, far_own, near_other, far_other],
        [
            jax.ShapeDtypeStruct((blocks, half, pairs), f32),
            jax.ShapeDtypeStruct((blocks, half, pairs), bf16),
        ],
        [in_vmem] * 2,
    )
    sends = call(
        functools.partial(scatter_coulomb_kernel, n, blocks, cap),
        "scatter_coulomb",
        out_table,
        [keeping, mine, swap(theirs)],
        [jax.ShapeDtypeStruct((2 * cap, half, pairs), bf16)] * n,
        [in_vmem] * n,
        scratch=[pltpu.VMEM((blocks, half, pairs), bf16)],
    )
    received = [sends[0]] + [shift(sends[d], d) for d in range(1, n)]
    return call(
        functools.partial(gather_coulomb_kernel, n, blocks, shell, cap),
        "gather_coulomb",
        in_table,
        received,
        [jax.ShapeDtypeStruct((blocks, pairs, half), bf16)] * 2,
        [anywhere] * 2,
        scratch=[
            pltpu.VMEM((2, blocks, half, pairs), bf16),
            pltpu.VMEM((2, blocks, pairs, half), bf16),
            pltpu.SemaphoreType.DMA((2, blocks)),
        ],
    )


def solution(mesh):
    in_specs = (
        P(("mol", "pair"), None, "aux"),
        P(("mol", "pair"), None, None),
        P(("mol", "pair"), None),
        P(("mol", "pair"), None),
        P("mol"),
        P("mol"),
    )
    out_specs = (P(("mol", "pair"), None, "aux"), P(("mol", "pair"), None, "aux"))
    return jax.shard_map(local, mesh=mesh, in_specs=in_specs, out_specs=out_specs, check_vma=False)
```

time: 197 us -> 185 us (0.939)
  the two profiles are of different devices: /device:TPU:14 before, /device:TPU:15 now
where the time goes in v6:
time: 185 us
  waiting for transfers between devices  115 us (62%)
  starting transfers between devices  41.9 us (23%)
  Pallas kernels  17.3 us (9%)
  local copies, waits for them, and re-layouts  5.73 us (3%)
  other arithmetic  3.93 us (2%)
    ppermute x14, waiting for transfers between devices, shift(): return lax.ppermute(x, 'pair', [(s, (s + d) % n) for s in range(n)])  89.7 us
    ppermute x12, waiting for transfers between devices, flip(): return lax.ppermute(x, 'pair', [(s, s ^ bit) for s in range(n)])  23.7 us
    ppermute x14, starting transfers between devices, shift(): return lax.ppermute(x, 'pair', [(s, (s + d) % n) for s in range(n)])  19.5 us
    ppermute x12, starting transfers between devices, flip(): return lax.ppermute(x, 'pair', [(s, s ^ bit) for s in range(n)])  17.4 us
    pallas_call x6, Pallas kernels, call(): pl.pallas_call(kernel, out_shape=out_shape, grid_spec=pltpu.PrefetchScala...  15.4 us
    unnamed x8, local copies, waits for them, and re-layouts  5.6 us
    ppermute x2, starting transfers between devices, swap(): return lax.ppermute(x, 'aux', [(s, (s + 1) % cores) for s in range(cores)])  5.03 us
  transfers between devices with their start and end apart: 28, of which 22 were waited for; matrix products, arithmetic and copies ran while one was open for 1% of the time, Pallas kernels for 2%

profile of v6, /device:TPU:15, one launch (start us, length us, event | category | flops | bytes accessed | tf_op | source)
XLA Modules:
  0.0 184.9 jit_solution(462231488050498899)
XLA Ops:
  3.5 5.2 %copy-done = bf16[14,256,2048]{2,1,0:T(8,128)(2,1)S(1)} copy-done((bf16[14,256,2048]{2,1,0:T(8,128)(2,1)S(1)}, bf16[14,256,2048]{2,1,0:T(8,128)(2,1)}, u32[]{:S(2)}) %copy-start) | copy-done | bytes 14680088
  11.5 2.1 %collective-permute-start = (bf16[3,128,256]{2,1,0:T(8,128)(2,1)S(1)}, bf16[3,128,256]{2,1,0:T(8,128)(2,1)S(1)}, u32[]{:S(2)}, u32[]{:S(2)}) collective-permute-start(bf16[3,128,256]{2,1,0:T(8,128)(2,1)S(1)} %get-tuple-element.45), channel_id=1, source_target_pairs={{0,2},{2,4},{4,6},{6,8},{8,10},{10,12},{12,14},{14,0},{1,3},{3,5},... | collective-permute-start | bytes 589832 | tf_op jit(solution)/shard_map/ppermute | solution.py:182
  15.0 3.2 %collective-permute-start.2 = (bf16[3,128,256]{2,1,0:T(8,128)(2,1)S(1)}, bf16[3,128,256]{2,1,0:T(8,128)(2,1)S(1)}, u32[]{:S(2)}, u32[]{:S(2)}) collective-permute-start(bf16[3,128,256]{2,1,0:T(8,128)(2,1)S(1)} %get-tuple-element.47), channel_id=1, source_target_pairs={{0,6},{2,8},{4,10},{6,12},{8,14},{10,0},{12,2},{14,4},{1,7},{3,9},... | collective-permute-start | bytes 589832 | tf_op jit(solution)/shard_map/ppermute | solution.py:182
  18.1 3.0 %collective-permute-start.3 = (bf16[3,128,256]{2,1,0:T(8,128)(2,1)S(1)}, bf16[3,128,256]{2,1,0:T(8,128)(2,1)S(1)}, u32[]{:S(2)}, u32[]{:S(2)}) collective-permute-start(bf16[3,128,256]{2,1,0:T(8,128)(2,1)S(1)} %get-tuple-element.48), channel_id=1, source_target_pairs={{0,8},{2,10},{4,12},{6,14},{8,0},{10,2},{12,4},{14,6},{1,9},{3,11}... | collective-permute-start | bytes 589832 | tf_op jit(solution)/shard_map/ppermute | solution.py:182
  24.6 2.8 %collective-permute-done.1.rest_2_ = bf16[3,128,256]{2,1,0:T(8,128)(2,1)S(1)} collective-permute-done((bf16[3,128,256]{2,1,0:T(8,128)(2,1)S(1)}, bf16[3,128,256]{2,1,0:T(8,128)(2,1)S(1)}, u32[]{:S(2)}, u32[]{:S(2)}) %collective-permute-start.1) | collective-permute-done | bytes 196640 | tf_op jit(solution)/shard_map/ppermute | solution.py:182
  27.4 15.4 %collective-permute-done.2.rest_3_ = bf16[3,128,256]{2,1,0:T(8,128)(2,1)S(1)} collective-permute-done((bf16[3,128,256]{2,1,0:T(8,128)(2,1)S(1)}, bf16[3,128,256]{2,1,0:T(8,128)(2,1)S(1)}, u32[]{:S(2)}, u32[]{:S(2)}) %collective-permute-start.2) | collective-permute-done | bytes 196640 | tf_op jit(solution)/shard_map/ppermute | solution.py:182
  42.8 4.2 %collective-permute-done.3.rest_4_ = bf16[3,128,256]{2,1,0:T(8,128)(2,1)S(1)} collective-permute-done((bf16[3,128,256]{2,1,0:T(8,128)(2,1)S(1)}, bf16[3,128,256]{2,1,0:T(8,128)(2,1)S(1)}, u32[]{:S(2)}, u32[]{:S(2)}) %collective-permute-start.3) | collective-permute-done | bytes 196640 | tf_op jit(solution)/shard_map/ppermute | solution.py:182
  49.2 2.8 %fit.2 = (f32[4,128,256]{2,1,0:T(8,128)S(1)}, bf16[4,128,256]{2,1,0:T(8,128)(2,1)S(1)}) custom-call(s32[8]{0:T(128)S(1)} %iota_xor_fusion.table, bf16[14,1,256]{2,1,0:T(2,128)(2,1)S(1)} %copy.10.factor, bf16[14,128,256]{2,1,0:T(8,128)(2,1)S(1)} %gather_density.1.density, bf16[14,256,2048]{2,1,0:T(8,128)(2,1)S(1)} %load_integrals.1.integrals), custom_call_target="tpu_custom_call" | custom-call | tf_op jit(solution)/shard_map/fit/pallas_call | solution.py:167
  52.0 2.8 %fit.3 = (f32[4,128,256]{2,1,0:T(8,128)S(1)}, bf16[4,128,256]{2,1,0:T(8,128)(2,1)S(1)}) custom-call(s32[8]{0:T(128)S(1)} %iota_xor_fusion.table, bf16[14,1,256]{2,1,0:T(2,128)(2,1)S(1)} %copy.10.factor, bf16[14,128,256]{2,1,0:T(8,128)(2,1)S(1)} %collective-permute-done.7.density, bf16[14,256,2048]{2,1,0:T(8,128)(2,1)S(1)} %load_integrals.1.integrals, ...), custom_call_target="tpu_custom_call" | custom-call | tf_op jit(solution)/shard_map/fit/pallas_call | solution.py:167
  56.9 5.9 %collective-permute-done.9 = bf16[4,128,256]{2,1,0:T(8,128)(2,1)S(1)} collective-permute-done((bf16[4,128,256]{2,1,0:T(8,128)(2,1)S(1)}, bf16[4,128,256]{2,1,0:T(8,128)(2,1)S(1)}, u32[]{:S(2)}, u32[]{:S(2)}) %collective-permute-start.9) | collective-permute-done | bytes 262176 | tf_op jit(solution)/shard_map/ppermute | solution.py:185
  73.5 2.6 %collective-permute-done.12 = bf16[1,128,256]{2,1,0:T(8,128)(2,1)S(1)} collective-permute-done((bf16[1,128,256]{2,1,0:T(8,128)(2,1)S(1)}, bf16[1,128,256]{2,1,0:T(8,128)(2,1)S(1)}, u32[]{:S(2)}, u32[]{:S(2)}) %collective-permute-start.12) | collective-permute-done | bytes 65568 | tf_op jit(solution)/shard_map/ppermute | solution.py:185
  76.1 2.1 %collective-permute-start.15 = (bf16[1,128,256]{2,1,0:T(8,128)(2,1)S(1)}, bf16[1,128,256]{2,1,0:T(8,128)(2,1)S(1)}, u32[]{:S(2)}, u32[]{:S(2)}) collective-permute-start(bf16[1,128,256]{2,1,0:T(8,128)(2,1)S(1)} %add_convert_fusion), channel_id=1, source_target_pairs={{0,8},{2,10},{4,12},{6,14},{8,0},{10,2},{12,4},{14,6},{1,9},{3,11}... | collective-permute-start | bytes 196616 | tf_op jit(solution)/shard_map/ppermute | solution.py:185
  83.7 3.2 %collective-permute-start.16 = (bf16[2,128,256]{2,1,0:T(8,128)(2,1)S(1)}, bf16[2,128,256]{2,1,0:T(8,128)(2,1)S(1)}, u32[]{:S(2)}, u32[]{:S(2)}) collective-permute-start(bf16[2,128,256]{2,1,0:T(8,128)(2,1)S(1)} %pad_maximum_fusion.2), channel_id=1, source_target_pairs={{0,4},{2,6},{4,0},{6,2},{8,12},{10,14},{12,8},{14,10},{1,5},{3,7},... | collective-permute-start | bytes 393224 | tf_op jit(solution)/shard_map/ppermute | solution.py:185
  86.9 2.3 %collective-permute-done.16 = bf16[2,128,256]{2,1,0:T(8,128)(2,1)S(1)} collective-permute-done((bf16[2,128,256]{2,1,0:T(8,128)(2,1)S(1)}, bf16[2,128,256]{2,1,0:T(8,128)(2,1)S(1)}, u32[]{:S(2)}, u32[]{:S(2)}) %collective-permute-start.16) | collective-permute-done | bytes 131104 | tf_op jit(solution)/shard_map/ppermute | solution.py:185
  92.4 2.2 %collective-permute-done.18.far = bf16[4,128,256]{2,1,0:T(8,128)(2,1)S(1)} collective-permute-done((bf16[4,128,256]{2,1,0:T(8,128)(2,1)S(1)}, bf16[4,128,256]{2,1,0:T(8,128)(2,1)S(1)}, u32[]{:S(2)}, u32[]{:S(2)}) %collective-permute-start.18) | collective-permute-done | bytes 262176 | tf_op jit(solution)/shard_map/ppermute | solution.py:185
  96.5 5.1 %apply.1 = (f32[14,128,256]{2,1,0:T(8,128)S(1)}, bf16[14,128,256]{2,1,0:T(8,128)(2,1)S(1)}) custom-call(s32[8]{0:T(128)S(1)} %iota_xor_fusion.table, bf16[14,256,2048]{2,1,0:T(8,128)(2,1)S(1)} %load_integrals.1.integrals, bf16[4,128,256]{2,1,0:T(8,128)(2,1)S(1)} %pad_maximum_fusion.near, bf16[4,128,256]{2,1,0:T(8,128)(2,1)S(1)} %collective-permute-done.18.far, ...), custom_call_target="tpu_custom_call" | custom-call | tf_op jit(solution)/shard_map/apply/pallas_call | solution.py:167
  101.5 3.7 %collective-permute-start.20 = (bf16[14,128,256]{2,1,0:T(8,128)(2,1)S(1)}, bf16[14,128,256]{2,1,0:T(8,128)(2,1)S(1)}, u32[]{:S(2)}, u32[]{:S(2)}) collective-permute-start(bf16[14,128,256]{2,1,0:T(8,128)(2,1)S(1)} %get-tuple-element.77), channel_id=1, source_target_pairs={{0,1},{1,0},{2,3},{3,2},{4,5},{5,4},{6,7},{7,6},{8,9},{9,8},{10,11... | collective-permute-start | bytes 2752520 | tf_op jit(solution)/shard_map/ppermute | solution.py:188
  108.3 2.7 %collective-permute-start.21 = (bf16[6,128,256]{2,1,0:T(8,128)(2,1)S(1)}, bf16[6,128,256]{2,1,0:T(8,128)(2,1)S(1)}, u32[]{:S(2)}, u32[]{:S(2)}) collective-permute-start(bf16[6,128,256]{2,1,0:T(8,128)(2,1)S(1)} %get-tuple-element.79), channel_id=1, source_target_pairs={{0,2},{2,4},{4,6},{6,8},{8,10},{10,12},{12,14},{14,0},{1,3},{3,5},... | collective-permute-start | bytes 1179656 | tf_op jit(solution)/shard_map/ppermute | solution.py:182
  115.3 3.9 %collective-permute-done.21.rest_1_ = bf16[6,128,256]{2,1,0:T(8,128)(2,1)S(1)} collective-permute-done((bf16[6,128,256]{2,1,0:T(8,128)(2,1)S(1)}, bf16[6,128,256]{2,1,0:T(8,128)(2,1)S(1)}, u32[]{:S(2)}, u32[]{:S(2)}) %collective-permute-start.21) | collective-permute-done | bytes 393248 | tf_op jit(solution)/shard_map/ppermute | solution.py:182
  120.4 7.7 %collective-permute-done.22.rest_2_ = bf16[6,128,256]{2,1,0:T(8,128)(2,1)S(1)} collective-permute-done((bf16[6,128,256]{2,1,0:T(8,128)(2,1)S(1)}, bf16[6,128,256]{2,1,0:T(8,128)(2,1)S(1)}, u32[]{:S(2)}, u32[]{:S(2)}) %collective-permute-start.22) | collective-permute-done | bytes 393248 | tf_op jit(solution)/shard_map/ppermute | solution.py:182
  128.4 41.4 %collective-permute-done.23.rest_3_ = bf16[6,128,256]{2,1,0:T(8,128)(2,1)S(1)} collective-permute-done((bf16[6,128,256]{2,1,0:T(8,128)(2,1)S(1)}, bf16[6,128,256]{2,1,0:T(8,128)(2,1)S(1)}, u32[]{:S(2)}, u32[]{:S(2)}) %collective-permute-start.23) | collective-permute-done | bytes 393248 | tf_op jit(solution)/shard_map/ppermute | solution.py:182
  169.8 8.4 %collective-permute-done.24.rest_4_ = bf16[6,128,256]{2,1,0:T(8,128)(2,1)S(1)} collective-permute-done((bf16[6,128,256]{2,1,0:T(8,128)(2,1)S(1)}, bf16[6,128,256]{2,1,0:T(8,128)(2,1)S(1)}, u32[]{:S(2)}, u32[]{:S(2)}) %collective-permute-start.24) | collective-permute-done | bytes 393248 | tf_op jit(solution)/shard_map/ppermute | solution.py:182
  178.2 2.3 %collective-permute-done.26.rest_6_ = bf16[6,128,256]{2,1,0:T(8,128)(2,1)S(1)} collective-permute-done((bf16[6,128,256]{2,1,0:T(8,128)(2,1)S(1)}, bf16[6,128,256]{2,1,0:T(8,128)(2,1)S(1)}, u32[]{:S(2)}, u32[]{:S(2)}) %collective-permute-start.26) | collective-permute-done | bytes 393248 | tf_op jit(solution)/shard_map/ppermute | solution.py:182
  181.9 3.0 %gather_coulomb.1 = (bf16[14,256,128]{2,1,0:T(8,128)(2,1)}, bf16[14,256,128]{2,1,0:T(8,128)(2,1)}) custom-call(s32[48]{0:T(128)S(1)} %pad_add_fusion.table, bf16[6,128,256]{2,1,0:T(8,128)(2,1)S(1)} %get-tuple-element.78.rest_0_, bf16[6,128,256]{2,1,0:T(8,128)(2,1)S(1)} %collective-permute-done.21.rest_1_, ...), custom_call_target="tpu_custom_call" | custom-call | tf_op jit(solution)/shard_map/gather_coulomb/pallas_call | solution.py:167
  (90 shorter events, 45.9 us)
Async XLA Ops:
  11.1 7.0 %collective-permute-start.5 = (bf16[3,128,256]{2,1,0:T(8,128)(2,1)S(1)}, bf16[3,128,256]{2,1,0:T(8,128)(2,1)S(1)}, u32[]{:S(2)}, u32[]{:S(2)}) collective-permute-start(bf16[3,128,256]{2,1,0:T(8,128)(2,1)S(1)} %get-tuple-element.51), channel_id=1, source_target_pairs={{0,12},{2,14},{4,0},{6,2},{8,4},{10,6},{12,8},{14,10},{1,13},{3,15... | collective-permute-start | bytes 589832 | tf_op jit(solution)/shard_map/ppermute | solution.py:182
  11.3 9.8 %collective-permute-start.6 = (bf16[3,128,256]{2,1,0:T(8,128)(2,1)S(1)}, bf16[3,128,256]{2,1,0:T(8,128)(2,1)S(1)}, u32[]{:S(2)}, u32[]{:S(2)}) collective-permute-start(bf16[3,128,256]{2,1,0:T(8,128)(2,1)S(1)} %get-tuple-element.53), channel_id=1, source_target_pairs={{0,14},{2,0},{4,2},{6,4},{8,6},{10,8},{12,10},{14,12},{1,15},{3,1}... | collective-permute-start | bytes 589832 | tf_op jit(solution)/shard_map/ppermute | solution.py:182
  11.5 13.1 %collective-permute-start = (bf16[3,128,256]{2,1,0:T(8,128)(2,1)S(1)}, bf16[3,128,256]{2,1,0:T(8,128)(2,1)S(1)}, u32[]{:S(2)}, u32[]{:S(2)}) collective-permute-start(bf16[3,128,256]{2,1,0:T(8,128)(2,1)S(1)} %get-tuple-element.45), channel_id=1, source_target_pairs={{0,2},{2,4},{4,6},{6,8},{8,10},{10,12},{12,14},{14,0},{1,3},{3,5},... | collective-permute-start | bytes 589832 | tf_op jit(solution)/shard_map/ppermute | solution.py:182
  13.7 13.8 %collective-permute-start.1 = (bf16[3,128,256]{2,1,0:T(8,128)(2,1)S(1)}, bf16[3,128,256]{2,1,0:T(8,128)(2,1)S(1)}, u32[]{:S(2)}, u32[]{:S(2)}) collective-permute-start(bf16[3,128,256]{2,1,0:T(8,128)(2,1)S(1)} %get-tuple-element.46), channel_id=1, source_target_pairs={{0,4},{2,6},{4,8},{6,10},{8,12},{10,14},{12,0},{14,2},{1,5},{3,7},... | collective-permute-start | bytes 589832 | tf_op jit(solution)/shard_map/ppermute | solution.py:182
  15.0 27.9 %collective-permute-start.2 = (bf16[3,128,256]{2,1,0:T(8,128)(2,1)S(1)}, bf16[3,128,256]{2,1,0:T(8,128)(2,1)S(1)}, u32[]{:S(2)}, u32[]{:S(2)}) collective-permute-start(bf16[3,128,256]{2,1,0:T(8,128)(2,1)S(1)} %get-tuple-element.47), channel_id=1, source_target_pairs={{0,6},{2,8},{4,10},{6,12},{8,14},{10,0},{12,2},{14,4},{1,7},{3,9},... | collective-permute-start | bytes 589832 | tf_op jit(solution)/shard_map/ppermute | solution.py:182
  18.1 28.9 %collective-permute-start.3 = (bf16[3,128,256]{2,1,0:T(8,128)(2,1)S(1)}, bf16[3,128,256]{2,1,0:T(8,128)(2,1)S(1)}, u32[]{:S(2)}, u32[]{:S(2)}) collective-permute-start(bf16[3,128,256]{2,1,0:T(8,128)(2,1)S(1)} %get-tuple-element.48), channel_id=1, source_target_pairs={{0,8},{2,10},{4,12},{6,14},{8,0},{10,2},{12,4},{14,6},{1,9},{3,11}... | collective-permute-start | bytes 589832 | tf_op jit(solution)/shard_map/ppermute | solution.py:182
  21.1 25.9 %collective-permute-start.4 = (bf16[3,128,256]{2,1,0:T(8,128)(2,1)S(1)}, bf16[3,128,256]{2,1,0:T(8,128)(2,1)S(1)}, u32[]{:S(2)}, u32[]{:S(2)}) collective-permute-start(bf16[3,128,256]{2,1,0:T(8,128)(2,1)S(1)} %get-tuple-element.49), channel_id=1, source_target_pairs={{0,10},{2,12},{4,14},{6,0},{8,2},{10,4},{12,6},{14,8},{1,11},{3,13... | collective-permute-start | bytes 589832 | tf_op jit(solution)/shard_map/ppermute | solution.py:182
  47.8 4.2 %collective-permute-start.7 = (bf16[14,128,256]{2,1,0:T(8,128)(2,1)S(1)}, bf16[14,128,256]{2,1,0:T(8,128)(2,1)S(1)}, u32[]{:S(2)}, u32[]{:S(2)}) collective-permute-start(bf16[14,128,256]{2,1,0:T(8,128)(2,1)S(1)} %gather_density.1.density), channel_id=1, source_target_pairs={{0,1},{1,0},{2,3},{3,2},{4,5},{5,4},{6,7},{7,6},{8,9},{9,8},{10,11... | collective-permute-start | bytes 2752520 | tf_op jit(solution)/shard_map/ppermute | solution.py:188
  54.9 8.0 %collective-permute-start.9 = (bf16[4,128,256]{2,1,0:T(8,128)(2,1)S(1)}, bf16[4,128,256]{2,1,0:T(8,128)(2,1)S(1)}, u32[]{:S(2)}, u32[]{:S(2)}) collective-permute-start(bf16[4,128,256]{2,1,0:T(8,128)(2,1)S(1)} %get-tuple-element.61), channel_id=1, source_target_pairs={{0,4},{2,6},{4,0},{6,2},{8,12},{10,14},{12,8},{14,10},{1,5},{3,7},... | collective-permute-start | bytes 786440 | tf_op jit(solution)/shard_map/ppermute | solution.py:185
  55.7 7.6 %collective-permute-start.8 = (bf16[4,128,256]{2,1,0:T(8,128)(2,1)S(1)}, bf16[4,128,256]{2,1,0:T(8,128)(2,1)S(1)}, u32[]{:S(2)}, u32[]{:S(2)}) collective-permute-start(bf16[4,128,256]{2,1,0:T(8,128)(2,1)S(1)} %get-tuple-element.59), channel_id=1, source_target_pairs={{0,2},{2,0},{4,6},{6,4},{8,10},{10,8},{12,14},{14,12},{1,3},{3,1},... | collective-permute-start | bytes 786440 | tf_op jit(solution)/shard_map/ppermute | solution.py:185
  69.3 4.2 %collective-permute-start.13 = (bf16[1,128,256]{2,1,0:T(8,128)(2,1)S(1)}, bf16[1,128,256]{2,1,0:T(8,128)(2,1)S(1)}, u32[]{:S(2)}, u32[]{:S(2)}) collective-permute-start(bf16[1,128,256]{2,1,0:T(8,128)(2,1)S(1)} %slice.56), channel_id=1, source_target_pairs={{0,8},{2,10},{4,12},{6,14},{8,0},{10,2},{12,4},{14,6},{1,9},{3,11}... | collective-permute-start | bytes 196616 | tf_op jit(solution)/shard_map/ppermute | solution.py:185
  71.4 4.7 %collective-permute-start.12 = (bf16[1,128,256]{2,1,0:T(8,128)(2,1)S(1)}, bf16[1,128,256]{2,1,0:T(8,128)(2,1)S(1)}, u32[]{:S(2)}, u32[]{:S(2)}) collective-permute-start(bf16[1,128,256]{2,1,0:T(8,128)(2,1)S(1)} %slice.57), channel_id=1, source_target_pairs={{0,8},{2,10},{4,12},{6,14},{8,0},{10,2},{12,4},{14,6},{1,9},{3,11}... | collective-permute-start | bytes 196616 | tf_op jit(solution)/shard_map/ppermute | solution.py:185
  82.3 4.6 %collective-permute-start.17 = (bf16[2,128,256]{2,1,0:T(8,128)(2,1)S(1)}, bf16[2,128,256]{2,1,0:T(8,128)(2,1)S(1)}, u32[]{:S(2)}, u32[]{:S(2)}) collective-permute-start(bf16[2,128,256]{2,1,0:T(8,128)(2,1)S(1)} %pad_maximum_fusion.3), channel_id=1, source_target_pairs={{0,2},{2,0},{4,6},{6,4},{8,10},{10,8},{12,14},{14,12},{1,3},{3,1},... | collective-permute-start | bytes 393224 | tf_op jit(solution)/shard_map/ppermute | solution.py:185
  83.7 5.6 %collective-permute-start.16 = (bf16[2,128,256]{2,1,0:T(8,128)(2,1)S(1)}, bf16[2,128,256]{2,1,0:T(8,128)(2,1)S(1)}, u32[]{:S(2)}, u32[]{:S(2)}) collective-permute-start(bf16[2,128,256]{2,1,0:T(8,128)(2,1)S(1)} %pad_maximum_fusion.2), channel_id=1, source_target_pairs={{0,4},{2,6},{4,0},{6,2},{8,12},{10,14},{12,8},{14,10},{1,5},{3,7},... | collective-permute-start | bytes 393224 | tf_op jit(solution)/shard_map/ppermute | solution.py:185
  89.3 5.3 %collective-permute-start.18 = (bf16[4,128,256]{2,1,0:T(8,128)(2,1)S(1)}, bf16[4,128,256]{2,1,0:T(8,128)(2,1)S(1)}, u32[]{:S(2)}, u32[]{:S(2)}) collective-permute-start(bf16[4,128,256]{2,1,0:T(8,128)(2,1)S(1)} %pad_maximum_fusion.near), channel_id=1, source_target_pairs={{0,2},{2,0},{4,6},{6,4},{8,10},{10,8},{12,14},{14,12},{1,3},{3,1},... | collective-permute-start | bytes 786440 | tf_op jit(solution)/shard_map/ppermute | solution.py:185
  90.7 5.8 %collective-permute-start.19 = (bf16[4,128,256]{2,1,0:T(8,128)(2,1)S(1)}, bf16[4,128,256]{2,1,0:T(8,128)(2,1)S(1)}, u32[]{:S(2)}, u32[]{:S(2)}) collective-permute-start(bf16[4,128,256]{2,1,0:T(8,128)(2,1)S(1)} %pad_maximum_fusion.1.near_other), channel_id=1, source_target_pairs={{0,4},{2,6},{4,0},{6,2},{8,12},{10,14},{12,8},{14,10},{1,5},{3,7},... | collective-permute-start | bytes 786440 | tf_op jit(solution)/shard_map/ppermute | solution.py:185
  101.5 5.8 %collective-permute-start.20 = (bf16[14,128,256]{2,1,0:T(8,128)(2,1)S(1)}, bf16[14,128,256]{2,1,0:T(8,128)(2,1)S(1)}, u32[]{:S(2)}, u32[]{:S(2)}) collective-permute-start(bf16[14,128,256]{2,1,0:T(8,128)(2,1)S(1)} %get-tuple-element.77), channel_id=1, source_target_pairs={{0,1},{1,0},{2,3},{3,2},{4,5},{5,4},{6,7},{7,6},{8,9},{9,8},{10,11... | collective-permute-start | bytes 2752520 | tf_op jit(solution)/shard_map/ppermute | solution.py:188
  108.3 10.9 %collective-permute-start.21 = (bf16[6,128,256]{2,1,0:T(8,128)(2,1)S(1)}, bf16[6,128,256]{2,1,0:T(8,128)(2,1)S(1)}, u32[]{:S(2)}, u32[]{:S(2)}) collective-permute-start(bf16[6,128,256]{2,1,0:T(8,128)(2,1)S(1)} %get-tuple-element.79), channel_id=1, source_target_pairs={{0,2},{2,4},{4,6},{6,8},{8,10},{10,12},{12,14},{14,0},{1,3},{3,5},... | collective-permute-start | bytes 1179656 | tf_op jit(solution)/shard_map/ppermute | solution.py:182
  111.1 17.0 %collective-permute-start.22 = (bf16[6,128,256]{2,1,0:T(8,128)(2,1)S(1)}, bf16[6,128,256]{2,1,0:T(8,128)(2,1)S(1)}, u32[]{:S(2)}, u32[]{:S(2)}) collective-permute-start(bf16[6,128,256]{2,1,0:T(8,128)(2,1)S(1)} %get-tuple-element.80), channel_id=1, source_target_pairs={{0,4},{2,6},{4,8},{6,10},{8,12},{10,14},{12,0},{14,2},{1,5},{3,7},... | collective-permute-start | bytes 1179656 | tf_op jit(solution)/shard_map/ppermute | solution.py:182
  112.9 56.9 %collective-permute-start.23 = (bf16[6,128,256]{2,1,0:T(8,128)(2,1)S(1)}, bf16[6,128,256]{2,1,0:T(8,128)(2,1)S(1)}, u32[]{:S(2)}, u32[]{:S(2)}) collective-permute-start(bf16[6,128,256]{2,1,0:T(8,128)(2,1)S(1)} %get-tuple-element.81), channel_id=1, source_target_pairs={{0,6},{2,8},{4,10},{6,12},{8,14},{10,0},{12,2},{14,4},{1,7},{3,9},... | collective-permute-start | bytes 1179656 | tf_op jit(solution)/shard_map/ppermute | solution.py:182
  113.3 64.8 %collective-permute-start.24 = (bf16[6,128,256]{2,1,0:T(8,128)(2,1)S(1)}, bf16[6,128,256]{2,1,0:T(8,128)(2,1)S(1)}, u32[]{:S(2)}, u32[]{:S(2)}) collective-permute-start(bf16[6,128,256]{2,1,0:T(8,128)(2,1)S(1)} %get-tuple-element.82), channel_id=1, source_target_pairs={{0,8},{2,10},{4,12},{6,14},{8,0},{10,2},{12,4},{14,6},{1,9},{3,11}... | collective-permute-start | bytes 1179656 | tf_op jit(solution)/shard_map/ppermute | solution.py:182
  113.5 64.7 %collective-permute-start.25 = (bf16[6,128,256]{2,1,0:T(8,128)(2,1)S(1)}, bf16[6,128,256]{2,1,0:T(8,128)(2,1)S(1)}, u32[]{:S(2)}, u32[]{:S(2)}) collective-permute-start(bf16[6,128,256]{2,1,0:T(8,128)(2,1)S(1)} %get-tuple-element.83), channel_id=1, source_target_pairs={{0,10},{2,12},{4,14},{6,0},{8,2},{10,4},{12,6},{14,8},{1,11},{3,13... | collective-permute-start | bytes 1179656 | tf_op jit(solution)/shard_map/ppermute | solution.py:182
  119.2 61.3 %collective-permute-start.26 = (bf16[6,128,256]{2,1,0:T(8,128)(2,1)S(1)}, bf16[6,128,256]{2,1,0:T(8,128)(2,1)S(1)}, u32[]{:S(2)}, u32[]{:S(2)}) collective-permute-start(bf16[6,128,256]{2,1,0:T(8,128)(2,1)S(1)} %get-tuple-element.84), channel_id=1, source_target_pairs={{0,12},{2,14},{4,0},{6,2},{8,4},{10,6},{12,8},{14,10},{1,13},{3,15... | collective-permute-start | bytes 1179656 | tf_op jit(solution)/shard_map/ppermute | solution.py:182
  128.1 53.8 %collective-permute-start.27 = (bf16[6,128,256]{2,1,0:T(8,128)(2,1)S(1)}, bf16[6,128,256]{2,1,0:T(8,128)(2,1)S(1)}, u32[]{:S(2)}, u32[]{:S(2)}) collective-permute-start(bf16[6,128,256]{2,1,0:T(8,128)(2,1)S(1)} %get-tuple-element.85), channel_id=1, source_target_pairs={{0,14},{2,0},{4,2},{6,4},{8,6},{10,8},{12,10},{14,12},{1,15},{3,1}... | collective-permute-start | bytes 1179656 | tf_op jit(solution)/shard_map/ppermute | solution.py:182
  (8 other events, 103.9 us)

commit v7 on v6

--- a/solution.py
+++ b/solution.py
@@ -34,7 +34,7 @@
     return jnp.max(jnp.where(held, numbers[None, :], -1), axis=1)
 
 
-def load_kernel(source, target, sem):
+def load_kernel(source, ready, target, sem):
     copy = pltpu.make_async_copy(source, target, sem)
     copy.start()
     copy.wait()
@@ -211,16 +211,6 @@
     factor = (screen.astype(f32) * weight[:, None]).astype(bf16)[:, None, :]
     keeping = screen.astype(f32)[:, None, :]
 
-    integrals = pl.pallas_call(
-        load_kernel,
-        out_shape=pltpu.VMEM((blocks, pairs, aux_dev), bf16),
-        in_specs=[anywhere],
-        out_specs=in_vmem,
-        scratch_shapes=[pltpu.SemaphoreType.DMA],
-        compiler_params=pltpu.CompilerParams(vmem_limit_bytes=2 * 1024 * 1024),
-        name="load_integrals",
-    )(three_index)
-
     sends = pl.pallas_call(
         functools.partial(scatter_density_kernel, n, blocks, cap),
         out_shape=[jax.ShapeDtypeStruct((cap, half, pairs), bf16)] * n,
@@ -234,9 +224,20 @@
         compiler_params=pltpu.CompilerParams(vmem_limit_bytes=VMEM_BYTES),
         name="scatter_density",
     )(send_table, density)
-    received = [sends[0]] + [
-        shift(after(sends[d], integrals) if d > n - 3 else sends[d], d) for d in range(1, n)
-    ]
+    steps = sorted(range(1, n), key=lambda d: abs(2 * d - n))
+    received = [sends[0]] + [None] * (n - 1)
+    for d in steps[:-1]:
+        received[d] = shift(sends[d], d)
+    integrals = pl.pallas_call(
+        load_kernel,
+        out_shape=pltpu.VMEM((blocks, pairs, aux_dev), bf16),
+        in_specs=[anywhere, anywhere],
+        out_specs=in_vmem,
+        scratch_shapes=[pltpu.SemaphoreType.DMA],
+        compiler_params=pltpu.CompilerParams(vmem_limit_bytes=2 * 1024 * 1024),
+        name="load_integrals",
+    )(three_index, received[steps[0]])
+    received[steps[-1]] = shift(after(sends[steps[-1]], integrals), steps[-1])
     own = call(
         functools.partial(gather_density_kernel, n, cap),
         "gather_density",
@@ -314,7 +315,9 @@
         [in_vmem] * n,
         scratch=[pltpu.VMEM((blocks, half, pairs), bf16)],
     )
-    received = [sends[0]] + [shift(sends[d], d) for d in range(1, n)]
+    for d in steps:
+        received[d] = shift(sends[d], d)
+    received[0] = sends[0]
     return call(
         functools.partial(gather_coulomb_kernel, n, blocks, shell, cap),
         "gather_coulomb",

time: 185 us -> 181 us (0.978)
  waiting for transfers between devices: 115 us -> 105 us
  starting transfers between devices: 41.9 us -> 46.3 us
    ppermute x14, waiting for transfers between devices: 89.7 us -> 78.1 us  [shift(): return lax.ppermute(x, 'pair', [(s, (s + d) % n) for s in range(n)])]
    ppermute x14, starting transfers between devices: 19.5 us -> 24.5 us  [shift(): return lax.ppermute(x, 'pair', [(s, (s + d) % n) for s in range(n)])]
    ppermute x12, starting transfers between devices: 17.4 us -> 13.1 us  [flip(): return lax.ppermute(x, 'pair', [(s, s ^ bit) for s in range(n)])]
    ppermute x2, starting transfers between devices: 5.03 us -> 8.61 us  [swap(): return lax.ppermute(x, 'aux', [(s, (s + 1) % cores) for s in range(cores)])]
  transfers between devices with their start and end apart: 28 -> 28, of which waited for: 22 -> 20; matrix products, arithmetic and copies ran while one was open for 1% -> 1% of each run, Pallas kernels for 2% -> 2%
where the time goes in v7:
time: 181 us; the launch traced here: 180 us
  waiting for transfers between devices  105 us (58%)
  starting transfers between devices  46.3 us (26%)
  Pallas kernels  17.3 us (10%)
  local copies, waits for them, and re-layouts  6.81 us (4%)
  other arithmetic  3.94 us (2%)
    ppermute x14, waiting for transfers between devices, shift(): return lax.ppermute(x, 'pair', [(s, (s + d) % n) for s in range(n)])  78.1 us
    ppermute x12, waiting for transfers between devices, flip(): return lax.ppermute(x, 'pair', [(s, s ^ bit) for s in range(n)])  25.3 us
    ppermute x14, starting transfers between devices, shift(): return lax.ppermute(x, 'pair', [(s, (s + d) % n) for s in range(n)])  24.5 us
    pallas_call x6, Pallas kernels, call(): pl.pallas_call(kernel, out_shape=out_shape, grid_spec=pltpu.PrefetchScala...  15.4 us
    ppermute x12, starting transfers between devices, flip(): return lax.ppermute(x, 'pair', [(s, s ^ bit) for s in range(n)])  13.1 us
    ppermute x2, starting transfers between devices, swap(): return lax.ppermute(x, 'aux', [(s, (s + 1) % cores) for s in range(cores)])  8.61 us
    unnamed x8, local copies, waits for them, and re-layouts  6.68 us
  transfers between devices with their start and end apart: 28, of which 20 were waited for; matrix products, arithmetic and copies ran while one was open for 1% of the time, Pallas kernels for 2%

profile of v7, /device:TPU:15, one launch (start us, length us, event | category | flops | bytes accessed | tf_op | source)
XLA Modules:
  0.0 180.4 jit_solution(11120392305340109887)
XLA Ops:
  6.0 2.4 %collective-permute-start = (bf16[3,128,256]{2,1,0:T(8,128)(2,1)S(1)}, bf16[3,128,256]{2,1,0:T(8,128)(2,1)S(1)}, u32[]{:S(2)}, u32[]{:S(2)}) collective-permute-start(bf16[3,128,256]{2,1,0:T(8,128)(2,1)S(1)} %get-tuple-element.43), channel_id=1, source_target_pairs={{0,8},{2,10},{4,12},{6,14},{8,0},{10,2},{12,4},{14,6},{1,9},{3,11}... | collective-permute-start | bytes 589832 | tf_op jit(solution)/shard_map/ppermute | solution.py:182
  8.7 3.1 %collective-permute-start.3 = (bf16[3,128,256]{2,1,0:T(8,128)(2,1)S(1)}, bf16[3,128,256]{2,1,0:T(8,128)(2,1)S(1)}, u32[]{:S(2)}, u32[]{:S(2)}) collective-permute-start(bf16[3,128,256]{2,1,0:T(8,128)(2,1)S(1)} %get-tuple-element.47), channel_id=1, source_target_pairs={{0,6},{2,8},{4,10},{6,12},{8,14},{10,0},{12,2},{14,4},{1,7},{3,9},... | collective-permute-start | bytes 589832 | tf_op jit(solution)/shard_map/ppermute | solution.py:182
  11.8 5.3 %collective-permute-done.ready.rest_4_ = bf16[3,128,256]{2,1,0:T(8,128)(2,1)S(1)} collective-permute-done((bf16[3,128,256]{2,1,0:T(8,128)(2,1)S(1)}, bf16[3,128,256]{2,1,0:T(8,128)(2,1)S(1)}, u32[]{:S(2)}, u32[]{:S(2)}) %collective-permute-start) | collective-permute-done | bytes 196640 | tf_op jit(solution)/shard_map/ppermute | solution.py:182
  17.1 12.7 %collective-permute-start.5 = (bf16[3,128,256]{2,1,0:T(8,128)(2,1)S(1)}, bf16[3,128,256]{2,1,0:T(8,128)(2,1)S(1)}, u32[]{:S(2)}, u32[]{:S(2)}) collective-permute-start(bf16[3,128,256]{2,1,0:T(8,128)(2,1)S(1)} %get-tuple-element.49), channel_id=1, source_target_pairs={{0,12},{2,14},{4,0},{6,2},{8,4},{10,6},{12,8},{14,10},{1,13},{3,15... | collective-permute-start | bytes 589832 | tf_op jit(solution)/shard_map/ppermute | solution.py:182
  29.8 5.2 %copy-done = bf16[14,256,2048]{2,1,0:T(8,128)(2,1)S(1)} copy-done((bf16[14,256,2048]{2,1,0:T(8,128)(2,1)S(1)}, bf16[14,256,2048]{2,1,0:T(8,128)(2,1)}, u32[]{:S(2)}) %copy-start) | copy-done | bytes 14680088
  38.2 4.2 %collective-permute-done.3.rest_3_ = bf16[3,128,256]{2,1,0:T(8,128)(2,1)S(1)} collective-permute-done((bf16[3,128,256]{2,1,0:T(8,128)(2,1)S(1)}, bf16[3,128,256]{2,1,0:T(8,128)(2,1)S(1)}, u32[]{:S(2)}, u32[]{:S(2)}) %collective-permute-start.3) | collective-permute-done | bytes 196640 | tf_op jit(solution)/shard_map/ppermute | solution.py:182
  43.2 3.2 %collective-permute-start.7 = (bf16[14,128,256]{2,1,0:T(8,128)(2,1)S(1)}, bf16[14,128,256]{2,1,0:T(8,128)(2,1)S(1)}, u32[]{:S(2)}, u32[]{:S(2)}) collective-permute-start(bf16[14,128,256]{2,1,0:T(8,128)(2,1)S(1)} %gather_density.1.density), channel_id=1, source_target_pairs={{0,1},{1,0},{2,3},{3,2},{4,5},{5,4},{6,7},{7,6},{8,9},{9,8},{10,11... | collective-permute-start | bytes 2752520 | tf_op jit(solution)/shard_map/ppermute | solution.py:188
  46.5 2.8 %fit.2 = (f32[4,128,256]{2,1,0:T(8,128)S(1)}, bf16[4,128,256]{2,1,0:T(8,128)(2,1)S(1)}) custom-call(s32[8]{0:T(128)S(1)} %iota_xor_fusion.table, bf16[14,1,256]{2,1,0:T(2,128)(2,1)S(1)} %copy.10.factor, bf16[14,128,256]{2,1,0:T(8,128)(2,1)S(1)} %gather_density.1.density, bf16[14,256,2048]{2,1,0:T(8,128)(2,1)S(1)} %load_integrals.1.integrals), custom_call_target="tpu_custom_call" | custom-call | tf_op jit(solution)/shard_map/fit/pallas_call | solution.py:167
  49.3 2.8 %fit.3 = (f32[4,128,256]{2,1,0:T(8,128)S(1)}, bf16[4,128,256]{2,1,0:T(8,128)(2,1)S(1)}) custom-call(s32[8]{0:T(128)S(1)} %iota_xor_fusion.table, bf16[14,1,256]{2,1,0:T(2,128)(2,1)S(1)} %copy.10.factor, bf16[14,128,256]{2,1,0:T(8,128)(2,1)S(1)} %collective-permute-done.7.density, bf16[14,256,2048]{2,1,0:T(8,128)(2,1)S(1)} %load_integrals.1.integrals, ...), custom_call_target="tpu_custom_call" | custom-call | tf_op jit(solution)/shard_map/fit/pallas_call | solution.py:167
  52.3 7.8 %collective-permute-done.9 = bf16[4,128,256]{2,1,0:T(8,128)(2,1)S(1)} collective-permute-done((bf16[4,128,256]{2,1,0:T(8,128)(2,1)S(1)}, bf16[4,128,256]{2,1,0:T(8,128)(2,1)S(1)}, u32[]{:S(2)}, u32[]{:S(2)}) %collective-permute-start.9) | collective-permute-done | bytes 262176 | tf_op jit(solution)/shard_map/ppermute | solution.py:185
  61.8 2.9 %collective-permute-done.11 = bf16[2,128,256]{2,1,0:T(8,128)(2,1)S(1)} collective-permute-done((bf16[2,128,256]{2,1,0:T(8,128)(2,1)S(1)}, bf16[2,128,256]{2,1,0:T(8,128)(2,1)S(1)}, u32[]{:S(2)}, u32[]{:S(2)}) %collective-permute-start.11) | collective-permute-done | bytes 131104 | tf_op jit(solution)/shard_map/ppermute | solution.py:185
  64.8 2.6 %collective-permute-start.13 = (bf16[1,128,256]{2,1,0:T(8,128)(2,1)S(1)}, bf16[1,128,256]{2,1,0:T(8,128)(2,1)S(1)}, u32[]{:S(2)}, u32[]{:S(2)}) collective-permute-start(bf16[1,128,256]{2,1,0:T(8,128)(2,1)S(1)} %slice.56), channel_id=1, source_target_pairs={{0,8},{2,10},{4,12},{6,14},{8,0},{10,2},{12,4},{14,6},{1,9},{3,11}... | collective-permute-start | bytes 196616 | tf_op jit(solution)/shard_map/ppermute | solution.py:185
  69.2 2.8 %collective-permute-done.12 = bf16[1,128,256]{2,1,0:T(8,128)(2,1)S(1)} collective-permute-done((bf16[1,128,256]{2,1,0:T(8,128)(2,1)S(1)}, bf16[1,128,256]{2,1,0:T(8,128)(2,1)S(1)}, u32[]{:S(2)}, u32[]{:S(2)}) %collective-permute-start.12) | collective-permute-done | bytes 65568 | tf_op jit(solution)/shard_map/ppermute | solution.py:185
  72.0 2.2 %collective-permute-start.15 = (bf16[1,128,256]{2,1,0:T(8,128)(2,1)S(1)}, bf16[1,128,256]{2,1,0:T(8,128)(2,1)S(1)}, u32[]{:S(2)}, u32[]{:S(2)}) collective-permute-start(bf16[1,128,256]{2,1,0:T(8,128)(2,1)S(1)} %add_convert_fusion), channel_id=1, source_target_pairs={{0,8},{2,10},{4,12},{6,14},{8,0},{10,2},{12,4},{14,6},{1,9},{3,11}... | collective-permute-start | bytes 196616 | tf_op jit(solution)/shard_map/ppermute | solution.py:185
  76.2 2.2 %collective-permute-done.14 = bf16[1,128,256]{2,1,0:T(8,128)(2,1)S(1)} collective-permute-done((bf16[1,128,256]{2,1,0:T(8,128)(2,1)S(1)}, bf16[1,128,256]{2,1,0:T(8,128)(2,1)S(1)}, u32[]{:S(2)}, u32[]{:S(2)}) %collective-permute-start.14) | collective-permute-done | bytes 65568 | tf_op jit(solution)/shard_map/ppermute | solution.py:185
  87.4 2.4 %collective-permute-done.18.far = bf16[4,128,256]{2,1,0:T(8,128)(2,1)S(1)} collective-permute-done((bf16[4,128,256]{2,1,0:T(8,128)(2,1)S(1)}, bf16[4,128,256]{2,1,0:T(8,128)(2,1)S(1)}, u32[]{:S(2)}, u32[]{:S(2)}) %collective-permute-start.18) | collective-permute-done | bytes 262176 | tf_op jit(solution)/shard_map/ppermute | solution.py:185
  91.1 5.1 %apply.1 = (f32[14,128,256]{2,1,0:T(8,128)S(1)}, bf16[14,128,256]{2,1,0:T(8,128)(2,1)S(1)}) custom-call(s32[8]{0:T(128)S(1)} %iota_xor_fusion.table, bf16[14,256,2048]{2,1,0:T(8,128)(2,1)S(1)} %load_integrals.1.integrals, bf16[4,128,256]{2,1,0:T(8,128)(2,1)S(1)} %pad_maximum_fusion.near, bf16[4,128,256]{2,1,0:T(8,128)(2,1)S(1)} %collective-permute-done.18.far, ...), custom_call_target="tpu_custom_call" | custom-call | tf_op jit(solution)/shard_map/apply/pallas_call | solution.py:167
  96.2 5.4 %collective-permute-start.20 = (bf16[14,128,256]{2,1,0:T(8,128)(2,1)S(1)}, bf16[14,128,256]{2,1,0:T(8,128)(2,1)S(1)}, u32[]{:S(2)}, u32[]{:S(2)}) collective-permute-start(bf16[14,128,256]{2,1,0:T(8,128)(2,1)S(1)} %get-tuple-element.75), channel_id=1, source_target_pairs={{0,1},{1,0},{2,3},{3,2},{4,5},{5,4},{6,7},{7,6},{8,9},{9,8},{10,11... | collective-permute-start | bytes 2752520 | tf_op jit(solution)/shard_map/ppermute | solution.py:188
  110.3 4.7 %collective-permute-done.21.rest_1_ = bf16[6,128,256]{2,1,0:T(8,128)(2,1)S(1)} collective-permute-done((bf16[6,128,256]{2,1,0:T(8,128)(2,1)S(1)}, bf16[6,128,256]{2,1,0:T(8,128)(2,1)S(1)}, u32[]{:S(2)}, u32[]{:S(2)}) %collective-permute-start.21) | collective-permute-done | bytes 393248 | tf_op jit(solution)/shard_map/ppermute | solution.py:182
  115.2 8.0 %collective-permute-done.22.rest_2_ = bf16[6,128,256]{2,1,0:T(8,128)(2,1)S(1)} collective-permute-done((bf16[6,128,256]{2,1,0:T(8,128)(2,1)S(1)}, bf16[6,128,256]{2,1,0:T(8,128)(2,1)S(1)}, u32[]{:S(2)}, u32[]{:S(2)}) %collective-permute-start.22) | collective-permute-done | bytes 393248 | tf_op jit(solution)/shard_map/ppermute | solution.py:182
  123.4 40.9 %collective-permute-done.23.rest_3_ = bf16[6,128,256]{2,1,0:T(8,128)(2,1)S(1)} collective-permute-done((bf16[6,128,256]{2,1,0:T(8,128)(2,1)S(1)}, bf16[6,128,256]{2,1,0:T(8,128)(2,1)S(1)}, u32[]{:S(2)}, u32[]{:S(2)}) %collective-permute-start.23) | collective-permute-done | bytes 393248 | tf_op jit(solution)/shard_map/ppermute | solution.py:182
  164.4 8.4 %collective-permute-done.24.rest_4_ = bf16[6,128,256]{2,1,0:T(8,128)(2,1)S(1)} collective-permute-done((bf16[6,128,256]{2,1,0:T(8,128)(2,1)S(1)}, bf16[6,128,256]{2,1,0:T(8,128)(2,1)S(1)}, u32[]{:S(2)}, u32[]{:S(2)}) %collective-permute-start.24) | collective-permute-done | bytes 393248 | tf_op jit(solution)/shard_map/ppermute | solution.py:182
  172.8 3.5 %collective-permute-done.26.rest_6_ = bf16[6,128,256]{2,1,0:T(8,128)(2,1)S(1)} collective-permute-done((bf16[6,128,256]{2,1,0:T(8,128)(2,1)S(1)}, bf16[6,128,256]{2,1,0:T(8,128)(2,1)S(1)}, u32[]{:S(2)}, u32[]{:S(2)}) %collective-permute-start.26) | collective-permute-done | bytes 393248 | tf_op jit(solution)/shard_map/ppermute | solution.py:182
  177.5 3.0 %gather_coulomb.1 = (bf16[14,256,128]{2,1,0:T(8,128)(2,1)}, bf16[14,256,128]{2,1,0:T(8,128)(2,1)}) custom-call(s32[48]{0:T(128)S(1)} %pad_add_fusion.table, bf16[6,128,256]{2,1,0:T(8,128)(2,1)S(1)} %get-tuple-element.76.rest_0_, bf16[6,128,256]{2,1,0:T(8,128)(2,1)S(1)} %collective-permute-done.21.rest_1_, ...), custom_call_target="tpu_custom_call" | custom-call | tf_op jit(solution)/shard_map/gather_coulomb/pallas_call | solution.py:167
  (90 shorter events, 35.8 us)
Async XLA Ops:
  6.0 11.1 %collective-permute-start = (bf16[3,128,256]{2,1,0:T(8,128)(2,1)S(1)}, bf16[3,128,256]{2,1,0:T(8,128)(2,1)S(1)}, u32[]{:S(2)}, u32[]{:S(2)}) collective-permute-start(bf16[3,128,256]{2,1,0:T(8,128)(2,1)S(1)} %get-tuple-element.43), channel_id=1, source_target_pairs={{0,8},{2,10},{4,12},{6,14},{8,0},{10,2},{12,4},{14,6},{1,9},{3,11}... | collective-permute-start | bytes 589832 | tf_op jit(solution)/shard_map/ppermute | solution.py:182
  8.4 27.6 %collective-permute-start.1 = (bf16[3,128,256]{2,1,0:T(8,128)(2,1)S(1)}, bf16[3,128,256]{2,1,0:T(8,128)(2,1)S(1)}, u32[]{:S(2)}, u32[]{:S(2)}) collective-permute-start(bf16[3,128,256]{2,1,0:T(8,128)(2,1)S(1)} %get-tuple-element.45), channel_id=1, source_target_pairs={{0,2},{2,4},{4,6},{6,8},{8,10},{10,12},{12,14},{14,0},{1,3},{3,5},... | collective-permute-start | bytes 589832 | tf_op jit(solution)/shard_map/ppermute | solution.py:182
  8.4 29.8 %collective-permute-start.2 = (bf16[3,128,256]{2,1,0:T(8,128)(2,1)S(1)}, bf16[3,128,256]{2,1,0:T(8,128)(2,1)S(1)}, u32[]{:S(2)}, u32[]{:S(2)}) collective-permute-start(bf16[3,128,256]{2,1,0:T(8,128)(2,1)S(1)} %get-tuple-element.46), channel_id=1, source_target_pairs={{0,4},{2,6},{4,8},{6,10},{8,12},{10,14},{12,0},{14,2},{1,5},{3,7},... | collective-permute-start | bytes 589832 | tf_op jit(solution)/shard_map/ppermute | solution.py:182
  8.7 33.8 %collective-permute-start.3 = (bf16[3,128,256]{2,1,0:T(8,128)(2,1)S(1)}, bf16[3,128,256]{2,1,0:T(8,128)(2,1)S(1)}, u32[]{:S(2)}, u32[]{:S(2)}) collective-permute-start(bf16[3,128,256]{2,1,0:T(8,128)(2,1)S(1)} %get-tuple-element.47), channel_id=1, source_target_pairs={{0,6},{2,8},{4,10},{6,12},{8,14},{10,0},{12,2},{14,4},{1,7},{3,9},... | collective-permute-start | bytes 589832 | tf_op jit(solution)/shard_map/ppermute | solution.py:182
  11.8 30.6 %collective-permute-start.4 = (bf16[3,128,256]{2,1,0:T(8,128)(2,1)S(1)}, bf16[3,128,256]{2,1,0:T(8,128)(2,1)S(1)}, u32[]{:S(2)}, u32[]{:S(2)}) collective-permute-start(bf16[3,128,256]{2,1,0:T(8,128)(2,1)S(1)} %get-tuple-element.48), channel_id=1, source_target_pairs={{0,10},{2,12},{4,14},{6,0},{8,2},{10,4},{12,6},{14,8},{1,11},{3,13... | collective-permute-start | bytes 589832 | tf_op jit(solution)/shard_map/ppermute | solution.py:182
  17.1 25.3 %collective-permute-start.5 = (bf16[3,128,256]{2,1,0:T(8,128)(2,1)S(1)}, bf16[3,128,256]{2,1,0:T(8,128)(2,1)S(1)}, u32[]{:S(2)}, u32[]{:S(2)}) collective-permute-start(bf16[3,128,256]{2,1,0:T(8,128)(2,1)S(1)} %get-tuple-element.49), channel_id=1, source_target_pairs={{0,12},{2,14},{4,0},{6,2},{8,4},{10,6},{12,8},{14,10},{1,13},{3,15... | collective-permute-start | bytes 589832 | tf_op jit(solution)/shard_map/ppermute | solution.py:182
  36.0 6.4 %collective-permute-start.6 = (bf16[3,128,256]{2,1,0:T(8,128)(2,1)S(1)}, bf16[3,128,256]{2,1,0:T(8,128)(2,1)S(1)}, u32[]{:S(2)}, u32[]{:S(2)}) collective-permute-start(bf16[3,128,256]{2,1,0:T(8,128)(2,1)S(1)} %get-tuple-element.51), channel_id=1, source_target_pairs={{0,14},{2,0},{4,2},{6,4},{8,6},{10,8},{12,10},{14,12},{1,15},{3,1}... | collective-permute-start | bytes 589832 | tf_op jit(solution)/shard_map/ppermute | solution.py:182
  43.2 6.1 %collective-permute-start.7 = (bf16[14,128,256]{2,1,0:T(8,128)(2,1)S(1)}, bf16[14,128,256]{2,1,0:T(8,128)(2,1)S(1)}, u32[]{:S(2)}, u32[]{:S(2)}) collective-permute-start(bf16[14,128,256]{2,1,0:T(8,128)(2,1)S(1)} %gather_density.1.density), channel_id=1, source_target_pairs={{0,1},{1,0},{2,3},{3,2},{4,5},{5,4},{6,7},{7,6},{8,9},{9,8},{10,11... | collective-permute-start | bytes 2752520 | tf_op jit(solution)/shard_map/ppermute | solution.py:188
  52.1 8.0 %collective-permute-start.9 = (bf16[4,128,256]{2,1,0:T(8,128)(2,1)S(1)}, bf16[4,128,256]{2,1,0:T(8,128)(2,1)S(1)}, u32[]{:S(2)}, u32[]{:S(2)}) collective-permute-start(bf16[4,128,256]{2,1,0:T(8,128)(2,1)S(1)} %get-tuple-element.59), channel_id=1, source_target_pairs={{0,4},{2,6},{4,0},{6,2},{8,12},{10,14},{12,8},{14,10},{1,5},{3,7},... | collective-permute-start | bytes 786440 | tf_op jit(solution)/shard_map/ppermute | solution.py:185
  52.2 8.0 %collective-permute-start.8 = (bf16[4,128,256]{2,1,0:T(8,128)(2,1)S(1)}, bf16[4,128,256]{2,1,0:T(8,128)(2,1)S(1)}, u32[]{:S(2)}, u32[]{:S(2)}) collective-permute-start(bf16[4,128,256]{2,1,0:T(8,128)(2,1)S(1)} %get-tuple-element.57), channel_id=1, source_target_pairs={{0,2},{2,0},{4,6},{6,4},{8,10},{10,8},{12,14},{14,12},{1,3},{3,1},... | collective-permute-start | bytes 786440 | tf_op jit(solution)/shard_map/ppermute | solution.py:185
  60.4 4.3 %collective-permute-start.11 = (bf16[2,128,256]{2,1,0:T(8,128)(2,1)S(1)}, bf16[2,128,256]{2,1,0:T(8,128)(2,1)S(1)}, u32[]{:S(2)}, u32[]{:S(2)}) collective-permute-start(bf16[2,128,256]{2,1,0:T(8,128)(2,1)S(1)} %slice.43), channel_id=1, source_target_pairs={{0,2},{2,0},{4,6},{6,4},{8,10},{10,8},{12,14},{14,12},{1,3},{3,1},... | collective-permute-start | bytes 393224 | tf_op jit(solution)/shard_map/ppermute | solution.py:185
  64.8 4.4 %collective-permute-start.13 = (bf16[1,128,256]{2,1,0:T(8,128)(2,1)S(1)}, bf16[1,128,256]{2,1,0:T(8,128)(2,1)S(1)}, u32[]{:S(2)}, u32[]{:S(2)}) collective-permute-start(bf16[1,128,256]{2,1,0:T(8,128)(2,1)S(1)} %slice.56), channel_id=1, source_target_pairs={{0,8},{2,10},{4,12},{6,14},{8,0},{10,2},{12,4},{14,6},{1,9},{3,11}... | collective-permute-start | bytes 196616 | tf_op jit(solution)/shard_map/ppermute | solution.py:185
  67.4 4.6 %collective-permute-start.12 = (bf16[1,128,256]{2,1,0:T(8,128)(2,1)S(1)}, bf16[1,128,256]{2,1,0:T(8,128)(2,1)S(1)}, u32[]{:S(2)}, u32[]{:S(2)}) collective-permute-start(bf16[1,128,256]{2,1,0:T(8,128)(2,1)S(1)} %slice.57), channel_id=1, source_target_pairs={{0,8},{2,10},{4,12},{6,14},{8,0},{10,2},{12,4},{14,6},{1,9},{3,11}... | collective-permute-start | bytes 196616 | tf_op jit(solution)/shard_map/ppermute | solution.py:185
  78.4 4.4 %collective-permute-start.17 = (bf16[2,128,256]{2,1,0:T(8,128)(2,1)S(1)}, bf16[2,128,256]{2,1,0:T(8,128)(2,1)S(1)}, u32[]{:S(2)}, u32[]{:S(2)}) collective-permute-start(bf16[2,128,256]{2,1,0:T(8,128)(2,1)S(1)} %pad_maximum_fusion.3), channel_id=1, source_target_pairs={{0,2},{2,0},{4,6},{6,4},{8,10},{10,8},{12,14},{14,12},{1,3},{3,1},... | collective-permute-start | bytes 393224 | tf_op jit(solution)/shard_map/ppermute | solution.py:185
  84.3 5.5 %collective-permute-start.18 = (bf16[4,128,256]{2,1,0:T(8,128)(2,1)S(1)}, bf16[4,128,256]{2,1,0:T(8,128)(2,1)S(1)}, u32[]{:S(2)}, u32[]{:S(2)}) collective-permute-start(bf16[4,128,256]{2,1,0:T(8,128)(2,1)S(1)} %pad_maximum_fusion.near), channel_id=1, source_target_pairs={{0,2},{2,0},{4,6},{6,4},{8,10},{10,8},{12,14},{14,12},{1,3},{3,1},... | collective-permute-start | bytes 786440 | tf_op jit(solution)/shard_map/ppermute | solution.py:185
  85.6 5.5 %collective-permute-start.19 = (bf16[4,128,256]{2,1,0:T(8,128)(2,1)S(1)}, bf16[4,128,256]{2,1,0:T(8,128)(2,1)S(1)}, u32[]{:S(2)}, u32[]{:S(2)}) collective-permute-start(bf16[4,128,256]{2,1,0:T(8,128)(2,1)S(1)} %pad_maximum_fusion.1.near_other), channel_id=1, source_target_pairs={{0,4},{2,6},{4,0},{6,2},{8,12},{10,14},{12,8},{14,10},{1,5},{3,7},... | collective-permute-start | bytes 786440 | tf_op jit(solution)/shard_map/ppermute | solution.py:185
  96.2 7.5 %collective-permute-start.20 = (bf16[14,128,256]{2,1,0:T(8,128)(2,1)S(1)}, bf16[14,128,256]{2,1,0:T(8,128)(2,1)S(1)}, u32[]{:S(2)}, u32[]{:S(2)}) collective-permute-start(bf16[14,128,256]{2,1,0:T(8,128)(2,1)S(1)} %get-tuple-element.75), channel_id=1, source_target_pairs={{0,1},{1,0},{2,3},{3,2},{4,5},{5,4},{6,7},{7,6},{8,9},{9,8},{10,11... | collective-permute-start | bytes 2752520 | tf_op jit(solution)/shard_map/ppermute | solution.py:188
  104.7 10.4 %collective-permute-start.21 = (bf16[6,128,256]{2,1,0:T(8,128)(2,1)S(1)}, bf16[6,128,256]{2,1,0:T(8,128)(2,1)S(1)}, u32[]{:S(2)}, u32[]{:S(2)}) collective-permute-start(bf16[6,128,256]{2,1,0:T(8,128)(2,1)S(1)} %get-tuple-element.77), channel_id=1, source_target_pairs={{0,2},{2,4},{4,6},{6,8},{8,10},{10,12},{12,14},{14,0},{1,3},{3,5},... | collective-permute-start | bytes 1179656 | tf_op jit(solution)/shard_map/ppermute | solution.py:182
  105.7 17.5 %collective-permute-start.22 = (bf16[6,128,256]{2,1,0:T(8,128)(2,1)S(1)}, bf16[6,128,256]{2,1,0:T(8,128)(2,1)S(1)}, u32[]{:S(2)}, u32[]{:S(2)}) collective-permute-start(bf16[6,128,256]{2,1,0:T(8,128)(2,1)S(1)} %get-tuple-element.78), channel_id=1, source_target_pairs={{0,4},{2,6},{4,8},{6,10},{8,12},{10,14},{12,0},{14,2},{1,5},{3,7},... | collective-permute-start | bytes 1179656 | tf_op jit(solution)/shard_map/ppermute | solution.py:182
  107.5 56.9 %collective-permute-start.23 = (bf16[6,128,256]{2,1,0:T(8,128)(2,1)S(1)}, bf16[6,128,256]{2,1,0:T(8,128)(2,1)S(1)}, u32[]{:S(2)}, u32[]{:S(2)}) collective-permute-start(bf16[6,128,256]{2,1,0:T(8,128)(2,1)S(1)} %get-tuple-element.79), channel_id=1, source_target_pairs={{0,6},{2,8},{4,10},{6,12},{8,14},{10,0},{12,2},{14,4},{1,7},{3,9},... | collective-permute-start | bytes 1179656 | tf_op jit(solution)/shard_map/ppermute | solution.py:182
  108.9 64.0 %collective-permute-start.24 = (bf16[6,128,256]{2,1,0:T(8,128)(2,1)S(1)}, bf16[6,128,256]{2,1,0:T(8,128)(2,1)S(1)}, u32[]{:S(2)}, u32[]{:S(2)}) collective-permute-start(bf16[6,128,256]{2,1,0:T(8,128)(2,1)S(1)} %get-tuple-element.80), channel_id=1, source_target_pairs={{0,8},{2,10},{4,12},{6,14},{8,0},{10,2},{12,4},{14,6},{1,9},{3,11}... | collective-permute-start | bytes 1179656 | tf_op jit(solution)/shard_map/ppermute | solution.py:182
  109.7 63.1 %collective-permute-start.25 = (bf16[6,128,256]{2,1,0:T(8,128)(2,1)S(1)}, bf16[6,128,256]{2,1,0:T(8,128)(2,1)S(1)}, u32[]{:S(2)}, u32[]{:S(2)}) collective-permute-start(bf16[6,128,256]{2,1,0:T(8,128)(2,1)S(1)} %get-tuple-element.81), channel_id=1, source_target_pairs={{0,10},{2,12},{4,14},{6,0},{8,2},{10,4},{12,6},{14,8},{1,11},{3,13... | collective-permute-start | bytes 1179656 | tf_op jit(solution)/shard_map/ppermute | solution.py:182
  115.1 61.3 %collective-permute-start.26 = (bf16[6,128,256]{2,1,0:T(8,128)(2,1)S(1)}, bf16[6,128,256]{2,1,0:T(8,128)(2,1)S(1)}, u32[]{:S(2)}, u32[]{:S(2)}) collective-permute-start(bf16[6,128,256]{2,1,0:T(8,128)(2,1)S(1)} %get-tuple-element.82), channel_id=1, source_target_pairs={{0,12},{2,14},{4,0},{6,2},{8,4},{10,6},{12,8},{14,10},{1,13},{3,15... | collective-permute-start | bytes 1179656 | tf_op jit(solution)/shard_map/ppermute | solution.py:182
  123.2 54.3 %collective-permute-start.27 = (bf16[6,128,256]{2,1,0:T(8,128)(2,1)S(1)}, bf16[6,128,256]{2,1,0:T(8,128)(2,1)S(1)}, u32[]{:S(2)}, u32[]{:S(2)}) collective-permute-start(bf16[6,128,256]{2,1,0:T(8,128)(2,1)S(1)} %get-tuple-element.83), channel_id=1, source_target_pairs={{0,14},{2,0},{4,2},{6,4},{8,6},{10,8},{12,10},{14,12},{1,15},{3,1}... | collective-permute-start | bytes 1179656 | tf_op jit(solution)/shard_map/ppermute | solution.py:182
  (8 other events, 45.7 us)

commit v8 on v7

--- a/solution.py
+++ b/solution.py
@@ -50,15 +50,15 @@
             sends[step][rank] = turned[row]
 
 
-def gather_density_kernel(devices, cap, table, *rest):
-    received, out = rest[:devices], rest[-1]
-    for step in range(devices):
+def gather_density_kernel(steps, cap, table, *rest):
+    out = rest[-1]
+    for step, piece in zip(steps, rest):
         for rank in range(cap):
             row = table[step * cap + rank]
 
             @pl.when(row >= 0)
             def _():
-                out[row] = received[step][rank]
+                out[row] = piece[rank]
 
 
 def fit_kernel(bits, blocks, table, factor, density, integrals, *rest):
@@ -112,18 +112,18 @@
                 sends[step][group * cap + rank] = ready[b]
 
 
-def gather_coulomb_kernel(devices, blocks, shell, cap, table, *rest):
-    received = rest[:devices]
+def gather_coulomb_kernel(steps, blocks, shell, cap, table, *rest):
+    devices = len(steps)
     rows, cols, landed, done, sems = rest[devices:]
     pairs = landed.shape[3]
-    for group in range(2):
-        for step in range(devices):
+    for step, piece in zip(steps, rest):
+        for group in range(2):
             for rank in range(cap):
                 row = table[(group * devices + step) * cap + rank]
 
                 @pl.when(row >= 0)
                 def _():
-                    landed[group, row] = received[step][group * cap + rank]
+                    landed[group, row] = piece[group * cap + rank]
 
     to = lax.broadcasted_iota(jnp.int32, (pairs, pairs), 0)
     source = lax.broadcasted_iota(jnp.int32, (pairs, pairs), 1)
@@ -191,22 +191,10 @@
         return lax.optimization_barrier((x, *others))[0]
 
     home_target, home_rank, home_source, home_row_rank = tables(home_slot, n, blocks, me)
-    mirror_target, mirror_rank, mirror_source, mirror_row_rank = tables(
-        mirror_slot, n, blocks, me
-    )
     held = functools.partial(slots_of, devices=n, cap=cap)
     send_table = ints([held((home_source - me) % n, home_row_rank), core[None].astype(jnp.int32)])
     pick_table = held((me - home_target) % n, home_rank)
     chunk_table = me ^ jnp.arange(n, dtype=jnp.int32)
-    out_table = ints(
-        [
-            held((home_target - me) % n, home_rank),
-            held((mirror_target - me) % n, mirror_rank),
-        ]
-    )
-    in_table = ints(
-        [held((me - home_source) % n, home_row_rank), held((me - mirror_source) % n, mirror_row_rank)]
-    )
     weight = jnp.where(pair_shells[:, 0] != pair_shells[:, 1], 2.0, 1.0)
     factor = (screen.astype(f32) * weight[:, None]).astype(bf16)[:, None, :]
     keeping = screen.astype(f32)[:, None, :]
@@ -225,9 +213,7 @@
         name="scatter_density",
     )(send_table, density)
     steps = sorted(range(1, n), key=lambda d: abs(2 * d - n))
-    received = [sends[0]] + [None] * (n - 1)
-    for d in steps[:-1]:
-        received[d] = shift(sends[d], d)
+    received = [shift(sends[d], d) for d in steps[:-1]]
     integrals = pl.pallas_call(
         load_kernel,
         out_shape=pltpu.VMEM((blocks, pairs, aux_dev), bf16),
@@ -236,10 +222,11 @@
         scratch_shapes=[pltpu.SemaphoreType.DMA],
         compiler_params=pltpu.CompilerParams(vmem_limit_bytes=2 * 1024 * 1024),
         name="load_integrals",
-    )(three_index, received[steps[0]])
-    received[steps[-1]] = shift(after(sends[steps[-1]], integrals), steps[-1])
+    )(three_index, received[0])
+    received += [shift(after(sends[steps[-1]], integrals), steps[-1]), sends[0]]
+    steps = (*steps, 0)
     own = call(
-        functools.partial(gather_density_kernel, n, cap),
+        functools.partial(gather_density_kernel, steps, cap),
         "gather_density",
         pick_table,
         received,
@@ -248,8 +235,21 @@
     )
     other = swap(own)
 
+    mirror_target, mirror_rank, mirror_source, mirror_row_rank = tables(
+        after(mirror_slot, own), n, blocks, me
+    )
+    out_table = ints(
+        [
+            held((home_target - me) % n, home_rank),
+            held((mirror_target - me) % n, mirror_rank),
+        ]
+    )
+    in_table = ints(
+        [held((me - home_source) % n, home_row_rank), held((me - mirror_source) % n, mirror_row_rank)]
+    )
+
     bits = [1 << j for j in range(n.bit_length() - 1)]
-    orders = (bits, bits[1::-1] + bits[2:])
+    orders = (bits[1::-1] + bits[2:], bits)
 
     def fit(value, bits, ready=()):
         return call(
@@ -289,10 +289,10 @@
                 return [(*pair, r) for pair, r in zip(zip(states, fars), relative)]
             states = [jnp.concatenate(pair, axis=0) for pair in zip(states, fars)]
 
-    fit_own = fit(own, orders[0])
-    fit_other = fit(other, orders[1], fit_own[:1])
-    (near_own, far_own, order_own), (near_other, far_other, order_other) = totals(
-        [tuple(fit_own), tuple(fit_other)]
+    fit_own = fit(own, orders[1])
+    fit_other = fit(other, orders[0], fit_own[:1])
+    (near_other, far_other, order_other), (near_own, far_own, order_own) = totals(
+        [tuple(fit_other), tuple(fit_own)]
     )
 
     mine, theirs = call(
@@ -315,11 +315,9 @@
         [in_vmem] * n,
         scratch=[pltpu.VMEM((blocks, half, pairs), bf16)],
     )
-    for d in steps:
-        received[d] = shift(sends[d], d)
-    received[0] = sends[0]
+    received = [shift(sends[d], d) if d else sends[d] for d in steps]
     return call(
-        functools.partial(gather_coulomb_kernel, n, blocks, shell, cap),
+        functools.partial(gather_coulomb_kernel, steps, blocks, shell, cap),
         "gather_coulomb",
         in_table,
         received,

time: 181 us -> 180 us (level)
  the two profiles are of different devices: /device:TPU:15 before, /device:TPU:0 now
where the time goes in v8:
time: 180 us
  waiting for transfers between devices  103 us (57%)
  starting transfers between devices  48.4 us (27%)
  Pallas kernels  17.2 us (10%)
  local copies, waits for them, and re-layouts  6.81 us (4%)
  other arithmetic  3.42 us (2%)
    ppermute x14, waiting for transfers between devices, shift(): return lax.ppermute(x, 'pair', [(s, (s + d) % n) for s in range(n)])  72.6 us
    ppermute x14, starting transfers between devices, shift(): return lax.ppermute(x, 'pair', [(s, (s + d) % n) for s in range(n)])  31.8 us
    ppermute x12, waiting for transfers between devices, flip(): return lax.ppermute(x, 'pair', [(s, s ^ bit) for s in range(n)])  28.9 us
    ppermute x12, starting transfers between devices, flip(): return lax.ppermute(x, 'pair', [(s, s ^ bit) for s in range(n)])  16.4 us
    pallas_call x6, Pallas kernels, call(): pl.pallas_call(kernel, out_shape=out_shape, grid_spec=pltpu.PrefetchScala...  15.2 us
    unnamed x10, local copies, waits for them, and re-layouts  6.69 us
  transfers between devices with their start and end apart: 28, of which 15 were waited for; matrix products, arithmetic and copies ran while one was open for 1% of the time, Pallas kernels for 2%

profile of v8, /device:TPU:0, one launch (start us, length us, event | category | flops | bytes accessed | tf_op | source)
XLA Modules:
  0.0 180.1 jit_solution(5864185854753960375)
XLA Ops:
  5.1 4.1 %collective-permute-start = (bf16[3,128,256]{2,1,0:T(8,128)(2,1)S(1)}, bf16[3,128,256]{2,1,0:T(8,128)(2,1)S(1)}, u32[]{:S(2)}, u32[]{:S(2)}) collective-permute-start(bf16[3,128,256]{2,1,0:T(8,128)(2,1)S(1)} %get-tuple-element.44), channel_id=1, source_target_pairs={{0,8},{2,10},{4,12},{6,14},{8,0},{10,2},{12,4},{14,6},{1,9},{3,11}... | collective-permute-start | bytes 589832 | tf_op jit(solution)/shard_map/ppermute | solution.py:182
  9.2 2.5 %collective-permute-start.1 = (bf16[3,128,256]{2,1,0:T(8,128)(2,1)S(1)}, bf16[3,128,256]{2,1,0:T(8,128)(2,1)S(1)}, u32[]{:S(2)}, u32[]{:S(2)}) collective-permute-start(bf16[3,128,256]{2,1,0:T(8,128)(2,1)S(1)} %get-tuple-element.45), channel_id=1, source_target_pairs={{0,6},{2,8},{4,10},{6,12},{8,14},{10,0},{12,2},{14,4},{1,7},{3,9},... | collective-permute-start | bytes 589832 | tf_op jit(solution)/shard_map/ppermute | solution.py:182
  14.6 2.2 %collective-permute-start.4 = (bf16[3,128,256]{2,1,0:T(8,128)(2,1)S(1)}, bf16[3,128,256]{2,1,0:T(8,128)(2,1)S(1)}, u32[]{:S(2)}, u32[]{:S(2)}) collective-permute-start(bf16[3,128,256]{2,1,0:T(8,128)(2,1)S(1)} %get-tuple-element.48), channel_id=1, source_target_pairs={{0,12},{2,14},{4,0},{6,2},{8,4},{10,6},{12,8},{14,10},{1,13},{3,15... | collective-permute-start | bytes 589832 | tf_op jit(solution)/shard_map/ppermute | solution.py:182
  16.8 15.0 %collective-permute-done.ready.rest_0_ = bf16[3,128,256]{2,1,0:T(8,128)(2,1)S(1)} collective-permute-done((bf16[3,128,256]{2,1,0:T(8,128)(2,1)S(1)}, bf16[3,128,256]{2,1,0:T(8,128)(2,1)S(1)}, u32[]{:S(2)}, u32[]{:S(2)}) %collective-permute-start) | collective-permute-done | bytes 196640 | tf_op jit(solution)/shard_map/ppermute | solution.py:182
  31.8 5.2 %copy-done = bf16[14,256,2048]{2,1,0:T(8,128)(2,1)S(1)} copy-done((bf16[14,256,2048]{2,1,0:T(8,128)(2,1)S(1)}, bf16[14,256,2048]{2,1,0:T(8,128)(2,1)}, u32[]{:S(2)}) %copy-start) | copy-done | bytes 14680088
  38.0 4.8 %collective-permute-start.6 = (bf16[3,128,256]{2,1,0:T(8,128)(2,1)S(1)}, bf16[3,128,256]{2,1,0:T(8,128)(2,1)S(1)}, u32[]{:S(2)}, u32[]{:S(2)}) collective-permute-start(bf16[3,128,256]{2,1,0:T(8,128)(2,1)S(1)} %get-tuple-element.51), channel_id=1, source_target_pairs={{0,14},{2,0},{4,2},{6,4},{8,6},{10,8},{12,10},{14,12},{1,15},{3,1}... | collective-permute-start | bytes 589832 | tf_op jit(solution)/shard_map/ppermute | solution.py:182
  42.9 3.1 %collective-permute-done.6.rest_6_ = bf16[3,128,256]{2,1,0:T(8,128)(2,1)S(1)} collective-permute-done((bf16[3,128,256]{2,1,0:T(8,128)(2,1)S(1)}, bf16[3,128,256]{2,1,0:T(8,128)(2,1)S(1)}, u32[]{:S(2)}, u32[]{:S(2)}) %collective-permute-start.6) | collective-permute-done | bytes 196640 | tf_op jit(solution)/shard_map/ppermute | solution.py:182
  46.9 2.8 %fit.2 = (f32[4,128,256]{2,1,0:T(8,128)S(1)}, bf16[4,128,256]{2,1,0:T(8,128)(2,1)S(1)}) custom-call(s32[8]{0:T(128)S(1)} %iota_xor_fusion.table, bf16[14,1,256]{2,1,0:T(2,128)(2,1)S(1)} %copy.11.factor, bf16[14,128,256]{2,1,0:T(8,128)(2,1)S(1)} %gather_density.1.density, bf16[14,256,2048]{2,1,0:T(8,128)(2,1)S(1)} %load_integrals.1.integrals), custom_call_target="tpu_custom_call" | custom-call | tf_op jit(solution)/shard_map/fit/pallas_call | solution.py:167
  49.7 2.7 %fit.3 = (f32[4,128,256]{2,1,0:T(8,128)S(1)}, bf16[4,128,256]{2,1,0:T(8,128)(2,1)S(1)}) custom-call(s32[8]{0:T(128)S(1)} %iota_xor_fusion.table, bf16[14,1,256]{2,1,0:T(2,128)(2,1)S(1)} %copy.11.factor, bf16[14,128,256]{2,1,0:T(8,128)(2,1)S(1)} %collective-permute-done.7.density, bf16[14,256,2048]{2,1,0:T(8,128)(2,1)S(1)} %load_integrals.1.integrals, ...), custom_call_target="tpu_custom_call" | custom-call | tf_op jit(solution)/shard_map/fit/pallas_call | solution.py:167
  52.9 8.3 %collective-permute-done.8 = bf16[4,128,256]{2,1,0:T(8,128)(2,1)S(1)} collective-permute-done((bf16[4,128,256]{2,1,0:T(8,128)(2,1)S(1)}, bf16[4,128,256]{2,1,0:T(8,128)(2,1)S(1)}, u32[]{:S(2)}, u32[]{:S(2)}) %collective-permute-start.8) | collective-permute-done | bytes 262176 | tf_op jit(solution)/shard_map/ppermute | solution.py:185
  63.5 3.2 %collective-permute-done.10 = bf16[2,128,256]{2,1,0:T(8,128)(2,1)S(1)} collective-permute-done((bf16[2,128,256]{2,1,0:T(8,128)(2,1)S(1)}, bf16[2,128,256]{2,1,0:T(8,128)(2,1)S(1)}, u32[]{:S(2)}, u32[]{:S(2)}) %collective-permute-start.10) | collective-permute-done | bytes 131104 | tf_op jit(solution)/shard_map/ppermute | solution.py:185
  66.8 5.8 %collective-permute-start.12 = (bf16[1,128,256]{2,1,0:T(8,128)(2,1)S(1)}, bf16[1,128,256]{2,1,0:T(8,128)(2,1)S(1)}, u32[]{:S(2)}, u32[]{:S(2)}) collective-permute-start(bf16[1,128,256]{2,1,0:T(8,128)(2,1)S(1)} %slice.57), channel_id=1, source_target_pairs={{0,8},{2,10},{4,12},{6,14},{8,0},{10,2},{12,4},{14,6},{1,9},{3,11}... | collective-permute-start | bytes 196616 | tf_op jit(solution)/shard_map/ppermute | solution.py:185
  72.7 4.1 %collective-permute-done.12 = bf16[1,128,256]{2,1,0:T(8,128)(2,1)S(1)} collective-permute-done((bf16[1,128,256]{2,1,0:T(8,128)(2,1)S(1)}, bf16[1,128,256]{2,1,0:T(8,128)(2,1)S(1)}, u32[]{:S(2)}, u32[]{:S(2)}) %collective-permute-start.12) | collective-permute-done | bytes 65568 | tf_op jit(solution)/shard_map/ppermute | solution.py:185
  78.7 2.7 %collective-permute-start.15 = (bf16[1,128,256]{2,1,0:T(8,128)(2,1)S(1)}, bf16[1,128,256]{2,1,0:T(8,128)(2,1)S(1)}, u32[]{:S(2)}, u32[]{:S(2)}) collective-permute-start(bf16[1,128,256]{2,1,0:T(8,128)(2,1)S(1)} %add_convert_fusion), channel_id=1, source_target_pairs={{0,8},{2,10},{4,12},{6,14},{8,0},{10,2},{12,4},{14,6},{1,9},{3,11}... | collective-permute-start | bytes 196616 | tf_op jit(solution)/shard_map/ppermute | solution.py:185
  81.4 2.7 %collective-permute-done.14 = bf16[1,128,256]{2,1,0:T(8,128)(2,1)S(1)} collective-permute-done((bf16[1,128,256]{2,1,0:T(8,128)(2,1)S(1)}, bf16[1,128,256]{2,1,0:T(8,128)(2,1)S(1)}, u32[]{:S(2)}, u32[]{:S(2)}) %collective-permute-start.14) | collective-permute-done | bytes 65568 | tf_op jit(solution)/shard_map/ppermute | solution.py:185
  86.5 3.3 %collective-permute-done.16 = bf16[2,128,256]{2,1,0:T(8,128)(2,1)S(1)} collective-permute-done((bf16[2,128,256]{2,1,0:T(8,128)(2,1)S(1)}, bf16[2,128,256]{2,1,0:T(8,128)(2,1)S(1)}, u32[]{:S(2)}, u32[]{:S(2)}) %collective-permute-start.16) | collective-permute-done | bytes 131104 | tf_op jit(solution)/shard_map/ppermute | solution.py:185
  93.5 3.0 %collective-permute-done.18.far = bf16[4,128,256]{2,1,0:T(8,128)(2,1)S(1)} collective-permute-done((bf16[4,128,256]{2,1,0:T(8,128)(2,1)S(1)}, bf16[4,128,256]{2,1,0:T(8,128)(2,1)S(1)}, u32[]{:S(2)}, u32[]{:S(2)}) %collective-permute-start.18) | collective-permute-done | bytes 262176 | tf_op jit(solution)/shard_map/ppermute | solution.py:185
  98.3 5.0 %apply.1 = (f32[14,128,256]{2,1,0:T(8,128)S(1)}, bf16[14,128,256]{2,1,0:T(8,128)(2,1)S(1)}) custom-call(s32[8]{0:T(128)S(1)} %iota_xor_fusion.table, bf16[14,256,2048]{2,1,0:T(8,128)(2,1)S(1)} %load_integrals.1.integrals, bf16[4,128,256]{2,1,0:T(8,128)(2,1)S(1)} %pad_maximum_fusion.1.near, bf16[4,128,256]{2,1,0:T(8,128)(2,1)S(1)} %collective-permute-done.18.far, ...), custom_call_target="tpu_custom_call" | custom-call | tf_op jit(solution)/shard_map/apply/pallas_call | solution.py:167
  106.8 2.9 %collective-permute-start.21 = (bf16[6,128,256]{2,1,0:T(8,128)(2,1)S(1)}, bf16[6,128,256]{2,1,0:T(8,128)(2,1)S(1)}, u32[]{:S(2)}, u32[]{:S(2)}) collective-permute-start(bf16[6,128,256]{2,1,0:T(8,128)(2,1)S(1)} %get-tuple-element.78), channel_id=1, source_target_pairs={{0,8},{2,10},{4,12},{6,14},{8,0},{10,2},{12,4},{14,6},{1,9},{3,11}... | collective-permute-start | bytes 1179656 | tf_op jit(solution)/shard_map/ppermute | solution.py:182
  111.6 2.2 %collective-permute-start.23 = (bf16[6,128,256]{2,1,0:T(8,128)(2,1)S(1)}, bf16[6,128,256]{2,1,0:T(8,128)(2,1)S(1)}, u32[]{:S(2)}, u32[]{:S(2)}) collective-permute-start(bf16[6,128,256]{2,1,0:T(8,128)(2,1)S(1)} %get-tuple-element.80), channel_id=1, source_target_pairs={{0,10},{2,12},{4,14},{6,0},{8,2},{10,4},{12,6},{14,8},{1,11},{3,13... | collective-permute-start | bytes 1179656 | tf_op jit(solution)/shard_map/ppermute | solution.py:182
  117.6 35.9 %collective-permute-done.21.rest_0_ = bf16[6,128,256]{2,1,0:T(8,128)(2,1)S(1)} collective-permute-done((bf16[6,128,256]{2,1,0:T(8,128)(2,1)S(1)}, bf16[6,128,256]{2,1,0:T(8,128)(2,1)S(1)}, u32[]{:S(2)}, u32[]{:S(2)}) %collective-permute-start.21) | collective-permute-done | bytes 393248 | tf_op jit(solution)/shard_map/ppermute | solution.py:182
  153.6 4.7 %collective-permute-start.27 = (bf16[6,128,256]{2,1,0:T(8,128)(2,1)S(1)}, bf16[6,128,256]{2,1,0:T(8,128)(2,1)S(1)}, u32[]{:S(2)}, u32[]{:S(2)}) collective-permute-start(bf16[6,128,256]{2,1,0:T(8,128)(2,1)S(1)} %get-tuple-element.84), channel_id=1, source_target_pairs={{0,14},{2,0},{4,2},{6,4},{8,6},{10,8},{12,10},{14,12},{1,15},{3,1}... | collective-permute-start | bytes 1179656 | tf_op jit(solution)/shard_map/ppermute | solution.py:182
  158.5 18.6 %collective-permute-done.26.rest_5_ = bf16[6,128,256]{2,1,0:T(8,128)(2,1)S(1)} collective-permute-done((bf16[6,128,256]{2,1,0:T(8,128)(2,1)S(1)}, bf16[6,128,256]{2,1,0:T(8,128)(2,1)S(1)}, u32[]{:S(2)}, u32[]{:S(2)}) %collective-permute-start.26) | collective-permute-done | bytes 393248 | tf_op jit(solution)/shard_map/ppermute | solution.py:182
  177.1 3.0 %gather_coulomb.1 = (bf16[14,256,128]{2,1,0:T(8,128)(2,1)}, bf16[14,256,128]{2,1,0:T(8,128)(2,1)}) custom-call(s32[48]{0:T(128)S(1)} %pad_add_fusion.1.table, bf16[6,128,256]{2,1,0:T(8,128)(2,1)S(1)} %collective-permute-done.21.rest_0_, bf16[6,128,256]{2,1,0:T(8,128)(2,1)S(1)} %collective-permute-done.22.rest_1_, ...), custom_call_target="tpu_custom_call" | custom-call | tf_op jit(solution)/shard_map/gather_coulomb/pallas_call | solution.py:167
  (94 shorter events, 31.2 us)
Async XLA Ops:
  5.1 26.7 %collective-permute-start = (bf16[3,128,256]{2,1,0:T(8,128)(2,1)S(1)}, bf16[3,128,256]{2,1,0:T(8,128)(2,1)S(1)}, u32[]{:S(2)}, u32[]{:S(2)}) collective-permute-start(bf16[3,128,256]{2,1,0:T(8,128)(2,1)S(1)} %get-tuple-element.44), channel_id=1, source_target_pairs={{0,8},{2,10},{4,12},{6,14},{8,0},{10,2},{12,4},{14,6},{1,9},{3,11}... | collective-permute-start | bytes 589832 | tf_op jit(solution)/shard_map/ppermute | solution.py:182
  9.2 28.8 %collective-permute-start.1 = (bf16[3,128,256]{2,1,0:T(8,128)(2,1)S(1)}, bf16[3,128,256]{2,1,0:T(8,128)(2,1)S(1)}, u32[]{:S(2)}, u32[]{:S(2)}) collective-permute-start(bf16[3,128,256]{2,1,0:T(8,128)(2,1)S(1)} %get-tuple-element.45), channel_id=1, source_target_pairs={{0,6},{2,8},{4,10},{6,12},{8,14},{10,0},{12,2},{14,4},{1,7},{3,9},... | collective-permute-start | bytes 589832 | tf_op jit(solution)/shard_map/ppermute | solution.py:182
  11.7 31.1 %collective-permute-start.2 = (bf16[3,128,256]{2,1,0:T(8,128)(2,1)S(1)}, bf16[3,128,256]{2,1,0:T(8,128)(2,1)S(1)}, u32[]{:S(2)}, u32[]{:S(2)}) collective-permute-start(bf16[3,128,256]{2,1,0:T(8,128)(2,1)S(1)} %get-tuple-element.46), channel_id=1, source_target_pairs={{0,10},{2,12},{4,14},{6,0},{8,2},{10,4},{12,6},{14,8},{1,11},{3,13... | collective-permute-start | bytes 589832 | tf_op jit(solution)/shard_map/ppermute | solution.py:182
  13.0 29.9 %collective-permute-start.3 = (bf16[3,128,256]{2,1,0:T(8,128)(2,1)S(1)}, bf16[3,128,256]{2,1,0:T(8,128)(2,1)S(1)}, u32[]{:S(2)}, u32[]{:S(2)}) collective-permute-start(bf16[3,128,256]{2,1,0:T(8,128)(2,1)S(1)} %get-tuple-element.47), channel_id=1, source_target_pairs={{0,4},{2,6},{4,8},{6,10},{8,12},{10,14},{12,0},{14,2},{1,5},{3,7},... | collective-permute-start | bytes 589832 | tf_op jit(solution)/shard_map/ppermute | solution.py:182
  14.6 28.3 %collective-permute-start.4 = (bf16[3,128,256]{2,1,0:T(8,128)(2,1)S(1)}, bf16[3,128,256]{2,1,0:T(8,128)(2,1)S(1)}, u32[]{:S(2)}, u32[]{:S(2)}) collective-permute-start(bf16[3,128,256]{2,1,0:T(8,128)(2,1)S(1)} %get-tuple-element.48), channel_id=1, source_target_pairs={{0,12},{2,14},{4,0},{6,2},{8,4},{10,6},{12,8},{14,10},{1,13},{3,15... | collective-permute-start | bytes 589832 | tf_op jit(solution)/shard_map/ppermute | solution.py:182
  31.8 11.1 %collective-permute-start.5 = (bf16[3,128,256]{2,1,0:T(8,128)(2,1)S(1)}, bf16[3,128,256]{2,1,0:T(8,128)(2,1)S(1)}, u32[]{:S(2)}, u32[]{:S(2)}) collective-permute-start(bf16[3,128,256]{2,1,0:T(8,128)(2,1)S(1)} %get-tuple-element.49), channel_id=1, source_target_pairs={{0,2},{2,4},{4,6},{6,8},{8,10},{10,12},{12,14},{14,0},{1,3},{3,5},... | collective-permute-start | bytes 589832 | tf_op jit(solution)/shard_map/ppermute | solution.py:182
  38.0 8.0 %collective-permute-start.6 = (bf16[3,128,256]{2,1,0:T(8,128)(2,1)S(1)}, bf16[3,128,256]{2,1,0:T(8,128)(2,1)S(1)}, u32[]{:S(2)}, u32[]{:S(2)}) collective-permute-start(bf16[3,128,256]{2,1,0:T(8,128)(2,1)S(1)} %get-tuple-element.51), channel_id=1, source_target_pairs={{0,14},{2,0},{4,2},{6,4},{8,6},{10,8},{12,10},{14,12},{1,15},{3,1}... | collective-permute-start | bytes 589832 | tf_op jit(solution)/shard_map/ppermute | solution.py:182
  52.5 8.8 %collective-permute-start.8 = (bf16[4,128,256]{2,1,0:T(8,128)(2,1)S(1)}, bf16[4,128,256]{2,1,0:T(8,128)(2,1)S(1)}, u32[]{:S(2)}, u32[]{:S(2)}) collective-permute-start(bf16[4,128,256]{2,1,0:T(8,128)(2,1)S(1)} %get-tuple-element.59), channel_id=1, source_target_pairs={{0,4},{2,6},{4,0},{6,2},{8,12},{10,14},{12,8},{14,10},{1,5},{3,7},... | collective-permute-start | bytes 786440 | tf_op jit(solution)/shard_map/ppermute | solution.py:185
  52.6 8.8 %collective-permute-start.9 = (bf16[4,128,256]{2,1,0:T(8,128)(2,1)S(1)}, bf16[4,128,256]{2,1,0:T(8,128)(2,1)S(1)}, u32[]{:S(2)}, u32[]{:S(2)}) collective-permute-start(bf16[4,128,256]{2,1,0:T(8,128)(2,1)S(1)} %get-tuple-element.61), channel_id=1, source_target_pairs={{0,2},{2,0},{4,6},{6,4},{8,10},{10,8},{12,14},{14,12},{1,3},{3,1},... | collective-permute-start | bytes 786440 | tf_op jit(solution)/shard_map/ppermute | solution.py:185
  61.5 5.2 %collective-permute-start.10 = (bf16[2,128,256]{2,1,0:T(8,128)(2,1)S(1)}, bf16[2,128,256]{2,1,0:T(8,128)(2,1)S(1)}, u32[]{:S(2)}, u32[]{:S(2)}) collective-permute-start(bf16[2,128,256]{2,1,0:T(8,128)(2,1)S(1)} %slice.41), channel_id=1, source_target_pairs={{0,2},{2,0},{4,6},{6,4},{8,10},{10,8},{12,14},{14,12},{1,3},{3,1},... | collective-permute-start | bytes 393224 | tf_op jit(solution)/shard_map/ppermute | solution.py:185
  66.8 10.0 %collective-permute-start.12 = (bf16[1,128,256]{2,1,0:T(8,128)(2,1)S(1)}, bf16[1,128,256]{2,1,0:T(8,128)(2,1)S(1)}, u32[]{:S(2)}, u32[]{:S(2)}) collective-permute-start(bf16[1,128,256]{2,1,0:T(8,128)(2,1)S(1)} %slice.57), channel_id=1, source_target_pairs={{0,8},{2,10},{4,12},{6,14},{8,0},{10,2},{12,4},{14,6},{1,9},{3,11}... | collective-permute-start | bytes 196616 | tf_op jit(solution)/shard_map/ppermute | solution.py:185
  72.7 5.7 %collective-permute-start.13 = (bf16[1,128,256]{2,1,0:T(8,128)(2,1)S(1)}, bf16[1,128,256]{2,1,0:T(8,128)(2,1)S(1)}, u32[]{:S(2)}, u32[]{:S(2)}) collective-permute-start(bf16[1,128,256]{2,1,0:T(8,128)(2,1)S(1)} %slice.56), channel_id=1, source_target_pairs={{0,8},{2,10},{4,12},{6,14},{8,0},{10,2},{12,4},{14,6},{1,9},{3,11}... | collective-permute-start | bytes 196616 | tf_op jit(solution)/shard_map/ppermute | solution.py:185
  78.4 5.7 %collective-permute-start.14 = (bf16[1,128,256]{2,1,0:T(8,128)(2,1)S(1)}, bf16[1,128,256]{2,1,0:T(8,128)(2,1)S(1)}, u32[]{:S(2)}, u32[]{:S(2)}) collective-permute-start(bf16[1,128,256]{2,1,0:T(8,128)(2,1)S(1)} %add_convert_fusion.1), channel_id=1, source_target_pairs={{0,8},{2,10},{4,12},{6,14},{8,0},{10,2},{12,4},{14,6},{1,9},{3,11}... | collective-permute-start | bytes 196616 | tf_op jit(solution)/shard_map/ppermute | solution.py:185
  78.7 6.1 %collective-permute-start.15 = (bf16[1,128,256]{2,1,0:T(8,128)(2,1)S(1)}, bf16[1,128,256]{2,1,0:T(8,128)(2,1)S(1)}, u32[]{:S(2)}, u32[]{:S(2)}) collective-permute-start(bf16[1,128,256]{2,1,0:T(8,128)(2,1)S(1)} %add_convert_fusion), channel_id=1, source_target_pairs={{0,8},{2,10},{4,12},{6,14},{8,0},{10,2},{12,4},{14,6},{1,9},{3,11}... | collective-permute-start | bytes 196616 | tf_op jit(solution)/shard_map/ppermute | solution.py:185
  84.8 5.0 %collective-permute-start.16 = (bf16[2,128,256]{2,1,0:T(8,128)(2,1)S(1)}, bf16[2,128,256]{2,1,0:T(8,128)(2,1)S(1)}, u32[]{:S(2)}, u32[]{:S(2)}) collective-permute-start(bf16[2,128,256]{2,1,0:T(8,128)(2,1)S(1)} %pad_maximum_fusion.2), channel_id=1, source_target_pairs={{0,2},{2,0},{4,6},{6,4},{8,10},{10,8},{12,14},{14,12},{1,3},{3,1},... | collective-permute-start | bytes 393224 | tf_op jit(solution)/shard_map/ppermute | solution.py:185
  90.1 6.4 %collective-permute-start.18 = (bf16[4,128,256]{2,1,0:T(8,128)(2,1)S(1)}, bf16[4,128,256]{2,1,0:T(8,128)(2,1)S(1)}, u32[]{:S(2)}, u32[]{:S(2)}) collective-permute-start(bf16[4,128,256]{2,1,0:T(8,128)(2,1)S(1)} %pad_maximum_fusion.1.near), channel_id=1, source_target_pairs={{0,2},{2,0},{4,6},{6,4},{8,10},{10,8},{12,14},{14,12},{1,3},{3,1},... | collective-permute-start | bytes 786440 | tf_op jit(solution)/shard_map/ppermute | solution.py:185
  92.0 6.4 %collective-permute-start.19 = (bf16[4,128,256]{2,1,0:T(8,128)(2,1)S(1)}, bf16[4,128,256]{2,1,0:T(8,128)(2,1)S(1)}, u32[]{:S(2)}, u32[]{:S(2)}) collective-permute-start(bf16[4,128,256]{2,1,0:T(8,128)(2,1)S(1)} %pad_maximum_fusion.near_other), channel_id=1, source_target_pairs={{0,4},{2,6},{4,0},{6,2},{8,12},{10,14},{12,8},{14,10},{1,5},{3,7},... | collective-permute-start | bytes 786440 | tf_op jit(solution)/shard_map/ppermute | solution.py:185
  106.8 46.8 %collective-permute-start.21 = (bf16[6,128,256]{2,1,0:T(8,128)(2,1)S(1)}, bf16[6,128,256]{2,1,0:T(8,128)(2,1)S(1)}, u32[]{:S(2)}, u32[]{:S(2)}) collective-permute-start(bf16[6,128,256]{2,1,0:T(8,128)(2,1)S(1)} %get-tuple-element.78), channel_id=1, source_target_pairs={{0,8},{2,10},{4,12},{6,14},{8,0},{10,2},{12,4},{14,6},{1,9},{3,11}... | collective-permute-start | bytes 1179656 | tf_op jit(solution)/shard_map/ppermute | solution.py:182
  109.7 43.9 %collective-permute-start.22 = (bf16[6,128,256]{2,1,0:T(8,128)(2,1)S(1)}, bf16[6,128,256]{2,1,0:T(8,128)(2,1)S(1)}, u32[]{:S(2)}, u32[]{:S(2)}) collective-permute-start(bf16[6,128,256]{2,1,0:T(8,128)(2,1)S(1)} %get-tuple-element.79), channel_id=1, source_target_pairs={{0,6},{2,8},{4,10},{6,12},{8,14},{10,0},{12,2},{14,4},{1,7},{3,9},... | collective-permute-start | bytes 1179656 | tf_op jit(solution)/shard_map/ppermute | solution.py:182
  111.6 46.9 %collective-permute-start.23 = (bf16[6,128,256]{2,1,0:T(8,128)(2,1)S(1)}, bf16[6,128,256]{2,1,0:T(8,128)(2,1)S(1)}, u32[]{:S(2)}, u32[]{:S(2)}) collective-permute-start(bf16[6,128,256]{2,1,0:T(8,128)(2,1)S(1)} %get-tuple-element.80), channel_id=1, source_target_pairs={{0,10},{2,12},{4,14},{6,0},{8,2},{10,4},{12,6},{14,8},{1,11},{3,13... | collective-permute-start | bytes 1179656 | tf_op jit(solution)/shard_map/ppermute | solution.py:182
  113.8 44.7 %collective-permute-start.24 = (bf16[6,128,256]{2,1,0:T(8,128)(2,1)S(1)}, bf16[6,128,256]{2,1,0:T(8,128)(2,1)S(1)}, u32[]{:S(2)}, u32[]{:S(2)}) collective-permute-start(bf16[6,128,256]{2,1,0:T(8,128)(2,1)S(1)} %get-tuple-element.81), channel_id=1, source_target_pairs={{0,4},{2,6},{4,8},{6,10},{8,12},{10,14},{12,0},{14,2},{1,5},{3,7},... | collective-permute-start | bytes 1179656 | tf_op jit(solution)/shard_map/ppermute | solution.py:182
  115.9 42.6 %collective-permute-start.25 = (bf16[6,128,256]{2,1,0:T(8,128)(2,1)S(1)}, bf16[6,128,256]{2,1,0:T(8,128)(2,1)S(1)}, u32[]{:S(2)}, u32[]{:S(2)}) collective-permute-start(bf16[6,128,256]{2,1,0:T(8,128)(2,1)S(1)} %get-tuple-element.82), channel_id=1, source_target_pairs={{0,12},{2,14},{4,0},{6,2},{8,4},{10,6},{12,8},{14,10},{1,13},{3,15... | collective-permute-start | bytes 1179656 | tf_op jit(solution)/shard_map/ppermute | solution.py:182
  153.6 23.5 %collective-permute-start.26 = (bf16[6,128,256]{2,1,0:T(8,128)(2,1)S(1)}, bf16[6,128,256]{2,1,0:T(8,128)(2,1)S(1)}, u32[]{:S(2)}, u32[]{:S(2)}) collective-permute-start(bf16[6,128,256]{2,1,0:T(8,128)(2,1)S(1)} %get-tuple-element.83), channel_id=1, source_target_pairs={{0,2},{2,4},{4,6},{6,8},{8,10},{10,12},{12,14},{14,0},{1,3},{3,5},... | collective-permute-start | bytes 1179656 | tf_op jit(solution)/shard_map/ppermute | solution.py:182
  153.6 23.5 %collective-permute-start.27 = (bf16[6,128,256]{2,1,0:T(8,128)(2,1)S(1)}, bf16[6,128,256]{2,1,0:T(8,128)(2,1)S(1)}, u32[]{:S(2)}, u32[]{:S(2)}) collective-permute-start(bf16[6,128,256]{2,1,0:T(8,128)(2,1)S(1)} %get-tuple-element.84), channel_id=1, source_target_pairs={{0,14},{2,0},{4,2},{6,4},{8,6},{10,8},{12,10},{14,12},{1,15},{3,1}... | collective-permute-start | bytes 1179656 | tf_op jit(solution)/shard_map/ppermute | solution.py:182
  (9 other events, 92.8 us)

commit v9 on v8

--- a/solution.py
+++ b/solution.py
@@ -19,13 +19,15 @@
     joined = source * devices + target
     earlier = (joined[:, None] == joined[None, :]) & (numbers[None, :] < numbers[:, None])
     rank = jnp.sum(earlier.astype(jnp.int32), axis=1)
-    own_target = lax.dynamic_slice_in_dim(target, me * blocks_dev, blocks_dev, 0)
-    own_rank = lax.dynamic_slice_in_dim(rank, me * blocks_dev, blocks_dev, 0)
+    held = []
+    for device in (me, me ^ (devices // 2)):
+        for values in (target, rank):
+            held.append(lax.dynamic_slice_in_dim(values, device * blocks_dev, blocks_dev, 0))
     rows = me * blocks_dev + jnp.arange(blocks_dev, dtype=jnp.int32)
     hot = slots[None, :] == rows[:, None]
     row_source = jnp.sum(jnp.where(hot, source[None, :], 0), axis=1)
     row_rank = jnp.sum(jnp.where(hot, rank[None, :], 0), axis=1)
-    return own_target, own_rank, row_source, row_rank
+    return held[:2], held[2:], (row_source, row_rank)
 
 
 def slots_of(steps, ranks, devices, cap):
@@ -101,29 +103,49 @@
 
 
 def scatter_coulomb_kernel(devices, blocks, cap, table, screen, own, other, *rest):
-    sends, ready = rest[:devices], rest[devices]
+    near, far, whole, ready = rest[: devices // 2], rest[devices // 2 : devices], rest[-2], rest[-1]
+    part = whole.shape[2]
     for b in range(blocks):
         value = (own[b] + other[b].astype(jnp.float32)) * screen[b]
         ready[b] = value.astype(jnp.bfloat16)
+        whole[b] = ready[b, :, pl.ds(0, part)]
     for group in range(2):
         for step in range(devices):
             for rank in range(cap):
                 b = jnp.maximum(table[(group * devices + step) * cap + rank], 0)
-                sends[step][group * cap + rank] = ready[b]
-
-
-def gather_coulomb_kernel(steps, blocks, shell, cap, table, *rest):
-    devices = len(steps)
-    rows, cols, landed, done, sems = rest[devices:]
+                if step < devices // 2:
+                    near[step][group * cap + rank] = ready[b]
+                else:
+                    far[step - devices // 2][group * cap + rank] = ready[b, :, pl.ds(part, part)]
+
+
+def pass_on_kernel(devices, cap, table, whole, *outs):
+    for group in range(2):
+        for step in range(devices // 2):
+            for rank in range(cap):
+                b = jnp.maximum(table[(group * devices + devices // 2 + step) * cap + rank], 0)
+                outs[step][group * cap + rank] = whole[b]
+
+
+def gather_coulomb_kernel(devices, blocks, shell, cap, table, *rest):
+    half = devices // 2
+    near, far, passed = rest[:half], rest[half:devices], rest[devices : devices + half]
+    rows, cols, landed, done, sems = rest[devices + half :]
     pairs = landed.shape[3]
-    for step, piece in zip(steps, rest):
+    part = far[0].shape[2]
+    for step in range(devices):
         for group in range(2):
             for rank in range(cap):
                 row = table[(group * devices + step) * cap + rank]
+                at = group * cap + rank
 
                 @pl.when(row >= 0)
                 def _():
-                    landed[group, row] = piece[group * cap + rank]
+                    if step < half:
+                        landed[group, row] = near[step][at]
+                    else:
+                        landed[group, row, :, pl.ds(0, part)] = passed[step - half][at]
+                        landed[group, row, :, pl.ds(part, part)] = far[step - half][at]
 
     to = lax.broadcasted_iota(jnp.int32, (pairs, pairs), 0)
     source = lax.broadcasted_iota(jnp.int32, (pairs, pairs), 1)
@@ -156,6 +178,7 @@
     me = lax.axis_index("pair")
     core = lax.axis_index("aux")
     half = ndens // cores
+    part = pairs // 2
     width = aux_dev // n
     cap = 2 + (blocks - 1) // n
     bf16, f32 = jnp.bfloat16, jnp.float32
@@ -178,9 +201,6 @@
             name=name,
         )(table, *args, *ready)
 
-    def shift(x, d):
-        return lax.ppermute(x, "pair", [(s, (s + d) % n) for s in range(n)])
-
     def flip(x, bit):
         return lax.ppermute(x, "pair", [(s, s ^ bit) for s in range(n)])
 
@@ -190,10 +210,12 @@
     def after(x, *others):
         return lax.optimization_barrier((x, *others))[0]
 
-    home_target, home_rank, home_source, home_row_rank = tables(home_slot, n, blocks, me)
-    held = functools.partial(slots_of, devices=n, cap=cap)
-    send_table = ints([held((home_source - me) % n, home_row_rank), core[None].astype(jnp.int32)])
-    pick_table = held((me - home_target) % n, home_rank)
+    def slots(peers, ranks, device):
+        return slots_of(peers ^ device, ranks, n, cap)
+
+    home_held, home_passed, home_rows = tables(home_slot, n, blocks, me)
+    send_table = ints([slots(*home_rows, me), core[None].astype(jnp.int32)])
+    pick_table = slots(*home_held, me)
     chunk_table = me ^ jnp.arange(n, dtype=jnp.int32)
     weight = jnp.where(pair_shells[:, 0] != pair_shells[:, 1], 2.0, 1.0)
     factor = (screen.astype(f32) * weight[:, None]).astype(bf16)[:, None, :]
@@ -212,8 +234,8 @@
         compiler_params=pltpu.CompilerParams(vmem_limit_bytes=VMEM_BYTES),
         name="scatter_density",
     )(send_table, density)
-    steps = sorted(range(1, n), key=lambda d: abs(2 * d - n))
-    received = [shift(sends[d], d) for d in steps[:-1]]
+    steps = [*range(n // 2, n), *range(1, n // 2)]
+    received = [flip(sends[d], d) for d in steps[:-1]]
     integrals = pl.pallas_call(
         load_kernel,
         out_shape=pltpu.VMEM((blocks, pairs, aux_dev), bf16),
@@ -223,7 +245,7 @@
         compiler_params=pltpu.CompilerParams(vmem_limit_bytes=2 * 1024 * 1024),
         name="load_integrals",
     )(three_index, received[0])
-    received += [shift(after(sends[steps[-1]], integrals), steps[-1]), sends[0]]
+    received += [flip(after(sends[steps[-1]], integrals), steps[-1]), sends[0]]
     steps = (*steps, 0)
     own = call(
         functools.partial(gather_density_kernel, steps, cap),
@@ -235,18 +257,10 @@
     )
     other = swap(own)
 
-    mirror_target, mirror_rank, mirror_source, mirror_row_rank = tables(
-        after(mirror_slot, own), n, blocks, me
-    )
-    out_table = ints(
-        [
-            held((home_target - me) % n, home_rank),
-            held((mirror_target - me) % n, mirror_rank),
-        ]
-    )
-    in_table = ints(
-        [held((me - home_source) % n, home_row_rank), held((me - mirror_source) % n, mirror_row_rank)]
-    )
+    mirror_held, mirror_passed, mirror_rows = tables(after(mirror_slot, own), n, blocks, me)
+    out_table = ints([slots(*home_held, me), slots(*mirror_held, me)])
+    pass_table = ints([slots(*held, me ^ (n // 2)) for held in (home_passed, mirror_passed)])
+    in_table = ints([slots(*home_rows, me), slots(*mirror_rows, me)])
 
     bits = [1 << j for j in range(n.bit_length() - 1)]
     orders = (bits[1::-1] + bits[2:], bits)
@@ -311,16 +325,29 @@
         "scatter_coulomb",
         out_table,
         [keeping, mine, swap(theirs)],
-        [jax.ShapeDtypeStruct((2 * cap, half, pairs), bf16)] * n,
-        [in_vmem] * n,
+        [jax.ShapeDtypeStruct((2 * cap, half, pairs), bf16)] * (n // 2)
+        + [jax.ShapeDtypeStruct((2 * cap, half, part), bf16)] * (n // 2)
+        + [jax.ShapeDtypeStruct((blocks, half, part), bf16)],
+        [in_vmem] * (n + 1),
         scratch=[pltpu.VMEM((blocks, half, pairs), bf16)],
     )
-    received = [shift(sends[d], d) if d else sends[d] for d in steps]
+    whole = flip(sends[n], n // 2)
+    far = [flip(sends[d], d) for d in range(n // 2, n)]
+    near = [sends[0]] + [flip(sends[d], d) for d in range(1, n // 2)]
+    passed = call(
+        functools.partial(pass_on_kernel, n, cap),
+        "pass_on",
+        pass_table,
+        [whole],
+        [jax.ShapeDtypeStruct((2 * cap, half, part), bf16)] * (n // 2),
+        [in_vmem] * (n // 2),
+    )
+    passed = [passed[0]] + [flip(passed[d], d) for d in range(1, n // 2)]
     return call(
-        functools.partial(gather_coulomb_kernel, steps, blocks, shell, cap),
+        functools.partial(gather_coulomb_kernel, n, blocks, shell, cap),
         "gather_coulomb",
         in_table,
-        received,
+        [*near, *far, *passed],
         [jax.ShapeDtypeStruct((blocks, pairs, half), bf16)] * 2,
         [anywhere] * 2,
         scratch=[

time: 180 us -> 187 us (1.039)
  waiting for transfers between devices: 103 us -> 108 us
    ppermute x12 -> x30, waiting for transfers between devices: 28.9 us -> 106 us  [flip(): return lax.ppermute(x, 'pair', [(s, s ^ bit) for s in range(n)])]
    ppermute x14 -> x0, waiting for transfers between devices: 72.6 us -> none  [shift(): return lax.ppermute(x, 'pair', [(s, (s + d) % n) for s in range(n)])]
    ppermute x12 -> x30, starting transfers between devices: 16.4 us -> 49.5 us  [flip(): return lax.ppermute(x, 'pair', [(s, s ^ bit) for s in range(n)])]
    ppermute x14 -> x0, starting transfers between devices: 31.8 us -> none  [shift(): return lax.ppermute(x, 'pair', [(s, (s + d) % n) for s in range(n)])]
    pallas_call x6 -> x7, Pallas kernels: 15.2 us -> 16 us  [call(): pl.pallas_call(kernel, out_shape=out_shape, grid_spec=pltpu.PrefetchScala...]
  transfers between devices with their start and end apart: 28 -> 32, of which waited for: 15 -> 21; matrix products, arithmetic and copies ran while one was open for 1% -> 1% of each run, Pallas kernels for 2% -> 2%
where the time goes in v9:
time: 187 us
  waiting for transfers between devices  108 us (58%)
  starting transfers between devices  49.6 us (27%)
  Pallas kernels  17.9 us (10%)
  local copies, waits for them, and re-layouts  6.81 us (4%)
  other arithmetic  3.47 us (2%)
    ppermute x30, waiting for transfers between devices, flip(): return lax.ppermute(x, 'pair', [(s, s ^ bit) for s in range(n)])  106 us
    ppermute x30, starting transfers between devices, flip(): return lax.ppermute(x, 'pair', [(s, s ^ bit) for s in range(n)])  49.5 us
    pallas_call x7, Pallas kernels, call(): pl.pallas_call(kernel, out_shape=out_shape, grid_spec=pltpu.PrefetchScala...  16 us
    unnamed x10, local copies, waits for them, and re-layouts  6.69 us
  transfers between devices with their start and end apart: 32, of which 21 were waited for; matrix products, arithmetic and copies ran while one was open for 1% of the time, Pallas kernels for 2%

profile of v9, /device:TPU:0, one launch (start us, length us, event | category | flops | bytes accessed | tf_op | source)
XLA Modules:
  0.0 186.8 jit_solution(5349795412570155600)
XLA Ops:
  5.1 4.1 %collective-permute-start = (bf16[3,128,256]{2,1,0:T(8,128)(2,1)S(1)}, bf16[3,128,256]{2,1,0:T(8,128)(2,1)S(1)}, u32[]{:S(2)}, u32[]{:S(2)}) collective-permute-start(bf16[3,128,256]{2,1,0:T(8,128)(2,1)S(1)} %get-tuple-element.49), channel_id=1, source_target_pairs={{0,8},{2,10},{4,12},{6,14},{8,0},{10,2},{12,4},{14,6},{1,9},{3,11}... | collective-permute-start | bytes 589832 | tf_op jit(solution)/shard_map/ppermute | solution.py:205
  10.5 3.6 %collective-permute-start.2 = (bf16[3,128,256]{2,1,0:T(8,128)(2,1)S(1)}, bf16[3,128,256]{2,1,0:T(8,128)(2,1)S(1)}, u32[]{:S(2)}, u32[]{:S(2)}) collective-permute-start(bf16[3,128,256]{2,1,0:T(8,128)(2,1)S(1)} %get-tuple-element.51), channel_id=1, source_target_pairs={{0,12},{2,14},{4,8},{6,10},{8,4},{10,6},{12,0},{14,2},{1,13},{3,15... | collective-permute-start | bytes 589832 | tf_op jit(solution)/shard_map/ppermute | solution.py:205
  15.8 16.0 %collective-permute-done.ready.rest_0_ = bf16[3,128,256]{2,1,0:T(8,128)(2,1)S(1)} collective-permute-done((bf16[3,128,256]{2,1,0:T(8,128)(2,1)S(1)}, bf16[3,128,256]{2,1,0:T(8,128)(2,1)S(1)}, u32[]{:S(2)}, u32[]{:S(2)}) %collective-permute-start) | collective-permute-done | bytes 196640 | tf_op jit(solution)/shard_map/ppermute | solution.py:205
  31.8 5.2 %copy-done = bf16[14,256,2048]{2,1,0:T(8,128)(2,1)S(1)} copy-done((bf16[14,256,2048]{2,1,0:T(8,128)(2,1)S(1)}, bf16[14,256,2048]{2,1,0:T(8,128)(2,1)}, u32[]{:S(2)}) %copy-start) | copy-done | bytes 14680088
  38.0 3.4 %collective-permute-start.6 = (bf16[3,128,256]{2,1,0:T(8,128)(2,1)S(1)}, bf16[3,128,256]{2,1,0:T(8,128)(2,1)S(1)}, u32[]{:S(2)}, u32[]{:S(2)}) collective-permute-start(bf16[3,128,256]{2,1,0:T(8,128)(2,1)S(1)} %get-tuple-element.56), channel_id=1, source_target_pairs={{0,6},{2,4},{4,2},{6,0},{8,14},{10,12},{12,10},{14,8},{1,7},{3,5},... | collective-permute-start | bytes 589832 | tf_op jit(solution)/shard_map/ppermute | solution.py:205
  41.5 4.4 %collective-permute-done.6.rest_6_ = bf16[3,128,256]{2,1,0:T(8,128)(2,1)S(1)} collective-permute-done((bf16[3,128,256]{2,1,0:T(8,128)(2,1)S(1)}, bf16[3,128,256]{2,1,0:T(8,128)(2,1)S(1)}, u32[]{:S(2)}, u32[]{:S(2)}) %collective-permute-start.6) | collective-permute-done | bytes 196640 | tf_op jit(solution)/shard_map/ppermute | solution.py:205
  46.8 2.8 %fit.2 = (f32[4,128,256]{2,1,0:T(8,128)S(1)}, bf16[4,128,256]{2,1,0:T(8,128)(2,1)S(1)}) custom-call(s32[8]{0:T(128)S(1)} %iota_xor_fusion.table, bf16[14,1,256]{2,1,0:T(2,128)(2,1)S(1)} %copy.11.factor, bf16[14,128,256]{2,1,0:T(8,128)(2,1)S(1)} %gather_density.1.density, bf16[14,256,2048]{2,1,0:T(8,128)(2,1)S(1)} %load_integrals.1.integrals), custom_call_target="tpu_custom_call" | custom-call | tf_op jit(solution)/shard_map/fit/pallas_call | solution.py:190
  49.6 2.7 %fit.3 = (f32[4,128,256]{2,1,0:T(8,128)S(1)}, bf16[4,128,256]{2,1,0:T(8,128)(2,1)S(1)}) custom-call(s32[8]{0:T(128)S(1)} %iota_xor_fusion.table, bf16[14,1,256]{2,1,0:T(2,128)(2,1)S(1)} %copy.11.factor, bf16[14,128,256]{2,1,0:T(8,128)(2,1)S(1)} %collective-permute-done.7.density, bf16[14,256,2048]{2,1,0:T(8,128)(2,1)S(1)} %load_integrals.1.integrals, ...), custom_call_target="tpu_custom_call" | custom-call | tf_op jit(solution)/shard_map/fit/pallas_call | solution.py:190
  52.3 3.5 %collective-permute-start.8 = (bf16[4,128,256]{2,1,0:T(8,128)(2,1)S(1)}, bf16[4,128,256]{2,1,0:T(8,128)(2,1)S(1)}, u32[]{:S(2)}, u32[]{:S(2)}) collective-permute-start(bf16[4,128,256]{2,1,0:T(8,128)(2,1)S(1)} %get-tuple-element.64), channel_id=1, source_target_pairs={{0,4},{2,6},{4,0},{6,2},{8,12},{10,14},{12,8},{14,10},{1,5},{3,7},... | collective-permute-start | bytes 786440 | tf_op jit(solution)/shard_map/ppermute | solution.py:205
  56.5 6.3 %collective-permute-done.8 = bf16[4,128,256]{2,1,0:T(8,128)(2,1)S(1)} collective-permute-done((bf16[4,128,256]{2,1,0:T(8,128)(2,1)S(1)}, bf16[4,128,256]{2,1,0:T(8,128)(2,1)S(1)}, u32[]{:S(2)}, u32[]{:S(2)}) %collective-permute-start.8) | collective-permute-done | bytes 262176 | tf_op jit(solution)/shard_map/ppermute | solution.py:205
  65.5 3.9 %collective-permute-done.10 = bf16[2,128,256]{2,1,0:T(8,128)(2,1)S(1)} collective-permute-done((bf16[2,128,256]{2,1,0:T(8,128)(2,1)S(1)}, bf16[2,128,256]{2,1,0:T(8,128)(2,1)S(1)}, u32[]{:S(2)}, u32[]{:S(2)}) %collective-permute-start.10) | collective-permute-done | bytes 131104 | tf_op jit(solution)/shard_map/ppermute | solution.py:205
  73.1 4.1 %collective-permute-done.12 = bf16[1,128,256]{2,1,0:T(8,128)(2,1)S(1)} collective-permute-done((bf16[1,128,256]{2,1,0:T(8,128)(2,1)S(1)}, bf16[1,128,256]{2,1,0:T(8,128)(2,1)S(1)}, u32[]{:S(2)}, u32[]{:S(2)}) %collective-permute-start.12) | collective-permute-done | bytes 65568 | tf_op jit(solution)/shard_map/ppermute | solution.py:205
  80.9 3.9 %collective-permute-done.14 = bf16[1,128,256]{2,1,0:T(8,128)(2,1)S(1)} collective-permute-done((bf16[1,128,256]{2,1,0:T(8,128)(2,1)S(1)}, bf16[1,128,256]{2,1,0:T(8,128)(2,1)S(1)}, u32[]{:S(2)}, u32[]{:S(2)}) %collective-permute-start.14) | collective-permute-done | bytes 65568 | tf_op jit(solution)/shard_map/ppermute | solution.py:205
  90.7 2.6 %collective-permute-done.17 = bf16[2,128,256]{2,1,0:T(8,128)(2,1)S(1)} collective-permute-done((bf16[2,128,256]{2,1,0:T(8,128)(2,1)S(1)}, bf16[2,128,256]{2,1,0:T(8,128)(2,1)S(1)}, u32[]{:S(2)}, u32[]{:S(2)}) %collective-permute-start.17) | collective-permute-done | bytes 131104 | tf_op jit(solution)/shard_map/ppermute | solution.py:205
  94.1 5.6 %collective-permute-done.18.far = bf16[4,128,256]{2,1,0:T(8,128)(2,1)S(1)} collective-permute-done((bf16[4,128,256]{2,1,0:T(8,128)(2,1)S(1)}, bf16[4,128,256]{2,1,0:T(8,128)(2,1)S(1)}, u32[]{:S(2)}, u32[]{:S(2)}) %collective-permute-start.18) | collective-permute-done | bytes 262176 | tf_op jit(solution)/shard_map/ppermute | solution.py:205
  99.8 5.0 %apply.1 = (f32[14,128,256]{2,1,0:T(8,128)S(1)}, bf16[14,128,256]{2,1,0:T(8,128)(2,1)S(1)}) custom-call(s32[8]{0:T(128)S(1)} %iota_xor_fusion.table, bf16[14,256,2048]{2,1,0:T(8,128)(2,1)S(1)} %load_integrals.1.integrals, bf16[4,128,256]{2,1,0:T(8,128)(2,1)S(1)} %pad_maximum_fusion.1.near, bf16[4,128,256]{2,1,0:T(8,128)(2,1)S(1)} %collective-permute-done.18.far, ...), custom_call_target="tpu_custom_call" | custom-call | tf_op jit(solution)/shard_map/apply/pallas_call | solution.py:190
  113.8 2.6 %collective-permute-start.26 = (bf16[6,128,128]{2,1,0:T(8,128)(2,1)S(1)}, bf16[6,128,128]{2,1,0:T(8,128)(2,1)S(1)}, u32[]{:S(2)}, u32[]{:S(2)}) collective-permute-start(bf16[6,128,128]{2,1,0:T(8,128)(2,1)S(1)} %get-tuple-element.89), channel_id=1, source_target_pairs={{0,12},{2,14},{4,8},{6,10},{8,4},{10,6},{12,0},{14,2},{1,13},{3,15... | collective-permute-start | bytes 589832 | tf_op jit(solution)/shard_map/ppermute | solution.py:205
  116.3 32.6 %collective-permute-done.24.rest_4_ = bf16[6,128,128]{2,1,0:T(8,128)(2,1)S(1)} collective-permute-done((bf16[6,128,128]{2,1,0:T(8,128)(2,1)S(1)}, bf16[6,128,128]{2,1,0:T(8,128)(2,1)S(1)}, u32[]{:S(2)}, u32[]{:S(2)}) %collective-permute-start.24) | collective-permute-done | bytes 196640 | tf_op jit(solution)/shard_map/ppermute | solution.py:205
  151.3 6.7 %collective-permute-done.25.rest_5_ = bf16[6,128,128]{2,1,0:T(8,128)(2,1)S(1)} collective-permute-done((bf16[6,128,128]{2,1,0:T(8,128)(2,1)S(1)}, bf16[6,128,128]{2,1,0:T(8,128)(2,1)S(1)}, u32[]{:S(2)}, u32[]{:S(2)}) %collective-permute-start.25) | collective-permute-done | bytes 196640 | tf_op jit(solution)/shard_map/ppermute | solution.py:205
  158.8 3.5 %collective-permute-start.29 = (bf16[6,128,128]{2,1,0:T(8,128)(2,1)S(1)}, bf16[6,128,128]{2,1,0:T(8,128)(2,1)S(1)}, u32[]{:S(2)}, u32[]{:S(2)}) collective-permute-start(bf16[6,128,128]{2,1,0:T(8,128)(2,1)S(1)} %get-tuple-element.93), channel_id=1, source_target_pairs={{0,2},{2,0},{4,6},{6,4},{8,10},{10,8},{12,14},{14,12},{1,3},{3,1},... | collective-permute-start | bytes 589832 | tf_op jit(solution)/shard_map/ppermute | solution.py:205
  162.3 6.8 %collective-permute-start.30 = (bf16[6,128,128]{2,1,0:T(8,128)(2,1)S(1)}, bf16[6,128,128]{2,1,0:T(8,128)(2,1)S(1)}, u32[]{:S(2)}, u32[]{:S(2)}) collective-permute-start(bf16[6,128,128]{2,1,0:T(8,128)(2,1)S(1)} %get-tuple-element.94), channel_id=1, source_target_pairs={{0,4},{2,6},{4,0},{6,2},{8,12},{10,14},{12,8},{14,10},{1,5},{3,7},... | collective-permute-start | bytes 589832 | tf_op jit(solution)/shard_map/ppermute | solution.py:205
  170.0 6.0 %collective-permute-done.23.rest_3_ = bf16[6,128,256]{2,1,0:T(8,128)(2,1)S(1)} collective-permute-done((bf16[6,128,256]{2,1,0:T(8,128)(2,1)S(1)}, bf16[6,128,256]{2,1,0:T(8,128)(2,1)S(1)}, u32[]{:S(2)}, u32[]{:S(2)}) %collective-permute-start.23) | collective-permute-done | bytes 393248 | tf_op jit(solution)/shard_map/ppermute | solution.py:205
  176.0 6.6 %collective-permute-done.30.rest_10_ = bf16[6,128,128]{2,1,0:T(8,128)(2,1)S(1)} collective-permute-done((bf16[6,128,128]{2,1,0:T(8,128)(2,1)S(1)}, bf16[6,128,128]{2,1,0:T(8,128)(2,1)S(1)}, u32[]{:S(2)}, u32[]{:S(2)}) %collective-permute-start.30) | collective-permute-done | bytes 196640 | tf_op jit(solution)/shard_map/ppermute | solution.py:205
  183.7 3.1 %gather_coulomb.1 = (bf16[14,256,128]{2,1,0:T(8,128)(2,1)}, bf16[14,256,128]{2,1,0:T(8,128)(2,1)}) custom-call(s32[48]{0:T(128)S(1)} %pad_add_fusion.1.table, bf16[6,128,256]{2,1,0:T(8,128)(2,1)S(1)} %get-tuple-element.83.rest_0_, bf16[6,128,256]{2,1,0:T(8,128)(2,1)S(1)} %collective-permute-done.21.rest_1_, ...), custom_call_target="tpu_custom_call" | custom-call | tf_op jit(solution)/shard_map/gather_coulomb/pallas_call | solution.py:190
  (104 shorter events, 40.8 us)
Async XLA Ops:
  5.1 26.7 %collective-permute-start = (bf16[3,128,256]{2,1,0:T(8,128)(2,1)S(1)}, bf16[3,128,256]{2,1,0:T(8,128)(2,1)S(1)}, u32[]{:S(2)}, u32[]{:S(2)}) collective-permute-start(bf16[3,128,256]{2,1,0:T(8,128)(2,1)S(1)} %get-tuple-element.49), channel_id=1, source_target_pairs={{0,8},{2,10},{4,12},{6,14},{8,0},{10,2},{12,4},{14,6},{1,9},{3,11}... | collective-permute-start | bytes 589832 | tf_op jit(solution)/shard_map/ppermute | solution.py:205
  9.2 28.8 %collective-permute-start.1 = (bf16[3,128,256]{2,1,0:T(8,128)(2,1)S(1)}, bf16[3,128,256]{2,1,0:T(8,128)(2,1)S(1)}, u32[]{:S(2)}, u32[]{:S(2)}) collective-permute-start(bf16[3,128,256]{2,1,0:T(8,128)(2,1)S(1)} %get-tuple-element.50), channel_id=1, source_target_pairs={{0,10},{2,8},{4,14},{6,12},{8,2},{10,0},{12,6},{14,4},{1,11},{3,9}... | collective-permute-start | bytes 589832 | tf_op jit(solution)/shard_map/ppermute | solution.py:205
  10.5 31.0 %collective-permute-start.2 = (bf16[3,128,256]{2,1,0:T(8,128)(2,1)S(1)}, bf16[3,128,256]{2,1,0:T(8,128)(2,1)S(1)}, u32[]{:S(2)}, u32[]{:S(2)}) collective-permute-start(bf16[3,128,256]{2,1,0:T(8,128)(2,1)S(1)} %get-tuple-element.51), channel_id=1, source_target_pairs={{0,12},{2,14},{4,8},{6,10},{8,4},{10,6},{12,0},{14,2},{1,13},{3,15... | collective-permute-start | bytes 589832 | tf_op jit(solution)/shard_map/ppermute | solution.py:205
  14.1 27.4 %collective-permute-start.3 = (bf16[3,128,256]{2,1,0:T(8,128)(2,1)S(1)}, bf16[3,128,256]{2,1,0:T(8,128)(2,1)S(1)}, u32[]{:S(2)}, u32[]{:S(2)}) collective-permute-start(bf16[3,128,256]{2,1,0:T(8,128)(2,1)S(1)} %get-tuple-element.52), channel_id=1, source_target_pairs={{0,14},{2,12},{4,10},{6,8},{8,6},{10,4},{12,2},{14,0},{1,15},{3,13... | collective-permute-start | bytes 589832 | tf_op jit(solution)/shard_map/ppermute | solution.py:205
  14.1 27.4 %collective-permute-start.4 = (bf16[3,128,256]{2,1,0:T(8,128)(2,1)S(1)}, bf16[3,128,256]{2,1,0:T(8,128)(2,1)S(1)}, u32[]{:S(2)}, u32[]{:S(2)}) collective-permute-start(bf16[3,128,256]{2,1,0:T(8,128)(2,1)S(1)} %get-tuple-element.53), channel_id=1, source_target_pairs={{0,2},{2,0},{4,6},{6,4},{8,10},{10,8},{12,14},{14,12},{1,3},{3,1},... | collective-permute-start | bytes 589832 | tf_op jit(solution)/shard_map/ppermute | solution.py:205
  31.8 9.7 %collective-permute-start.5 = (bf16[3,128,256]{2,1,0:T(8,128)(2,1)S(1)}, bf16[3,128,256]{2,1,0:T(8,128)(2,1)S(1)}, u32[]{:S(2)}, u32[]{:S(2)}) collective-permute-start(bf16[3,128,256]{2,1,0:T(8,128)(2,1)S(1)} %get-tuple-element.54), channel_id=1, source_target_pairs={{0,4},{2,6},{4,0},{6,2},{8,12},{10,14},{12,8},{14,10},{1,5},{3,7},... | collective-permute-start | bytes 589832 | tf_op jit(solution)/shard_map/ppermute | solution.py:205
  38.0 7.9 %collective-permute-start.6 = (bf16[3,128,256]{2,1,0:T(8,128)(2,1)S(1)}, bf16[3,128,256]{2,1,0:T(8,128)(2,1)S(1)}, u32[]{:S(2)}, u32[]{:S(2)}) collective-permute-start(bf16[3,128,256]{2,1,0:T(8,128)(2,1)S(1)} %get-tuple-element.56), channel_id=1, source_target_pairs={{0,6},{2,4},{4,2},{6,0},{8,14},{10,12},{12,10},{14,8},{1,7},{3,5},... | collective-permute-start | bytes 589832 | tf_op jit(solution)/shard_map/ppermute | solution.py:205
  52.3 10.5 %collective-permute-start.8 = (bf16[4,128,256]{2,1,0:T(8,128)(2,1)S(1)}, bf16[4,128,256]{2,1,0:T(8,128)(2,1)S(1)}, u32[]{:S(2)}, u32[]{:S(2)}) collective-permute-start(bf16[4,128,256]{2,1,0:T(8,128)(2,1)S(1)} %get-tuple-element.64), channel_id=1, source_target_pairs={{0,4},{2,6},{4,0},{6,2},{8,12},{10,14},{12,8},{14,10},{1,5},{3,7},... | collective-permute-start | bytes 786440 | tf_op jit(solution)/shard_map/ppermute | solution.py:205
  55.9 8.4 %collective-permute-start.9 = (bf16[4,128,256]{2,1,0:T(8,128)(2,1)S(1)}, bf16[4,128,256]{2,1,0:T(8,128)(2,1)S(1)}, u32[]{:S(2)}, u32[]{:S(2)}) collective-permute-start(bf16[4,128,256]{2,1,0:T(8,128)(2,1)S(1)} %get-tuple-element.66), channel_id=1, source_target_pairs={{0,2},{2,0},{4,6},{6,4},{8,10},{10,8},{12,14},{14,12},{1,3},{3,1},... | collective-permute-start | bytes 786440 | tf_op jit(solution)/shard_map/ppermute | solution.py:205
  70.2 7.1 %collective-permute-start.12 = (bf16[1,128,256]{2,1,0:T(8,128)(2,1)S(1)}, bf16[1,128,256]{2,1,0:T(8,128)(2,1)S(1)}, u32[]{:S(2)}, u32[]{:S(2)}) collective-permute-start(bf16[1,128,256]{2,1,0:T(8,128)(2,1)S(1)} %slice.57), channel_id=1, source_target_pairs={{0,8},{2,10},{4,12},{6,14},{8,0},{10,2},{12,4},{14,6},{1,9},{3,11}... | collective-permute-start | bytes 196616 | tf_op jit(solution)/shard_map/ppermute | solution.py:205
  78.0 6.9 %collective-permute-start.14 = (bf16[1,128,256]{2,1,0:T(8,128)(2,1)S(1)}, bf16[1,128,256]{2,1,0:T(8,128)(2,1)S(1)}, u32[]{:S(2)}, u32[]{:S(2)}) collective-permute-start(bf16[1,128,256]{2,1,0:T(8,128)(2,1)S(1)} %add_convert_fusion.1), channel_id=1, source_target_pairs={{0,8},{2,10},{4,12},{6,14},{8,0},{10,2},{12,4},{14,6},{1,9},{3,11}... | collective-permute-start | bytes 196616 | tf_op jit(solution)/shard_map/ppermute | solution.py:205
  78.7 6.9 %collective-permute-start.15 = (bf16[1,128,256]{2,1,0:T(8,128)(2,1)S(1)}, bf16[1,128,256]{2,1,0:T(8,128)(2,1)S(1)}, u32[]{:S(2)}, u32[]{:S(2)}) collective-permute-start(bf16[1,128,256]{2,1,0:T(8,128)(2,1)S(1)} %add_convert_fusion), channel_id=1, source_target_pairs={{0,8},{2,10},{4,12},{6,14},{8,0},{10,2},{12,4},{14,6},{1,9},{3,11}... | collective-permute-start | bytes 196616 | tf_op jit(solution)/shard_map/ppermute | solution.py:205
  93.3 6.4 %collective-permute-start.18 = (bf16[4,128,256]{2,1,0:T(8,128)(2,1)S(1)}, bf16[4,128,256]{2,1,0:T(8,128)(2,1)S(1)}, u32[]{:S(2)}, u32[]{:S(2)}) collective-permute-start(bf16[4,128,256]{2,1,0:T(8,128)(2,1)S(1)} %pad_maximum_fusion.1.near), channel_id=1, source_target_pairs={{0,2},{2,0},{4,6},{6,4},{8,10},{10,8},{12,14},{14,12},{1,3},{3,1},... | collective-permute-start | bytes 786440 | tf_op jit(solution)/shard_map/ppermute | solution.py:205
  108.4 49.6 %collective-permute-start.28 = (bf16[14,128,128]{2,1,0:T(8,128)(2,1)S(1)}, bf16[14,128,128]{2,1,0:T(8,128)(2,1)S(1)}, u32[]{:S(2)}, u32[]{:S(2)}) collective-permute-start(bf16[14,128,128]{2,1,0:T(8,128)(2,1)S(1)} %get-tuple-element.91), channel_id=1, source_target_pairs={{0,8},{2,10},{4,12},{6,14},{8,0},{10,2},{12,4},{14,6},{1,9},{3,11}... | collective-permute-start | bytes 1376264 | tf_op jit(solution)/shard_map/ppermute | solution.py:205
  109.3 39.6 %collective-permute-start.24 = (bf16[6,128,128]{2,1,0:T(8,128)(2,1)S(1)}, bf16[6,128,128]{2,1,0:T(8,128)(2,1)S(1)}, u32[]{:S(2)}, u32[]{:S(2)}) collective-permute-start(bf16[6,128,128]{2,1,0:T(8,128)(2,1)S(1)} %get-tuple-element.87), channel_id=1, source_target_pairs={{0,8},{2,10},{4,12},{6,14},{8,0},{10,2},{12,4},{14,6},{1,9},{3,11}... | collective-permute-start | bytes 589832 | tf_op jit(solution)/shard_map/ppermute | solution.py:205
  111.7 46.3 %collective-permute-start.25 = (bf16[6,128,128]{2,1,0:T(8,128)(2,1)S(1)}, bf16[6,128,128]{2,1,0:T(8,128)(2,1)S(1)}, u32[]{:S(2)}, u32[]{:S(2)}) collective-permute-start(bf16[6,128,128]{2,1,0:T(8,128)(2,1)S(1)} %get-tuple-element.88), channel_id=1, source_target_pairs={{0,10},{2,8},{4,14},{6,12},{8,2},{10,0},{12,6},{14,4},{1,11},{3,9}... | collective-permute-start | bytes 589832 | tf_op jit(solution)/shard_map/ppermute | solution.py:205
  113.3 55.9 %collective-permute-start.21 = (bf16[6,128,256]{2,1,0:T(8,128)(2,1)S(1)}, bf16[6,128,256]{2,1,0:T(8,128)(2,1)S(1)}, u32[]{:S(2)}, u32[]{:S(2)}) collective-permute-start(bf16[6,128,256]{2,1,0:T(8,128)(2,1)S(1)} %get-tuple-element.84), channel_id=1, source_target_pairs={{0,2},{2,0},{4,6},{6,4},{8,10},{10,8},{12,14},{14,12},{1,3},{3,1},... | collective-permute-start | bytes 1179656 | tf_op jit(solution)/shard_map/ppermute | solution.py:205
  113.8 45.0 %collective-permute-start.26 = (bf16[6,128,128]{2,1,0:T(8,128)(2,1)S(1)}, bf16[6,128,128]{2,1,0:T(8,128)(2,1)S(1)}, u32[]{:S(2)}, u32[]{:S(2)}) collective-permute-start(bf16[6,128,128]{2,1,0:T(8,128)(2,1)S(1)} %get-tuple-element.89), channel_id=1, source_target_pairs={{0,12},{2,14},{4,8},{6,10},{8,4},{10,6},{12,0},{14,2},{1,13},{3,15... | collective-permute-start | bytes 589832 | tf_op jit(solution)/shard_map/ppermute | solution.py:205
  148.9 13.4 %collective-permute-start.27 = (bf16[6,128,128]{2,1,0:T(8,128)(2,1)S(1)}, bf16[6,128,128]{2,1,0:T(8,128)(2,1)S(1)}, u32[]{:S(2)}, u32[]{:S(2)}) collective-permute-start(bf16[6,128,128]{2,1,0:T(8,128)(2,1)S(1)} %get-tuple-element.90), channel_id=1, source_target_pairs={{0,14},{2,12},{4,10},{6,8},{8,6},{10,4},{12,2},{14,0},{1,15},{3,13... | collective-permute-start | bytes 589832 | tf_op jit(solution)/shard_map/ppermute | solution.py:205
  158.0 12.1 %collective-permute-start.22 = (bf16[6,128,256]{2,1,0:T(8,128)(2,1)S(1)}, bf16[6,128,256]{2,1,0:T(8,128)(2,1)S(1)}, u32[]{:S(2)}, u32[]{:S(2)}) collective-permute-start(bf16[6,128,256]{2,1,0:T(8,128)(2,1)S(1)} %get-tuple-element.85), channel_id=1, source_target_pairs={{0,4},{2,6},{4,0},{6,2},{8,12},{10,14},{12,8},{14,10},{1,5},{3,7},... | collective-permute-start | bytes 1179656 | tf_op jit(solution)/shard_map/ppermute | solution.py:205
  158.0 18.0 %collective-permute-start.23 = (bf16[6,128,256]{2,1,0:T(8,128)(2,1)S(1)}, bf16[6,128,256]{2,1,0:T(8,128)(2,1)S(1)}, u32[]{:S(2)}, u32[]{:S(2)}) collective-permute-start(bf16[6,128,256]{2,1,0:T(8,128)(2,1)S(1)} %get-tuple-element.86), channel_id=1, source_target_pairs={{0,6},{2,4},{4,2},{6,0},{8,14},{10,12},{12,10},{14,8},{1,7},{3,5},... | collective-permute-start | bytes 1179656 | tf_op jit(solution)/shard_map/ppermute | solution.py:205
  158.8 17.3 %collective-permute-start.29 = (bf16[6,128,128]{2,1,0:T(8,128)(2,1)S(1)}, bf16[6,128,128]{2,1,0:T(8,128)(2,1)S(1)}, u32[]{:S(2)}, u32[]{:S(2)}) collective-permute-start(bf16[6,128,128]{2,1,0:T(8,128)(2,1)S(1)} %get-tuple-element.93), channel_id=1, source_target_pairs={{0,2},{2,0},{4,6},{6,4},{8,10},{10,8},{12,14},{14,12},{1,3},{3,1},... | collective-permute-start | bytes 589832 | tf_op jit(solution)/shard_map/ppermute | solution.py:205
  162.3 20.4 %collective-permute-start.30 = (bf16[6,128,128]{2,1,0:T(8,128)(2,1)S(1)}, bf16[6,128,128]{2,1,0:T(8,128)(2,1)S(1)}, u32[]{:S(2)}, u32[]{:S(2)}) collective-permute-start(bf16[6,128,128]{2,1,0:T(8,128)(2,1)S(1)} %get-tuple-element.94), channel_id=1, source_target_pairs={{0,4},{2,6},{4,0},{6,2},{8,12},{10,14},{12,8},{14,10},{1,5},{3,7},... | collective-permute-start | bytes 589832 | tf_op jit(solution)/shard_map/ppermute | solution.py:205
  169.2 14.6 %collective-permute-start.31 = (bf16[6,128,128]{2,1,0:T(8,128)(2,1)S(1)}, bf16[6,128,128]{2,1,0:T(8,128)(2,1)S(1)}, u32[]{:S(2)}, u32[]{:S(2)}) collective-permute-start(bf16[6,128,128]{2,1,0:T(8,128)(2,1)S(1)} %get-tuple-element.95), channel_id=1, source_target_pairs={{0,6},{2,4},{4,2},{6,0},{8,14},{10,12},{12,10},{14,8},{1,7},{3,5},... | collective-permute-start | bytes 589832 | tf_op jit(solution)/shard_map/ppermute | solution.py:205
  (13 other events, 117.0 us)

commit v10 on v9

--- a/solution.py
+++ b/solution.py
@@ -129,7 +129,7 @@
 
 def gather_coulomb_kernel(devices, blocks, shell, cap, table, *rest):
     half = devices // 2
-    near, far, passed = rest[:half], rest[half:devices], rest[devices : devices + half]
+    near, passed, far = rest[:half], rest[half:devices], rest[devices : devices + half]
     rows, cols, landed, done, sems = rest[devices + half :]
     pairs = landed.shape[3]
     part = far[0].shape[2]
@@ -234,7 +234,7 @@
         compiler_params=pltpu.CompilerParams(vmem_limit_bytes=VMEM_BYTES),
         name="scatter_density",
     )(send_table, density)
-    steps = [*range(n // 2, n), *range(1, n // 2)]
+    steps = range(1, n)
     received = [flip(sends[d], d) for d in steps[:-1]]
     integrals = pl.pallas_call(
         load_kernel,
@@ -244,7 +244,7 @@
         scratch_shapes=[pltpu.SemaphoreType.DMA],
         compiler_params=pltpu.CompilerParams(vmem_limit_bytes=2 * 1024 * 1024),
         name="load_integrals",
-    )(three_index, received[0])
+    )(three_index, received[1])
     received += [flip(after(sends[steps[-1]], integrals), steps[-1]), sends[0]]
     steps = (*steps, 0)
     own = call(
@@ -332,7 +332,6 @@
         scratch=[pltpu.VMEM((blocks, half, pairs), bf16)],
     )
     whole = flip(sends[n], n // 2)
-    far = [flip(sends[d], d) for d in range(n // 2, n)]
     near = [sends[0]] + [flip(sends[d], d) for d in range(1, n // 2)]
     passed = call(
         functools.partial(pass_on_kernel, n, cap),
@@ -343,11 +342,14 @@
         [in_vmem] * (n // 2),
     )
     passed = [passed[0]] + [flip(passed[d], d) for d in range(1, n // 2)]
+    far = [flip(sends[n // 2], n // 2)]
+    for i in range(1, n // 2):
+        far.append(flip(after(sends[n // 2 + i], near[1] if i == 1 else passed[i - 1]), n // 2 + i))
     return call(
         functools.partial(gather_coulomb_kernel, n, blocks, shell, cap),
         "gather_coulomb",
         in_table,
-        [*near, *far, *passed],
+        [*near, *passed, *far],
         [jax.ShapeDtypeStruct((blocks, pairs, half), bf16)] * 2,
         [anywhere] * 2,
         scratch=[

time: 187 us -> 176 us (0.941)
  the two profiles are of different devices: /device:TPU:0 before, /device:TPU:23 now
where the time goes in v10:
time: 176 us; the launch traced here: 175 us
  waiting for transfers between devices  105 us (60%)
  starting transfers between devices  41.4 us (24%)
  Pallas kernels  18 us (10%)
  local copies, waits for them, and re-layouts  6.82 us (4%)
  other arithmetic  3.47 us (2%)
    ppermute x30, waiting for transfers between devices, flip(): return lax.ppermute(x, 'pair', [(s, s ^ bit) for s in range(n)])  103 us
    ppermute x30, starting transfers between devices, flip(): return lax.ppermute(x, 'pair', [(s, s ^ bit) for s in range(n)])  35.6 us
    pallas_call x7, Pallas kernels, call(): pl.pallas_call(kernel, out_shape=out_shape, grid_spec=pltpu.PrefetchScala...  16.1 us
    unnamed x10, local copies, waits for them, and re-layouts  6.69 us
    ppermute x2, starting transfers between devices, swap(): return lax.ppermute(x, 'aux', [(s, (s + 1) % cores) for s in range(cores)])  5.78 us
  transfers between devices with their start and end apart: 32, of which 24 were waited for; matrix products, arithmetic and copies ran while one was open for 1% of the time, Pallas kernels for 2%

profile of v10, /device:TPU:23, one launch (start us, length us, event | category | flops | bytes accessed | tf_op | source)
XLA Modules:
  0.0 175.5 jit_solution(4083266639009790647)
XLA Ops:
  11.1 5.2 %copy-done = bf16[14,256,2048]{2,1,0:T(8,128)(2,1)S(1)} copy-done((bf16[14,256,2048]{2,1,0:T(8,128)(2,1)S(1)}, bf16[14,256,2048]{2,1,0:T(8,128)(2,1)}, u32[]{:S(2)}) %copy-start) | copy-done | bytes 14680088
  19.3 4.2 %collective-permute-done.4.rest_4_ = bf16[3,128,256]{2,1,0:T(8,128)(2,1)S(1)} collective-permute-done((bf16[3,128,256]{2,1,0:T(8,128)(2,1)S(1)}, bf16[3,128,256]{2,1,0:T(8,128)(2,1)S(1)}, u32[]{:S(2)}, u32[]{:S(2)}) %collective-permute-start.4) | collective-permute-done | bytes 196640 | tf_op jit(solution)/shard_map/ppermute | solution.py:205
  23.5 15.6 %collective-permute-done.5.rest_5_ = bf16[3,128,256]{2,1,0:T(8,128)(2,1)S(1)} collective-permute-done((bf16[3,128,256]{2,1,0:T(8,128)(2,1)S(1)}, bf16[3,128,256]{2,1,0:T(8,128)(2,1)S(1)}, u32[]{:S(2)}, u32[]{:S(2)}) %collective-permute-start.5) | collective-permute-done | bytes 196640 | tf_op jit(solution)/shard_map/ppermute | solution.py:205
  39.1 4.2 %collective-permute-done.6.rest_6_ = bf16[3,128,256]{2,1,0:T(8,128)(2,1)S(1)} collective-permute-done((bf16[3,128,256]{2,1,0:T(8,128)(2,1)S(1)}, bf16[3,128,256]{2,1,0:T(8,128)(2,1)S(1)}, u32[]{:S(2)}, u32[]{:S(2)}) %collective-permute-start.6) | collective-permute-done | bytes 196640 | tf_op jit(solution)/shard_map/ppermute | solution.py:205
  44.0 2.5 %collective-permute-start.7 = (bf16[14,128,256]{2,1,0:T(8,128)(2,1)S(1)}, bf16[14,128,256]{2,1,0:T(8,128)(2,1)S(1)}, u32[]{:S(2)}, u32[]{:S(2)}) collective-permute-start(bf16[14,128,256]{2,1,0:T(8,128)(2,1)S(1)} %gather_density.1.density), channel_id=1, source_target_pairs={{0,1},{1,0},{2,3},{3,2},{4,5},{5,4},{6,7},{7,6},{8,9},{9,8},{10,11... | collective-permute-start | bytes 2752520 | tf_op jit(solution)/shard_map/ppermute | solution.py:208
  46.6 2.8 %fit.2 = (f32[4,128,256]{2,1,0:T(8,128)S(1)}, bf16[4,128,256]{2,1,0:T(8,128)(2,1)S(1)}) custom-call(s32[8]{0:T(128)S(1)} %iota_xor_fusion.table, bf16[14,1,256]{2,1,0:T(2,128)(2,1)S(1)} %copy.11.factor, bf16[14,128,256]{2,1,0:T(8,128)(2,1)S(1)} %gather_density.1.density, bf16[14,256,2048]{2,1,0:T(8,128)(2,1)S(1)} %load_integrals.1.integrals), custom_call_target="tpu_custom_call" | custom-call | tf_op jit(solution)/shard_map/fit/pallas_call | solution.py:190
  49.4 2.8 %fit.3 = (f32[4,128,256]{2,1,0:T(8,128)S(1)}, bf16[4,128,256]{2,1,0:T(8,128)(2,1)S(1)}) custom-call(s32[8]{0:T(128)S(1)} %iota_xor_fusion.table, bf16[14,1,256]{2,1,0:T(2,128)(2,1)S(1)} %copy.11.factor, bf16[14,128,256]{2,1,0:T(8,128)(2,1)S(1)} %collective-permute-done.7.density, bf16[14,256,2048]{2,1,0:T(8,128)(2,1)S(1)} %load_integrals.1.integrals, ...), custom_call_target="tpu_custom_call" | custom-call | tf_op jit(solution)/shard_map/fit/pallas_call | solution.py:190
  53.5 6.6 %collective-permute-done.8 = bf16[4,128,256]{2,1,0:T(8,128)(2,1)S(1)} collective-permute-done((bf16[4,128,256]{2,1,0:T(8,128)(2,1)S(1)}, bf16[4,128,256]{2,1,0:T(8,128)(2,1)S(1)}, u32[]{:S(2)}, u32[]{:S(2)}) %collective-permute-start.8) | collective-permute-done | bytes 262176 | tf_op jit(solution)/shard_map/ppermute | solution.py:205
  71.2 3.3 %collective-permute-start.14 = (bf16[1,128,256]{2,1,0:T(8,128)(2,1)S(1)}, bf16[1,128,256]{2,1,0:T(8,128)(2,1)S(1)}, u32[]{:S(2)}, u32[]{:S(2)}) collective-permute-start(bf16[1,128,256]{2,1,0:T(8,128)(2,1)S(1)} %add_convert_fusion.1), channel_id=1, source_target_pairs={{0,8},{2,10},{4,12},{6,14},{8,0},{10,2},{12,4},{14,6},{1,9},{3,11}... | collective-permute-start | bytes 196616 | tf_op jit(solution)/shard_map/ppermute | solution.py:205
  76.5 2.7 %collective-permute-done.15 = bf16[1,128,256]{2,1,0:T(8,128)(2,1)S(1)} collective-permute-done((bf16[1,128,256]{2,1,0:T(8,128)(2,1)S(1)}, bf16[1,128,256]{2,1,0:T(8,128)(2,1)S(1)}, u32[]{:S(2)}, u32[]{:S(2)}) %collective-permute-start.15) | collective-permute-done | bytes 65568 | tf_op jit(solution)/shard_map/ppermute | solution.py:205
  79.7 3.1 %collective-permute-start.17 = (bf16[2,128,256]{2,1,0:T(8,128)(2,1)S(1)}, bf16[2,128,256]{2,1,0:T(8,128)(2,1)S(1)}, u32[]{:S(2)}, u32[]{:S(2)}) collective-permute-start(bf16[2,128,256]{2,1,0:T(8,128)(2,1)S(1)} %pad_maximum_fusion.3), channel_id=1, source_target_pairs={{0,4},{2,6},{4,0},{6,2},{8,12},{10,14},{12,8},{14,10},{1,5},{3,7},... | collective-permute-start | bytes 393224 | tf_op jit(solution)/shard_map/ppermute | solution.py:205
  83.1 2.4 %collective-permute-done.17 = bf16[2,128,256]{2,1,0:T(8,128)(2,1)S(1)} collective-permute-done((bf16[2,128,256]{2,1,0:T(8,128)(2,1)S(1)}, bf16[2,128,256]{2,1,0:T(8,128)(2,1)S(1)}, u32[]{:S(2)}, u32[]{:S(2)}) %collective-permute-start.17) | collective-permute-done | bytes 131104 | tf_op jit(solution)/shard_map/ppermute | solution.py:205
  88.3 3.0 %collective-permute-done.18.far = bf16[4,128,256]{2,1,0:T(8,128)(2,1)S(1)} collective-permute-done((bf16[4,128,256]{2,1,0:T(8,128)(2,1)S(1)}, bf16[4,128,256]{2,1,0:T(8,128)(2,1)S(1)}, u32[]{:S(2)}, u32[]{:S(2)}) %collective-permute-start.18) | collective-permute-done | bytes 262176 | tf_op jit(solution)/shard_map/ppermute | solution.py:205
  92.3 5.0 %apply.1 = (f32[14,128,256]{2,1,0:T(8,128)S(1)}, bf16[14,128,256]{2,1,0:T(8,128)(2,1)S(1)}) custom-call(s32[8]{0:T(128)S(1)} %iota_xor_fusion.table, bf16[14,256,2048]{2,1,0:T(8,128)(2,1)S(1)} %load_integrals.1.integrals, bf16[4,128,256]{2,1,0:T(8,128)(2,1)S(1)} %pad_maximum_fusion.1.near, bf16[4,128,256]{2,1,0:T(8,128)(2,1)S(1)} %collective-permute-done.18.far, ...), custom_call_target="tpu_custom_call" | custom-call | tf_op jit(solution)/shard_map/apply/pallas_call | solution.py:190
  97.3 3.3 %collective-permute-start.20 = (bf16[14,128,256]{2,1,0:T(8,128)(2,1)S(1)}, bf16[14,128,256]{2,1,0:T(8,128)(2,1)S(1)}, u32[]{:S(2)}, u32[]{:S(2)}) collective-permute-start(bf16[14,128,256]{2,1,0:T(8,128)(2,1)S(1)} %get-tuple-element.85), channel_id=1, source_target_pairs={{0,1},{1,0},{2,3},{3,2},{4,5},{5,4},{6,7},{7,6},{8,9},{9,8},{10,11... | collective-permute-start | bytes 2752520 | tf_op jit(solution)/shard_map/ppermute | solution.py:208
  103.8 2.5 %collective-permute-start.24 = (bf16[14,128,128]{2,1,0:T(8,128)(2,1)S(1)}, bf16[14,128,128]{2,1,0:T(8,128)(2,1)S(1)}, u32[]{:S(2)}, u32[]{:S(2)}) collective-permute-start(bf16[14,128,128]{2,1,0:T(8,128)(2,1)S(1)} %get-tuple-element.90), channel_id=1, source_target_pairs={{0,8},{2,10},{4,12},{6,14},{8,0},{10,2},{12,4},{14,6},{1,9},{3,11}... | collective-permute-start | bytes 1376264 | tf_op jit(solution)/shard_map/ppermute | solution.py:205
  109.8 20.4 %collective-permute-done.24.whole = bf16[14,128,128]{2,1,0:T(8,128)(2,1)S(1)} collective-permute-done((bf16[14,128,128]{2,1,0:T(8,128)(2,1)S(1)}, bf16[14,128,128]{2,1,0:T(8,128)(2,1)S(1)}, u32[]{:S(2)}, u32[]{:S(2)}) %collective-permute-start.24) | collective-permute-done | bytes 458784 | tf_op jit(solution)/shard_map/ppermute | solution.py:205
  130.8 2.6 %collective-permute-start.26 = (bf16[6,128,128]{2,1,0:T(8,128)(2,1)S(1)}, bf16[6,128,128]{2,1,0:T(8,128)(2,1)S(1)}, u32[]{:S(2)}, u32[]{:S(2)}) collective-permute-start(bf16[6,128,128]{2,1,0:T(8,128)(2,1)S(1)} %get-tuple-element.93), channel_id=1, source_target_pairs={{0,4},{2,6},{4,0},{6,2},{8,12},{10,14},{12,8},{14,10},{1,5},{3,7},... | collective-permute-start | bytes 589832 | tf_op jit(solution)/shard_map/ppermute | solution.py:205
  133.4 9.2 %collective-permute-done.25.rest_5_ = bf16[6,128,128]{2,1,0:T(8,128)(2,1)S(1)} collective-permute-done((bf16[6,128,128]{2,1,0:T(8,128)(2,1)S(1)}, bf16[6,128,128]{2,1,0:T(8,128)(2,1)S(1)}, u32[]{:S(2)}, u32[]{:S(2)}) %collective-permute-start.25) | collective-permute-done | bytes 196640 | tf_op jit(solution)/shard_map/ppermute | solution.py:205
  147.9 2.9 %collective-permute-done.29.rest_9_ = bf16[6,128,128]{2,1,0:T(8,128)(2,1)S(1)} collective-permute-done((bf16[6,128,128]{2,1,0:T(8,128)(2,1)S(1)}, bf16[6,128,128]{2,1,0:T(8,128)(2,1)S(1)}, u32[]{:S(2)}, u32[]{:S(2)}) %collective-permute-start.29) | collective-permute-done | bytes 196640 | tf_op jit(solution)/shard_map/ppermute | solution.py:205
  150.8 3.9 %collective-permute-done.27.rest_7_ = bf16[6,128,128]{2,1,0:T(8,128)(2,1)S(1)} collective-permute-done((bf16[6,128,128]{2,1,0:T(8,128)(2,1)S(1)}, bf16[6,128,128]{2,1,0:T(8,128)(2,1)S(1)}, u32[]{:S(2)}, u32[]{:S(2)}) %collective-permute-start.27) | collective-permute-done | bytes 196640 | tf_op jit(solution)/shard_map/ppermute | solution.py:205
  154.7 10.0 %collective-permute-done.30.rest_10_ = bf16[6,128,128]{2,1,0:T(8,128)(2,1)S(1)} collective-permute-done((bf16[6,128,128]{2,1,0:T(8,128)(2,1)S(1)}, bf16[6,128,128]{2,1,0:T(8,128)(2,1)S(1)}, u32[]{:S(2)}, u32[]{:S(2)}) %collective-permute-start.30) | collective-permute-done | bytes 196640 | tf_op jit(solution)/shard_map/ppermute | solution.py:205
  164.7 7.7 %collective-permute-done.31.rest_11_ = bf16[6,128,128]{2,1,0:T(8,128)(2,1)S(1)} collective-permute-done((bf16[6,128,128]{2,1,0:T(8,128)(2,1)S(1)}, bf16[6,128,128]{2,1,0:T(8,128)(2,1)S(1)}, u32[]{:S(2)}, u32[]{:S(2)}) %collective-permute-start.31) | collective-permute-done | bytes 196640 | tf_op jit(solution)/shard_map/ppermute | solution.py:205
  172.4 3.1 %gather_coulomb.1 = (bf16[14,256,128]{2,1,0:T(8,128)(2,1)}, bf16[14,256,128]{2,1,0:T(8,128)(2,1)}) custom-call(s32[48]{0:T(128)S(1)} %pad_add_fusion.1.table, bf16[6,128,256]{2,1,0:T(8,128)(2,1)S(1)} %get-tuple-element.86.rest_0_, bf16[6,128,256]{2,1,0:T(8,128)(2,1)S(1)} %collective-permute-done.21.rest_1_, ...), custom_call_target="tpu_custom_call" | custom-call | tf_op jit(solution)/shard_map/gather_coulomb/pallas_call | solution.py:190
  (104 shorter events, 45.6 us)
Async XLA Ops:
  5.1 5.8 %collective-permute-start.1 = (bf16[3,128,256]{2,1,0:T(8,128)(2,1)S(1)}, bf16[3,128,256]{2,1,0:T(8,128)(2,1)S(1)}, u32[]{:S(2)}, u32[]{:S(2)}) collective-permute-start(bf16[3,128,256]{2,1,0:T(8,128)(2,1)S(1)} %get-tuple-element.53), channel_id=1, source_target_pairs={{0,4},{2,6},{4,0},{6,2},{8,12},{10,14},{12,8},{14,10},{1,5},{3,7},... | collective-permute-start | bytes 589832 | tf_op jit(solution)/shard_map/ppermute | solution.py:205
  6.4 10.8 %collective-permute-start = (bf16[3,128,256]{2,1,0:T(8,128)(2,1)S(1)}, bf16[3,128,256]{2,1,0:T(8,128)(2,1)S(1)}, u32[]{:S(2)}, u32[]{:S(2)}) collective-permute-start(bf16[3,128,256]{2,1,0:T(8,128)(2,1)S(1)} %get-tuple-element.52), channel_id=1, source_target_pairs={{0,2},{2,0},{4,6},{6,4},{8,10},{10,8},{12,14},{14,12},{1,3},{3,1},... | collective-permute-start | bytes 589832 | tf_op jit(solution)/shard_map/ppermute | solution.py:205
  6.7 12.3 %collective-permute-start.2 = (bf16[3,128,256]{2,1,0:T(8,128)(2,1)S(1)}, bf16[3,128,256]{2,1,0:T(8,128)(2,1)S(1)}, u32[]{:S(2)}, u32[]{:S(2)}) collective-permute-start(bf16[3,128,256]{2,1,0:T(8,128)(2,1)S(1)} %get-tuple-element.54), channel_id=1, source_target_pairs={{0,6},{2,4},{4,2},{6,0},{8,14},{10,12},{12,10},{14,8},{1,7},{3,5},... | collective-permute-start | bytes 589832 | tf_op jit(solution)/shard_map/ppermute | solution.py:205
  7.8 11.5 %collective-permute-start.3 = (bf16[3,128,256]{2,1,0:T(8,128)(2,1)S(1)}, bf16[3,128,256]{2,1,0:T(8,128)(2,1)S(1)}, u32[]{:S(2)}, u32[]{:S(2)}) collective-permute-start(bf16[3,128,256]{2,1,0:T(8,128)(2,1)S(1)} %get-tuple-element.55), channel_id=1, source_target_pairs={{0,8},{2,10},{4,12},{6,14},{8,0},{10,2},{12,4},{14,6},{1,9},{3,11}... | collective-permute-start | bytes 589832 | tf_op jit(solution)/shard_map/ppermute | solution.py:205
  7.9 15.6 %collective-permute-start.4 = (bf16[3,128,256]{2,1,0:T(8,128)(2,1)S(1)}, bf16[3,128,256]{2,1,0:T(8,128)(2,1)S(1)}, u32[]{:S(2)}, u32[]{:S(2)}) collective-permute-start(bf16[3,128,256]{2,1,0:T(8,128)(2,1)S(1)} %get-tuple-element.56), channel_id=1, source_target_pairs={{0,10},{2,8},{4,14},{6,12},{8,2},{10,0},{12,6},{14,4},{1,11},{3,9}... | collective-permute-start | bytes 589832 | tf_op jit(solution)/shard_map/ppermute | solution.py:205
  10.9 28.1 %collective-permute-start.5 = (bf16[3,128,256]{2,1,0:T(8,128)(2,1)S(1)}, bf16[3,128,256]{2,1,0:T(8,128)(2,1)S(1)}, u32[]{:S(2)}, u32[]{:S(2)}) collective-permute-start(bf16[3,128,256]{2,1,0:T(8,128)(2,1)S(1)} %get-tuple-element.57), channel_id=1, source_target_pairs={{0,12},{2,14},{4,8},{6,10},{8,4},{10,6},{12,0},{14,2},{1,13},{3,15... | collective-permute-start | bytes 589832 | tf_op jit(solution)/shard_map/ppermute | solution.py:205
  17.3 25.9 %collective-permute-start.6 = (bf16[3,128,256]{2,1,0:T(8,128)(2,1)S(1)}, bf16[3,128,256]{2,1,0:T(8,128)(2,1)S(1)}, u32[]{:S(2)}, u32[]{:S(2)}) collective-permute-start(bf16[3,128,256]{2,1,0:T(8,128)(2,1)S(1)} %get-tuple-element.59), channel_id=1, source_target_pairs={{0,14},{2,12},{4,10},{6,8},{8,6},{10,4},{12,2},{14,0},{1,15},{3,13... | collective-permute-start | bytes 589832 | tf_op jit(solution)/shard_map/ppermute | solution.py:205
  52.1 8.0 %collective-permute-start.8 = (bf16[4,128,256]{2,1,0:T(8,128)(2,1)S(1)}, bf16[4,128,256]{2,1,0:T(8,128)(2,1)S(1)}, u32[]{:S(2)}, u32[]{:S(2)}) collective-permute-start(bf16[4,128,256]{2,1,0:T(8,128)(2,1)S(1)} %get-tuple-element.67), channel_id=1, source_target_pairs={{0,4},{2,6},{4,0},{6,2},{8,12},{10,14},{12,8},{14,10},{1,5},{3,7},... | collective-permute-start | bytes 786440 | tf_op jit(solution)/shard_map/ppermute | solution.py:205
  52.2 8.0 %collective-permute-start.9 = (bf16[4,128,256]{2,1,0:T(8,128)(2,1)S(1)}, bf16[4,128,256]{2,1,0:T(8,128)(2,1)S(1)}, u32[]{:S(2)}, u32[]{:S(2)}) collective-permute-start(bf16[4,128,256]{2,1,0:T(8,128)(2,1)S(1)} %get-tuple-element.69), channel_id=1, source_target_pairs={{0,2},{2,0},{4,6},{6,4},{8,10},{10,8},{12,14},{14,12},{1,3},{3,1},... | collective-permute-start | bytes 786440 | tf_op jit(solution)/shard_map/ppermute | solution.py:205
  79.7 5.7 %collective-permute-start.17 = (bf16[2,128,256]{2,1,0:T(8,128)(2,1)S(1)}, bf16[2,128,256]{2,1,0:T(8,128)(2,1)S(1)}, u32[]{:S(2)}, u32[]{:S(2)}) collective-permute-start(bf16[2,128,256]{2,1,0:T(8,128)(2,1)S(1)} %pad_maximum_fusion.3), channel_id=1, source_target_pairs={{0,4},{2,6},{4,0},{6,2},{8,12},{10,14},{12,8},{14,10},{1,5},{3,7},... | collective-permute-start | bytes 393224 | tf_op jit(solution)/shard_map/ppermute | solution.py:205
  85.5 5.7 %collective-permute-start.18 = (bf16[4,128,256]{2,1,0:T(8,128)(2,1)S(1)}, bf16[4,128,256]{2,1,0:T(8,128)(2,1)S(1)}, u32[]{:S(2)}, u32[]{:S(2)}) collective-permute-start(bf16[4,128,256]{2,1,0:T(8,128)(2,1)S(1)} %pad_maximum_fusion.1.near), channel_id=1, source_target_pairs={{0,2},{2,0},{4,6},{6,4},{8,10},{10,8},{12,14},{14,12},{1,3},{3,1},... | collective-permute-start | bytes 786440 | tf_op jit(solution)/shard_map/ppermute | solution.py:205
  86.5 5.8 %collective-permute-start.19 = (bf16[4,128,256]{2,1,0:T(8,128)(2,1)S(1)}, bf16[4,128,256]{2,1,0:T(8,128)(2,1)S(1)}, u32[]{:S(2)}, u32[]{:S(2)}) collective-permute-start(bf16[4,128,256]{2,1,0:T(8,128)(2,1)S(1)} %pad_maximum_fusion.near_other), channel_id=1, source_target_pairs={{0,4},{2,6},{4,0},{6,2},{8,12},{10,14},{12,8},{14,10},{1,5},{3,7},... | collective-permute-start | bytes 786440 | tf_op jit(solution)/shard_map/ppermute | solution.py:205
  97.3 5.4 %collective-permute-start.20 = (bf16[14,128,256]{2,1,0:T(8,128)(2,1)S(1)}, bf16[14,128,256]{2,1,0:T(8,128)(2,1)S(1)}, u32[]{:S(2)}, u32[]{:S(2)}) collective-permute-start(bf16[14,128,256]{2,1,0:T(8,128)(2,1)S(1)} %get-tuple-element.85), channel_id=1, source_target_pairs={{0,1},{1,0},{2,3},{3,2},{4,5},{5,4},{6,7},{7,6},{8,9},{9,8},{10,11... | collective-permute-start | bytes 2752520 | tf_op jit(solution)/shard_map/ppermute | solution.py:208
  103.8 26.3 %collective-permute-start.24 = (bf16[14,128,128]{2,1,0:T(8,128)(2,1)S(1)}, bf16[14,128,128]{2,1,0:T(8,128)(2,1)S(1)}, u32[]{:S(2)}, u32[]{:S(2)}) collective-permute-start(bf16[14,128,128]{2,1,0:T(8,128)(2,1)S(1)} %get-tuple-element.90), channel_id=1, source_target_pairs={{0,8},{2,10},{4,12},{6,14},{8,0},{10,2},{12,4},{14,6},{1,9},{3,11}... | collective-permute-start | bytes 1376264 | tf_op jit(solution)/shard_map/ppermute | solution.py:205
  106.4 24.5 %collective-permute-start.21 = (bf16[6,128,256]{2,1,0:T(8,128)(2,1)S(1)}, bf16[6,128,256]{2,1,0:T(8,128)(2,1)S(1)}, u32[]{:S(2)}, u32[]{:S(2)}) collective-permute-start(bf16[6,128,256]{2,1,0:T(8,128)(2,1)S(1)} %get-tuple-element.87), channel_id=1, source_target_pairs={{0,2},{2,0},{4,6},{6,4},{8,10},{10,8},{12,14},{14,12},{1,3},{3,1},... | collective-permute-start | bytes 1179656 | tf_op jit(solution)/shard_map/ppermute | solution.py:205
  106.5 39.7 %collective-permute-start.22 = (bf16[6,128,256]{2,1,0:T(8,128)(2,1)S(1)}, bf16[6,128,256]{2,1,0:T(8,128)(2,1)S(1)}, u32[]{:S(2)}, u32[]{:S(2)}) collective-permute-start(bf16[6,128,256]{2,1,0:T(8,128)(2,1)S(1)} %get-tuple-element.88), channel_id=1, source_target_pairs={{0,4},{2,6},{4,0},{6,2},{8,12},{10,14},{12,8},{14,10},{1,5},{3,7},... | collective-permute-start | bytes 1179656 | tf_op jit(solution)/shard_map/ppermute | solution.py:205
  107.3 37.6 %collective-permute-start.28 = (bf16[6,128,128]{2,1,0:T(8,128)(2,1)S(1)}, bf16[6,128,128]{2,1,0:T(8,128)(2,1)S(1)}, u32[]{:S(2)}, u32[]{:S(2)}) collective-permute-start(bf16[6,128,128]{2,1,0:T(8,128)(2,1)S(1)} %get-tuple-element.95), channel_id=1, source_target_pairs={{0,8},{2,10},{4,12},{6,14},{8,0},{10,2},{12,4},{14,6},{1,9},{3,11}... | collective-permute-start | bytes 589832 | tf_op jit(solution)/shard_map/ppermute | solution.py:205
  108.9 39.0 %collective-permute-start.23 = (bf16[6,128,256]{2,1,0:T(8,128)(2,1)S(1)}, bf16[6,128,256]{2,1,0:T(8,128)(2,1)S(1)}, u32[]{:S(2)}, u32[]{:S(2)}) collective-permute-start(bf16[6,128,256]{2,1,0:T(8,128)(2,1)S(1)} %get-tuple-element.89), channel_id=1, source_target_pairs={{0,6},{2,4},{4,2},{6,0},{8,14},{10,12},{12,10},{14,8},{1,7},{3,5},... | collective-permute-start | bytes 1179656 | tf_op jit(solution)/shard_map/ppermute | solution.py:205
  130.7 11.9 %collective-permute-start.25 = (bf16[6,128,128]{2,1,0:T(8,128)(2,1)S(1)}, bf16[6,128,128]{2,1,0:T(8,128)(2,1)S(1)}, u32[]{:S(2)}, u32[]{:S(2)}) collective-permute-start(bf16[6,128,128]{2,1,0:T(8,128)(2,1)S(1)} %get-tuple-element.92), channel_id=1, source_target_pairs={{0,2},{2,0},{4,6},{6,4},{8,10},{10,8},{12,14},{14,12},{1,3},{3,1},... | collective-permute-start | bytes 589832 | tf_op jit(solution)/shard_map/ppermute | solution.py:205
  130.8 12.1 %collective-permute-start.26 = (bf16[6,128,128]{2,1,0:T(8,128)(2,1)S(1)}, bf16[6,128,128]{2,1,0:T(8,128)(2,1)S(1)}, u32[]{:S(2)}, u32[]{:S(2)}) collective-permute-start(bf16[6,128,128]{2,1,0:T(8,128)(2,1)S(1)} %get-tuple-element.93), channel_id=1, source_target_pairs={{0,4},{2,6},{4,0},{6,2},{8,12},{10,14},{12,8},{14,10},{1,5},{3,7},... | collective-permute-start | bytes 589832 | tf_op jit(solution)/shard_map/ppermute | solution.py:205
  142.7 8.1 %collective-permute-start.29 = (bf16[6,128,128]{2,1,0:T(8,128)(2,1)S(1)}, bf16[6,128,128]{2,1,0:T(8,128)(2,1)S(1)}, u32[]{:S(2)}, u32[]{:S(2)}) collective-permute-start(bf16[6,128,128]{2,1,0:T(8,128)(2,1)S(1)} %get-tuple-element.97), channel_id=1, source_target_pairs={{0,10},{2,8},{4,14},{6,12},{8,2},{10,0},{12,6},{14,4},{1,11},{3,9}... | collective-permute-start | bytes 589832 | tf_op jit(solution)/shard_map/ppermute | solution.py:205
  142.9 11.8 %collective-permute-start.27 = (bf16[6,128,128]{2,1,0:T(8,128)(2,1)S(1)}, bf16[6,128,128]{2,1,0:T(8,128)(2,1)S(1)}, u32[]{:S(2)}, u32[]{:S(2)}) collective-permute-start(bf16[6,128,128]{2,1,0:T(8,128)(2,1)S(1)} %get-tuple-element.94), channel_id=1, source_target_pairs={{0,6},{2,4},{4,2},{6,0},{8,14},{10,12},{12,10},{14,8},{1,7},{3,5},... | collective-permute-start | bytes 589832 | tf_op jit(solution)/shard_map/ppermute | solution.py:205
  144.9 19.8 %collective-permute-start.30 = (bf16[6,128,128]{2,1,0:T(8,128)(2,1)S(1)}, bf16[6,128,128]{2,1,0:T(8,128)(2,1)S(1)}, u32[]{:S(2)}, u32[]{:S(2)}) collective-permute-start(bf16[6,128,128]{2,1,0:T(8,128)(2,1)S(1)} %get-tuple-element.99), channel_id=1, source_target_pairs={{0,12},{2,14},{4,8},{6,10},{8,4},{10,6},{12,0},{14,2},{1,13},{3,15... | collective-permute-start | bytes 589832 | tf_op jit(solution)/shard_map/ppermute | solution.py:205
  146.2 26.2 %collective-permute-start.31 = (bf16[6,128,128]{2,1,0:T(8,128)(2,1)S(1)}, bf16[6,128,128]{2,1,0:T(8,128)(2,1)S(1)}, u32[]{:S(2)}, u32[]{:S(2)}) collective-permute-start(bf16[6,128,128]{2,1,0:T(8,128)(2,1)S(1)} %get-tuple-element.101), channel_id=1, source_target_pairs={{0,14},{2,12},{4,10},{6,8},{8,6},{10,4},{12,2},{14,0},{1,15},{3,13... | collective-permute-start | bytes 589832 | tf_op jit(solution)/shard_map/ppermute | solution.py:205
  (13 other events, 152.6 us)

commit v11 on v10

--- a/solution.py
+++ b/solution.py
@@ -119,7 +119,8 @@
                     far[step - devices // 2][group * cap + rank] = ready[b, :, pl.ds(part, part)]
 
 
-def pass_on_kernel(devices, cap, table, whole, *outs):
+def pass_on_kernel(devices, cap, table, whole, *rest):
+    outs = rest[-(devices // 2) :]
     for group in range(2):
         for step in range(devices // 2):
             for rank in range(cap):
@@ -234,8 +235,13 @@
         compiler_params=pltpu.CompilerParams(vmem_limit_bytes=VMEM_BYTES),
         name="scatter_density",
     )(send_table, density)
-    steps = range(1, n)
-    received = [flip(sends[d], d) for d in steps[:-1]]
+    steps = [n // 2, n // 2 + 1, *range(1, n // 2), *range(n // 2 + 2, n)]
+    received = []
+    for i, d in enumerate(steps[:-1]):
+        send = sends[d]
+        if d > n // 2 + 1:
+            send = after(send, received[i - n // 2 + 1])
+        received.append(flip(send, d))
     integrals = pl.pallas_call(
         load_kernel,
         out_shape=pltpu.VMEM((blocks, pairs, aux_dev), bf16),
@@ -244,8 +250,8 @@
         scratch_shapes=[pltpu.SemaphoreType.DMA],
         compiler_params=pltpu.CompilerParams(vmem_limit_bytes=2 * 1024 * 1024),
         name="load_integrals",
-    )(three_index, received[1])
-    received += [flip(after(sends[steps[-1]], integrals), steps[-1]), sends[0]]
+    )(three_index, received[2])
+    received += [flip(after(sends[steps[-1]], received[3], integrals), steps[-1]), sends[0]]
     steps = (*steps, 0)
     own = call(
         functools.partial(gather_density_kernel, steps, cap),
@@ -331,8 +337,14 @@
         [in_vmem] * (n + 1),
         scratch=[pltpu.VMEM((blocks, half, pairs), bf16)],
     )
+    def direct(i, ready):
+        return flip(after(sends[n // 2 + i], ready), n // 2 + i)
+
     whole = flip(sends[n], n // 2)
     near = [sends[0]] + [flip(sends[d], d) for d in range(1, n // 2)]
+    far = [direct(0, sends[0])]
+    for i in range(1, 3):
+        far.append(direct(i, far[i - 1]))
     passed = call(
         functools.partial(pass_on_kernel, n, cap),
         "pass_on",
@@ -340,11 +352,11 @@
         [whole],
         [jax.ShapeDtypeStruct((2 * cap, half, part), bf16)] * (n // 2),
         [in_vmem] * (n // 2),
+        far[1:2],
     )
     passed = [passed[0]] + [flip(passed[d], d) for d in range(1, n // 2)]
-    far = [flip(sends[n // 2], n // 2)]
-    for i in range(1, n // 2):
-        far.append(flip(after(sends[n // 2 + i], near[1] if i == 1 else passed[i - 1]), n // 2 + i))
+    for i in range(3, n // 2):
+        far.append(direct(i, passed[i - 2]))
     return call(
         functools.partial(gather_coulomb_kernel, n, blocks, shell, cap),
         "gather_coulomb",

time: 176 us -> 181 us (1.028)
  the two profiles are of different devices: /device:TPU:23 before, /device:TPU:0 now
where the time goes in v11:
time: 181 us; the launch traced here: 180 us
  waiting for transfers between devices  98 us (54%)
  starting transfers between devices  53.1 us (29%)
  Pallas kernels  17.9 us (10%)
  local copies, waits for them, and re-layouts  6.81 us (4%)
  other arithmetic  3.47 us (2%)
    ppermute x30, waiting for transfers between devices, flip(): return lax.ppermute(x, 'pair', [(s, s ^ bit) for s in range(n)])  96 us
    ppermute x30, starting transfers between devices, flip(): return lax.ppermute(x, 'pair', [(s, s ^ bit) for s in range(n)])  53 us
    pallas_call x7, Pallas kernels, call(): pl.pallas_call(kernel, out_shape=out_shape, grid_spec=pltpu.PrefetchScala...  16 us
    unnamed x10, local copies, waits for them, and re-layouts  6.69 us
  transfers between devices with their start and end apart: 32, of which 21 were waited for; matrix products, arithmetic and copies ran while one was open for 1% of the time, Pallas kernels for 2%

profile of v11, /device:TPU:0, one launch (start us, length us, event | category | flops | bytes accessed | tf_op | source)
XLA Modules:
  0.0 180.3 jit_solution(5696638166832242533)
XLA Ops:
  5.1 3.0 %collective-permute-start.2 = (bf16[3,128,256]{2,1,0:T(8,128)(2,1)S(1)}, bf16[3,128,256]{2,1,0:T(8,128)(2,1)S(1)}, u32[]{:S(2)}, u32[]{:S(2)}) collective-permute-start(bf16[3,128,256]{2,1,0:T(8,128)(2,1)S(1)} %get-tuple-element.56), channel_id=1, source_target_pairs={{0,2},{2,0},{4,6},{6,4},{8,10},{10,8},{12,14},{14,12},{1,3},{3,1},... | collective-permute-start | bytes 589832 | tf_op jit(solution)/shard_map/ppermute | solution.py:206
  14.0 3.6 %collective-permute-start.5 = (bf16[3,128,256]{2,1,0:T(8,128)(2,1)S(1)}, bf16[3,128,256]{2,1,0:T(8,128)(2,1)S(1)}, u32[]{:S(2)}, u32[]{:S(2)}) collective-permute-start(bf16[3,128,256]{2,1,0:T(8,128)(2,1)S(1)} %get-tuple-element.60), channel_id=1, source_target_pairs={{0,12},{2,14},{4,8},{6,10},{8,4},{10,6},{12,0},{14,2},{1,13},{3,15... | collective-permute-start | bytes 589832 | tf_op jit(solution)/shard_map/ppermute | solution.py:206
  17.6 5.2 %copy-done = bf16[14,256,2048]{2,1,0:T(8,128)(2,1)S(1)} copy-done((bf16[14,256,2048]{2,1,0:T(8,128)(2,1)S(1)}, bf16[14,256,2048]{2,1,0:T(8,128)(2,1)}, u32[]{:S(2)}) %copy-start) | copy-done | bytes 14680088
  26.9 12.1 %collective-permute-done.1.rest_1_ = bf16[3,128,256]{2,1,0:T(8,128)(2,1)S(1)} collective-permute-done((bf16[3,128,256]{2,1,0:T(8,128)(2,1)S(1)}, bf16[3,128,256]{2,1,0:T(8,128)(2,1)S(1)}, u32[]{:S(2)}, u32[]{:S(2)}) %collective-permute-start.1) | collective-permute-done | bytes 196640 | tf_op jit(solution)/shard_map/ppermute | solution.py:206
  40.0 2.8 %fit.2 = (f32[4,128,256]{2,1,0:T(8,128)S(1)}, bf16[4,128,256]{2,1,0:T(8,128)(2,1)S(1)}) custom-call(s32[8]{0:T(128)S(1)} %iota_xor_fusion.table, bf16[14,1,256]{2,1,0:T(2,128)(2,1)S(1)} %copy.11.factor, bf16[14,128,256]{2,1,0:T(8,128)(2,1)S(1)} %gather_density.1.density, bf16[14,256,2048]{2,1,0:T(8,128)(2,1)S(1)} %load_integrals.1.integrals), custom_call_target="tpu_custom_call" | custom-call | tf_op jit(solution)/shard_map/fit/pallas_call | solution.py:191
  42.8 2.7 %fit.3 = (f32[4,128,256]{2,1,0:T(8,128)S(1)}, bf16[4,128,256]{2,1,0:T(8,128)(2,1)S(1)}) custom-call(s32[8]{0:T(128)S(1)} %iota_xor_fusion.table, bf16[14,1,256]{2,1,0:T(2,128)(2,1)S(1)} %copy.11.factor, bf16[14,128,256]{2,1,0:T(8,128)(2,1)S(1)} %collective-permute-done.7.density, bf16[14,256,2048]{2,1,0:T(8,128)(2,1)S(1)} %load_integrals.1.integrals, ...), custom_call_target="tpu_custom_call" | custom-call | tf_op jit(solution)/shard_map/fit/pallas_call | solution.py:191
  45.5 7.9 %collective-permute-start.8 = (bf16[4,128,256]{2,1,0:T(8,128)(2,1)S(1)}, bf16[4,128,256]{2,1,0:T(8,128)(2,1)S(1)}, u32[]{:S(2)}, u32[]{:S(2)}) collective-permute-start(bf16[4,128,256]{2,1,0:T(8,128)(2,1)S(1)} %get-tuple-element.70), channel_id=1, source_target_pairs={{0,4},{2,6},{4,0},{6,2},{8,12},{10,14},{12,8},{14,10},{1,5},{3,7},... | collective-permute-start | bytes 786440 | tf_op jit(solution)/shard_map/ppermute | solution.py:206
  54.9 5.4 %collective-permute-done.8 = bf16[4,128,256]{2,1,0:T(8,128)(2,1)S(1)} collective-permute-done((bf16[4,128,256]{2,1,0:T(8,128)(2,1)S(1)}, bf16[4,128,256]{2,1,0:T(8,128)(2,1)S(1)}, u32[]{:S(2)}, u32[]{:S(2)}) %collective-permute-start.8) | collective-permute-done | bytes 262176 | tf_op jit(solution)/shard_map/ppermute | solution.py:206
  64.0 3.0 %collective-permute-done.10 = bf16[2,128,256]{2,1,0:T(8,128)(2,1)S(1)} collective-permute-done((bf16[2,128,256]{2,1,0:T(8,128)(2,1)S(1)}, bf16[2,128,256]{2,1,0:T(8,128)(2,1)S(1)}, u32[]{:S(2)}, u32[]{:S(2)}) %collective-permute-start.10) | collective-permute-done | bytes 131104 | tf_op jit(solution)/shard_map/ppermute | solution.py:206
  71.6 3.0 %collective-permute-done.12 = bf16[1,128,256]{2,1,0:T(8,128)(2,1)S(1)} collective-permute-done((bf16[1,128,256]{2,1,0:T(8,128)(2,1)S(1)}, bf16[1,128,256]{2,1,0:T(8,128)(2,1)S(1)}, u32[]{:S(2)}, u32[]{:S(2)}) %collective-permute-start.12) | collective-permute-done | bytes 65568 | tf_op jit(solution)/shard_map/ppermute | solution.py:206
  78.3 3.5 %collective-permute-done.14 = bf16[1,128,256]{2,1,0:T(8,128)(2,1)S(1)} collective-permute-done((bf16[1,128,256]{2,1,0:T(8,128)(2,1)S(1)}, bf16[1,128,256]{2,1,0:T(8,128)(2,1)S(1)}, u32[]{:S(2)}, u32[]{:S(2)}) %collective-permute-start.14) | collective-permute-done | bytes 65568 | tf_op jit(solution)/shard_map/ppermute | solution.py:206
  82.7 3.0 %collective-permute-start.17 = (bf16[2,128,256]{2,1,0:T(8,128)(2,1)S(1)}, bf16[2,128,256]{2,1,0:T(8,128)(2,1)S(1)}, u32[]{:S(2)}, u32[]{:S(2)}) collective-permute-start(bf16[2,128,256]{2,1,0:T(8,128)(2,1)S(1)} %pad_maximum_fusion.3), channel_id=1, source_target_pairs={{0,4},{2,6},{4,0},{6,2},{8,12},{10,14},{12,8},{14,10},{1,5},{3,7},... | collective-permute-start | bytes 393224 | tf_op jit(solution)/shard_map/ppermute | solution.py:206
  85.7 3.0 %collective-permute-done.16 = bf16[2,128,256]{2,1,0:T(8,128)(2,1)S(1)} collective-permute-done((bf16[2,128,256]{2,1,0:T(8,128)(2,1)S(1)}, bf16[2,128,256]{2,1,0:T(8,128)(2,1)S(1)}, u32[]{:S(2)}, u32[]{:S(2)}) %collective-permute-start.16) | collective-permute-done | bytes 131104 | tf_op jit(solution)/shard_map/ppermute | solution.py:206
  93.9 2.6 %collective-permute-done.18.far = bf16[4,128,256]{2,1,0:T(8,128)(2,1)S(1)} collective-permute-done((bf16[4,128,256]{2,1,0:T(8,128)(2,1)S(1)}, bf16[4,128,256]{2,1,0:T(8,128)(2,1)S(1)}, u32[]{:S(2)}, u32[]{:S(2)}) %collective-permute-start.18) | collective-permute-done | bytes 262176 | tf_op jit(solution)/shard_map/ppermute | solution.py:206
  98.4 5.0 %apply.1 = (f32[14,128,256]{2,1,0:T(8,128)S(1)}, bf16[14,128,256]{2,1,0:T(8,128)(2,1)S(1)}) custom-call(s32[8]{0:T(128)S(1)} %iota_xor_fusion.table, bf16[14,256,2048]{2,1,0:T(8,128)(2,1)S(1)} %load_integrals.1.integrals, bf16[4,128,256]{2,1,0:T(8,128)(2,1)S(1)} %pad_maximum_fusion.1.near, bf16[4,128,256]{2,1,0:T(8,128)(2,1)S(1)} %collective-permute-done.18.far, ...), custom_call_target="tpu_custom_call" | custom-call | tf_op jit(solution)/shard_map/apply/pallas_call | solution.py:191
  112.5 26.4 %collective-permute-done.25.rest_8_ = bf16[6,128,128]{2,1,0:T(8,128)(2,1)S(1)} collective-permute-done((bf16[6,128,128]{2,1,0:T(8,128)(2,1)S(1)}, bf16[6,128,128]{2,1,0:T(8,128)(2,1)S(1)}, u32[]{:S(2)}, u32[]{:S(2)}) %collective-permute-start.25) | collective-permute-done | bytes 196640 | tf_op jit(solution)/shard_map/ppermute | solution.py:206
  139.1 3.3 %collective-permute-start.23 = (bf16[6,128,256]{2,1,0:T(8,128)(2,1)S(1)}, bf16[6,128,256]{2,1,0:T(8,128)(2,1)S(1)}, u32[]{:S(2)}, u32[]{:S(2)}) collective-permute-start(bf16[6,128,256]{2,1,0:T(8,128)(2,1)S(1)} %get-tuple-element.92), channel_id=1, source_target_pairs={{0,6},{2,4},{4,2},{6,0},{8,14},{10,12},{12,10},{14,8},{1,7},{3,5},... | collective-permute-start | bytes 1179656 | tf_op jit(solution)/shard_map/ppermute | solution.py:206
  142.4 7.8 %collective-permute-done.26.rest_0_.rest_9_ = bf16[6,128,128]{2,1,0:T(8,128)(2,1)S(1)} collective-permute-done((bf16[6,128,128]{2,1,0:T(8,128)(2,1)S(1)}, bf16[6,128,128]{2,1,0:T(8,128)(2,1)S(1)}, u32[]{:S(2)}, u32[]{:S(2)}) %collective-permute-start.26) | collective-permute-done | bytes 196640 | tf_op jit(solution)/shard_map/ppermute | solution.py:206
  153.5 6.3 %collective-permute-done.27.rest_5_ = bf16[6,128,128]{2,1,0:T(8,128)(2,1)S(1)} collective-permute-done((bf16[6,128,128]{2,1,0:T(8,128)(2,1)S(1)}, bf16[6,128,128]{2,1,0:T(8,128)(2,1)S(1)}, u32[]{:S(2)}, u32[]{:S(2)}) %collective-permute-start.27) | collective-permute-done | bytes 196640 | tf_op jit(solution)/shard_map/ppermute | solution.py:206
  161.1 3.2 %collective-permute-start.31 = (bf16[6,128,128]{2,1,0:T(8,128)(2,1)S(1)}, bf16[6,128,128]{2,1,0:T(8,128)(2,1)S(1)}, u32[]{:S(2)}, u32[]{:S(2)}) collective-permute-start(bf16[6,128,128]{2,1,0:T(8,128)(2,1)S(1)} %get-tuple-element.105), channel_id=1, source_target_pairs={{0,14},{2,12},{4,10},{6,8},{8,6},{10,4},{12,2},{14,0},{1,15},{3,13... | collective-permute-start | bytes 589832 | tf_op jit(solution)/shard_map/ppermute | solution.py:206
  164.4 3.2 %collective-permute-done.28.rest_6_ = bf16[6,128,128]{2,1,0:T(8,128)(2,1)S(1)} collective-permute-done((bf16[6,128,128]{2,1,0:T(8,128)(2,1)S(1)}, bf16[6,128,128]{2,1,0:T(8,128)(2,1)S(1)}, u32[]{:S(2)}, u32[]{:S(2)}) %collective-permute-start.28) | collective-permute-done | bytes 196640 | tf_op jit(solution)/shard_map/ppermute | solution.py:206
  167.5 4.0 %collective-permute-done.29.rest_7_ = bf16[6,128,128]{2,1,0:T(8,128)(2,1)S(1)} collective-permute-done((bf16[6,128,128]{2,1,0:T(8,128)(2,1)S(1)}, bf16[6,128,128]{2,1,0:T(8,128)(2,1)S(1)}, u32[]{:S(2)}, u32[]{:S(2)}) %collective-permute-start.29) | collective-permute-done | bytes 196640 | tf_op jit(solution)/shard_map/ppermute | solution.py:206
  171.6 5.7 %collective-permute-done.31.rest_11_ = bf16[6,128,128]{2,1,0:T(8,128)(2,1)S(1)} collective-permute-done((bf16[6,128,128]{2,1,0:T(8,128)(2,1)S(1)}, bf16[6,128,128]{2,1,0:T(8,128)(2,1)S(1)}, u32[]{:S(2)}, u32[]{:S(2)}) %collective-permute-start.31) | collective-permute-done | bytes 196640 | tf_op jit(solution)/shard_map/ppermute | solution.py:206
  177.3 3.1 %gather_coulomb.1 = (bf16[14,256,128]{2,1,0:T(8,128)(2,1)}, bf16[14,256,128]{2,1,0:T(8,128)(2,1)}) custom-call(s32[48]{0:T(128)S(1)} %pad_add_fusion.1.table, bf16[6,128,256]{2,1,0:T(8,128)(2,1)S(1)} %get-tuple-element.89.rest_0_, bf16[6,128,256]{2,1,0:T(8,128)(2,1)S(1)} %collective-permute-done.21.rest_1_, ...), custom_call_target="tpu_custom_call" | custom-call | tf_op jit(solution)/shard_map/gather_coulomb/pallas_call | solution.py:191
  (104 shorter events, 50.6 us)
Async XLA Ops:
  5.1 8.9 %collective-permute-start.2 = (bf16[3,128,256]{2,1,0:T(8,128)(2,1)S(1)}, bf16[3,128,256]{2,1,0:T(8,128)(2,1)S(1)}, u32[]{:S(2)}, u32[]{:S(2)}) collective-permute-start(bf16[3,128,256]{2,1,0:T(8,128)(2,1)S(1)} %get-tuple-element.56), channel_id=1, source_target_pairs={{0,2},{2,0},{4,6},{6,4},{8,10},{10,8},{12,14},{14,12},{1,3},{3,1},... | collective-permute-start | bytes 589832 | tf_op jit(solution)/shard_map/ppermute | solution.py:206
  8.1 15.6 %collective-permute-start.3 = (bf16[3,128,256]{2,1,0:T(8,128)(2,1)S(1)}, bf16[3,128,256]{2,1,0:T(8,128)(2,1)S(1)}, u32[]{:S(2)}, u32[]{:S(2)}) collective-permute-start(bf16[3,128,256]{2,1,0:T(8,128)(2,1)S(1)} %get-tuple-element.57), channel_id=1, source_target_pairs={{0,4},{2,6},{4,0},{6,2},{8,12},{10,14},{12,8},{14,10},{1,5},{3,7},... | collective-permute-start | bytes 589832 | tf_op jit(solution)/shard_map/ppermute | solution.py:206
  9.7 17.2 %collective-permute-start = (bf16[3,128,256]{2,1,0:T(8,128)(2,1)S(1)}, bf16[3,128,256]{2,1,0:T(8,128)(2,1)S(1)}, u32[]{:S(2)}, u32[]{:S(2)}) collective-permute-start(bf16[3,128,256]{2,1,0:T(8,128)(2,1)S(1)} %get-tuple-element.54), channel_id=1, source_target_pairs={{0,8},{2,10},{4,12},{6,14},{8,0},{10,2},{12,4},{14,6},{1,9},{3,11}... | collective-permute-start | bytes 589832 | tf_op jit(solution)/shard_map/ppermute | solution.py:206
  12.3 26.7 %collective-permute-start.1 = (bf16[3,128,256]{2,1,0:T(8,128)(2,1)S(1)}, bf16[3,128,256]{2,1,0:T(8,128)(2,1)S(1)}, u32[]{:S(2)}, u32[]{:S(2)}) collective-permute-start(bf16[3,128,256]{2,1,0:T(8,128)(2,1)S(1)} %get-tuple-element.55), channel_id=1, source_target_pairs={{0,10},{2,8},{4,14},{6,12},{8,2},{10,0},{12,6},{14,4},{1,11},{3,9}... | collective-permute-start | bytes 589832 | tf_op jit(solution)/shard_map/ppermute | solution.py:206
  12.6 26.4 %collective-permute-start.4 = (bf16[3,128,256]{2,1,0:T(8,128)(2,1)S(1)}, bf16[3,128,256]{2,1,0:T(8,128)(2,1)S(1)}, u32[]{:S(2)}, u32[]{:S(2)}) collective-permute-start(bf16[3,128,256]{2,1,0:T(8,128)(2,1)S(1)} %get-tuple-element.58), channel_id=1, source_target_pairs={{0,6},{2,4},{4,2},{6,0},{8,14},{10,12},{12,10},{14,8},{1,7},{3,5},... | collective-permute-start | bytes 589832 | tf_op jit(solution)/shard_map/ppermute | solution.py:206
  14.0 25.0 %collective-permute-start.5 = (bf16[3,128,256]{2,1,0:T(8,128)(2,1)S(1)}, bf16[3,128,256]{2,1,0:T(8,128)(2,1)S(1)}, u32[]{:S(2)}, u32[]{:S(2)}) collective-permute-start(bf16[3,128,256]{2,1,0:T(8,128)(2,1)S(1)} %get-tuple-element.60), channel_id=1, source_target_pairs={{0,12},{2,14},{4,8},{6,10},{8,4},{10,6},{12,0},{14,2},{1,13},{3,15... | collective-permute-start | bytes 589832 | tf_op jit(solution)/shard_map/ppermute | solution.py:206
  23.8 15.2 %collective-permute-start.6 = (bf16[3,128,256]{2,1,0:T(8,128)(2,1)S(1)}, bf16[3,128,256]{2,1,0:T(8,128)(2,1)S(1)}, u32[]{:S(2)}, u32[]{:S(2)}) collective-permute-start(bf16[3,128,256]{2,1,0:T(8,128)(2,1)S(1)} %get-tuple-element.62), channel_id=1, source_target_pairs={{0,14},{2,12},{4,10},{6,8},{8,6},{10,4},{12,2},{14,0},{1,15},{3,13... | collective-permute-start | bytes 589832 | tf_op jit(solution)/shard_map/ppermute | solution.py:206
  45.5 14.8 %collective-permute-start.8 = (bf16[4,128,256]{2,1,0:T(8,128)(2,1)S(1)}, bf16[4,128,256]{2,1,0:T(8,128)(2,1)S(1)}, u32[]{:S(2)}, u32[]{:S(2)}) collective-permute-start(bf16[4,128,256]{2,1,0:T(8,128)(2,1)S(1)} %get-tuple-element.70), channel_id=1, source_target_pairs={{0,4},{2,6},{4,0},{6,2},{8,12},{10,14},{12,8},{14,10},{1,5},{3,7},... | collective-permute-start | bytes 786440 | tf_op jit(solution)/shard_map/ppermute | solution.py:206
  53.4 8.4 %collective-permute-start.9 = (bf16[4,128,256]{2,1,0:T(8,128)(2,1)S(1)}, bf16[4,128,256]{2,1,0:T(8,128)(2,1)S(1)}, u32[]{:S(2)}, u32[]{:S(2)}) collective-permute-start(bf16[4,128,256]{2,1,0:T(8,128)(2,1)S(1)} %get-tuple-element.72), channel_id=1, source_target_pairs={{0,2},{2,0},{4,6},{6,4},{8,10},{10,8},{12,14},{14,12},{1,3},{3,1},... | collective-permute-start | bytes 786440 | tf_op jit(solution)/shard_map/ppermute | solution.py:206
  75.3 6.5 %collective-permute-start.14 = (bf16[1,128,256]{2,1,0:T(8,128)(2,1)S(1)}, bf16[1,128,256]{2,1,0:T(8,128)(2,1)S(1)}, u32[]{:S(2)}, u32[]{:S(2)}) collective-permute-start(bf16[1,128,256]{2,1,0:T(8,128)(2,1)S(1)} %add_convert_fusion.1), channel_id=1, source_target_pairs={{0,8},{2,10},{4,12},{6,14},{8,0},{10,2},{12,4},{14,6},{1,9},{3,11}... | collective-permute-start | bytes 196616 | tf_op jit(solution)/shard_map/ppermute | solution.py:206
  82.7 7.3 %collective-permute-start.17 = (bf16[2,128,256]{2,1,0:T(8,128)(2,1)S(1)}, bf16[2,128,256]{2,1,0:T(8,128)(2,1)S(1)}, u32[]{:S(2)}, u32[]{:S(2)}) collective-permute-start(bf16[2,128,256]{2,1,0:T(8,128)(2,1)S(1)} %pad_maximum_fusion.3), channel_id=1, source_target_pairs={{0,4},{2,6},{4,0},{6,2},{8,12},{10,14},{12,8},{14,10},{1,5},{3,7},... | collective-permute-start | bytes 393224 | tf_op jit(solution)/shard_map/ppermute | solution.py:206
  90.1 6.4 %collective-permute-start.18 = (bf16[4,128,256]{2,1,0:T(8,128)(2,1)S(1)}, bf16[4,128,256]{2,1,0:T(8,128)(2,1)S(1)}, u32[]{:S(2)}, u32[]{:S(2)}) collective-permute-start(bf16[4,128,256]{2,1,0:T(8,128)(2,1)S(1)} %pad_maximum_fusion.1.near), channel_id=1, source_target_pairs={{0,2},{2,0},{4,6},{6,4},{8,10},{10,8},{12,14},{14,12},{1,3},{3,1},... | collective-permute-start | bytes 786440 | tf_op jit(solution)/shard_map/ppermute | solution.py:206
  92.1 6.4 %collective-permute-start.19 = (bf16[4,128,256]{2,1,0:T(8,128)(2,1)S(1)}, bf16[4,128,256]{2,1,0:T(8,128)(2,1)S(1)}, u32[]{:S(2)}, u32[]{:S(2)}) collective-permute-start(bf16[4,128,256]{2,1,0:T(8,128)(2,1)S(1)} %pad_maximum_fusion.near_other), channel_id=1, source_target_pairs={{0,4},{2,6},{4,0},{6,2},{8,12},{10,14},{12,8},{14,10},{1,5},{3,7},... | collective-permute-start | bytes 786440 | tf_op jit(solution)/shard_map/ppermute | solution.py:206
  107.1 43.1 %collective-permute-start.24 = (bf16[14,128,128]{2,1,0:T(8,128)(2,1)S(1)}, bf16[14,128,128]{2,1,0:T(8,128)(2,1)S(1)}, u32[]{:S(2)}, u32[]{:S(2)}) collective-permute-start(bf16[14,128,128]{2,1,0:T(8,128)(2,1)S(1)} %get-tuple-element.93), channel_id=1, source_target_pairs={{0,8},{2,10},{4,12},{6,14},{8,0},{10,2},{12,4},{14,6},{1,9},{3,11}... | collective-permute-start | bytes 1376264 | tf_op jit(solution)/shard_map/ppermute | solution.py:206
  108.0 30.9 %collective-permute-start.25 = (bf16[6,128,128]{2,1,0:T(8,128)(2,1)S(1)}, bf16[6,128,128]{2,1,0:T(8,128)(2,1)S(1)}, u32[]{:S(2)}, u32[]{:S(2)}) collective-permute-start(bf16[6,128,128]{2,1,0:T(8,128)(2,1)S(1)} %get-tuple-element.96), channel_id=1, source_target_pairs={{0,8},{2,10},{4,12},{6,14},{8,0},{10,2},{12,4},{14,6},{1,9},{3,11}... | collective-permute-start | bytes 589832 | tf_op jit(solution)/shard_map/ppermute | solution.py:206
  110.2 49.6 %collective-permute-start.21 = (bf16[6,128,256]{2,1,0:T(8,128)(2,1)S(1)}, bf16[6,128,256]{2,1,0:T(8,128)(2,1)S(1)}, u32[]{:S(2)}, u32[]{:S(2)}) collective-permute-start(bf16[6,128,256]{2,1,0:T(8,128)(2,1)S(1)} %get-tuple-element.90), channel_id=1, source_target_pairs={{0,2},{2,0},{4,6},{6,4},{8,10},{10,8},{12,14},{14,12},{1,3},{3,1},... | collective-permute-start | bytes 1179656 | tf_op jit(solution)/shard_map/ppermute | solution.py:206
  110.4 50.7 %collective-permute-start.22 = (bf16[6,128,256]{2,1,0:T(8,128)(2,1)S(1)}, bf16[6,128,256]{2,1,0:T(8,128)(2,1)S(1)}, u32[]{:S(2)}, u32[]{:S(2)}) collective-permute-start(bf16[6,128,256]{2,1,0:T(8,128)(2,1)S(1)} %get-tuple-element.91), channel_id=1, source_target_pairs={{0,4},{2,6},{4,0},{6,2},{8,12},{10,14},{12,8},{14,10},{1,5},{3,7},... | collective-permute-start | bytes 1179656 | tf_op jit(solution)/shard_map/ppermute | solution.py:206
  138.8 11.3 %collective-permute-start.26 = (bf16[6,128,128]{2,1,0:T(8,128)(2,1)S(1)}, bf16[6,128,128]{2,1,0:T(8,128)(2,1)S(1)}, u32[]{:S(2)}, u32[]{:S(2)}) collective-permute-start(bf16[6,128,128]{2,1,0:T(8,128)(2,1)S(1)} %get-tuple-element.97), channel_id=1, source_target_pairs={{0,10},{2,8},{4,14},{6,12},{8,2},{10,0},{12,6},{14,4},{1,11},{3,9}... | collective-permute-start | bytes 589832 | tf_op jit(solution)/shard_map/ppermute | solution.py:206
  139.1 25.3 %collective-permute-start.23 = (bf16[6,128,256]{2,1,0:T(8,128)(2,1)S(1)}, bf16[6,128,256]{2,1,0:T(8,128)(2,1)S(1)}, u32[]{:S(2)}, u32[]{:S(2)}) collective-permute-start(bf16[6,128,256]{2,1,0:T(8,128)(2,1)S(1)} %get-tuple-element.92), channel_id=1, source_target_pairs={{0,6},{2,4},{4,2},{6,0},{8,14},{10,12},{12,10},{14,8},{1,7},{3,5},... | collective-permute-start | bytes 1179656 | tf_op jit(solution)/shard_map/ppermute | solution.py:206
  150.8 9.0 %collective-permute-start.27 = (bf16[6,128,128]{2,1,0:T(8,128)(2,1)S(1)}, bf16[6,128,128]{2,1,0:T(8,128)(2,1)S(1)}, u32[]{:S(2)}, u32[]{:S(2)}) collective-permute-start(bf16[6,128,128]{2,1,0:T(8,128)(2,1)S(1)} %get-tuple-element.99), channel_id=1, source_target_pairs={{0,2},{2,0},{4,6},{6,4},{8,10},{10,8},{12,14},{14,12},{1,3},{3,1},... | collective-permute-start | bytes 589832 | tf_op jit(solution)/shard_map/ppermute | solution.py:206
  151.9 12.5 %collective-permute-start.30 = (bf16[6,128,128]{2,1,0:T(8,128)(2,1)S(1)}, bf16[6,128,128]{2,1,0:T(8,128)(2,1)S(1)}, u32[]{:S(2)}, u32[]{:S(2)}) collective-permute-start(bf16[6,128,128]{2,1,0:T(8,128)(2,1)S(1)} %get-tuple-element.103), channel_id=1, source_target_pairs={{0,12},{2,14},{4,8},{6,10},{8,4},{10,6},{12,0},{14,2},{1,13},{3,15... | collective-permute-start | bytes 589832 | tf_op jit(solution)/shard_map/ppermute | solution.py:206
  159.8 7.8 %collective-permute-start.28 = (bf16[6,128,128]{2,1,0:T(8,128)(2,1)S(1)}, bf16[6,128,128]{2,1,0:T(8,128)(2,1)S(1)}, u32[]{:S(2)}, u32[]{:S(2)}) collective-permute-start(bf16[6,128,128]{2,1,0:T(8,128)(2,1)S(1)} %get-tuple-element.100), channel_id=1, source_target_pairs={{0,4},{2,6},{4,0},{6,2},{8,12},{10,14},{12,8},{14,10},{1,5},{3,7},... | collective-permute-start | bytes 589832 | tf_op jit(solution)/shard_map/ppermute | solution.py:206
  159.8 11.8 %collective-permute-start.29 = (bf16[6,128,128]{2,1,0:T(8,128)(2,1)S(1)}, bf16[6,128,128]{2,1,0:T(8,128)(2,1)S(1)}, u32[]{:S(2)}, u32[]{:S(2)}) collective-permute-start(bf16[6,128,128]{2,1,0:T(8,128)(2,1)S(1)} %get-tuple-element.101), channel_id=1, source_target_pairs={{0,6},{2,4},{4,2},{6,0},{8,14},{10,12},{12,10},{14,8},{1,7},{3,5},... | collective-permute-start | bytes 589832 | tf_op jit(solution)/shard_map/ppermute | solution.py:206
  161.1 16.2 %collective-permute-start.31 = (bf16[6,128,128]{2,1,0:T(8,128)(2,1)S(1)}, bf16[6,128,128]{2,1,0:T(8,128)(2,1)S(1)}, u32[]{:S(2)}, u32[]{:S(2)}) collective-permute-start(bf16[6,128,128]{2,1,0:T(8,128)(2,1)S(1)} %get-tuple-element.105), channel_id=1, source_target_pairs={{0,14},{2,12},{4,10},{6,8},{8,6},{10,4},{12,2},{14,0},{1,15},{3,13... | collective-permute-start | bytes 589832 | tf_op jit(solution)/shard_map/ppermute | solution.py:206
  (13 other events, 137.6 us)

commit v12 on v10

--- a/solution.py
+++ b/solution.py
@@ -119,7 +119,8 @@
                     far[step - devices // 2][group * cap + rank] = ready[b, :, pl.ds(part, part)]
 
 
-def pass_on_kernel(devices, cap, table, whole, *outs):
+def pass_on_kernel(devices, cap, table, whole, *rest):
+    outs = rest[-(devices // 2) :]
     for group in range(2):
         for step in range(devices // 2):
             for rank in range(cap):
@@ -201,6 +202,9 @@
             name=name,
         )(table, *args, *ready)
 
+    def shift(x, d):
+        return lax.ppermute(x, "pair", [(s, (s + d) % n) for s in range(n)])
+
     def flip(x, bit):
         return lax.ppermute(x, "pair", [(s, s ^ bit) for s in range(n)])
 
@@ -214,8 +218,10 @@
         return slots_of(peers ^ device, ranks, n, cap)
 
     home_held, home_passed, home_rows = tables(home_slot, n, blocks, me)
-    send_table = ints([slots(*home_rows, me), core[None].astype(jnp.int32)])
-    pick_table = slots(*home_held, me)
+    send_table = ints(
+        [slots_of((home_rows[0] - me) % n, home_rows[1], n, cap), core[None].astype(jnp.int32)]
+    )
+    pick_table = slots_of((me - home_held[0]) % n, home_held[1], n, cap)
     chunk_table = me ^ jnp.arange(n, dtype=jnp.int32)
     weight = jnp.where(pair_shells[:, 0] != pair_shells[:, 1], 2.0, 1.0)
     factor = (screen.astype(f32) * weight[:, None]).astype(bf16)[:, None, :]
@@ -234,8 +240,8 @@
         compiler_params=pltpu.CompilerParams(vmem_limit_bytes=VMEM_BYTES),
         name="scatter_density",
     )(send_table, density)
-    steps = range(1, n)
-    received = [flip(sends[d], d) for d in steps[:-1]]
+    steps = sorted(range(1, n), key=lambda d: abs(2 * d - n))
+    received = [shift(sends[d], d) for d in steps[:-1]]
     integrals = pl.pallas_call(
         load_kernel,
         out_shape=pltpu.VMEM((blocks, pairs, aux_dev), bf16),
@@ -244,8 +250,8 @@
         scratch_shapes=[pltpu.SemaphoreType.DMA],
         compiler_params=pltpu.CompilerParams(vmem_limit_bytes=2 * 1024 * 1024),
         name="load_integrals",
-    )(three_index, received[1])
-    received += [flip(after(sends[steps[-1]], integrals), steps[-1]), sends[0]]
+    )(three_index, received[0])
+    received += [shift(after(sends[steps[-1]], integrals), steps[-1]), sends[0]]
     steps = (*steps, 0)
     own = call(
         functools.partial(gather_density_kernel, steps, cap),
@@ -331,8 +337,12 @@
         [in_vmem] * (n + 1),
         scratch=[pltpu.VMEM((blocks, half, pairs), bf16)],
     )
+    def direct(i, *ready):
+        return flip(after(sends[n // 2 + i], *ready), n // 2 + i)
+
     whole = flip(sends[n], n // 2)
     near = [sends[0]] + [flip(sends[d], d) for d in range(1, n // 2)]
+    far = [direct(0), direct(1, near[1]), direct(2, near[2])]
     passed = call(
         functools.partial(pass_on_kernel, n, cap),
         "pass_on",
@@ -340,11 +350,11 @@
         [whole],
         [jax.ShapeDtypeStruct((2 * cap, half, part), bf16)] * (n // 2),
         [in_vmem] * (n // 2),
+        near[1:],
     )
     passed = [passed[0]] + [flip(passed[d], d) for d in range(1, n // 2)]
-    far = [flip(sends[n // 2], n // 2)]
-    for i in range(1, n // 2):
-        far.append(flip(after(sends[n // 2 + i], near[1] if i == 1 else passed[i - 1]), n // 2 + i))
+    for i in range(3, n // 2):
+        far.append(direct(i, passed[i - 2]))
     return call(
         functools.partial(gather_coulomb_kernel, n, blocks, shell, cap),
         "gather_coulomb",

time: 176 us -> 174 us (0.989)
  the two profiles are of different devices: /device:TPU:23 before, /device:TPU:0 now
where the time goes in v12:
time: 174 us; the launch traced here: 173 us
  waiting for transfers between devices  93.5 us (54%)
  starting transfers between devices  50.2 us (29%)
  Pallas kernels  18 us (10%)
  local copies, waits for them, and re-layouts  6.81 us (4%)
  other arithmetic  3.66 us (2%)
    ppermute x23, waiting for transfers between devices, flip(): return lax.ppermute(x, 'pair', [(s, s ^ bit) for s in range(n)])  73.5 us
    ppermute x23, starting transfers between devices, flip(): return lax.ppermute(x, 'pair', [(s, s ^ bit) for s in range(n)])  33.6 us
    ppermute x7, waiting for transfers between devices, shift(): return lax.ppermute(x, 'pair', [(s, (s + d) % n) for s in range(n)])  18.1 us
    ppermute x7, starting transfers between devices, shift(): return lax.ppermute(x, 'pair', [(s, (s + d) % n) for s in range(n)])  16.5 us
    pallas_call x7, Pallas kernels, call(): pl.pallas_call(kernel, out_shape=out_shape, grid_spec=pltpu.PrefetchScala...  16 us
    unnamed x10, local copies, waits for them, and re-layouts  6.69 us
  transfers between devices with their start and end apart: 32, of which 20 were waited for; matrix products, arithmetic and copies ran while one was open for 1% of the time, Pallas kernels for 3%

profile of v12, /device:TPU:0, one launch (start us, length us, event | category | flops | bytes accessed | tf_op | source)
XLA Modules:
  0.0 173.2 jit_solution(137021709532967197)
XLA Ops:
  5.1 4.1 %collective-permute-start = (bf16[3,128,256]{2,1,0:T(8,128)(2,1)S(1)}, bf16[3,128,256]{2,1,0:T(8,128)(2,1)S(1)}, u32[]{:S(2)}, u32[]{:S(2)}) collective-permute-start(bf16[3,128,256]{2,1,0:T(8,128)(2,1)S(1)} %get-tuple-element.52), channel_id=1, source_target_pairs={{0,8},{2,10},{4,12},{6,14},{8,0},{10,2},{12,4},{14,6},{1,9},{3,11}... | collective-permute-start | bytes 589832 | tf_op jit(solution)/shard_map/ppermute | solution.py:206
  16.8 15.0 %collective-permute-done.ready.rest_0_ = bf16[3,128,256]{2,1,0:T(8,128)(2,1)S(1)} collective-permute-done((bf16[3,128,256]{2,1,0:T(8,128)(2,1)S(1)}, bf16[3,128,256]{2,1,0:T(8,128)(2,1)S(1)}, u32[]{:S(2)}, u32[]{:S(2)}) %collective-permute-start) | collective-permute-done | bytes 196640 | tf_op jit(solution)/shard_map/ppermute | solution.py:206
  31.8 5.2 %copy-done = bf16[14,256,2048]{2,1,0:T(8,128)(2,1)S(1)} copy-done((bf16[14,256,2048]{2,1,0:T(8,128)(2,1)S(1)}, bf16[14,256,2048]{2,1,0:T(8,128)(2,1)}, u32[]{:S(2)}) %copy-start) | copy-done | bytes 14680088
  38.0 4.8 %collective-permute-start.6 = (bf16[3,128,256]{2,1,0:T(8,128)(2,1)S(1)}, bf16[3,128,256]{2,1,0:T(8,128)(2,1)S(1)}, u32[]{:S(2)}, u32[]{:S(2)}) collective-permute-start(bf16[3,128,256]{2,1,0:T(8,128)(2,1)S(1)} %get-tuple-element.59), channel_id=1, source_target_pairs={{0,14},{2,0},{4,2},{6,4},{8,6},{10,8},{12,10},{14,12},{1,15},{3,1}... | collective-permute-start | bytes 589832 | tf_op jit(solution)/shard_map/ppermute | solution.py:206
  42.9 3.1 %collective-permute-done.6.rest_6_ = bf16[3,128,256]{2,1,0:T(8,128)(2,1)S(1)} collective-permute-done((bf16[3,128,256]{2,1,0:T(8,128)(2,1)S(1)}, bf16[3,128,256]{2,1,0:T(8,128)(2,1)S(1)}, u32[]{:S(2)}, u32[]{:S(2)}) %collective-permute-start.6) | collective-permute-done | bytes 196640 | tf_op jit(solution)/shard_map/ppermute | solution.py:206
  46.9 2.8 %fit.2 = (f32[4,128,256]{2,1,0:T(8,128)S(1)}, bf16[4,128,256]{2,1,0:T(8,128)(2,1)S(1)}) custom-call(s32[8]{0:T(128)S(1)} %iota_xor_fusion.table, bf16[14,1,256]{2,1,0:T(2,128)(2,1)S(1)} %copy.11.factor, bf16[14,128,256]{2,1,0:T(8,128)(2,1)S(1)} %gather_density.1.density, bf16[14,256,2048]{2,1,0:T(8,128)(2,1)S(1)} %load_integrals.1.integrals), custom_call_target="tpu_custom_call" | custom-call | tf_op jit(solution)/shard_map/fit/pallas_call | solution.py:191
  49.7 2.7 %fit.3 = (f32[4,128,256]{2,1,0:T(8,128)S(1)}, bf16[4,128,256]{2,1,0:T(8,128)(2,1)S(1)}) custom-call(s32[8]{0:T(128)S(1)} %iota_xor_fusion.table, bf16[14,1,256]{2,1,0:T(2,128)(2,1)S(1)} %copy.11.factor, bf16[14,128,256]{2,1,0:T(8,128)(2,1)S(1)} %collective-permute-done.7.density, bf16[14,256,2048]{2,1,0:T(8,128)(2,1)S(1)} %load_integrals.1.integrals, ...), custom_call_target="tpu_custom_call" | custom-call | tf_op jit(solution)/shard_map/fit/pallas_call | solution.py:191
  52.9 8.3 %collective-permute-done.8 = bf16[4,128,256]{2,1,0:T(8,128)(2,1)S(1)} collective-permute-done((bf16[4,128,256]{2,1,0:T(8,128)(2,1)S(1)}, bf16[4,128,256]{2,1,0:T(8,128)(2,1)S(1)}, u32[]{:S(2)}, u32[]{:S(2)}) %collective-permute-start.8) | collective-permute-done | bytes 262176 | tf_op jit(solution)/shard_map/ppermute | solution.py:209
  63.5 3.2 %collective-permute-done.10 = bf16[2,128,256]{2,1,0:T(8,128)(2,1)S(1)} collective-permute-done((bf16[2,128,256]{2,1,0:T(8,128)(2,1)S(1)}, bf16[2,128,256]{2,1,0:T(8,128)(2,1)S(1)}, u32[]{:S(2)}, u32[]{:S(2)}) %collective-permute-start.10) | collective-permute-done | bytes 131104 | tf_op jit(solution)/shard_map/ppermute | solution.py:209
  66.8 5.8 %collective-permute-start.12 = (bf16[1,128,256]{2,1,0:T(8,128)(2,1)S(1)}, bf16[1,128,256]{2,1,0:T(8,128)(2,1)S(1)}, u32[]{:S(2)}, u32[]{:S(2)}) collective-permute-start(bf16[1,128,256]{2,1,0:T(8,128)(2,1)S(1)} %slice.57), channel_id=1, source_target_pairs={{0,8},{2,10},{4,12},{6,14},{8,0},{10,2},{12,4},{14,6},{1,9},{3,11}... | collective-permute-start | bytes 196616 | tf_op jit(solution)/shard_map/ppermute | solution.py:209
  72.7 4.1 %collective-permute-done.12 = bf16[1,128,256]{2,1,0:T(8,128)(2,1)S(1)} collective-permute-done((bf16[1,128,256]{2,1,0:T(8,128)(2,1)S(1)}, bf16[1,128,256]{2,1,0:T(8,128)(2,1)S(1)}, u32[]{:S(2)}, u32[]{:S(2)}) %collective-permute-start.12) | collective-permute-done | bytes 65568 | tf_op jit(solution)/shard_map/ppermute | solution.py:209
  78.7 2.7 %collective-permute-start.15 = (bf16[1,128,256]{2,1,0:T(8,128)(2,1)S(1)}, bf16[1,128,256]{2,1,0:T(8,128)(2,1)S(1)}, u32[]{:S(2)}, u32[]{:S(2)}) collective-permute-start(bf16[1,128,256]{2,1,0:T(8,128)(2,1)S(1)} %add_convert_fusion), channel_id=1, source_target_pairs={{0,8},{2,10},{4,12},{6,14},{8,0},{10,2},{12,4},{14,6},{1,9},{3,11}... | collective-permute-start | bytes 196616 | tf_op jit(solution)/shard_map/ppermute | solution.py:209
  86.5 3.3 %collective-permute-done.16 = bf16[2,128,256]{2,1,0:T(8,128)(2,1)S(1)} collective-permute-done((bf16[2,128,256]{2,1,0:T(8,128)(2,1)S(1)}, bf16[2,128,256]{2,1,0:T(8,128)(2,1)S(1)}, u32[]{:S(2)}, u32[]{:S(2)}) %collective-permute-start.16) | collective-permute-done | bytes 131104 | tf_op jit(solution)/shard_map/ppermute | solution.py:209
  93.5 3.0 %collective-permute-done.18.far = bf16[4,128,256]{2,1,0:T(8,128)(2,1)S(1)} collective-permute-done((bf16[4,128,256]{2,1,0:T(8,128)(2,1)S(1)}, bf16[4,128,256]{2,1,0:T(8,128)(2,1)S(1)}, u32[]{:S(2)}, u32[]{:S(2)}) %collective-permute-start.18) | collective-permute-done | bytes 262176 | tf_op jit(solution)/shard_map/ppermute | solution.py:209
  98.3 5.0 %apply.1 = (f32[14,128,256]{2,1,0:T(8,128)S(1)}, bf16[14,128,256]{2,1,0:T(8,128)(2,1)S(1)}) custom-call(s32[8]{0:T(128)S(1)} %iota_xor_fusion.table, bf16[14,256,2048]{2,1,0:T(8,128)(2,1)S(1)} %load_integrals.1.integrals, bf16[4,128,256]{2,1,0:T(8,128)(2,1)S(1)} %pad_maximum_fusion.1.near, bf16[4,128,256]{2,1,0:T(8,128)(2,1)S(1)} %collective-permute-done.18.far, ...), custom_call_target="tpu_custom_call" | custom-call | tf_op jit(solution)/shard_map/apply/pallas_call | solution.py:191
  106.9 2.9 %collective-permute-start.24 = (bf16[14,128,128]{2,1,0:T(8,128)(2,1)S(1)}, bf16[14,128,128]{2,1,0:T(8,128)(2,1)S(1)}, u32[]{:S(2)}, u32[]{:S(2)}) collective-permute-start(bf16[14,128,128]{2,1,0:T(8,128)(2,1)S(1)} %get-tuple-element.90), channel_id=1, source_target_pairs={{0,8},{2,10},{4,12},{6,14},{8,0},{10,2},{12,4},{14,6},{1,9},{3,11}... | collective-permute-start | bytes 1376264 | tf_op jit(solution)/shard_map/ppermute | solution.py:209
  114.1 6.8 %collective-permute-done.21.rest_0_.rest_1_ = bf16[6,128,256]{2,1,0:T(8,128)(2,1)S(1)} collective-permute-done((bf16[6,128,256]{2,1,0:T(8,128)(2,1)S(1)}, bf16[6,128,256]{2,1,0:T(8,128)(2,1)S(1)}, u32[]{:S(2)}, u32[]{:S(2)}) %collective-permute-start.21) | collective-permute-done | bytes 393248 | tf_op jit(solution)/shard_map/ppermute | solution.py:209
  120.8 8.3 %collective-permute-done.22.rest_1_.rest_2_ = bf16[6,128,256]{2,1,0:T(8,128)(2,1)S(1)} collective-permute-done((bf16[6,128,256]{2,1,0:T(8,128)(2,1)S(1)}, bf16[6,128,256]{2,1,0:T(8,128)(2,1)S(1)}, u32[]{:S(2)}, u32[]{:S(2)}) %collective-permute-start.22) | collective-permute-done | bytes 393248 | tf_op jit(solution)/shard_map/ppermute | solution.py:209
  129.1 14.1 %collective-permute-done.23.rest_2_.rest_3_ = bf16[6,128,256]{2,1,0:T(8,128)(2,1)S(1)} collective-permute-done((bf16[6,128,256]{2,1,0:T(8,128)(2,1)S(1)}, bf16[6,128,256]{2,1,0:T(8,128)(2,1)S(1)}, u32[]{:S(2)}, u32[]{:S(2)}) %collective-permute-start.23) | collective-permute-done | bytes 393248 | tf_op jit(solution)/shard_map/ppermute | solution.py:209
  152.2 3.4 %collective-permute-start.31 = (bf16[6,128,128]{2,1,0:T(8,128)(2,1)S(1)}, bf16[6,128,128]{2,1,0:T(8,128)(2,1)S(1)}, u32[]{:S(2)}, u32[]{:S(2)}) collective-permute-start(bf16[6,128,128]{2,1,0:T(8,128)(2,1)S(1)} %get-tuple-element.101), channel_id=1, source_target_pairs={{0,14},{2,12},{4,10},{6,8},{8,6},{10,4},{12,2},{14,0},{1,15},{3,13... | collective-permute-start | bytes 589832 | tf_op jit(solution)/shard_map/ppermute | solution.py:209
  155.7 5.0 %collective-permute-done.29.rest_9_ = bf16[6,128,128]{2,1,0:T(8,128)(2,1)S(1)} collective-permute-done((bf16[6,128,128]{2,1,0:T(8,128)(2,1)S(1)}, bf16[6,128,128]{2,1,0:T(8,128)(2,1)S(1)}, u32[]{:S(2)}, u32[]{:S(2)}) %collective-permute-start.29) | collective-permute-done | bytes 196640 | tf_op jit(solution)/shard_map/ppermute | solution.py:209
  160.8 2.8 %collective-permute-done.26.rest_6_ = bf16[6,128,128]{2,1,0:T(8,128)(2,1)S(1)} collective-permute-done((bf16[6,128,128]{2,1,0:T(8,128)(2,1)S(1)}, bf16[6,128,128]{2,1,0:T(8,128)(2,1)S(1)}, u32[]{:S(2)}, u32[]{:S(2)}) %collective-permute-start.26) | collective-permute-done | bytes 196640 | tf_op jit(solution)/shard_map/ppermute | solution.py:209
  163.5 6.5 %collective-permute-done.27.rest_7_ = bf16[6,128,128]{2,1,0:T(8,128)(2,1)S(1)} collective-permute-done((bf16[6,128,128]{2,1,0:T(8,128)(2,1)S(1)}, bf16[6,128,128]{2,1,0:T(8,128)(2,1)S(1)}, u32[]{:S(2)}, u32[]{:S(2)}) %collective-permute-start.27) | collective-permute-done | bytes 196640 | tf_op jit(solution)/shard_map/ppermute | solution.py:209
  170.1 3.1 %gather_coulomb.1 = (bf16[14,256,128]{2,1,0:T(8,128)(2,1)}, bf16[14,256,128]{2,1,0:T(8,128)(2,1)}) custom-call(s32[48]{0:T(128)S(1)} %pad_add_fusion.1.table, bf16[6,128,256]{2,1,0:T(8,128)(2,1)S(1)} %get-tuple-element.86.rest_0_, bf16[6,128,256]{2,1,0:T(8,128)(2,1)S(1)} %collective-permute-done.21.rest_0_.rest_1_, ...), custom_call_target="tpu_custom_call" | custom-call | tf_op jit(solution)/shard_map/gather_coulomb/pallas_call | solution.py:191
  (106 shorter events, 46.3 us)
Async XLA Ops:
  5.1 26.7 %collective-permute-start = (bf16[3,128,256]{2,1,0:T(8,128)(2,1)S(1)}, bf16[3,128,256]{2,1,0:T(8,128)(2,1)S(1)}, u32[]{:S(2)}, u32[]{:S(2)}) collective-permute-start(bf16[3,128,256]{2,1,0:T(8,128)(2,1)S(1)} %get-tuple-element.52), channel_id=1, source_target_pairs={{0,8},{2,10},{4,12},{6,14},{8,0},{10,2},{12,4},{14,6},{1,9},{3,11}... | collective-permute-start | bytes 589832 | tf_op jit(solution)/shard_map/ppermute | solution.py:206
  9.2 28.8 %collective-permute-start.1 = (bf16[3,128,256]{2,1,0:T(8,128)(2,1)S(1)}, bf16[3,128,256]{2,1,0:T(8,128)(2,1)S(1)}, u32[]{:S(2)}, u32[]{:S(2)}) collective-permute-start(bf16[3,128,256]{2,1,0:T(8,128)(2,1)S(1)} %get-tuple-element.53), channel_id=1, source_target_pairs={{0,6},{2,8},{4,10},{6,12},{8,14},{10,0},{12,2},{14,4},{1,7},{3,9},... | collective-permute-start | bytes 589832 | tf_op jit(solution)/shard_map/ppermute | solution.py:206
  11.7 31.1 %collective-permute-start.2 = (bf16[3,128,256]{2,1,0:T(8,128)(2,1)S(1)}, bf16[3,128,256]{2,1,0:T(8,128)(2,1)S(1)}, u32[]{:S(2)}, u32[]{:S(2)}) collective-permute-start(bf16[3,128,256]{2,1,0:T(8,128)(2,1)S(1)} %get-tuple-element.54), channel_id=1, source_target_pairs={{0,10},{2,12},{4,14},{6,0},{8,2},{10,4},{12,6},{14,8},{1,11},{3,13... | collective-permute-start | bytes 589832 | tf_op jit(solution)/shard_map/ppermute | solution.py:206
  13.0 29.9 %collective-permute-start.3 = (bf16[3,128,256]{2,1,0:T(8,128)(2,1)S(1)}, bf16[3,128,256]{2,1,0:T(8,128)(2,1)S(1)}, u32[]{:S(2)}, u32[]{:S(2)}) collective-permute-start(bf16[3,128,256]{2,1,0:T(8,128)(2,1)S(1)} %get-tuple-element.55), channel_id=1, source_target_pairs={{0,4},{2,6},{4,8},{6,10},{8,12},{10,14},{12,0},{14,2},{1,5},{3,7},... | collective-permute-start | bytes 589832 | tf_op jit(solution)/shard_map/ppermute | solution.py:206
  14.6 28.3 %collective-permute-start.4 = (bf16[3,128,256]{2,1,0:T(8,128)(2,1)S(1)}, bf16[3,128,256]{2,1,0:T(8,128)(2,1)S(1)}, u32[]{:S(2)}, u32[]{:S(2)}) collective-permute-start(bf16[3,128,256]{2,1,0:T(8,128)(2,1)S(1)} %get-tuple-element.56), channel_id=1, source_target_pairs={{0,12},{2,14},{4,0},{6,2},{8,4},{10,6},{12,8},{14,10},{1,13},{3,15... | collective-permute-start | bytes 589832 | tf_op jit(solution)/shard_map/ppermute | solution.py:206
  31.8 11.1 %collective-permute-start.5 = (bf16[3,128,256]{2,1,0:T(8,128)(2,1)S(1)}, bf16[3,128,256]{2,1,0:T(8,128)(2,1)S(1)}, u32[]{:S(2)}, u32[]{:S(2)}) collective-permute-start(bf16[3,128,256]{2,1,0:T(8,128)(2,1)S(1)} %get-tuple-element.57), channel_id=1, source_target_pairs={{0,2},{2,4},{4,6},{6,8},{8,10},{10,12},{12,14},{14,0},{1,3},{3,5},... | collective-permute-start | bytes 589832 | tf_op jit(solution)/shard_map/ppermute | solution.py:206
  38.0 8.0 %collective-permute-start.6 = (bf16[3,128,256]{2,1,0:T(8,128)(2,1)S(1)}, bf16[3,128,256]{2,1,0:T(8,128)(2,1)S(1)}, u32[]{:S(2)}, u32[]{:S(2)}) collective-permute-start(bf16[3,128,256]{2,1,0:T(8,128)(2,1)S(1)} %get-tuple-element.59), channel_id=1, source_target_pairs={{0,14},{2,0},{4,2},{6,4},{8,6},{10,8},{12,10},{14,12},{1,15},{3,1}... | collective-permute-start | bytes 589832 | tf_op jit(solution)/shard_map/ppermute | solution.py:206
  52.5 8.8 %collective-permute-start.8 = (bf16[4,128,256]{2,1,0:T(8,128)(2,1)S(1)}, bf16[4,128,256]{2,1,0:T(8,128)(2,1)S(1)}, u32[]{:S(2)}, u32[]{:S(2)}) collective-permute-start(bf16[4,128,256]{2,1,0:T(8,128)(2,1)S(1)} %get-tuple-element.67), channel_id=1, source_target_pairs={{0,4},{2,6},{4,0},{6,2},{8,12},{10,14},{12,8},{14,10},{1,5},{3,7},... | collective-permute-start | bytes 786440 | tf_op jit(solution)/shard_map/ppermute | solution.py:209
  52.6 8.8 %collective-permute-start.9 = (bf16[4,128,256]{2,1,0:T(8,128)(2,1)S(1)}, bf16[4,128,256]{2,1,0:T(8,128)(2,1)S(1)}, u32[]{:S(2)}, u32[]{:S(2)}) collective-permute-start(bf16[4,128,256]{2,1,0:T(8,128)(2,1)S(1)} %get-tuple-element.69), channel_id=1, source_target_pairs={{0,2},{2,0},{4,6},{6,4},{8,10},{10,8},{12,14},{14,12},{1,3},{3,1},... | collective-permute-start | bytes 786440 | tf_op jit(solution)/shard_map/ppermute | solution.py:209
  66.8 10.0 %collective-permute-start.12 = (bf16[1,128,256]{2,1,0:T(8,128)(2,1)S(1)}, bf16[1,128,256]{2,1,0:T(8,128)(2,1)S(1)}, u32[]{:S(2)}, u32[]{:S(2)}) collective-permute-start(bf16[1,128,256]{2,1,0:T(8,128)(2,1)S(1)} %slice.57), channel_id=1, source_target_pairs={{0,8},{2,10},{4,12},{6,14},{8,0},{10,2},{12,4},{14,6},{1,9},{3,11}... | collective-permute-start | bytes 196616 | tf_op jit(solution)/shard_map/ppermute | solution.py:209
  78.7 6.1 %collective-permute-start.15 = (bf16[1,128,256]{2,1,0:T(8,128)(2,1)S(1)}, bf16[1,128,256]{2,1,0:T(8,128)(2,1)S(1)}, u32[]{:S(2)}, u32[]{:S(2)}) collective-permute-start(bf16[1,128,256]{2,1,0:T(8,128)(2,1)S(1)} %add_convert_fusion), channel_id=1, source_target_pairs={{0,8},{2,10},{4,12},{6,14},{8,0},{10,2},{12,4},{14,6},{1,9},{3,11}... | collective-permute-start | bytes 196616 | tf_op jit(solution)/shard_map/ppermute | solution.py:209
  90.1 6.4 %collective-permute-start.18 = (bf16[4,128,256]{2,1,0:T(8,128)(2,1)S(1)}, bf16[4,128,256]{2,1,0:T(8,128)(2,1)S(1)}, u32[]{:S(2)}, u32[]{:S(2)}) collective-permute-start(bf16[4,128,256]{2,1,0:T(8,128)(2,1)S(1)} %pad_maximum_fusion.1.near), channel_id=1, source_target_pairs={{0,2},{2,0},{4,6},{6,4},{8,10},{10,8},{12,14},{14,12},{1,3},{3,1},... | collective-permute-start | bytes 786440 | tf_op jit(solution)/shard_map/ppermute | solution.py:209
  92.0 6.4 %collective-permute-start.19 = (bf16[4,128,256]{2,1,0:T(8,128)(2,1)S(1)}, bf16[4,128,256]{2,1,0:T(8,128)(2,1)S(1)}, u32[]{:S(2)}, u32[]{:S(2)}) collective-permute-start(bf16[4,128,256]{2,1,0:T(8,128)(2,1)S(1)} %pad_maximum_fusion.near_other), channel_id=1, source_target_pairs={{0,4},{2,6},{4,0},{6,2},{8,12},{10,14},{12,8},{14,10},{1,5},{3,7},... | collective-permute-start | bytes 786440 | tf_op jit(solution)/shard_map/ppermute | solution.py:209
  106.9 36.3 %collective-permute-start.24 = (bf16[14,128,128]{2,1,0:T(8,128)(2,1)S(1)}, bf16[14,128,128]{2,1,0:T(8,128)(2,1)S(1)}, u32[]{:S(2)}, u32[]{:S(2)}) collective-permute-start(bf16[14,128,128]{2,1,0:T(8,128)(2,1)S(1)} %get-tuple-element.90), channel_id=1, source_target_pairs={{0,8},{2,10},{4,12},{6,14},{8,0},{10,2},{12,4},{14,6},{1,9},{3,11}... | collective-permute-start | bytes 1376264 | tf_op jit(solution)/shard_map/ppermute | solution.py:209
  109.9 10.9 %collective-permute-start.21 = (bf16[6,128,256]{2,1,0:T(8,128)(2,1)S(1)}, bf16[6,128,256]{2,1,0:T(8,128)(2,1)S(1)}, u32[]{:S(2)}, u32[]{:S(2)}) collective-permute-start(bf16[6,128,256]{2,1,0:T(8,128)(2,1)S(1)} %get-tuple-element.87), channel_id=1, source_target_pairs={{0,2},{2,0},{4,6},{6,4},{8,10},{10,8},{12,14},{14,12},{1,3},{3,1},... | collective-permute-start | bytes 1179656 | tf_op jit(solution)/shard_map/ppermute | solution.py:209
  110.1 19.1 %collective-permute-start.22 = (bf16[6,128,256]{2,1,0:T(8,128)(2,1)S(1)}, bf16[6,128,256]{2,1,0:T(8,128)(2,1)S(1)}, u32[]{:S(2)}, u32[]{:S(2)}) collective-permute-start(bf16[6,128,256]{2,1,0:T(8,128)(2,1)S(1)} %get-tuple-element.88), channel_id=1, source_target_pairs={{0,4},{2,6},{4,0},{6,2},{8,12},{10,14},{12,8},{14,10},{1,5},{3,7},... | collective-permute-start | bytes 1179656 | tf_op jit(solution)/shard_map/ppermute | solution.py:209
  112.1 31.1 %collective-permute-start.23 = (bf16[6,128,256]{2,1,0:T(8,128)(2,1)S(1)}, bf16[6,128,256]{2,1,0:T(8,128)(2,1)S(1)}, u32[]{:S(2)}, u32[]{:S(2)}) collective-permute-start(bf16[6,128,256]{2,1,0:T(8,128)(2,1)S(1)} %get-tuple-element.89), channel_id=1, source_target_pairs={{0,6},{2,4},{4,2},{6,0},{8,14},{10,12},{12,10},{14,8},{1,7},{3,5},... | collective-permute-start | bytes 1179656 | tf_op jit(solution)/shard_map/ppermute | solution.py:209
  113.9 38.3 %collective-permute-start.28 = (bf16[6,128,128]{2,1,0:T(8,128)(2,1)S(1)}, bf16[6,128,128]{2,1,0:T(8,128)(2,1)S(1)}, u32[]{:S(2)}, u32[]{:S(2)}) collective-permute-start(bf16[6,128,128]{2,1,0:T(8,128)(2,1)S(1)} %get-tuple-element.95), channel_id=1, source_target_pairs={{0,8},{2,10},{4,12},{6,14},{8,0},{10,2},{12,4},{14,6},{1,9},{3,11}... | collective-permute-start | bytes 589832 | tf_op jit(solution)/shard_map/ppermute | solution.py:209
  143.8 6.2 %collective-permute-start.25 = (bf16[6,128,128]{2,1,0:T(8,128)(2,1)S(1)}, bf16[6,128,128]{2,1,0:T(8,128)(2,1)S(1)}, u32[]{:S(2)}, u32[]{:S(2)}) collective-permute-start(bf16[6,128,128]{2,1,0:T(8,128)(2,1)S(1)} %get-tuple-element.92), channel_id=1, source_target_pairs={{0,2},{2,0},{4,6},{6,4},{8,10},{10,8},{12,14},{14,12},{1,3},{3,1},... | collective-permute-start | bytes 589832 | tf_op jit(solution)/shard_map/ppermute | solution.py:209
  144.2 16.5 %collective-permute-start.29 = (bf16[6,128,128]{2,1,0:T(8,128)(2,1)S(1)}, bf16[6,128,128]{2,1,0:T(8,128)(2,1)S(1)}, u32[]{:S(2)}, u32[]{:S(2)}) collective-permute-start(bf16[6,128,128]{2,1,0:T(8,128)(2,1)S(1)} %get-tuple-element.97), channel_id=1, source_target_pairs={{0,10},{2,8},{4,14},{6,12},{8,2},{10,0},{12,6},{14,4},{1,11},{3,9}... | collective-permute-start | bytes 589832 | tf_op jit(solution)/shard_map/ppermute | solution.py:209
  145.4 15.3 %collective-permute-start.30 = (bf16[6,128,128]{2,1,0:T(8,128)(2,1)S(1)}, bf16[6,128,128]{2,1,0:T(8,128)(2,1)S(1)}, u32[]{:S(2)}, u32[]{:S(2)}) collective-permute-start(bf16[6,128,128]{2,1,0:T(8,128)(2,1)S(1)} %get-tuple-element.99), channel_id=1, source_target_pairs={{0,12},{2,14},{4,8},{6,10},{8,4},{10,6},{12,0},{14,2},{1,13},{3,15... | collective-permute-start | bytes 589832 | tf_op jit(solution)/shard_map/ppermute | solution.py:209
  147.3 16.2 %collective-permute-start.26 = (bf16[6,128,128]{2,1,0:T(8,128)(2,1)S(1)}, bf16[6,128,128]{2,1,0:T(8,128)(2,1)S(1)}, u32[]{:S(2)}, u32[]{:S(2)}) collective-permute-start(bf16[6,128,128]{2,1,0:T(8,128)(2,1)S(1)} %get-tuple-element.93), channel_id=1, source_target_pairs={{0,4},{2,6},{4,0},{6,2},{8,12},{10,14},{12,8},{14,10},{1,5},{3,7},... | collective-permute-start | bytes 589832 | tf_op jit(solution)/shard_map/ppermute | solution.py:209
  150.1 20.0 %collective-permute-start.27 = (bf16[6,128,128]{2,1,0:T(8,128)(2,1)S(1)}, bf16[6,128,128]{2,1,0:T(8,128)(2,1)S(1)}, u32[]{:S(2)}, u32[]{:S(2)}) collective-permute-start(bf16[6,128,128]{2,1,0:T(8,128)(2,1)S(1)} %get-tuple-element.94), channel_id=1, source_target_pairs={{0,6},{2,4},{4,2},{6,0},{8,14},{10,12},{12,10},{14,8},{1,7},{3,5},... | collective-permute-start | bytes 589832 | tf_op jit(solution)/shard_map/ppermute | solution.py:209
  152.2 17.9 %collective-permute-start.31 = (bf16[6,128,128]{2,1,0:T(8,128)(2,1)S(1)}, bf16[6,128,128]{2,1,0:T(8,128)(2,1)S(1)}, u32[]{:S(2)}, u32[]{:S(2)}) collective-permute-start(bf16[6,128,128]{2,1,0:T(8,128)(2,1)S(1)} %get-tuple-element.101), channel_id=1, source_target_pairs={{0,14},{2,12},{4,10},{6,8},{8,6},{10,4},{12,2},{14,0},{1,15},{3,13... | collective-permute-start | bytes 589832 | tf_op jit(solution)/shard_map/ppermute | solution.py:209
  (13 other events, 114.4 us)

commit v13 on v12

--- a/solution.py
+++ b/solution.py
@@ -341,7 +341,9 @@
         return flip(after(sends[n // 2 + i], *ready), n // 2 + i)
 
     whole = flip(sends[n], n // 2)
-    near = [sends[0]] + [flip(sends[d], d) for d in range(1, n // 2)]
+    near = [sends[0], flip(sends[1], 1), flip(sends[2], 2)]
+    for d in range(3, n // 2):
+        near.append(flip(after(sends[d], near[d - 1]), d))
     far = [direct(0), direct(1, near[1]), direct(2, near[2])]
     passed = call(
         functools.partial(pass_on_kernel, n, cap),
@@ -350,7 +352,7 @@
         [whole],
         [jax.ShapeDtypeStruct((2 * cap, half, part), bf16)] * (n // 2),
         [in_vmem] * (n // 2),
-        near[1:],
+        near[1:3],
     )
     passed = [passed[0]] + [flip(passed[d], d) for d in range(1, n // 2)]
     for i in range(3, n // 2):

time: 174 us -> 171 us (0.983)
  waiting for transfers between devices: 93.5 us -> 90.5 us
    ppermute x23, waiting for transfers between devices: 73.5 us -> 70.5 us  [flip(): return lax.ppermute(x, 'pair', [(s, s ^ bit) for s in range(n)])]
  transfers between devices with their start and end apart: 32 -> 32, of which waited for: 20 -> 19; matrix products, arithmetic and copies ran while one was open for 1% -> 1% of each run, Pallas kernels for 3% -> 3%
where the time goes in v13:
time: 171 us; the launch traced here: 170 us
  waiting for transfers between devices  90.5 us (53%)
  starting transfers between devices  49.9 us (29%)
  Pallas kernels  18 us (11%)
  local copies, waits for them, and re-layouts  6.81 us (4%)
  other arithmetic  3.66 us (2%)
    ppermute x23, waiting for transfers between devices, flip(): return lax.ppermute(x, 'pair', [(s, s ^ bit) for s in range(n)])  70.5 us
    ppermute x23, starting transfers between devices, flip(): return lax.ppermute(x, 'pair', [(s, s ^ bit) for s in range(n)])  33.3 us
    ppermute x7, waiting for transfers between devices, shift(): return lax.ppermute(x, 'pair', [(s, (s + d) % n) for s in range(n)])  18.1 us
    ppermute x7, starting transfers between devices, shift(): return lax.ppermute(x, 'pair', [(s, (s + d) % n) for s in range(n)])  16.5 us
    pallas_call x7, Pallas kernels, call(): pl.pallas_call(kernel, out_shape=out_shape, grid_spec=pltpu.PrefetchScala...  16 us
    unnamed x10, local copies, waits for them, and re-layouts  6.69 us
  transfers between devices with their start and end apart: 32, of which 19 were waited for; matrix products, arithmetic and copies ran while one was open for 1% of the time, Pallas kernels for 3%

profile of v13, /device:TPU:0, one launch (start us, length us, event | category | flops | bytes accessed | tf_op | source)
XLA Modules:
  0.0 169.9 jit_solution(11244978623364997379)
XLA Ops:
  5.1 4.1 %collective-permute-start = (bf16[3,128,256]{2,1,0:T(8,128)(2,1)S(1)}, bf16[3,128,256]{2,1,0:T(8,128)(2,1)S(1)}, u32[]{:S(2)}, u32[]{:S(2)}) collective-permute-start(bf16[3,128,256]{2,1,0:T(8,128)(2,1)S(1)} %get-tuple-element.53), channel_id=1, source_target_pairs={{0,8},{2,10},{4,12},{6,14},{8,0},{10,2},{12,4},{14,6},{1,9},{3,11}... | collective-permute-start | bytes 589832 | tf_op jit(solution)/shard_map/ppermute | solution.py:206
  16.8 15.0 %collective-permute-done.ready.rest_0_ = bf16[3,128,256]{2,1,0:T(8,128)(2,1)S(1)} collective-permute-done((bf16[3,128,256]{2,1,0:T(8,128)(2,1)S(1)}, bf16[3,128,256]{2,1,0:T(8,128)(2,1)S(1)}, u32[]{:S(2)}, u32[]{:S(2)}) %collective-permute-start) | collective-permute-done | bytes 196640 | tf_op jit(solution)/shard_map/ppermute | solution.py:206
  31.8 5.2 %copy-done = bf16[14,256,2048]{2,1,0:T(8,128)(2,1)S(1)} copy-done((bf16[14,256,2048]{2,1,0:T(8,128)(2,1)S(1)}, bf16[14,256,2048]{2,1,0:T(8,128)(2,1)}, u32[]{:S(2)}) %copy-start) | copy-done | bytes 14680088
  38.0 4.8 %collective-permute-start.6 = (bf16[3,128,256]{2,1,0:T(8,128)(2,1)S(1)}, bf16[3,128,256]{2,1,0:T(8,128)(2,1)S(1)}, u32[]{:S(2)}, u32[]{:S(2)}) collective-permute-start(bf16[3,128,256]{2,1,0:T(8,128)(2,1)S(1)} %get-tuple-element.60), channel_id=1, source_target_pairs={{0,14},{2,0},{4,2},{6,4},{8,6},{10,8},{12,10},{14,12},{1,15},{3,1}... | collective-permute-start | bytes 589832 | tf_op jit(solution)/shard_map/ppermute | solution.py:206
  42.9 3.1 %collective-permute-done.6.rest_6_ = bf16[3,128,256]{2,1,0:T(8,128)(2,1)S(1)} collective-permute-done((bf16[3,128,256]{2,1,0:T(8,128)(2,1)S(1)}, bf16[3,128,256]{2,1,0:T(8,128)(2,1)S(1)}, u32[]{:S(2)}, u32[]{:S(2)}) %collective-permute-start.6) | collective-permute-done | bytes 196640 | tf_op jit(solution)/shard_map/ppermute | solution.py:206
  46.9 2.8 %fit.2 = (f32[4,128,256]{2,1,0:T(8,128)S(1)}, bf16[4,128,256]{2,1,0:T(8,128)(2,1)S(1)}) custom-call(s32[8]{0:T(128)S(1)} %iota_xor_fusion.table, bf16[14,1,256]{2,1,0:T(2,128)(2,1)S(1)} %copy.11.factor, bf16[14,128,256]{2,1,0:T(8,128)(2,1)S(1)} %gather_density.1.density, bf16[14,256,2048]{2,1,0:T(8,128)(2,1)S(1)} %load_integrals.1.integrals), custom_call_target="tpu_custom_call" | custom-call | tf_op jit(solution)/shard_map/fit/pallas_call | solution.py:191
  49.7 2.7 %fit.3 = (f32[4,128,256]{2,1,0:T(8,128)S(1)}, bf16[4,128,256]{2,1,0:T(8,128)(2,1)S(1)}) custom-call(s32[8]{0:T(128)S(1)} %iota_xor_fusion.table, bf16[14,1,256]{2,1,0:T(2,128)(2,1)S(1)} %copy.11.factor, bf16[14,128,256]{2,1,0:T(8,128)(2,1)S(1)} %collective-permute-done.7.density, bf16[14,256,2048]{2,1,0:T(8,128)(2,1)S(1)} %load_integrals.1.integrals, ...), custom_call_target="tpu_custom_call" | custom-call | tf_op jit(solution)/shard_map/fit/pallas_call | solution.py:191
  52.9 8.3 %collective-permute-done.8 = bf16[4,128,256]{2,1,0:T(8,128)(2,1)S(1)} collective-permute-done((bf16[4,128,256]{2,1,0:T(8,128)(2,1)S(1)}, bf16[4,128,256]{2,1,0:T(8,128)(2,1)S(1)}, u32[]{:S(2)}, u32[]{:S(2)}) %collective-permute-start.8) | collective-permute-done | bytes 262176 | tf_op jit(solution)/shard_map/ppermute | solution.py:209
  63.5 3.2 %collective-permute-done.10 = bf16[2,128,256]{2,1,0:T(8,128)(2,1)S(1)} collective-permute-done((bf16[2,128,256]{2,1,0:T(8,128)(2,1)S(1)}, bf16[2,128,256]{2,1,0:T(8,128)(2,1)S(1)}, u32[]{:S(2)}, u32[]{:S(2)}) %collective-permute-start.10) | collective-permute-done | bytes 131104 | tf_op jit(solution)/shard_map/ppermute | solution.py:209
  66.8 5.8 %collective-permute-start.12 = (bf16[1,128,256]{2,1,0:T(8,128)(2,1)S(1)}, bf16[1,128,256]{2,1,0:T(8,128)(2,1)S(1)}, u32[]{:S(2)}, u32[]{:S(2)}) collective-permute-start(bf16[1,128,256]{2,1,0:T(8,128)(2,1)S(1)} %slice.57), channel_id=1, source_target_pairs={{0,8},{2,10},{4,12},{6,14},{8,0},{10,2},{12,4},{14,6},{1,9},{3,11}... | collective-permute-start | bytes 196616 | tf_op jit(solution)/shard_map/ppermute | solution.py:209
  72.7 4.1 %collective-permute-done.12 = bf16[1,128,256]{2,1,0:T(8,128)(2,1)S(1)} collective-permute-done((bf16[1,128,256]{2,1,0:T(8,128)(2,1)S(1)}, bf16[1,128,256]{2,1,0:T(8,128)(2,1)S(1)}, u32[]{:S(2)}, u32[]{:S(2)}) %collective-permute-start.12) | collective-permute-done | bytes 65568 | tf_op jit(solution)/shard_map/ppermute | solution.py:209
  78.7 2.7 %collective-permute-start.15 = (bf16[1,128,256]{2,1,0:T(8,128)(2,1)S(1)}, bf16[1,128,256]{2,1,0:T(8,128)(2,1)S(1)}, u32[]{:S(2)}, u32[]{:S(2)}) collective-permute-start(bf16[1,128,256]{2,1,0:T(8,128)(2,1)S(1)} %add_convert_fusion), channel_id=1, source_target_pairs={{0,8},{2,10},{4,12},{6,14},{8,0},{10,2},{12,4},{14,6},{1,9},{3,11}... | collective-permute-start | bytes 196616 | tf_op jit(solution)/shard_map/ppermute | solution.py:209
  86.5 3.3 %collective-permute-done.16 = bf16[2,128,256]{2,1,0:T(8,128)(2,1)S(1)} collective-permute-done((bf16[2,128,256]{2,1,0:T(8,128)(2,1)S(1)}, bf16[2,128,256]{2,1,0:T(8,128)(2,1)S(1)}, u32[]{:S(2)}, u32[]{:S(2)}) %collective-permute-start.16) | collective-permute-done | bytes 131104 | tf_op jit(solution)/shard_map/ppermute | solution.py:209
  93.5 3.0 %collective-permute-done.18.far = bf16[4,128,256]{2,1,0:T(8,128)(2,1)S(1)} collective-permute-done((bf16[4,128,256]{2,1,0:T(8,128)(2,1)S(1)}, bf16[4,128,256]{2,1,0:T(8,128)(2,1)S(1)}, u32[]{:S(2)}, u32[]{:S(2)}) %collective-permute-start.18) | collective-permute-done | bytes 262176 | tf_op jit(solution)/shard_map/ppermute | solution.py:209
  98.3 5.0 %apply.1 = (f32[14,128,256]{2,1,0:T(8,128)S(1)}, bf16[14,128,256]{2,1,0:T(8,128)(2,1)S(1)}) custom-call(s32[8]{0:T(128)S(1)} %iota_xor_fusion.table, bf16[14,256,2048]{2,1,0:T(8,128)(2,1)S(1)} %load_integrals.1.integrals, bf16[4,128,256]{2,1,0:T(8,128)(2,1)S(1)} %pad_maximum_fusion.1.near, bf16[4,128,256]{2,1,0:T(8,128)(2,1)S(1)} %collective-permute-done.18.far, ...), custom_call_target="tpu_custom_call" | custom-call | tf_op jit(solution)/shard_map/apply/pallas_call | solution.py:191
  106.9 2.9 %collective-permute-start.24 = (bf16[14,128,128]{2,1,0:T(8,128)(2,1)S(1)}, bf16[14,128,128]{2,1,0:T(8,128)(2,1)S(1)}, u32[]{:S(2)}, u32[]{:S(2)}) collective-permute-start(bf16[14,128,128]{2,1,0:T(8,128)(2,1)S(1)} %get-tuple-element.92), channel_id=1, source_target_pairs={{0,8},{2,10},{4,12},{6,14},{8,0},{10,2},{12,4},{14,6},{1,9},{3,11}... | collective-permute-start | bytes 1376264 | tf_op jit(solution)/shard_map/ppermute | solution.py:209
  112.6 8.2 %collective-permute-done.21.rest_0_.rest_1_ = bf16[6,128,256]{2,1,0:T(8,128)(2,1)S(1)} collective-permute-done((bf16[6,128,256]{2,1,0:T(8,128)(2,1)S(1)}, bf16[6,128,256]{2,1,0:T(8,128)(2,1)S(1)}, u32[]{:S(2)}, u32[]{:S(2)}) %collective-permute-start.21) | collective-permute-done | bytes 393248 | tf_op jit(solution)/shard_map/ppermute | solution.py:209
  120.8 8.3 %collective-permute-done.22.rest_1_.rest_2_ = bf16[6,128,256]{2,1,0:T(8,128)(2,1)S(1)} collective-permute-done((bf16[6,128,256]{2,1,0:T(8,128)(2,1)S(1)}, bf16[6,128,256]{2,1,0:T(8,128)(2,1)S(1)}, u32[]{:S(2)}, u32[]{:S(2)}) %collective-permute-start.22) | collective-permute-done | bytes 393248 | tf_op jit(solution)/shard_map/ppermute | solution.py:209
  131.2 8.2 %collective-permute-done.24.whole = bf16[14,128,128]{2,1,0:T(8,128)(2,1)S(1)} collective-permute-done((bf16[14,128,128]{2,1,0:T(8,128)(2,1)S(1)}, bf16[14,128,128]{2,1,0:T(8,128)(2,1)S(1)}, u32[]{:S(2)}, u32[]{:S(2)}) %collective-permute-start.24) | collective-permute-done | bytes 458784 | tf_op jit(solution)/shard_map/ppermute | solution.py:209
  140.6 2.8 %collective-permute-start.30 = (bf16[6,128,128]{2,1,0:T(8,128)(2,1)S(1)}, bf16[6,128,128]{2,1,0:T(8,128)(2,1)S(1)}, u32[]{:S(2)}, u32[]{:S(2)}) collective-permute-start(bf16[6,128,128]{2,1,0:T(8,128)(2,1)S(1)} %get-tuple-element.101), channel_id=1, source_target_pairs={{0,12},{2,14},{4,8},{6,10},{8,4},{10,6},{12,0},{14,2},{1,13},{3,15... | collective-permute-start | bytes 589832 | tf_op jit(solution)/shard_map/ppermute | solution.py:209
  143.4 6.5 %collective-permute-done.25.rest_5_ = bf16[6,128,128]{2,1,0:T(8,128)(2,1)S(1)} collective-permute-done((bf16[6,128,128]{2,1,0:T(8,128)(2,1)S(1)}, bf16[6,128,128]{2,1,0:T(8,128)(2,1)S(1)}, u32[]{:S(2)}, u32[]{:S(2)}) %collective-permute-start.25) | collective-permute-done | bytes 196640 | tf_op jit(solution)/shard_map/ppermute | solution.py:209
  153.2 2.9 %collective-permute-start.31 = (bf16[6,128,128]{2,1,0:T(8,128)(2,1)S(1)}, bf16[6,128,128]{2,1,0:T(8,128)(2,1)S(1)}, u32[]{:S(2)}, u32[]{:S(2)}) collective-permute-start(bf16[6,128,128]{2,1,0:T(8,128)(2,1)S(1)} %get-tuple-element.103), channel_id=1, source_target_pairs={{0,14},{2,12},{4,10},{6,8},{8,6},{10,4},{12,2},{14,0},{1,15},{3,13... | collective-permute-start | bytes 589832 | tf_op jit(solution)/shard_map/ppermute | solution.py:209
  157.6 9.1 %collective-permute-done.27.rest_7_ = bf16[6,128,128]{2,1,0:T(8,128)(2,1)S(1)} collective-permute-done((bf16[6,128,128]{2,1,0:T(8,128)(2,1)S(1)}, bf16[6,128,128]{2,1,0:T(8,128)(2,1)S(1)}, u32[]{:S(2)}, u32[]{:S(2)}) %collective-permute-start.27) | collective-permute-done | bytes 196640 | tf_op jit(solution)/shard_map/ppermute | solution.py:209
  166.8 3.1 %gather_coulomb.1 = (bf16[14,256,128]{2,1,0:T(8,128)(2,1)}, bf16[14,256,128]{2,1,0:T(8,128)(2,1)}) custom-call(s32[48]{0:T(128)S(1)} %pad_add_fusion.1.table, bf16[6,128,256]{2,1,0:T(8,128)(2,1)S(1)} %get-tuple-element.87.rest_0_, bf16[6,128,256]{2,1,0:T(8,128)(2,1)S(1)} %collective-permute-done.21.rest_0_.rest_1_, ...), custom_call_target="tpu_custom_call" | custom-call | tf_op jit(solution)/shard_map/gather_coulomb/pallas_call | solution.py:191
  (106 shorter events, 43.8 us)
Async XLA Ops:
  5.1 26.7 %collective-permute-start = (bf16[3,128,256]{2,1,0:T(8,128)(2,1)S(1)}, bf16[3,128,256]{2,1,0:T(8,128)(2,1)S(1)}, u32[]{:S(2)}, u32[]{:S(2)}) collective-permute-start(bf16[3,128,256]{2,1,0:T(8,128)(2,1)S(1)} %get-tuple-element.53), channel_id=1, source_target_pairs={{0,8},{2,10},{4,12},{6,14},{8,0},{10,2},{12,4},{14,6},{1,9},{3,11}... | collective-permute-start | bytes 589832 | tf_op jit(solution)/shard_map/ppermute | solution.py:206
  9.2 28.8 %collective-permute-start.1 = (bf16[3,128,256]{2,1,0:T(8,128)(2,1)S(1)}, bf16[3,128,256]{2,1,0:T(8,128)(2,1)S(1)}, u32[]{:S(2)}, u32[]{:S(2)}) collective-permute-start(bf16[3,128,256]{2,1,0:T(8,128)(2,1)S(1)} %get-tuple-element.54), channel_id=1, source_target_pairs={{0,6},{2,8},{4,10},{6,12},{8,14},{10,0},{12,2},{14,4},{1,7},{3,9},... | collective-permute-start | bytes 589832 | tf_op jit(solution)/shard_map/ppermute | solution.py:206
  11.7 31.1 %collective-permute-start.2 = (bf16[3,128,256]{2,1,0:T(8,128)(2,1)S(1)}, bf16[3,128,256]{2,1,0:T(8,128)(2,1)S(1)}, u32[]{:S(2)}, u32[]{:S(2)}) collective-permute-start(bf16[3,128,256]{2,1,0:T(8,128)(2,1)S(1)} %get-tuple-element.55), channel_id=1, source_target_pairs={{0,10},{2,12},{4,14},{6,0},{8,2},{10,4},{12,6},{14,8},{1,11},{3,13... | collective-permute-start | bytes 589832 | tf_op jit(solution)/shard_map/ppermute | solution.py:206
  13.0 29.9 %collective-permute-start.3 = (bf16[3,128,256]{2,1,0:T(8,128)(2,1)S(1)}, bf16[3,128,256]{2,1,0:T(8,128)(2,1)S(1)}, u32[]{:S(2)}, u32[]{:S(2)}) collective-permute-start(bf16[3,128,256]{2,1,0:T(8,128)(2,1)S(1)} %get-tuple-element.56), channel_id=1, source_target_pairs={{0,4},{2,6},{4,8},{6,10},{8,12},{10,14},{12,0},{14,2},{1,5},{3,7},... | collective-permute-start | bytes 589832 | tf_op jit(solution)/shard_map/ppermute | solution.py:206
  14.6 28.3 %collective-permute-start.4 = (bf16[3,128,256]{2,1,0:T(8,128)(2,1)S(1)}, bf16[3,128,256]{2,1,0:T(8,128)(2,1)S(1)}, u32[]{:S(2)}, u32[]{:S(2)}) collective-permute-start(bf16[3,128,256]{2,1,0:T(8,128)(2,1)S(1)} %get-tuple-element.57), channel_id=1, source_target_pairs={{0,12},{2,14},{4,0},{6,2},{8,4},{10,6},{12,8},{14,10},{1,13},{3,15... | collective-permute-start | bytes 589832 | tf_op jit(solution)/shard_map/ppermute | solution.py:206
  31.8 11.1 %collective-permute-start.5 = (bf16[3,128,256]{2,1,0:T(8,128)(2,1)S(1)}, bf16[3,128,256]{2,1,0:T(8,128)(2,1)S(1)}, u32[]{:S(2)}, u32[]{:S(2)}) collective-permute-start(bf16[3,128,256]{2,1,0:T(8,128)(2,1)S(1)} %get-tuple-element.58), channel_id=1, source_target_pairs={{0,2},{2,4},{4,6},{6,8},{8,10},{10,12},{12,14},{14,0},{1,3},{3,5},... | collective-permute-start | bytes 589832 | tf_op jit(solution)/shard_map/ppermute | solution.py:206
  38.0 8.0 %collective-permute-start.6 = (bf16[3,128,256]{2,1,0:T(8,128)(2,1)S(1)}, bf16[3,128,256]{2,1,0:T(8,128)(2,1)S(1)}, u32[]{:S(2)}, u32[]{:S(2)}) collective-permute-start(bf16[3,128,256]{2,1,0:T(8,128)(2,1)S(1)} %get-tuple-element.60), channel_id=1, source_target_pairs={{0,14},{2,0},{4,2},{6,4},{8,6},{10,8},{12,10},{14,12},{1,15},{3,1}... | collective-permute-start | bytes 589832 | tf_op jit(solution)/shard_map/ppermute | solution.py:206
  52.5 8.8 %collective-permute-start.8 = (bf16[4,128,256]{2,1,0:T(8,128)(2,1)S(1)}, bf16[4,128,256]{2,1,0:T(8,128)(2,1)S(1)}, u32[]{:S(2)}, u32[]{:S(2)}) collective-permute-start(bf16[4,128,256]{2,1,0:T(8,128)(2,1)S(1)} %get-tuple-element.68), channel_id=1, source_target_pairs={{0,4},{2,6},{4,0},{6,2},{8,12},{10,14},{12,8},{14,10},{1,5},{3,7},... | collective-permute-start | bytes 786440 | tf_op jit(solution)/shard_map/ppermute | solution.py:209
  52.6 8.8 %collective-permute-start.9 = (bf16[4,128,256]{2,1,0:T(8,128)(2,1)S(1)}, bf16[4,128,256]{2,1,0:T(8,128)(2,1)S(1)}, u32[]{:S(2)}, u32[]{:S(2)}) collective-permute-start(bf16[4,128,256]{2,1,0:T(8,128)(2,1)S(1)} %get-tuple-element.70), channel_id=1, source_target_pairs={{0,2},{2,0},{4,6},{6,4},{8,10},{10,8},{12,14},{14,12},{1,3},{3,1},... | collective-permute-start | bytes 786440 | tf_op jit(solution)/shard_map/ppermute | solution.py:209
  66.8 10.0 %collective-permute-start.12 = (bf16[1,128,256]{2,1,0:T(8,128)(2,1)S(1)}, bf16[1,128,256]{2,1,0:T(8,128)(2,1)S(1)}, u32[]{:S(2)}, u32[]{:S(2)}) collective-permute-start(bf16[1,128,256]{2,1,0:T(8,128)(2,1)S(1)} %slice.57), channel_id=1, source_target_pairs={{0,8},{2,10},{4,12},{6,14},{8,0},{10,2},{12,4},{14,6},{1,9},{3,11}... | collective-permute-start | bytes 196616 | tf_op jit(solution)/shard_map/ppermute | solution.py:209
  78.7 6.1 %collective-permute-start.15 = (bf16[1,128,256]{2,1,0:T(8,128)(2,1)S(1)}, bf16[1,128,256]{2,1,0:T(8,128)(2,1)S(1)}, u32[]{:S(2)}, u32[]{:S(2)}) collective-permute-start(bf16[1,128,256]{2,1,0:T(8,128)(2,1)S(1)} %add_convert_fusion), channel_id=1, source_target_pairs={{0,8},{2,10},{4,12},{6,14},{8,0},{10,2},{12,4},{14,6},{1,9},{3,11}... | collective-permute-start | bytes 196616 | tf_op jit(solution)/shard_map/ppermute | solution.py:209
  90.1 6.4 %collective-permute-start.18 = (bf16[4,128,256]{2,1,0:T(8,128)(2,1)S(1)}, bf16[4,128,256]{2,1,0:T(8,128)(2,1)S(1)}, u32[]{:S(2)}, u32[]{:S(2)}) collective-permute-start(bf16[4,128,256]{2,1,0:T(8,128)(2,1)S(1)} %pad_maximum_fusion.1.near), channel_id=1, source_target_pairs={{0,2},{2,0},{4,6},{6,4},{8,10},{10,8},{12,14},{14,12},{1,3},{3,1},... | collective-permute-start | bytes 786440 | tf_op jit(solution)/shard_map/ppermute | solution.py:209
  92.0 6.4 %collective-permute-start.19 = (bf16[4,128,256]{2,1,0:T(8,128)(2,1)S(1)}, bf16[4,128,256]{2,1,0:T(8,128)(2,1)S(1)}, u32[]{:S(2)}, u32[]{:S(2)}) collective-permute-start(bf16[4,128,256]{2,1,0:T(8,128)(2,1)S(1)} %pad_maximum_fusion.near_other), channel_id=1, source_target_pairs={{0,4},{2,6},{4,0},{6,2},{8,12},{10,14},{12,8},{14,10},{1,5},{3,7},... | collective-permute-start | bytes 786440 | tf_op jit(solution)/shard_map/ppermute | solution.py:209
  106.9 32.5 %collective-permute-start.24 = (bf16[14,128,128]{2,1,0:T(8,128)(2,1)S(1)}, bf16[14,128,128]{2,1,0:T(8,128)(2,1)S(1)}, u32[]{:S(2)}, u32[]{:S(2)}) collective-permute-start(bf16[14,128,128]{2,1,0:T(8,128)(2,1)S(1)} %get-tuple-element.92), channel_id=1, source_target_pairs={{0,8},{2,10},{4,12},{6,14},{8,0},{10,2},{12,4},{14,6},{1,9},{3,11}... | collective-permute-start | bytes 1376264 | tf_op jit(solution)/shard_map/ppermute | solution.py:209
  109.9 10.9 %collective-permute-start.21 = (bf16[6,128,256]{2,1,0:T(8,128)(2,1)S(1)}, bf16[6,128,256]{2,1,0:T(8,128)(2,1)S(1)}, u32[]{:S(2)}, u32[]{:S(2)}) collective-permute-start(bf16[6,128,256]{2,1,0:T(8,128)(2,1)S(1)} %get-tuple-element.88), channel_id=1, source_target_pairs={{0,2},{2,0},{4,6},{6,4},{8,10},{10,8},{12,14},{14,12},{1,3},{3,1},... | collective-permute-start | bytes 1179656 | tf_op jit(solution)/shard_map/ppermute | solution.py:209
  110.1 19.1 %collective-permute-start.22 = (bf16[6,128,256]{2,1,0:T(8,128)(2,1)S(1)}, bf16[6,128,256]{2,1,0:T(8,128)(2,1)S(1)}, u32[]{:S(2)}, u32[]{:S(2)}) collective-permute-start(bf16[6,128,256]{2,1,0:T(8,128)(2,1)S(1)} %get-tuple-element.89), channel_id=1, source_target_pairs={{0,4},{2,6},{4,0},{6,2},{8,12},{10,14},{12,8},{14,10},{1,5},{3,7},... | collective-permute-start | bytes 1179656 | tf_op jit(solution)/shard_map/ppermute | solution.py:209
  112.6 39.3 %collective-permute-start.28 = (bf16[6,128,128]{2,1,0:T(8,128)(2,1)S(1)}, bf16[6,128,128]{2,1,0:T(8,128)(2,1)S(1)}, u32[]{:S(2)}, u32[]{:S(2)}) collective-permute-start(bf16[6,128,128]{2,1,0:T(8,128)(2,1)S(1)} %get-tuple-element.97), channel_id=1, source_target_pairs={{0,8},{2,10},{4,12},{6,14},{8,0},{10,2},{12,4},{14,6},{1,9},{3,11}... | collective-permute-start | bytes 589832 | tf_op jit(solution)/shard_map/ppermute | solution.py:209
  120.8 32.4 %collective-permute-start.29 = (bf16[6,128,128]{2,1,0:T(8,128)(2,1)S(1)}, bf16[6,128,128]{2,1,0:T(8,128)(2,1)S(1)}, u32[]{:S(2)}, u32[]{:S(2)}) collective-permute-start(bf16[6,128,128]{2,1,0:T(8,128)(2,1)S(1)} %get-tuple-element.99), channel_id=1, source_target_pairs={{0,10},{2,8},{4,14},{6,12},{8,2},{10,0},{12,6},{14,4},{1,11},{3,9}... | collective-permute-start | bytes 589832 | tf_op jit(solution)/shard_map/ppermute | solution.py:209
  129.1 37.6 %collective-permute-start.23 = (bf16[6,128,256]{2,1,0:T(8,128)(2,1)S(1)}, bf16[6,128,256]{2,1,0:T(8,128)(2,1)S(1)}, u32[]{:S(2)}, u32[]{:S(2)}) collective-permute-start(bf16[6,128,256]{2,1,0:T(8,128)(2,1)S(1)} %get-tuple-element.91), channel_id=1, source_target_pairs={{0,6},{2,4},{4,2},{6,0},{8,14},{10,12},{12,10},{14,8},{1,7},{3,5},... | collective-permute-start | bytes 1179656 | tf_op jit(solution)/shard_map/ppermute | solution.py:209
  140.1 9.8 %collective-permute-start.25 = (bf16[6,128,128]{2,1,0:T(8,128)(2,1)S(1)}, bf16[6,128,128]{2,1,0:T(8,128)(2,1)S(1)}, u32[]{:S(2)}, u32[]{:S(2)}) collective-permute-start(bf16[6,128,128]{2,1,0:T(8,128)(2,1)S(1)} %get-tuple-element.94), channel_id=1, source_target_pairs={{0,2},{2,0},{4,6},{6,4},{8,10},{10,8},{12,14},{14,12},{1,3},{3,1},... | collective-permute-start | bytes 589832 | tf_op jit(solution)/shard_map/ppermute | solution.py:209
  140.6 15.7 %collective-permute-start.30 = (bf16[6,128,128]{2,1,0:T(8,128)(2,1)S(1)}, bf16[6,128,128]{2,1,0:T(8,128)(2,1)S(1)}, u32[]{:S(2)}, u32[]{:S(2)}) collective-permute-start(bf16[6,128,128]{2,1,0:T(8,128)(2,1)S(1)} %get-tuple-element.101), channel_id=1, source_target_pairs={{0,12},{2,14},{4,8},{6,10},{8,4},{10,6},{12,0},{14,2},{1,13},{3,15... | collective-permute-start | bytes 589832 | tf_op jit(solution)/shard_map/ppermute | solution.py:209
  149.9 7.7 %collective-permute-start.26 = (bf16[6,128,128]{2,1,0:T(8,128)(2,1)S(1)}, bf16[6,128,128]{2,1,0:T(8,128)(2,1)S(1)}, u32[]{:S(2)}, u32[]{:S(2)}) collective-permute-start(bf16[6,128,128]{2,1,0:T(8,128)(2,1)S(1)} %get-tuple-element.95), channel_id=1, source_target_pairs={{0,4},{2,6},{4,0},{6,2},{8,12},{10,14},{12,8},{14,10},{1,5},{3,7},... | collective-permute-start | bytes 589832 | tf_op jit(solution)/shard_map/ppermute | solution.py:209
  151.9 14.9 %collective-permute-start.27 = (bf16[6,128,128]{2,1,0:T(8,128)(2,1)S(1)}, bf16[6,128,128]{2,1,0:T(8,128)(2,1)S(1)}, u32[]{:S(2)}, u32[]{:S(2)}) collective-permute-start(bf16[6,128,128]{2,1,0:T(8,128)(2,1)S(1)} %get-tuple-element.96), channel_id=1, source_target_pairs={{0,6},{2,4},{4,2},{6,0},{8,14},{10,12},{12,10},{14,8},{1,7},{3,5},... | collective-permute-start | bytes 589832 | tf_op jit(solution)/shard_map/ppermute | solution.py:209
  153.2 13.5 %collective-permute-start.31 = (bf16[6,128,128]{2,1,0:T(8,128)(2,1)S(1)}, bf16[6,128,128]{2,1,0:T(8,128)(2,1)S(1)}, u32[]{:S(2)}, u32[]{:S(2)}) collective-permute-start(bf16[6,128,128]{2,1,0:T(8,128)(2,1)S(1)} %get-tuple-element.103), channel_id=1, source_target_pairs={{0,14},{2,12},{4,10},{6,8},{8,6},{10,4},{12,2},{14,0},{1,15},{3,13... | collective-permute-start | bytes 589832 | tf_op jit(solution)/shard_map/ppermute | solution.py:209
  (13 other events, 114.4 us)

commit v14 on v13

--- a/solution.py
+++ b/solution.py
@@ -290,18 +290,24 @@
         return jax.tree.unflatten(tree, lax.optimization_barrier(flat))
 
     def totals(states):
-        for j in range(len(bits)):
+        last = len(bits) - 1
+        for j in range(last):
             states = step_together(states)
             found = []
             for (keep, send), order in zip(states, orders):
                 value = keep + flip(send, order[j]).astype(f32)
-                if j < len(bits) - 1:
+                if j < last - 1:
                     found.append((value[0::2], value[1::2].astype(bf16)))
                 else:
-                    found.append(value.astype(bf16))
+                    found.append((value, value[::-1].astype(bf16)))
             states = found
-        relative = [[0] for _ in orders]
-        for j in reversed(range(len(bits))):
+        states = step_together(states)
+        states = [
+            (keep + flip(send, order[last]).astype(f32)).astype(bf16)
+            for (keep, send), order in zip(states, orders)
+        ]
+        relative = [[0, order[last]] for order in orders]
+        for j in reversed(range(last)):
             states = step_together(states)
             fars = [flip(near, order[j]) for near, order in zip(states, orders)]
             relative = [r + [e ^ order[j] for e in r] for r, order in zip(relative, orders)]

time: 171 us -> 176 us (1.029)
  waiting for transfers between devices: 90.5 us -> 98.2 us
  starting transfers between devices: 49.9 us -> 42.6 us
  local copies, waits for them, and re-layouts: 6.81 us -> 12 us
    ppermute x23 -> x21, waiting for transfers between devices: 70.5 us -> 78.3 us  [flip(): return lax.ppermute(x, 'pair', [(s, s ^ bit) for s in range(n)])]
    ppermute x23 -> x21, starting transfers between devices: 33.3 us -> 26 us  [flip(): return lax.ppermute(x, 'pair', [(s, s ^ bit) for s in range(n)])]
    unnamed x10 -> x14, local copies, waits for them, and re-layouts: 6.69 us -> 11.9 us
  transfers between devices with their start and end apart: 32 -> 30, of which waited for: 19 -> 18; matrix products, arithmetic and copies ran while one was open for 1% -> 1% of each run, Pallas kernels for 3% -> 2%
where the time goes in v14:
time: 176 us; the launch traced here: 175 us
  waiting for transfers between devices  98.2 us (56%)
  starting transfers between devices  42.6 us (24%)
  Pallas kernels  18 us (10%)
  local copies, waits for them, and re-layouts  12 us (7%)
  other arithmetic  3.64 us (2%)
    ppermute x21, waiting for transfers between devices, flip(): return lax.ppermute(x, 'pair', [(s, s ^ bit) for s in range(n)])  78.3 us
    ppermute x21, starting transfers between devices, flip(): return lax.ppermute(x, 'pair', [(s, s ^ bit) for s in range(n)])  26 us
    ppermute x7, waiting for transfers between devices, shift(): return lax.ppermute(x, 'pair', [(s, (s + d) % n) for s in range(n)])  18.1 us
    ppermute x7, starting transfers between devices, shift(): return lax.ppermute(x, 'pair', [(s, (s + d) % n) for s in range(n)])  16.5 us
    pallas_call x7, Pallas kernels, call(): pl.pallas_call(kernel, out_shape=out_shape, grid_spec=pltpu.PrefetchScala...  16.1 us
    unnamed x14, local copies, waits for them, and re-layouts  11.9 us
  transfers between devices with their start and end apart: 30, of which 18 were waited for; matrix products, arithmetic and copies ran while one was open for 1% of the time, Pallas kernels for 2%

profile of v14, /device:TPU:0, one launch (start us, length us, event | category | flops | bytes accessed | tf_op | source)
XLA Modules:
  0.0 175.5 jit_solution(279643633595250593)
XLA Ops:
  5.1 4.1 %collective-permute-start = (bf16[3,128,256]{2,1,0:T(8,128)(2,1)S(1)}, bf16[3,128,256]{2,1,0:T(8,128)(2,1)S(1)}, u32[]{:S(2)}, u32[]{:S(2)}) collective-permute-start(bf16[3,128,256]{2,1,0:T(8,128)(2,1)S(1)} %get-tuple-element.51), channel_id=1, source_target_pairs={{0,8},{2,10},{4,12},{6,14},{8,0},{10,2},{12,4},{14,6},{1,9},{3,11}... | collective-permute-start | bytes 589832 | tf_op jit(solution)/shard_map/ppermute | solution.py:206
  16.8 15.0 %collective-permute-done.ready.rest_0_ = bf16[3,128,256]{2,1,0:T(8,128)(2,1)S(1)} collective-permute-done((bf16[3,128,256]{2,1,0:T(8,128)(2,1)S(1)}, bf16[3,128,256]{2,1,0:T(8,128)(2,1)S(1)}, u32[]{:S(2)}, u32[]{:S(2)}) %collective-permute-start) | collective-permute-done | bytes 196640 | tf_op jit(solution)/shard_map/ppermute | solution.py:206
  31.8 5.2 %copy-done.2 = bf16[14,256,2048]{2,1,0:T(8,128)(2,1)S(1)} copy-done((bf16[14,256,2048]{2,1,0:T(8,128)(2,1)S(1)}, bf16[14,256,2048]{2,1,0:T(8,128)(2,1)}, u32[]{:S(2)}) %copy-start.2) | copy-done | bytes 14680088
  38.0 4.8 %collective-permute-start.6 = (bf16[3,128,256]{2,1,0:T(8,128)(2,1)S(1)}, bf16[3,128,256]{2,1,0:T(8,128)(2,1)S(1)}, u32[]{:S(2)}, u32[]{:S(2)}) collective-permute-start(bf16[3,128,256]{2,1,0:T(8,128)(2,1)S(1)} %get-tuple-element.58), channel_id=1, source_target_pairs={{0,14},{2,0},{4,2},{6,4},{8,6},{10,8},{12,10},{14,12},{1,15},{3,1}... | collective-permute-start | bytes 589832 | tf_op jit(solution)/shard_map/ppermute | solution.py:206
  42.9 3.1 %collective-permute-done.6.rest_6_ = bf16[3,128,256]{2,1,0:T(8,128)(2,1)S(1)} collective-permute-done((bf16[3,128,256]{2,1,0:T(8,128)(2,1)S(1)}, bf16[3,128,256]{2,1,0:T(8,128)(2,1)S(1)}, u32[]{:S(2)}, u32[]{:S(2)}) %collective-permute-start.6) | collective-permute-done | bytes 196640 | tf_op jit(solution)/shard_map/ppermute | solution.py:206
  47.0 2.8 %fit.2 = (f32[4,128,256]{2,1,0:T(8,128)S(1)}, bf16[4,128,256]{2,1,0:T(8,128)(2,1)S(1)}) custom-call(s32[8]{0:T(128)S(1)} %iota_xor_fusion.table, bf16[14,1,256]{2,1,0:T(2,128)(2,1)S(1)} %copy.11.factor, bf16[14,128,256]{2,1,0:T(8,128)(2,1)S(1)} %gather_density.1.density, bf16[14,256,2048]{2,1,0:T(8,128)(2,1)S(1)} %load_integrals.1.integrals), custom_call_target="tpu_custom_call" | custom-call | tf_op jit(solution)/shard_map/fit/pallas_call | solution.py:191
  49.7 2.7 %fit.3 = (f32[4,128,256]{2,1,0:T(8,128)S(1)}, bf16[4,128,256]{2,1,0:T(8,128)(2,1)S(1)}) custom-call(s32[8]{0:T(128)S(1)} %iota_xor_fusion.table, bf16[14,1,256]{2,1,0:T(2,128)(2,1)S(1)} %copy.11.factor, bf16[14,128,256]{2,1,0:T(8,128)(2,1)S(1)} %collective-permute-done.7.density, bf16[14,256,2048]{2,1,0:T(8,128)(2,1)S(1)} %load_integrals.1.integrals, ...), custom_call_target="tpu_custom_call" | custom-call | tf_op jit(solution)/shard_map/fit/pallas_call | solution.py:191
  52.9 8.4 %collective-permute-done.8 = bf16[4,128,256]{2,1,0:T(8,128)(2,1)S(1)} collective-permute-done((bf16[4,128,256]{2,1,0:T(8,128)(2,1)S(1)}, bf16[4,128,256]{2,1,0:T(8,128)(2,1)S(1)}, u32[]{:S(2)}, u32[]{:S(2)}) %collective-permute-start.8) | collective-permute-done | bytes 262176 | tf_op jit(solution)/shard_map/ppermute | solution.py:209
  63.5 3.2 %collective-permute-done.10 = bf16[2,128,256]{2,1,0:T(8,128)(2,1)S(1)} collective-permute-done((bf16[2,128,256]{2,1,0:T(8,128)(2,1)S(1)}, bf16[2,128,256]{2,1,0:T(8,128)(2,1)S(1)}, u32[]{:S(2)}, u32[]{:S(2)}) %collective-permute-start.10) | collective-permute-done | bytes 131104 | tf_op jit(solution)/shard_map/ppermute | solution.py:209
  66.8 5.8 %collective-permute-start.12 = (bf16[2,128,256]{2,1,0:T(8,128)(2,1)S(1)}, bf16[2,128,256]{2,1,0:T(8,128)(2,1)S(1)}, u32[]{:S(2)}, u32[]{:S(2)}) collective-permute-start(bf16[2,128,256]{2,1,0:T(8,128)(2,1)S(1)} %rev.11), channel_id=1, source_target_pairs={{0,8},{2,10},{4,12},{6,14},{8,0},{10,2},{12,4},{14,6},{1,9},{3,11}... | collective-permute-start | bytes 393224 | tf_op jit(solution)/shard_map/ppermute | solution.py:209
  72.7 8.5 %collective-permute-done.12 = bf16[2,128,256]{2,1,0:T(8,128)(2,1)S(1)} collective-permute-done((bf16[2,128,256]{2,1,0:T(8,128)(2,1)S(1)}, bf16[2,128,256]{2,1,0:T(8,128)(2,1)S(1)}, u32[]{:S(2)}, u32[]{:S(2)}) %collective-permute-start.12) | collective-permute-done | bytes 131104 | tf_op jit(solution)/shard_map/ppermute | solution.py:209
  83.7 4.4 %collective-permute-done.14 = bf16[2,128,256]{2,1,0:T(8,128)(2,1)S(1)} collective-permute-done((bf16[2,128,256]{2,1,0:T(8,128)(2,1)S(1)}, bf16[2,128,256]{2,1,0:T(8,128)(2,1)S(1)}, u32[]{:S(2)}, u32[]{:S(2)}) %collective-permute-start.14) | collective-permute-done | bytes 131104 | tf_op jit(solution)/shard_map/ppermute | solution.py:209
  90.2 5.0 %collective-permute-done.16.far = bf16[4,128,256]{2,1,0:T(8,128)(2,1)S(1)} collective-permute-done((bf16[4,128,256]{2,1,0:T(8,128)(2,1)S(1)}, bf16[4,128,256]{2,1,0:T(8,128)(2,1)S(1)}, u32[]{:S(2)}, u32[]{:S(2)}) %collective-permute-start.16) | collective-permute-done | bytes 262176 | tf_op jit(solution)/shard_map/ppermute | solution.py:209
  96.5 5.2 %copy-done.1 = bf16[14,256,2048]{2,1,0:T(8,128)(2,1)S(1)} copy-done((bf16[14,256,2048]{2,1,0:T(8,128)(2,1)S(1)}, bf16[14,256,2048]{2,1,0:T(8,128)(2,1)}, u32[]{:S(2)}) %copy-start.1) | copy-done | bytes 14680088
  101.7 5.0 %apply.1 = (f32[14,128,256]{2,1,0:T(8,128)S(1)}, bf16[14,128,256]{2,1,0:T(8,128)(2,1)S(1)}) custom-call(s32[8]{0:T(128)S(1)} %iota_xor_fusion.table, bf16[14,256,2048]{2,1,0:T(8,128)(2,1)S(1)} %copy-done.1, bf16[4,128,256]{2,1,0:T(8,128)(2,1)S(1)} %pad_maximum_fusion.1.near, bf16[4,128,256]{2,1,0:T(8,128)(2,1)S(1)} %collective-permute-done.16.far, ...), custom_call_target="tpu_custom_call" | custom-call | tf_op jit(solution)/shard_map/apply/pallas_call | solution.py:191
  114.9 7.9 %collective-permute-done.19.rest_0_.rest_1_ = bf16[6,128,256]{2,1,0:T(8,128)(2,1)S(1)} collective-permute-done((bf16[6,128,256]{2,1,0:T(8,128)(2,1)S(1)}, bf16[6,128,256]{2,1,0:T(8,128)(2,1)S(1)}, u32[]{:S(2)}, u32[]{:S(2)}) %collective-permute-start.19) | collective-permute-done | bytes 393248 | tf_op jit(solution)/shard_map/ppermute | solution.py:209
  124.4 6.7 %collective-permute-done.20.rest_1_.rest_2_ = bf16[6,128,256]{2,1,0:T(8,128)(2,1)S(1)} collective-permute-done((bf16[6,128,256]{2,1,0:T(8,128)(2,1)S(1)}, bf16[6,128,256]{2,1,0:T(8,128)(2,1)S(1)}, u32[]{:S(2)}, u32[]{:S(2)}) %collective-permute-start.20) | collective-permute-done | bytes 393248 | tf_op jit(solution)/shard_map/ppermute | solution.py:209
  133.5 9.0 %collective-permute-done.22.whole = bf16[14,128,128]{2,1,0:T(8,128)(2,1)S(1)} collective-permute-done((bf16[14,128,128]{2,1,0:T(8,128)(2,1)S(1)}, bf16[14,128,128]{2,1,0:T(8,128)(2,1)S(1)}, u32[]{:S(2)}, u32[]{:S(2)}) %collective-permute-start.22) | collective-permute-done | bytes 458784 | tf_op jit(solution)/shard_map/ppermute | solution.py:209
  145.7 7.4 %collective-permute-done.23.rest_5_ = bf16[6,128,128]{2,1,0:T(8,128)(2,1)S(1)} collective-permute-done((bf16[6,128,128]{2,1,0:T(8,128)(2,1)S(1)}, bf16[6,128,128]{2,1,0:T(8,128)(2,1)S(1)}, u32[]{:S(2)}, u32[]{:S(2)}) %collective-permute-start.23) | collective-permute-done | bytes 196640 | tf_op jit(solution)/shard_map/ppermute | solution.py:209
  155.5 2.6 %collective-permute-start.29 = (bf16[6,128,128]{2,1,0:T(8,128)(2,1)S(1)}, bf16[6,128,128]{2,1,0:T(8,128)(2,1)S(1)}, u32[]{:S(2)}, u32[]{:S(2)}) collective-permute-start(bf16[6,128,128]{2,1,0:T(8,128)(2,1)S(1)} %get-tuple-element.99), channel_id=1, source_target_pairs={{0,14},{2,12},{4,10},{6,8},{8,6},{10,4},{12,2},{14,0},{1,15},{3,13... | collective-permute-start | bytes 589832 | tf_op jit(solution)/shard_map/ppermute | solution.py:209
  158.3 2.7 %collective-permute-done.24.rest_6_ = bf16[6,128,128]{2,1,0:T(8,128)(2,1)S(1)} collective-permute-done((bf16[6,128,128]{2,1,0:T(8,128)(2,1)S(1)}, bf16[6,128,128]{2,1,0:T(8,128)(2,1)S(1)}, u32[]{:S(2)}, u32[]{:S(2)}) %collective-permute-start.24) | collective-permute-done | bytes 196640 | tf_op jit(solution)/shard_map/ppermute | solution.py:209
  160.9 4.6 %collective-permute-done.25.rest_7_ = bf16[6,128,128]{2,1,0:T(8,128)(2,1)S(1)} collective-permute-done((bf16[6,128,128]{2,1,0:T(8,128)(2,1)S(1)}, bf16[6,128,128]{2,1,0:T(8,128)(2,1)S(1)}, u32[]{:S(2)}, u32[]{:S(2)}) %collective-permute-start.25) | collective-permute-done | bytes 196640 | tf_op jit(solution)/shard_map/ppermute | solution.py:209
  165.6 6.8 %collective-permute-done.29.rest_11_ = bf16[6,128,128]{2,1,0:T(8,128)(2,1)S(1)} collective-permute-done((bf16[6,128,128]{2,1,0:T(8,128)(2,1)S(1)}, bf16[6,128,128]{2,1,0:T(8,128)(2,1)S(1)}, u32[]{:S(2)}, u32[]{:S(2)}) %collective-permute-start.29) | collective-permute-done | bytes 196640 | tf_op jit(solution)/shard_map/ppermute | solution.py:209
  172.4 3.1 %gather_coulomb.1 = (bf16[14,256,128]{2,1,0:T(8,128)(2,1)}, bf16[14,256,128]{2,1,0:T(8,128)(2,1)}) custom-call(s32[48]{0:T(128)S(1)} %pad_add_fusion.1.table, bf16[6,128,256]{2,1,0:T(8,128)(2,1)S(1)} %get-tuple-element.83.rest_0_, bf16[6,128,256]{2,1,0:T(8,128)(2,1)S(1)} %collective-permute-done.19.rest_0_.rest_1_, ...), custom_call_target="tpu_custom_call" | custom-call | tf_op jit(solution)/shard_map/gather_coulomb/pallas_call | solution.py:191
  (102 shorter events, 40.6 us)
Async XLA Ops:
  5.1 26.7 %collective-permute-start = (bf16[3,128,256]{2,1,0:T(8,128)(2,1)S(1)}, bf16[3,128,256]{2,1,0:T(8,128)(2,1)S(1)}, u32[]{:S(2)}, u32[]{:S(2)}) collective-permute-start(bf16[3,128,256]{2,1,0:T(8,128)(2,1)S(1)} %get-tuple-element.51), channel_id=1, source_target_pairs={{0,8},{2,10},{4,12},{6,14},{8,0},{10,2},{12,4},{14,6},{1,9},{3,11}... | collective-permute-start | bytes 589832 | tf_op jit(solution)/shard_map/ppermute | solution.py:206
  9.2 28.8 %collective-permute-start.1 = (bf16[3,128,256]{2,1,0:T(8,128)(2,1)S(1)}, bf16[3,128,256]{2,1,0:T(8,128)(2,1)S(1)}, u32[]{:S(2)}, u32[]{:S(2)}) collective-permute-start(bf16[3,128,256]{2,1,0:T(8,128)(2,1)S(1)} %get-tuple-element.52), channel_id=1, source_target_pairs={{0,6},{2,8},{4,10},{6,12},{8,14},{10,0},{12,2},{14,4},{1,7},{3,9},... | collective-permute-start | bytes 589832 | tf_op jit(solution)/shard_map/ppermute | solution.py:206
  11.7 31.1 %collective-permute-start.2 = (bf16[3,128,256]{2,1,0:T(8,128)(2,1)S(1)}, bf16[3,128,256]{2,1,0:T(8,128)(2,1)S(1)}, u32[]{:S(2)}, u32[]{:S(2)}) collective-permute-start(bf16[3,128,256]{2,1,0:T(8,128)(2,1)S(1)} %get-tuple-element.53), channel_id=1, source_target_pairs={{0,10},{2,12},{4,14},{6,0},{8,2},{10,4},{12,6},{14,8},{1,11},{3,13... | collective-permute-start | bytes 589832 | tf_op jit(solution)/shard_map/ppermute | solution.py:206
  13.0 29.9 %collective-permute-start.3 = (bf16[3,128,256]{2,1,0:T(8,128)(2,1)S(1)}, bf16[3,128,256]{2,1,0:T(8,128)(2,1)S(1)}, u32[]{:S(2)}, u32[]{:S(2)}) collective-permute-start(bf16[3,128,256]{2,1,0:T(8,128)(2,1)S(1)} %get-tuple-element.54), channel_id=1, source_target_pairs={{0,4},{2,6},{4,8},{6,10},{8,12},{10,14},{12,0},{14,2},{1,5},{3,7},... | collective-permute-start | bytes 589832 | tf_op jit(solution)/shard_map/ppermute | solution.py:206
  14.6 28.3 %collective-permute-start.4 = (bf16[3,128,256]{2,1,0:T(8,128)(2,1)S(1)}, bf16[3,128,256]{2,1,0:T(8,128)(2,1)S(1)}, u32[]{:S(2)}, u32[]{:S(2)}) collective-permute-start(bf16[3,128,256]{2,1,0:T(8,128)(2,1)S(1)} %get-tuple-element.55), channel_id=1, source_target_pairs={{0,12},{2,14},{4,0},{6,2},{8,4},{10,6},{12,8},{14,10},{1,13},{3,15... | collective-permute-start | bytes 589832 | tf_op jit(solution)/shard_map/ppermute | solution.py:206
  31.8 11.1 %collective-permute-start.5 = (bf16[3,128,256]{2,1,0:T(8,128)(2,1)S(1)}, bf16[3,128,256]{2,1,0:T(8,128)(2,1)S(1)}, u32[]{:S(2)}, u32[]{:S(2)}) collective-permute-start(bf16[3,128,256]{2,1,0:T(8,128)(2,1)S(1)} %get-tuple-element.56), channel_id=1, source_target_pairs={{0,2},{2,4},{4,6},{6,8},{8,10},{10,12},{12,14},{14,0},{1,3},{3,5},... | collective-permute-start | bytes 589832 | tf_op jit(solution)/shard_map/ppermute | solution.py:206
  38.0 8.0 %collective-permute-start.6 = (bf16[3,128,256]{2,1,0:T(8,128)(2,1)S(1)}, bf16[3,128,256]{2,1,0:T(8,128)(2,1)S(1)}, u32[]{:S(2)}, u32[]{:S(2)}) collective-permute-start(bf16[3,128,256]{2,1,0:T(8,128)(2,1)S(1)} %get-tuple-element.58), channel_id=1, source_target_pairs={{0,14},{2,0},{4,2},{6,4},{8,6},{10,8},{12,10},{14,12},{1,15},{3,1}... | collective-permute-start | bytes 589832 | tf_op jit(solution)/shard_map/ppermute | solution.py:206
  52.5 8.8 %collective-permute-start.8 = (bf16[4,128,256]{2,1,0:T(8,128)(2,1)S(1)}, bf16[4,128,256]{2,1,0:T(8,128)(2,1)S(1)}, u32[]{:S(2)}, u32[]{:S(2)}) collective-permute-start(bf16[4,128,256]{2,1,0:T(8,128)(2,1)S(1)} %get-tuple-element.66), channel_id=1, source_target_pairs={{0,4},{2,6},{4,0},{6,2},{8,12},{10,14},{12,8},{14,10},{1,5},{3,7},... | collective-permute-start | bytes 786440 | tf_op jit(solution)/shard_map/ppermute | solution.py:209
  52.6 8.8 %collective-permute-start.9 = (bf16[4,128,256]{2,1,0:T(8,128)(2,1)S(1)}, bf16[4,128,256]{2,1,0:T(8,128)(2,1)S(1)}, u32[]{:S(2)}, u32[]{:S(2)}) collective-permute-start(bf16[4,128,256]{2,1,0:T(8,128)(2,1)S(1)} %get-tuple-element.68), channel_id=1, source_target_pairs={{0,2},{2,0},{4,6},{6,4},{8,10},{10,8},{12,14},{14,12},{1,3},{3,1},... | collective-permute-start | bytes 786440 | tf_op jit(solution)/shard_map/ppermute | solution.py:209
  66.8 14.4 %collective-permute-start.12 = (bf16[2,128,256]{2,1,0:T(8,128)(2,1)S(1)}, bf16[2,128,256]{2,1,0:T(8,128)(2,1)S(1)}, u32[]{:S(2)}, u32[]{:S(2)}) collective-permute-start(bf16[2,128,256]{2,1,0:T(8,128)(2,1)S(1)} %rev.11), channel_id=1, source_target_pairs={{0,8},{2,10},{4,12},{6,14},{8,0},{10,2},{12,4},{14,6},{1,9},{3,11}... | collective-permute-start | bytes 393224 | tf_op jit(solution)/shard_map/ppermute | solution.py:209
  72.6 10.3 %collective-permute-start.13 = (bf16[2,128,256]{2,1,0:T(8,128)(2,1)S(1)}, bf16[2,128,256]{2,1,0:T(8,128)(2,1)S(1)}, u32[]{:S(2)}, u32[]{:S(2)}) collective-permute-start(bf16[2,128,256]{2,1,0:T(8,128)(2,1)S(1)} %rev.10), channel_id=1, source_target_pairs={{0,8},{2,10},{4,12},{6,14},{8,0},{10,2},{12,4},{14,6},{1,9},{3,11}... | collective-permute-start | bytes 393224 | tf_op jit(solution)/shard_map/ppermute | solution.py:209
  88.7 6.5 %collective-permute-start.16 = (bf16[4,128,256]{2,1,0:T(8,128)(2,1)S(1)}, bf16[4,128,256]{2,1,0:T(8,128)(2,1)S(1)}, u32[]{:S(2)}, u32[]{:S(2)}) collective-permute-start(bf16[4,128,256]{2,1,0:T(8,128)(2,1)S(1)} %pad_maximum_fusion.1.near), channel_id=1, source_target_pairs={{0,2},{2,0},{4,6},{6,4},{8,10},{10,8},{12,14},{14,12},{1,3},{3,1},... | collective-permute-start | bytes 786440 | tf_op jit(solution)/shard_map/ppermute | solution.py:209
  90.2 6.4 %collective-permute-start.17 = (bf16[4,128,256]{2,1,0:T(8,128)(2,1)S(1)}, bf16[4,128,256]{2,1,0:T(8,128)(2,1)S(1)}, u32[]{:S(2)}, u32[]{:S(2)}) collective-permute-start(bf16[4,128,256]{2,1,0:T(8,128)(2,1)S(1)} %pad_maximum_fusion.near_other), channel_id=1, source_target_pairs={{0,4},{2,6},{4,0},{6,2},{8,12},{10,14},{12,8},{14,10},{1,5},{3,7},... | collective-permute-start | bytes 786440 | tf_op jit(solution)/shard_map/ppermute | solution.py:209
  110.4 32.1 %collective-permute-start.22 = (bf16[14,128,128]{2,1,0:T(8,128)(2,1)S(1)}, bf16[14,128,128]{2,1,0:T(8,128)(2,1)S(1)}, u32[]{:S(2)}, u32[]{:S(2)}) collective-permute-start(bf16[14,128,128]{2,1,0:T(8,128)(2,1)S(1)} %get-tuple-element.88), channel_id=1, source_target_pairs={{0,8},{2,10},{4,12},{6,14},{8,0},{10,2},{12,4},{14,6},{1,9},{3,11}... | collective-permute-start | bytes 1376264 | tf_op jit(solution)/shard_map/ppermute | solution.py:209
  111.9 10.9 %collective-permute-start.19 = (bf16[6,128,256]{2,1,0:T(8,128)(2,1)S(1)}, bf16[6,128,256]{2,1,0:T(8,128)(2,1)S(1)}, u32[]{:S(2)}, u32[]{:S(2)}) collective-permute-start(bf16[6,128,256]{2,1,0:T(8,128)(2,1)S(1)} %get-tuple-element.84), channel_id=1, source_target_pairs={{0,2},{2,0},{4,6},{6,4},{8,10},{10,8},{12,14},{14,12},{1,3},{3,1},... | collective-permute-start | bytes 1179656 | tf_op jit(solution)/shard_map/ppermute | solution.py:209
  112.4 18.7 %collective-permute-start.20 = (bf16[6,128,256]{2,1,0:T(8,128)(2,1)S(1)}, bf16[6,128,256]{2,1,0:T(8,128)(2,1)S(1)}, u32[]{:S(2)}, u32[]{:S(2)}) collective-permute-start(bf16[6,128,256]{2,1,0:T(8,128)(2,1)S(1)} %get-tuple-element.85), channel_id=1, source_target_pairs={{0,4},{2,6},{4,0},{6,2},{8,12},{10,14},{12,8},{14,10},{1,5},{3,7},... | collective-permute-start | bytes 1179656 | tf_op jit(solution)/shard_map/ppermute | solution.py:209
  114.8 39.3 %collective-permute-start.26 = (bf16[6,128,128]{2,1,0:T(8,128)(2,1)S(1)}, bf16[6,128,128]{2,1,0:T(8,128)(2,1)S(1)}, u32[]{:S(2)}, u32[]{:S(2)}) collective-permute-start(bf16[6,128,128]{2,1,0:T(8,128)(2,1)S(1)} %get-tuple-element.93), channel_id=1, source_target_pairs={{0,8},{2,10},{4,12},{6,14},{8,0},{10,2},{12,4},{14,6},{1,9},{3,11}... | collective-permute-start | bytes 589832 | tf_op jit(solution)/shard_map/ppermute | solution.py:209
  122.8 32.7 %collective-permute-start.27 = (bf16[6,128,128]{2,1,0:T(8,128)(2,1)S(1)}, bf16[6,128,128]{2,1,0:T(8,128)(2,1)S(1)}, u32[]{:S(2)}, u32[]{:S(2)}) collective-permute-start(bf16[6,128,128]{2,1,0:T(8,128)(2,1)S(1)} %get-tuple-element.95), channel_id=1, source_target_pairs={{0,10},{2,8},{4,14},{6,12},{8,2},{10,0},{12,6},{14,4},{1,11},{3,9}... | collective-permute-start | bytes 589832 | tf_op jit(solution)/shard_map/ppermute | solution.py:209
  131.1 34.5 %collective-permute-start.21 = (bf16[6,128,256]{2,1,0:T(8,128)(2,1)S(1)}, bf16[6,128,256]{2,1,0:T(8,128)(2,1)S(1)}, u32[]{:S(2)}, u32[]{:S(2)}) collective-permute-start(bf16[6,128,256]{2,1,0:T(8,128)(2,1)S(1)} %get-tuple-element.87), channel_id=1, source_target_pairs={{0,6},{2,4},{4,2},{6,0},{8,14},{10,12},{12,10},{14,8},{1,7},{3,5},... | collective-permute-start | bytes 1179656 | tf_op jit(solution)/shard_map/ppermute | solution.py:209
  143.1 10.0 %collective-permute-start.23 = (bf16[6,128,128]{2,1,0:T(8,128)(2,1)S(1)}, bf16[6,128,128]{2,1,0:T(8,128)(2,1)S(1)}, u32[]{:S(2)}, u32[]{:S(2)}) collective-permute-start(bf16[6,128,128]{2,1,0:T(8,128)(2,1)S(1)} %get-tuple-element.90), channel_id=1, source_target_pairs={{0,2},{2,0},{4,6},{6,4},{8,10},{10,8},{12,14},{14,12},{1,3},{3,1},... | collective-permute-start | bytes 589832 | tf_op jit(solution)/shard_map/ppermute | solution.py:209
  143.6 14.6 %collective-permute-start.28 = (bf16[6,128,128]{2,1,0:T(8,128)(2,1)S(1)}, bf16[6,128,128]{2,1,0:T(8,128)(2,1)S(1)}, u32[]{:S(2)}, u32[]{:S(2)}) collective-permute-start(bf16[6,128,128]{2,1,0:T(8,128)(2,1)S(1)} %get-tuple-element.97), channel_id=1, source_target_pairs={{0,12},{2,14},{4,8},{6,10},{8,4},{10,6},{12,0},{14,2},{1,13},{3,15... | collective-permute-start | bytes 589832 | tf_op jit(solution)/shard_map/ppermute | solution.py:209
  153.1 7.8 %collective-permute-start.24 = (bf16[6,128,128]{2,1,0:T(8,128)(2,1)S(1)}, bf16[6,128,128]{2,1,0:T(8,128)(2,1)S(1)}, u32[]{:S(2)}, u32[]{:S(2)}) collective-permute-start(bf16[6,128,128]{2,1,0:T(8,128)(2,1)S(1)} %get-tuple-element.91), channel_id=1, source_target_pairs={{0,4},{2,6},{4,0},{6,2},{8,12},{10,14},{12,8},{14,10},{1,5},{3,7},... | collective-permute-start | bytes 589832 | tf_op jit(solution)/shard_map/ppermute | solution.py:209
  154.1 11.5 %collective-permute-start.25 = (bf16[6,128,128]{2,1,0:T(8,128)(2,1)S(1)}, bf16[6,128,128]{2,1,0:T(8,128)(2,1)S(1)}, u32[]{:S(2)}, u32[]{:S(2)}) collective-permute-start(bf16[6,128,128]{2,1,0:T(8,128)(2,1)S(1)} %get-tuple-element.92), channel_id=1, source_target_pairs={{0,6},{2,4},{4,2},{6,0},{8,14},{10,12},{12,10},{14,8},{1,7},{3,5},... | collective-permute-start | bytes 589832 | tf_op jit(solution)/shard_map/ppermute | solution.py:209
  155.5 16.9 %collective-permute-start.29 = (bf16[6,128,128]{2,1,0:T(8,128)(2,1)S(1)}, bf16[6,128,128]{2,1,0:T(8,128)(2,1)S(1)}, u32[]{:S(2)}, u32[]{:S(2)}) collective-permute-start(bf16[6,128,128]{2,1,0:T(8,128)(2,1)S(1)} %get-tuple-element.99), channel_id=1, source_target_pairs={{0,14},{2,12},{4,10},{6,8},{8,6},{10,4},{12,2},{14,0},{1,15},{3,13... | collective-permute-start | bytes 589832 | tf_op jit(solution)/shard_map/ppermute | solution.py:209
  (13 other events, 126.1 us)

commit v15 on v14

--- a/solution.py
+++ b/solution.py
@@ -299,7 +299,8 @@
                 if j < last - 1:
                     found.append((value[0::2], value[1::2].astype(bf16)))
                 else:
-                    found.append((value, value[::-1].astype(bf16)))
+                    turned = jnp.concatenate([value[1:], value[:1]], axis=0)
+                    found.append((value, turned.astype(bf16)))
             states = found
         states = step_together(states)
         states = [

time: 176 us -> 171 us (0.972)
  local copies, waits for them, and re-layouts: 12 us -> 6.8 us
    unnamed x14 -> x10, local copies, waits for them, and re-layouts: 11.9 us -> 6.69 us
  transfers between devices with their start and end apart: 30 -> 30, of which waited for: 18 -> 18; matrix products, arithmetic and copies ran while one was open for 1% -> 1% of each run, Pallas kernels for 2% -> 3%
where the time goes in v15:
time: 171 us; the launch traced here: 170 us
  waiting for transfers between devices  97.9 us (57%)
  starting transfers between devices  42.9 us (25%)
  Pallas kernels  18 us (11%)
  local copies, waits for them, and re-layouts  6.8 us (4%)
  other arithmetic  3.72 us (2%)
    ppermute x21, waiting for transfers between devices, flip(): return lax.ppermute(x, 'pair', [(s, s ^ bit) for s in range(n)])  78 us
    ppermute x21, starting transfers between devices, flip(): return lax.ppermute(x, 'pair', [(s, s ^ bit) for s in range(n)])  26.3 us
    ppermute x7, waiting for transfers between devices, shift(): return lax.ppermute(x, 'pair', [(s, (s + d) % n) for s in range(n)])  18.1 us
    ppermute x7, starting transfers between devices, shift(): return lax.ppermute(x, 'pair', [(s, (s + d) % n) for s in range(n)])  16.5 us
    pallas_call x7, Pallas kernels, call(): pl.pallas_call(kernel, out_shape=out_shape, grid_spec=pltpu.PrefetchScala...  16 us
    unnamed x10, local copies, waits for them, and re-layouts  6.69 us
  transfers between devices with their start and end apart: 30, of which 18 were waited for; matrix products, arithmetic and copies ran while one was open for 1% of the time, Pallas kernels for 3%

profile of v15, /device:TPU:0, one launch (start us, length us, event | category | flops | bytes accessed | tf_op | source)
XLA Modules:
  0.0 170.3 jit_solution(10681915592974377575)
XLA Ops:
  5.1 4.1 %collective-permute-start = (bf16[3,128,256]{2,1,0:T(8,128)(2,1)S(1)}, bf16[3,128,256]{2,1,0:T(8,128)(2,1)S(1)}, u32[]{:S(2)}, u32[]{:S(2)}) collective-permute-start(bf16[3,128,256]{2,1,0:T(8,128)(2,1)S(1)} %get-tuple-element.51), channel_id=1, source_target_pairs={{0,8},{2,10},{4,12},{6,14},{8,0},{10,2},{12,4},{14,6},{1,9},{3,11}... | collective-permute-start | bytes 589832 | tf_op jit(solution)/shard_map/ppermute | solution.py:206
  9.2 2.5 %collective-permute-start.1 = (bf16[3,128,256]{2,1,0:T(8,128)(2,1)S(1)}, bf16[3,128,256]{2,1,0:T(8,128)(2,1)S(1)}, u32[]{:S(2)}, u32[]{:S(2)}) collective-permute-start(bf16[3,128,256]{2,1,0:T(8,128)(2,1)S(1)} %get-tuple-element.52), channel_id=1, source_target_pairs={{0,6},{2,8},{4,10},{6,12},{8,14},{10,0},{12,2},{14,4},{1,7},{3,9},... | collective-permute-start | bytes 589832 | tf_op jit(solution)/shard_map/ppermute | solution.py:206
  16.8 15.0 %collective-permute-done.ready.rest_0_ = bf16[3,128,256]{2,1,0:T(8,128)(2,1)S(1)} collective-permute-done((bf16[3,128,256]{2,1,0:T(8,128)(2,1)S(1)}, bf16[3,128,256]{2,1,0:T(8,128)(2,1)S(1)}, u32[]{:S(2)}, u32[]{:S(2)}) %collective-permute-start) | collective-permute-done | bytes 196640 | tf_op jit(solution)/shard_map/ppermute | solution.py:206
  31.8 5.2 %copy-done = bf16[14,256,2048]{2,1,0:T(8,128)(2,1)S(1)} copy-done((bf16[14,256,2048]{2,1,0:T(8,128)(2,1)S(1)}, bf16[14,256,2048]{2,1,0:T(8,128)(2,1)}, u32[]{:S(2)}) %copy-start) | copy-done | bytes 14680088
  38.0 4.8 %collective-permute-start.6 = (bf16[3,128,256]{2,1,0:T(8,128)(2,1)S(1)}, bf16[3,128,256]{2,1,0:T(8,128)(2,1)S(1)}, u32[]{:S(2)}, u32[]{:S(2)}) collective-permute-start(bf16[3,128,256]{2,1,0:T(8,128)(2,1)S(1)} %get-tuple-element.58), channel_id=1, source_target_pairs={{0,14},{2,0},{4,2},{6,4},{8,6},{10,8},{12,10},{14,12},{1,15},{3,1}... | collective-permute-start | bytes 589832 | tf_op jit(solution)/shard_map/ppermute | solution.py:206
  42.9 3.1 %collective-permute-done.6.rest_6_ = bf16[3,128,256]{2,1,0:T(8,128)(2,1)S(1)} collective-permute-done((bf16[3,128,256]{2,1,0:T(8,128)(2,1)S(1)}, bf16[3,128,256]{2,1,0:T(8,128)(2,1)S(1)}, u32[]{:S(2)}, u32[]{:S(2)}) %collective-permute-start.6) | collective-permute-done | bytes 196640 | tf_op jit(solution)/shard_map/ppermute | solution.py:206
  46.9 2.8 %fit.2 = (f32[4,128,256]{2,1,0:T(8,128)S(1)}, bf16[4,128,256]{2,1,0:T(8,128)(2,1)S(1)}) custom-call(s32[8]{0:T(128)S(1)} %iota_xor_fusion.table, bf16[14,1,256]{2,1,0:T(2,128)(2,1)S(1)} %copy.11.factor, bf16[14,128,256]{2,1,0:T(8,128)(2,1)S(1)} %gather_density.1.density, bf16[14,256,2048]{2,1,0:T(8,128)(2,1)S(1)} %load_integrals.1.integrals), custom_call_target="tpu_custom_call" | custom-call | tf_op jit(solution)/shard_map/fit/pallas_call | solution.py:191
  49.7 2.7 %fit.3 = (f32[4,128,256]{2,1,0:T(8,128)S(1)}, bf16[4,128,256]{2,1,0:T(8,128)(2,1)S(1)}) custom-call(s32[8]{0:T(128)S(1)} %iota_xor_fusion.table, bf16[14,1,256]{2,1,0:T(2,128)(2,1)S(1)} %copy.11.factor, bf16[14,128,256]{2,1,0:T(8,128)(2,1)S(1)} %collective-permute-done.7.density, bf16[14,256,2048]{2,1,0:T(8,128)(2,1)S(1)} %load_integrals.1.integrals, ...), custom_call_target="tpu_custom_call" | custom-call | tf_op jit(solution)/shard_map/fit/pallas_call | solution.py:191
  52.9 8.3 %collective-permute-done.8 = bf16[4,128,256]{2,1,0:T(8,128)(2,1)S(1)} collective-permute-done((bf16[4,128,256]{2,1,0:T(8,128)(2,1)S(1)}, bf16[4,128,256]{2,1,0:T(8,128)(2,1)S(1)}, u32[]{:S(2)}, u32[]{:S(2)}) %collective-permute-start.8) | collective-permute-done | bytes 262176 | tf_op jit(solution)/shard_map/ppermute | solution.py:209
  63.5 3.2 %collective-permute-done.10 = bf16[2,128,256]{2,1,0:T(8,128)(2,1)S(1)} collective-permute-done((bf16[2,128,256]{2,1,0:T(8,128)(2,1)S(1)}, bf16[2,128,256]{2,1,0:T(8,128)(2,1)S(1)}, u32[]{:S(2)}, u32[]{:S(2)}) %collective-permute-start.10) | collective-permute-done | bytes 131104 | tf_op jit(solution)/shard_map/ppermute | solution.py:209
  66.9 5.8 %collective-permute-start.12 = (bf16[2,128,256]{2,1,0:T(8,128)(2,1)S(1)}, bf16[2,128,256]{2,1,0:T(8,128)(2,1)S(1)}, u32[]{:S(2)}, u32[]{:S(2)}) collective-permute-start(bf16[2,128,256]{2,1,0:T(8,128)(2,1)S(1)} %pad_maximum_fusion.2), channel_id=1, source_target_pairs={{0,8},{2,10},{4,12},{6,14},{8,0},{10,2},{12,4},{14,6},{1,9},{3,11}... | collective-permute-start | bytes 393224 | tf_op jit(solution)/shard_map/ppermute | solution.py:209
  72.8 8.5 %collective-permute-done.12 = bf16[2,128,256]{2,1,0:T(8,128)(2,1)S(1)} collective-permute-done((bf16[2,128,256]{2,1,0:T(8,128)(2,1)S(1)}, bf16[2,128,256]{2,1,0:T(8,128)(2,1)S(1)}, u32[]{:S(2)}, u32[]{:S(2)}) %collective-permute-start.12) | collective-permute-done | bytes 131104 | tf_op jit(solution)/shard_map/ppermute | solution.py:209
  83.7 4.4 %collective-permute-done.14 = bf16[2,128,256]{2,1,0:T(8,128)(2,1)S(1)} collective-permute-done((bf16[2,128,256]{2,1,0:T(8,128)(2,1)S(1)}, bf16[2,128,256]{2,1,0:T(8,128)(2,1)S(1)}, u32[]{:S(2)}, u32[]{:S(2)}) %collective-permute-start.14) | collective-permute-done | bytes 131104 | tf_op jit(solution)/shard_map/ppermute | solution.py:209
  90.2 5.0 %collective-permute-done.16.far = bf16[4,128,256]{2,1,0:T(8,128)(2,1)S(1)} collective-permute-done((bf16[4,128,256]{2,1,0:T(8,128)(2,1)S(1)}, bf16[4,128,256]{2,1,0:T(8,128)(2,1)S(1)}, u32[]{:S(2)}, u32[]{:S(2)}) %collective-permute-start.16) | collective-permute-done | bytes 262176 | tf_op jit(solution)/shard_map/ppermute | solution.py:209
  96.6 5.0 %apply.1 = (f32[14,128,256]{2,1,0:T(8,128)S(1)}, bf16[14,128,256]{2,1,0:T(8,128)(2,1)S(1)}) custom-call(s32[8]{0:T(128)S(1)} %iota_xor_fusion.table, bf16[14,256,2048]{2,1,0:T(8,128)(2,1)S(1)} %load_integrals.1.integrals, bf16[4,128,256]{2,1,0:T(8,128)(2,1)S(1)} %pad_maximum_fusion.1.near, bf16[4,128,256]{2,1,0:T(8,128)(2,1)S(1)} %collective-permute-done.16.far, ...), custom_call_target="tpu_custom_call" | custom-call | tf_op jit(solution)/shard_map/apply/pallas_call | solution.py:191
  109.8 7.8 %collective-permute-done.19.rest_0_.rest_1_ = bf16[6,128,256]{2,1,0:T(8,128)(2,1)S(1)} collective-permute-done((bf16[6,128,256]{2,1,0:T(8,128)(2,1)S(1)}, bf16[6,128,256]{2,1,0:T(8,128)(2,1)S(1)}, u32[]{:S(2)}, u32[]{:S(2)}) %collective-permute-start.19) | collective-permute-done | bytes 393248 | tf_op jit(solution)/shard_map/ppermute | solution.py:209
  119.3 6.7 %collective-permute-done.20.rest_1_.rest_2_ = bf16[6,128,256]{2,1,0:T(8,128)(2,1)S(1)} collective-permute-done((bf16[6,128,256]{2,1,0:T(8,128)(2,1)S(1)}, bf16[6,128,256]{2,1,0:T(8,128)(2,1)S(1)}, u32[]{:S(2)}, u32[]{:S(2)}) %collective-permute-start.20) | collective-permute-done | bytes 393248 | tf_op jit(solution)/shard_map/ppermute | solution.py:209
  128.4 9.0 %collective-permute-done.22.whole = bf16[14,128,128]{2,1,0:T(8,128)(2,1)S(1)} collective-permute-done((bf16[14,128,128]{2,1,0:T(8,128)(2,1)S(1)}, bf16[14,128,128]{2,1,0:T(8,128)(2,1)S(1)}, u32[]{:S(2)}, u32[]{:S(2)}) %collective-permute-start.22) | collective-permute-done | bytes 458784 | tf_op jit(solution)/shard_map/ppermute | solution.py:209
  140.6 7.3 %collective-permute-done.23.rest_5_ = bf16[6,128,128]{2,1,0:T(8,128)(2,1)S(1)} collective-permute-done((bf16[6,128,128]{2,1,0:T(8,128)(2,1)S(1)}, bf16[6,128,128]{2,1,0:T(8,128)(2,1)S(1)}, u32[]{:S(2)}, u32[]{:S(2)}) %collective-permute-start.23) | collective-permute-done | bytes 196640 | tf_op jit(solution)/shard_map/ppermute | solution.py:209
  150.4 2.6 %collective-permute-start.29 = (bf16[6,128,128]{2,1,0:T(8,128)(2,1)S(1)}, bf16[6,128,128]{2,1,0:T(8,128)(2,1)S(1)}, u32[]{:S(2)}, u32[]{:S(2)}) collective-permute-start(bf16[6,128,128]{2,1,0:T(8,128)(2,1)S(1)} %get-tuple-element.99), channel_id=1, source_target_pairs={{0,14},{2,12},{4,10},{6,8},{8,6},{10,4},{12,2},{14,0},{1,15},{3,13... | collective-permute-start | bytes 589832 | tf_op jit(solution)/shard_map/ppermute | solution.py:209
  153.2 2.5 %collective-permute-done.24.rest_6_ = bf16[6,128,128]{2,1,0:T(8,128)(2,1)S(1)} collective-permute-done((bf16[6,128,128]{2,1,0:T(8,128)(2,1)S(1)}, bf16[6,128,128]{2,1,0:T(8,128)(2,1)S(1)}, u32[]{:S(2)}, u32[]{:S(2)}) %collective-permute-start.24) | collective-permute-done | bytes 196640 | tf_op jit(solution)/shard_map/ppermute | solution.py:209
  155.7 4.9 %collective-permute-done.25.rest_7_ = bf16[6,128,128]{2,1,0:T(8,128)(2,1)S(1)} collective-permute-done((bf16[6,128,128]{2,1,0:T(8,128)(2,1)S(1)}, bf16[6,128,128]{2,1,0:T(8,128)(2,1)S(1)}, u32[]{:S(2)}, u32[]{:S(2)}) %collective-permute-start.25) | collective-permute-done | bytes 196640 | tf_op jit(solution)/shard_map/ppermute | solution.py:209
  160.5 6.7 %collective-permute-done.29.rest_11_ = bf16[6,128,128]{2,1,0:T(8,128)(2,1)S(1)} collective-permute-done((bf16[6,128,128]{2,1,0:T(8,128)(2,1)S(1)}, bf16[6,128,128]{2,1,0:T(8,128)(2,1)S(1)}, u32[]{:S(2)}, u32[]{:S(2)}) %collective-permute-start.29) | collective-permute-done | bytes 196640 | tf_op jit(solution)/shard_map/ppermute | solution.py:209
  167.2 3.1 %gather_coulomb.1 = (bf16[14,256,128]{2,1,0:T(8,128)(2,1)}, bf16[14,256,128]{2,1,0:T(8,128)(2,1)}) custom-call(s32[48]{0:T(128)S(1)} %pad_add_fusion.1.table, bf16[6,128,256]{2,1,0:T(8,128)(2,1)S(1)} %get-tuple-element.83.rest_0_, bf16[6,128,256]{2,1,0:T(8,128)(2,1)S(1)} %collective-permute-done.19.rest_0_.rest_1_, ...), custom_call_target="tpu_custom_call" | custom-call | tf_op jit(solution)/shard_map/gather_coulomb/pallas_call | solution.py:191
  (100 shorter events, 38.3 us)
Async XLA Ops:
  5.1 26.7 %collective-permute-start = (bf16[3,128,256]{2,1,0:T(8,128)(2,1)S(1)}, bf16[3,128,256]{2,1,0:T(8,128)(2,1)S(1)}, u32[]{:S(2)}, u32[]{:S(2)}) collective-permute-start(bf16[3,128,256]{2,1,0:T(8,128)(2,1)S(1)} %get-tuple-element.51), channel_id=1, source_target_pairs={{0,8},{2,10},{4,12},{6,14},{8,0},{10,2},{12,4},{14,6},{1,9},{3,11}... | collective-permute-start | bytes 589832 | tf_op jit(solution)/shard_map/ppermute | solution.py:206
  9.2 28.8 %collective-permute-start.1 = (bf16[3,128,256]{2,1,0:T(8,128)(2,1)S(1)}, bf16[3,128,256]{2,1,0:T(8,128)(2,1)S(1)}, u32[]{:S(2)}, u32[]{:S(2)}) collective-permute-start(bf16[3,128,256]{2,1,0:T(8,128)(2,1)S(1)} %get-tuple-element.52), channel_id=1, source_target_pairs={{0,6},{2,8},{4,10},{6,12},{8,14},{10,0},{12,2},{14,4},{1,7},{3,9},... | collective-permute-start | bytes 589832 | tf_op jit(solution)/shard_map/ppermute | solution.py:206
  11.7 31.1 %collective-permute-start.2 = (bf16[3,128,256]{2,1,0:T(8,128)(2,1)S(1)}, bf16[3,128,256]{2,1,0:T(8,128)(2,1)S(1)}, u32[]{:S(2)}, u32[]{:S(2)}) collective-permute-start(bf16[3,128,256]{2,1,0:T(8,128)(2,1)S(1)} %get-tuple-element.53), channel_id=1, source_target_pairs={{0,10},{2,12},{4,14},{6,0},{8,2},{10,4},{12,6},{14,8},{1,11},{3,13... | collective-permute-start | bytes 589832 | tf_op jit(solution)/shard_map/ppermute | solution.py:206
  13.0 29.9 %collective-permute-start.3 = (bf16[3,128,256]{2,1,0:T(8,128)(2,1)S(1)}, bf16[3,128,256]{2,1,0:T(8,128)(2,1)S(1)}, u32[]{:S(2)}, u32[]{:S(2)}) collective-permute-start(bf16[3,128,256]{2,1,0:T(8,128)(2,1)S(1)} %get-tuple-element.54), channel_id=1, source_target_pairs={{0,4},{2,6},{4,8},{6,10},{8,12},{10,14},{12,0},{14,2},{1,5},{3,7},... | collective-permute-start | bytes 589832 | tf_op jit(solution)/shard_map/ppermute | solution.py:206
  14.6 28.3 %collective-permute-start.4 = (bf16[3,128,256]{2,1,0:T(8,128)(2,1)S(1)}, bf16[3,128,256]{2,1,0:T(8,128)(2,1)S(1)}, u32[]{:S(2)}, u32[]{:S(2)}) collective-permute-start(bf16[3,128,256]{2,1,0:T(8,128)(2,1)S(1)} %get-tuple-element.55), channel_id=1, source_target_pairs={{0,12},{2,14},{4,0},{6,2},{8,4},{10,6},{12,8},{14,10},{1,13},{3,15... | collective-permute-start | bytes 589832 | tf_op jit(solution)/shard_map/ppermute | solution.py:206
  31.8 11.1 %collective-permute-start.5 = (bf16[3,128,256]{2,1,0:T(8,128)(2,1)S(1)}, bf16[3,128,256]{2,1,0:T(8,128)(2,1)S(1)}, u32[]{:S(2)}, u32[]{:S(2)}) collective-permute-start(bf16[3,128,256]{2,1,0:T(8,128)(2,1)S(1)} %get-tuple-element.56), channel_id=1, source_target_pairs={{0,2},{2,4},{4,6},{6,8},{8,10},{10,12},{12,14},{14,0},{1,3},{3,5},... | collective-permute-start | bytes 589832 | tf_op jit(solution)/shard_map/ppermute | solution.py:206
  38.0 8.0 %collective-permute-start.6 = (bf16[3,128,256]{2,1,0:T(8,128)(2,1)S(1)}, bf16[3,128,256]{2,1,0:T(8,128)(2,1)S(1)}, u32[]{:S(2)}, u32[]{:S(2)}) collective-permute-start(bf16[3,128,256]{2,1,0:T(8,128)(2,1)S(1)} %get-tuple-element.58), channel_id=1, source_target_pairs={{0,14},{2,0},{4,2},{6,4},{8,6},{10,8},{12,10},{14,12},{1,15},{3,1}... | collective-permute-start | bytes 589832 | tf_op jit(solution)/shard_map/ppermute | solution.py:206
  52.5 8.8 %collective-permute-start.8 = (bf16[4,128,256]{2,1,0:T(8,128)(2,1)S(1)}, bf16[4,128,256]{2,1,0:T(8,128)(2,1)S(1)}, u32[]{:S(2)}, u32[]{:S(2)}) collective-permute-start(bf16[4,128,256]{2,1,0:T(8,128)(2,1)S(1)} %get-tuple-element.66), channel_id=1, source_target_pairs={{0,4},{2,6},{4,0},{6,2},{8,12},{10,14},{12,8},{14,10},{1,5},{3,7},... | collective-permute-start | bytes 786440 | tf_op jit(solution)/shard_map/ppermute | solution.py:209
  52.6 8.8 %collective-permute-start.9 = (bf16[4,128,256]{2,1,0:T(8,128)(2,1)S(1)}, bf16[4,128,256]{2,1,0:T(8,128)(2,1)S(1)}, u32[]{:S(2)}, u32[]{:S(2)}) collective-permute-start(bf16[4,128,256]{2,1,0:T(8,128)(2,1)S(1)} %get-tuple-element.68), channel_id=1, source_target_pairs={{0,2},{2,0},{4,6},{6,4},{8,10},{10,8},{12,14},{14,12},{1,3},{3,1},... | collective-permute-start | bytes 786440 | tf_op jit(solution)/shard_map/ppermute | solution.py:209
  66.9 14.4 %collective-permute-start.12 = (bf16[2,128,256]{2,1,0:T(8,128)(2,1)S(1)}, bf16[2,128,256]{2,1,0:T(8,128)(2,1)S(1)}, u32[]{:S(2)}, u32[]{:S(2)}) collective-permute-start(bf16[2,128,256]{2,1,0:T(8,128)(2,1)S(1)} %pad_maximum_fusion.2), channel_id=1, source_target_pairs={{0,8},{2,10},{4,12},{6,14},{8,0},{10,2},{12,4},{14,6},{1,9},{3,11}... | collective-permute-start | bytes 393224 | tf_op jit(solution)/shard_map/ppermute | solution.py:209
  72.7 10.3 %collective-permute-start.13 = (bf16[2,128,256]{2,1,0:T(8,128)(2,1)S(1)}, bf16[2,128,256]{2,1,0:T(8,128)(2,1)S(1)}, u32[]{:S(2)}, u32[]{:S(2)}) collective-permute-start(bf16[2,128,256]{2,1,0:T(8,128)(2,1)S(1)} %pad_maximum_fusion.3), channel_id=1, source_target_pairs={{0,8},{2,10},{4,12},{6,14},{8,0},{10,2},{12,4},{14,6},{1,9},{3,11}... | collective-permute-start | bytes 393224 | tf_op jit(solution)/shard_map/ppermute | solution.py:209
  88.7 6.5 %collective-permute-start.16 = (bf16[4,128,256]{2,1,0:T(8,128)(2,1)S(1)}, bf16[4,128,256]{2,1,0:T(8,128)(2,1)S(1)}, u32[]{:S(2)}, u32[]{:S(2)}) collective-permute-start(bf16[4,128,256]{2,1,0:T(8,128)(2,1)S(1)} %pad_maximum_fusion.1.near), channel_id=1, source_target_pairs={{0,2},{2,0},{4,6},{6,4},{8,10},{10,8},{12,14},{14,12},{1,3},{3,1},... | collective-permute-start | bytes 786440 | tf_op jit(solution)/shard_map/ppermute | solution.py:209
  90.2 6.4 %collective-permute-start.17 = (bf16[4,128,256]{2,1,0:T(8,128)(2,1)S(1)}, bf16[4,128,256]{2,1,0:T(8,128)(2,1)S(1)}, u32[]{:S(2)}, u32[]{:S(2)}) collective-permute-start(bf16[4,128,256]{2,1,0:T(8,128)(2,1)S(1)} %pad_maximum_fusion.near_other), channel_id=1, source_target_pairs={{0,4},{2,6},{4,0},{6,2},{8,12},{10,14},{12,8},{14,10},{1,5},{3,7},... | collective-permute-start | bytes 786440 | tf_op jit(solution)/shard_map/ppermute | solution.py:209
  105.2 32.2 %collective-permute-start.22 = (bf16[14,128,128]{2,1,0:T(8,128)(2,1)S(1)}, bf16[14,128,128]{2,1,0:T(8,128)(2,1)S(1)}, u32[]{:S(2)}, u32[]{:S(2)}) collective-permute-start(bf16[14,128,128]{2,1,0:T(8,128)(2,1)S(1)} %get-tuple-element.88), channel_id=1, source_target_pairs={{0,8},{2,10},{4,12},{6,14},{8,0},{10,2},{12,4},{14,6},{1,9},{3,11}... | collective-permute-start | bytes 1376264 | tf_op jit(solution)/shard_map/ppermute | solution.py:209
  106.7 10.9 %collective-permute-start.19 = (bf16[6,128,256]{2,1,0:T(8,128)(2,1)S(1)}, bf16[6,128,256]{2,1,0:T(8,128)(2,1)S(1)}, u32[]{:S(2)}, u32[]{:S(2)}) collective-permute-start(bf16[6,128,256]{2,1,0:T(8,128)(2,1)S(1)} %get-tuple-element.84), channel_id=1, source_target_pairs={{0,2},{2,0},{4,6},{6,4},{8,10},{10,8},{12,14},{14,12},{1,3},{3,1},... | collective-permute-start | bytes 1179656 | tf_op jit(solution)/shard_map/ppermute | solution.py:209
  107.2 18.7 %collective-permute-start.20 = (bf16[6,128,256]{2,1,0:T(8,128)(2,1)S(1)}, bf16[6,128,256]{2,1,0:T(8,128)(2,1)S(1)}, u32[]{:S(2)}, u32[]{:S(2)}) collective-permute-start(bf16[6,128,256]{2,1,0:T(8,128)(2,1)S(1)} %get-tuple-element.85), channel_id=1, source_target_pairs={{0,4},{2,6},{4,0},{6,2},{8,12},{10,14},{12,8},{14,10},{1,5},{3,7},... | collective-permute-start | bytes 1179656 | tf_op jit(solution)/shard_map/ppermute | solution.py:209
  109.7 39.3 %collective-permute-start.26 = (bf16[6,128,128]{2,1,0:T(8,128)(2,1)S(1)}, bf16[6,128,128]{2,1,0:T(8,128)(2,1)S(1)}, u32[]{:S(2)}, u32[]{:S(2)}) collective-permute-start(bf16[6,128,128]{2,1,0:T(8,128)(2,1)S(1)} %get-tuple-element.93), channel_id=1, source_target_pairs={{0,8},{2,10},{4,12},{6,14},{8,0},{10,2},{12,4},{14,6},{1,9},{3,11}... | collective-permute-start | bytes 589832 | tf_op jit(solution)/shard_map/ppermute | solution.py:209
  117.6 32.7 %collective-permute-start.27 = (bf16[6,128,128]{2,1,0:T(8,128)(2,1)S(1)}, bf16[6,128,128]{2,1,0:T(8,128)(2,1)S(1)}, u32[]{:S(2)}, u32[]{:S(2)}) collective-permute-start(bf16[6,128,128]{2,1,0:T(8,128)(2,1)S(1)} %get-tuple-element.95), channel_id=1, source_target_pairs={{0,10},{2,8},{4,14},{6,12},{8,2},{10,0},{12,6},{14,4},{1,11},{3,9}... | collective-permute-start | bytes 589832 | tf_op jit(solution)/shard_map/ppermute | solution.py:209
  126.0 34.6 %collective-permute-start.21 = (bf16[6,128,256]{2,1,0:T(8,128)(2,1)S(1)}, bf16[6,128,256]{2,1,0:T(8,128)(2,1)S(1)}, u32[]{:S(2)}, u32[]{:S(2)}) collective-permute-start(bf16[6,128,256]{2,1,0:T(8,128)(2,1)S(1)} %get-tuple-element.87), channel_id=1, source_target_pairs={{0,6},{2,4},{4,2},{6,0},{8,14},{10,12},{12,10},{14,8},{1,7},{3,5},... | collective-permute-start | bytes 1179656 | tf_op jit(solution)/shard_map/ppermute | solution.py:209
  138.0 9.8 %collective-permute-start.23 = (bf16[6,128,128]{2,1,0:T(8,128)(2,1)S(1)}, bf16[6,128,128]{2,1,0:T(8,128)(2,1)S(1)}, u32[]{:S(2)}, u32[]{:S(2)}) collective-permute-start(bf16[6,128,128]{2,1,0:T(8,128)(2,1)S(1)} %get-tuple-element.90), channel_id=1, source_target_pairs={{0,2},{2,0},{4,6},{6,4},{8,10},{10,8},{12,14},{14,12},{1,3},{3,1},... | collective-permute-start | bytes 589832 | tf_op jit(solution)/shard_map/ppermute | solution.py:209
  138.6 14.6 %collective-permute-start.28 = (bf16[6,128,128]{2,1,0:T(8,128)(2,1)S(1)}, bf16[6,128,128]{2,1,0:T(8,128)(2,1)S(1)}, u32[]{:S(2)}, u32[]{:S(2)}) collective-permute-start(bf16[6,128,128]{2,1,0:T(8,128)(2,1)S(1)} %get-tuple-element.97), channel_id=1, source_target_pairs={{0,12},{2,14},{4,8},{6,10},{8,4},{10,6},{12,0},{14,2},{1,13},{3,15... | collective-permute-start | bytes 589832 | tf_op jit(solution)/shard_map/ppermute | solution.py:209
  147.8 7.8 %collective-permute-start.24 = (bf16[6,128,128]{2,1,0:T(8,128)(2,1)S(1)}, bf16[6,128,128]{2,1,0:T(8,128)(2,1)S(1)}, u32[]{:S(2)}, u32[]{:S(2)}) collective-permute-start(bf16[6,128,128]{2,1,0:T(8,128)(2,1)S(1)} %get-tuple-element.91), channel_id=1, source_target_pairs={{0,4},{2,6},{4,0},{6,2},{8,12},{10,14},{12,8},{14,10},{1,5},{3,7},... | collective-permute-start | bytes 589832 | tf_op jit(solution)/shard_map/ppermute | solution.py:209
  149.1 11.5 %collective-permute-start.25 = (bf16[6,128,128]{2,1,0:T(8,128)(2,1)S(1)}, bf16[6,128,128]{2,1,0:T(8,128)(2,1)S(1)}, u32[]{:S(2)}, u32[]{:S(2)}) collective-permute-start(bf16[6,128,128]{2,1,0:T(8,128)(2,1)S(1)} %get-tuple-element.92), channel_id=1, source_target_pairs={{0,6},{2,4},{4,2},{6,0},{8,14},{10,12},{12,10},{14,8},{1,7},{3,5},... | collective-permute-start | bytes 589832 | tf_op jit(solution)/shard_map/ppermute | solution.py:209
  150.4 16.9 %collective-permute-start.29 = (bf16[6,128,128]{2,1,0:T(8,128)(2,1)S(1)}, bf16[6,128,128]{2,1,0:T(8,128)(2,1)S(1)}, u32[]{:S(2)}, u32[]{:S(2)}) collective-permute-start(bf16[6,128,128]{2,1,0:T(8,128)(2,1)S(1)} %get-tuple-element.99), channel_id=1, source_target_pairs={{0,14},{2,12},{4,10},{6,8},{8,6},{10,4},{12,2},{14,0},{1,15},{3,13... | collective-permute-start | bytes 589832 | tf_op jit(solution)/shard_map/ppermute | solution.py:209
  (11 other events, 101.3 us)

commit v16 on v15

--- a/solution.py
+++ b/solution.py
@@ -240,8 +240,10 @@
         compiler_params=pltpu.CompilerParams(vmem_limit_bytes=VMEM_BYTES),
         name="scatter_density",
     )(send_table, density)
-    steps = sorted(range(1, n), key=lambda d: abs(2 * d - n))
-    received = [shift(sends[d], d) for d in steps[:-1]]
+    steps = sorted(range(1, n), key=lambda d: (min(d, n - d) > 1, abs(2 * d - n)))
+    received = []
+    for i, d in enumerate(steps):
+        received.append(shift(after(sends[d], *received[: max(i - 4, 0)][-1:]), d))
     integrals = pl.pallas_call(
         load_kernel,
         out_shape=pltpu.VMEM((blocks, pairs, aux_dev), bf16),
@@ -250,8 +252,8 @@
         scratch_shapes=[pltpu.SemaphoreType.DMA],
         compiler_params=pltpu.CompilerParams(vmem_limit_bytes=2 * 1024 * 1024),
         name="load_integrals",
-    )(three_index, received[0])
-    received += [shift(after(sends[steps[-1]], integrals), steps[-1]), sends[0]]
+    )(three_index, received[1])
+    received.append(sends[0])
     steps = (*steps, 0)
     own = call(
         functools.partial(gather_density_kernel, steps, cap),
@@ -260,6 +262,7 @@
         received,
         jax.ShapeDtypeStruct((blocks, half, pairs), bf16),
         in_vmem,
+        [integrals],
     )
     other = swap(own)
 

time: 171 us -> 169 us (0.988)
  waiting for transfers between devices: 97.9 us -> 88.6 us
  starting transfers between devices: 42.9 us -> 50.6 us
    ppermute x21, starting transfers between devices: 26.3 us -> 34.5 us  [flip(): return lax.ppermute(x, 'pair', [(s, s ^ bit) for s in range(n)])]
    ppermute x7, waiting for transfers between devices: 18.1 us -> 10.6 us  [shift(): return lax.ppermute(x, 'pair', [(s, (s + d) % n) for s in range(n)])]
    ppermute x21, waiting for transfers between devices: 78 us -> 76.1 us  [flip(): return lax.ppermute(x, 'pair', [(s, s ^ bit) for s in range(n)])]
  transfers between devices with their start and end apart: 30 -> 30, of which waited for: 18 -> 22; matrix products, arithmetic and copies ran while one was open for 1% -> 1% of each run, Pallas kernels for 3% -> 3%
where the time goes in v16:
time: 169 us
  waiting for transfers between devices  88.6 us (52%)
  starting transfers between devices  50.6 us (30%)
  Pallas kernels  18 us (11%)
  local copies, waits for them, and re-layouts  6.79 us (4%)
  other arithmetic  3.71 us (2%)
    ppermute x21, waiting for transfers between devices, flip(): return lax.ppermute(x, 'pair', [(s, s ^ bit) for s in range(n)])  76.1 us
    ppermute x21, starting transfers between devices, flip(): return lax.ppermute(x, 'pair', [(s, s ^ bit) for s in range(n)])  34.5 us
    pallas_call x7, Pallas kernels, call(): pl.pallas_call(kernel, out_shape=out_shape, grid_spec=pltpu.PrefetchScala...  16 us
    ppermute x7, starting transfers between devices, shift(): return lax.ppermute(x, 'pair', [(s, (s + d) % n) for s in range(n)])  15.9 us
    ppermute x7, waiting for transfers between devices, shift(): return lax.ppermute(x, 'pair', [(s, (s + d) % n) for s in range(n)])  10.6 us
    unnamed x10, local copies, waits for them, and re-layouts  6.69 us
  transfers between devices with their start and end apart: 30, of which 22 were waited for; matrix products, arithmetic and copies ran while one was open for 1% of the time, Pallas kernels for 3%

profile of v16, /device:TPU:0, one launch (start us, length us, event | category | flops | bytes accessed | tf_op | source)
XLA Modules:
  0.0 168.7 jit_solution(6481607107489792999)
XLA Ops:
  5.1 6.1 %collective-permute-start.1 = (bf16[3,128,256]{2,1,0:T(8,128)(2,1)S(1)}, bf16[3,128,256]{2,1,0:T(8,128)(2,1)S(1)}, u32[]{:S(2)}, u32[]{:S(2)}) collective-permute-start(bf16[3,128,256]{2,1,0:T(8,128)(2,1)S(1)} %get-tuple-element.53), channel_id=1, source_target_pairs={{0,14},{2,0},{4,2},{6,4},{8,6},{10,8},{12,10},{14,12},{1,15},{3,1}... | collective-permute-start | bytes 589832 | tf_op jit(solution)/shard_map/ppermute | solution.py:206
  11.2 5.2 %collective-permute-start.3 = (bf16[3,128,256]{2,1,0:T(8,128)(2,1)S(1)}, bf16[3,128,256]{2,1,0:T(8,128)(2,1)S(1)}, u32[]{:S(2)}, u32[]{:S(2)}) collective-permute-start(bf16[3,128,256]{2,1,0:T(8,128)(2,1)S(1)} %get-tuple-element.55), channel_id=1, source_target_pairs={{0,6},{2,8},{4,10},{6,12},{8,14},{10,0},{12,2},{14,4},{1,7},{3,9},... | collective-permute-start | bytes 589832 | tf_op jit(solution)/shard_map/ppermute | solution.py:206
  16.5 4.6 %collective-permute-start.6 = (bf16[3,128,256]{2,1,0:T(8,128)(2,1)S(1)}, bf16[3,128,256]{2,1,0:T(8,128)(2,1)S(1)}, u32[]{:S(2)}, u32[]{:S(2)}) collective-permute-start(bf16[3,128,256]{2,1,0:T(8,128)(2,1)S(1)} %get-tuple-element.60), channel_id=1, source_target_pairs={{0,12},{2,14},{4,0},{6,2},{8,4},{10,6},{12,8},{14,10},{1,13},{3,15... | collective-permute-start | bytes 589832 | tf_op jit(solution)/shard_map/ppermute | solution.py:206
  21.8 5.2 %copy-done = bf16[14,256,2048]{2,1,0:T(8,128)(2,1)S(1)} copy-done((bf16[14,256,2048]{2,1,0:T(8,128)(2,1)S(1)}, bf16[14,256,2048]{2,1,0:T(8,128)(2,1)}, u32[]{:S(2)}) %copy-start) | copy-done | bytes 14680088
  28.0 5.7 %collective-permute-done.2.rest_2_ = bf16[3,128,256]{2,1,0:T(8,128)(2,1)S(1)} collective-permute-done((bf16[3,128,256]{2,1,0:T(8,128)(2,1)S(1)}, bf16[3,128,256]{2,1,0:T(8,128)(2,1)S(1)}, u32[]{:S(2)}, u32[]{:S(2)}) %collective-permute-start.2) | collective-permute-done | bytes 196640 | tf_op jit(solution)/shard_map/ppermute | solution.py:206
  38.9 2.8 %fit.2 = (f32[4,128,256]{2,1,0:T(8,128)S(1)}, bf16[4,128,256]{2,1,0:T(8,128)(2,1)S(1)}) custom-call(s32[8]{0:T(128)S(1)} %iota_xor_fusion.table, bf16[14,1,256]{2,1,0:T(2,128)(2,1)S(1)} %copy.11.factor, bf16[14,128,256]{2,1,0:T(8,128)(2,1)S(1)} %gather_density.1.density, bf16[14,256,2048]{2,1,0:T(8,128)(2,1)S(1)} %load_integrals.1.rest_8_.integrals), custom_call_target="tpu_custom_call" | custom-call | tf_op jit(solution)/shard_map/fit/pallas_call | solution.py:191
  41.7 2.7 %fit.3 = (f32[4,128,256]{2,1,0:T(8,128)S(1)}, bf16[4,128,256]{2,1,0:T(8,128)(2,1)S(1)}) custom-call(s32[8]{0:T(128)S(1)} %iota_xor_fusion.table, bf16[14,1,256]{2,1,0:T(2,128)(2,1)S(1)} %copy.11.factor, bf16[14,128,256]{2,1,0:T(8,128)(2,1)S(1)} %collective-permute-done.7.density, bf16[14,256,2048]{2,1,0:T(8,128)(2,1)S(1)} %load_integrals.1.rest_8_.integrals, ...), custom_call_target="tpu_custom_call" | custom-call | tf_op jit(solution)/shard_map/fit/pallas_call | solution.py:191
  44.5 8.1 %collective-permute-start.8 = (bf16[4,128,256]{2,1,0:T(8,128)(2,1)S(1)}, bf16[4,128,256]{2,1,0:T(8,128)(2,1)S(1)}, u32[]{:S(2)}, u32[]{:S(2)}) collective-permute-start(bf16[4,128,256]{2,1,0:T(8,128)(2,1)S(1)} %get-tuple-element.68), channel_id=1, source_target_pairs={{0,4},{2,6},{4,0},{6,2},{8,12},{10,14},{12,8},{14,10},{1,5},{3,7},... | collective-permute-start | bytes 786440 | tf_op jit(solution)/shard_map/ppermute | solution.py:209
  54.8 4.8 %collective-permute-done.8 = bf16[4,128,256]{2,1,0:T(8,128)(2,1)S(1)} collective-permute-done((bf16[4,128,256]{2,1,0:T(8,128)(2,1)S(1)}, bf16[4,128,256]{2,1,0:T(8,128)(2,1)S(1)}, u32[]{:S(2)}, u32[]{:S(2)}) %collective-permute-start.8) | collective-permute-done | bytes 262176 | tf_op jit(solution)/shard_map/ppermute | solution.py:209
  63.8 2.9 %collective-permute-done.10 = bf16[2,128,256]{2,1,0:T(8,128)(2,1)S(1)} collective-permute-done((bf16[2,128,256]{2,1,0:T(8,128)(2,1)S(1)}, bf16[2,128,256]{2,1,0:T(8,128)(2,1)S(1)}, u32[]{:S(2)}, u32[]{:S(2)}) %collective-permute-start.10) | collective-permute-done | bytes 131104 | tf_op jit(solution)/shard_map/ppermute | solution.py:209
  71.4 7.5 %collective-permute-done.12 = bf16[2,128,256]{2,1,0:T(8,128)(2,1)S(1)} collective-permute-done((bf16[2,128,256]{2,1,0:T(8,128)(2,1)S(1)}, bf16[2,128,256]{2,1,0:T(8,128)(2,1)S(1)}, u32[]{:S(2)}, u32[]{:S(2)}) %collective-permute-start.12) | collective-permute-done | bytes 131104 | tf_op jit(solution)/shard_map/ppermute | solution.py:209
  82.2 4.6 %collective-permute-done.14 = bf16[2,128,256]{2,1,0:T(8,128)(2,1)S(1)} collective-permute-done((bf16[2,128,256]{2,1,0:T(8,128)(2,1)S(1)}, bf16[2,128,256]{2,1,0:T(8,128)(2,1)S(1)}, u32[]{:S(2)}, u32[]{:S(2)}) %collective-permute-start.14) | collective-permute-done | bytes 131104 | tf_op jit(solution)/shard_map/ppermute | solution.py:209
  88.9 5.2 %collective-permute-done.16.far = bf16[4,128,256]{2,1,0:T(8,128)(2,1)S(1)} collective-permute-done((bf16[4,128,256]{2,1,0:T(8,128)(2,1)S(1)}, bf16[4,128,256]{2,1,0:T(8,128)(2,1)S(1)}, u32[]{:S(2)}, u32[]{:S(2)}) %collective-permute-start.16) | collective-permute-done | bytes 262176 | tf_op jit(solution)/shard_map/ppermute | solution.py:209
  95.3 5.0 %apply.1 = (f32[14,128,256]{2,1,0:T(8,128)S(1)}, bf16[14,128,256]{2,1,0:T(8,128)(2,1)S(1)}) custom-call(s32[8]{0:T(128)S(1)} %iota_xor_fusion.table, bf16[14,256,2048]{2,1,0:T(8,128)(2,1)S(1)} %load_integrals.1.rest_8_.integrals, bf16[4,128,256]{2,1,0:T(8,128)(2,1)S(1)} %pad_maximum_fusion.1.near, bf16[4,128,256]{2,1,0:T(8,128)(2,1)S(1)} %collective-permute-done.16.far, ...), custom_call_target="tpu_custom_call" | custom-call | tf_op jit(solution)/shard_map/apply/pallas_call | solution.py:191
  108.5 7.5 %collective-permute-done.19.rest_0_.rest_1_ = bf16[6,128,256]{2,1,0:T(8,128)(2,1)S(1)} collective-permute-done((bf16[6,128,256]{2,1,0:T(8,128)(2,1)S(1)}, bf16[6,128,256]{2,1,0:T(8,128)(2,1)S(1)}, u32[]{:S(2)}, u32[]{:S(2)}) %collective-permute-start.19) | collective-permute-done | bytes 393248 | tf_op jit(solution)/shard_map/ppermute | solution.py:209
  118.0 6.3 %collective-permute-done.20.rest_1_.rest_2_ = bf16[6,128,256]{2,1,0:T(8,128)(2,1)S(1)} collective-permute-done((bf16[6,128,256]{2,1,0:T(8,128)(2,1)S(1)}, bf16[6,128,256]{2,1,0:T(8,128)(2,1)S(1)}, u32[]{:S(2)}, u32[]{:S(2)}) %collective-permute-start.20) | collective-permute-done | bytes 393248 | tf_op jit(solution)/shard_map/ppermute | solution.py:209
  124.3 3.3 %collective-permute-start.21 = (bf16[6,128,256]{2,1,0:T(8,128)(2,1)S(1)}, bf16[6,128,256]{2,1,0:T(8,128)(2,1)S(1)}, u32[]{:S(2)}, u32[]{:S(2)}) collective-permute-start(bf16[6,128,256]{2,1,0:T(8,128)(2,1)S(1)} %get-tuple-element.89), channel_id=1, source_target_pairs={{0,6},{2,4},{4,2},{6,0},{8,14},{10,12},{12,10},{14,8},{1,7},{3,5},... | collective-permute-start | bytes 1179656 | tf_op jit(solution)/shard_map/ppermute | solution.py:209
  127.6 8.3 %collective-permute-done.22.whole = bf16[14,128,128]{2,1,0:T(8,128)(2,1)S(1)} collective-permute-done((bf16[14,128,128]{2,1,0:T(8,128)(2,1)S(1)}, bf16[14,128,128]{2,1,0:T(8,128)(2,1)S(1)}, u32[]{:S(2)}, u32[]{:S(2)}) %collective-permute-start.22) | collective-permute-done | bytes 458784 | tf_op jit(solution)/shard_map/ppermute | solution.py:209
  137.1 2.7 %collective-permute-start.28 = (bf16[6,128,128]{2,1,0:T(8,128)(2,1)S(1)}, bf16[6,128,128]{2,1,0:T(8,128)(2,1)S(1)}, u32[]{:S(2)}, u32[]{:S(2)}) collective-permute-start(bf16[6,128,128]{2,1,0:T(8,128)(2,1)S(1)} %get-tuple-element.99), channel_id=1, source_target_pairs={{0,12},{2,14},{4,8},{6,10},{8,4},{10,6},{12,0},{14,2},{1,13},{3,15... | collective-permute-start | bytes 589832 | tf_op jit(solution)/shard_map/ppermute | solution.py:209
  139.8 7.5 %collective-permute-done.23.rest_5_ = bf16[6,128,128]{2,1,0:T(8,128)(2,1)S(1)} collective-permute-done((bf16[6,128,128]{2,1,0:T(8,128)(2,1)S(1)}, bf16[6,128,128]{2,1,0:T(8,128)(2,1)S(1)}, u32[]{:S(2)}, u32[]{:S(2)}) %collective-permute-start.23) | collective-permute-done | bytes 196640 | tf_op jit(solution)/shard_map/ppermute | solution.py:209
  151.4 3.7 %collective-permute-done.24.rest_6_ = bf16[6,128,128]{2,1,0:T(8,128)(2,1)S(1)} collective-permute-done((bf16[6,128,128]{2,1,0:T(8,128)(2,1)S(1)}, bf16[6,128,128]{2,1,0:T(8,128)(2,1)S(1)}, u32[]{:S(2)}, u32[]{:S(2)}) %collective-permute-start.24) | collective-permute-done | bytes 196640 | tf_op jit(solution)/shard_map/ppermute | solution.py:209
  155.2 4.2 %collective-permute-done.25.rest_7_ = bf16[6,128,128]{2,1,0:T(8,128)(2,1)S(1)} collective-permute-done((bf16[6,128,128]{2,1,0:T(8,128)(2,1)S(1)}, bf16[6,128,128]{2,1,0:T(8,128)(2,1)S(1)}, u32[]{:S(2)}, u32[]{:S(2)}) %collective-permute-start.25) | collective-permute-done | bytes 196640 | tf_op jit(solution)/shard_map/ppermute | solution.py:209
  159.4 6.2 %collective-permute-done.29.rest_11_ = bf16[6,128,128]{2,1,0:T(8,128)(2,1)S(1)} collective-permute-done((bf16[6,128,128]{2,1,0:T(8,128)(2,1)S(1)}, bf16[6,128,128]{2,1,0:T(8,128)(2,1)S(1)}, u32[]{:S(2)}, u32[]{:S(2)}) %collective-permute-start.29) | collective-permute-done | bytes 196640 | tf_op jit(solution)/shard_map/ppermute | solution.py:209
  165.6 3.1 %gather_coulomb.1 = (bf16[14,256,128]{2,1,0:T(8,128)(2,1)}, bf16[14,256,128]{2,1,0:T(8,128)(2,1)}) custom-call(s32[48]{0:T(128)S(1)} %pad_add_fusion.1.table, bf16[6,128,256]{2,1,0:T(8,128)(2,1)S(1)} %get-tuple-element.85.rest_0_, bf16[6,128,256]{2,1,0:T(8,128)(2,1)S(1)} %collective-permute-done.19.rest_0_.rest_1_, ...), custom_call_target="tpu_custom_call" | custom-call | tf_op jit(solution)/shard_map/gather_coulomb/pallas_call | solution.py:191
  (100 shorter events, 44.4 us)
Async XLA Ops:
  5.1 11.4 %collective-permute-start.1 = (bf16[3,128,256]{2,1,0:T(8,128)(2,1)S(1)}, bf16[3,128,256]{2,1,0:T(8,128)(2,1)S(1)}, u32[]{:S(2)}, u32[]{:S(2)}) collective-permute-start(bf16[3,128,256]{2,1,0:T(8,128)(2,1)S(1)} %get-tuple-element.53), channel_id=1, source_target_pairs={{0,14},{2,0},{4,2},{6,4},{8,6},{10,8},{12,10},{14,12},{1,15},{3,1}... | collective-permute-start | bytes 589832 | tf_op jit(solution)/shard_map/ppermute | solution.py:206
  11.1 10.6 %collective-permute-start = (bf16[3,128,256]{2,1,0:T(8,128)(2,1)S(1)}, bf16[3,128,256]{2,1,0:T(8,128)(2,1)S(1)}, u32[]{:S(2)}, u32[]{:S(2)}) collective-permute-start(bf16[3,128,256]{2,1,0:T(8,128)(2,1)S(1)} %get-tuple-element.52), channel_id=1, source_target_pairs={{0,2},{2,4},{4,6},{6,8},{8,10},{10,12},{12,14},{14,0},{1,3},{3,5},... | collective-permute-start | bytes 589832 | tf_op jit(solution)/shard_map/ppermute | solution.py:206
  11.2 22.6 %collective-permute-start.2 = (bf16[3,128,256]{2,1,0:T(8,128)(2,1)S(1)}, bf16[3,128,256]{2,1,0:T(8,128)(2,1)S(1)}, u32[]{:S(2)}, u32[]{:S(2)}) collective-permute-start(bf16[3,128,256]{2,1,0:T(8,128)(2,1)S(1)} %get-tuple-element.54), channel_id=1, source_target_pairs={{0,8},{2,10},{4,12},{6,14},{8,0},{10,2},{12,4},{14,6},{1,9},{3,11}... | collective-permute-start | bytes 589832 | tf_op jit(solution)/shard_map/ppermute | solution.py:206
  11.2 25.2 %collective-permute-start.3 = (bf16[3,128,256]{2,1,0:T(8,128)(2,1)S(1)}, bf16[3,128,256]{2,1,0:T(8,128)(2,1)S(1)}, u32[]{:S(2)}, u32[]{:S(2)}) collective-permute-start(bf16[3,128,256]{2,1,0:T(8,128)(2,1)S(1)} %get-tuple-element.55), channel_id=1, source_target_pairs={{0,6},{2,8},{4,10},{6,12},{8,14},{10,0},{12,2},{14,4},{1,7},{3,9},... | collective-permute-start | bytes 589832 | tf_op jit(solution)/shard_map/ppermute | solution.py:206
  16.4 20.0 %collective-permute-start.4 = (bf16[3,128,256]{2,1,0:T(8,128)(2,1)S(1)}, bf16[3,128,256]{2,1,0:T(8,128)(2,1)S(1)}, u32[]{:S(2)}, u32[]{:S(2)}) collective-permute-start(bf16[3,128,256]{2,1,0:T(8,128)(2,1)S(1)} %get-tuple-element.56), channel_id=1, source_target_pairs={{0,10},{2,12},{4,14},{6,0},{8,2},{10,4},{12,6},{14,8},{1,11},{3,13... | collective-permute-start | bytes 589832 | tf_op jit(solution)/shard_map/ppermute | solution.py:206
  16.5 20.0 %collective-permute-start.6 = (bf16[3,128,256]{2,1,0:T(8,128)(2,1)S(1)}, bf16[3,128,256]{2,1,0:T(8,128)(2,1)S(1)}, u32[]{:S(2)}, u32[]{:S(2)}) collective-permute-start(bf16[3,128,256]{2,1,0:T(8,128)(2,1)S(1)} %get-tuple-element.60), channel_id=1, source_target_pairs={{0,12},{2,14},{4,0},{6,2},{8,4},{10,6},{12,8},{14,10},{1,13},{3,15... | collective-permute-start | bytes 589832 | tf_op jit(solution)/shard_map/ppermute | solution.py:206
  21.7 16.2 %collective-permute-start.5 = (bf16[3,128,256]{2,1,0:T(8,128)(2,1)S(1)}, bf16[3,128,256]{2,1,0:T(8,128)(2,1)S(1)}, u32[]{:S(2)}, u32[]{:S(2)}) collective-permute-start(bf16[3,128,256]{2,1,0:T(8,128)(2,1)S(1)} %get-tuple-element.58), channel_id=1, source_target_pairs={{0,4},{2,6},{4,8},{6,10},{8,12},{10,14},{12,0},{14,2},{1,5},{3,7},... | collective-permute-start | bytes 589832 | tf_op jit(solution)/shard_map/ppermute | solution.py:206
  44.5 15.1 %collective-permute-start.8 = (bf16[4,128,256]{2,1,0:T(8,128)(2,1)S(1)}, bf16[4,128,256]{2,1,0:T(8,128)(2,1)S(1)}, u32[]{:S(2)}, u32[]{:S(2)}) collective-permute-start(bf16[4,128,256]{2,1,0:T(8,128)(2,1)S(1)} %get-tuple-element.68), channel_id=1, source_target_pairs={{0,4},{2,6},{4,0},{6,2},{8,12},{10,14},{12,8},{14,10},{1,5},{3,7},... | collective-permute-start | bytes 786440 | tf_op jit(solution)/shard_map/ppermute | solution.py:209
  52.6 8.8 %collective-permute-start.9 = (bf16[4,128,256]{2,1,0:T(8,128)(2,1)S(1)}, bf16[4,128,256]{2,1,0:T(8,128)(2,1)S(1)}, u32[]{:S(2)}, u32[]{:S(2)}) collective-permute-start(bf16[4,128,256]{2,1,0:T(8,128)(2,1)S(1)} %get-tuple-element.70), channel_id=1, source_target_pairs={{0,2},{2,0},{4,6},{6,4},{8,10},{10,8},{12,14},{14,12},{1,3},{3,1},... | collective-permute-start | bytes 786440 | tf_op jit(solution)/shard_map/ppermute | solution.py:209
  68.4 10.5 %collective-permute-start.12 = (bf16[2,128,256]{2,1,0:T(8,128)(2,1)S(1)}, bf16[2,128,256]{2,1,0:T(8,128)(2,1)S(1)}, u32[]{:S(2)}, u32[]{:S(2)}) collective-permute-start(bf16[2,128,256]{2,1,0:T(8,128)(2,1)S(1)} %pad_maximum_fusion.2), channel_id=1, source_target_pairs={{0,8},{2,10},{4,12},{6,14},{8,0},{10,2},{12,4},{14,6},{1,9},{3,11}... | collective-permute-start | bytes 393224 | tf_op jit(solution)/shard_map/ppermute | solution.py:209
  68.8 12.7 %collective-permute-start.13 = (bf16[2,128,256]{2,1,0:T(8,128)(2,1)S(1)}, bf16[2,128,256]{2,1,0:T(8,128)(2,1)S(1)}, u32[]{:S(2)}, u32[]{:S(2)}) collective-permute-start(bf16[2,128,256]{2,1,0:T(8,128)(2,1)S(1)} %pad_maximum_fusion.3), channel_id=1, source_target_pairs={{0,8},{2,10},{4,12},{6,14},{8,0},{10,2},{12,4},{14,6},{1,9},{3,11}... | collective-permute-start | bytes 393224 | tf_op jit(solution)/shard_map/ppermute | solution.py:209
  87.2 6.9 %collective-permute-start.16 = (bf16[4,128,256]{2,1,0:T(8,128)(2,1)S(1)}, bf16[4,128,256]{2,1,0:T(8,128)(2,1)S(1)}, u32[]{:S(2)}, u32[]{:S(2)}) collective-permute-start(bf16[4,128,256]{2,1,0:T(8,128)(2,1)S(1)} %pad_maximum_fusion.1.near), channel_id=1, source_target_pairs={{0,2},{2,0},{4,6},{6,4},{8,10},{10,8},{12,14},{14,12},{1,3},{3,1},... | collective-permute-start | bytes 786440 | tf_op jit(solution)/shard_map/ppermute | solution.py:209
  88.7 6.6 %collective-permute-start.17 = (bf16[4,128,256]{2,1,0:T(8,128)(2,1)S(1)}, bf16[4,128,256]{2,1,0:T(8,128)(2,1)S(1)}, u32[]{:S(2)}, u32[]{:S(2)}) collective-permute-start(bf16[4,128,256]{2,1,0:T(8,128)(2,1)S(1)} %pad_maximum_fusion.near_other), channel_id=1, source_target_pairs={{0,4},{2,6},{4,0},{6,2},{8,12},{10,14},{12,8},{14,10},{1,5},{3,7},... | collective-permute-start | bytes 786440 | tf_op jit(solution)/shard_map/ppermute | solution.py:209
  103.9 32.0 %collective-permute-start.22 = (bf16[14,128,128]{2,1,0:T(8,128)(2,1)S(1)}, bf16[14,128,128]{2,1,0:T(8,128)(2,1)S(1)}, u32[]{:S(2)}, u32[]{:S(2)}) collective-permute-start(bf16[14,128,128]{2,1,0:T(8,128)(2,1)S(1)} %get-tuple-element.90), channel_id=1, source_target_pairs={{0,8},{2,10},{4,12},{6,14},{8,0},{10,2},{12,4},{14,6},{1,9},{3,11}... | collective-permute-start | bytes 1376264 | tf_op jit(solution)/shard_map/ppermute | solution.py:209
  105.0 10.9 %collective-permute-start.19 = (bf16[6,128,256]{2,1,0:T(8,128)(2,1)S(1)}, bf16[6,128,256]{2,1,0:T(8,128)(2,1)S(1)}, u32[]{:S(2)}, u32[]{:S(2)}) collective-permute-start(bf16[6,128,256]{2,1,0:T(8,128)(2,1)S(1)} %get-tuple-element.86), channel_id=1, source_target_pairs={{0,2},{2,0},{4,6},{6,4},{8,10},{10,8},{12,14},{14,12},{1,3},{3,1},... | collective-permute-start | bytes 1179656 | tf_op jit(solution)/shard_map/ppermute | solution.py:209
  106.5 17.8 %collective-permute-start.20 = (bf16[6,128,256]{2,1,0:T(8,128)(2,1)S(1)}, bf16[6,128,256]{2,1,0:T(8,128)(2,1)S(1)}, u32[]{:S(2)}, u32[]{:S(2)}) collective-permute-start(bf16[6,128,256]{2,1,0:T(8,128)(2,1)S(1)} %get-tuple-element.87), channel_id=1, source_target_pairs={{0,4},{2,6},{4,0},{6,2},{8,12},{10,14},{12,8},{14,10},{1,5},{3,7},... | collective-permute-start | bytes 1179656 | tf_op jit(solution)/shard_map/ppermute | solution.py:209
  108.3 39.6 %collective-permute-start.26 = (bf16[6,128,128]{2,1,0:T(8,128)(2,1)S(1)}, bf16[6,128,128]{2,1,0:T(8,128)(2,1)S(1)}, u32[]{:S(2)}, u32[]{:S(2)}) collective-permute-start(bf16[6,128,128]{2,1,0:T(8,128)(2,1)S(1)} %get-tuple-element.95), channel_id=1, source_target_pairs={{0,8},{2,10},{4,12},{6,14},{8,0},{10,2},{12,4},{14,6},{1,9},{3,11}... | collective-permute-start | bytes 589832 | tf_op jit(solution)/shard_map/ppermute | solution.py:209
  116.0 32.7 %collective-permute-start.27 = (bf16[6,128,128]{2,1,0:T(8,128)(2,1)S(1)}, bf16[6,128,128]{2,1,0:T(8,128)(2,1)S(1)}, u32[]{:S(2)}, u32[]{:S(2)}) collective-permute-start(bf16[6,128,128]{2,1,0:T(8,128)(2,1)S(1)} %get-tuple-element.97), channel_id=1, source_target_pairs={{0,10},{2,8},{4,14},{6,12},{8,2},{10,0},{12,6},{14,4},{1,11},{3,9}... | collective-permute-start | bytes 589832 | tf_op jit(solution)/shard_map/ppermute | solution.py:209
  124.3 35.1 %collective-permute-start.21 = (bf16[6,128,256]{2,1,0:T(8,128)(2,1)S(1)}, bf16[6,128,256]{2,1,0:T(8,128)(2,1)S(1)}, u32[]{:S(2)}, u32[]{:S(2)}) collective-permute-start(bf16[6,128,256]{2,1,0:T(8,128)(2,1)S(1)} %get-tuple-element.89), channel_id=1, source_target_pairs={{0,6},{2,4},{4,2},{6,0},{8,14},{10,12},{12,10},{14,8},{1,7},{3,5},... | collective-permute-start | bytes 1179656 | tf_op jit(solution)/shard_map/ppermute | solution.py:209
  136.5 10.8 %collective-permute-start.23 = (bf16[6,128,128]{2,1,0:T(8,128)(2,1)S(1)}, bf16[6,128,128]{2,1,0:T(8,128)(2,1)S(1)}, u32[]{:S(2)}, u32[]{:S(2)}) collective-permute-start(bf16[6,128,128]{2,1,0:T(8,128)(2,1)S(1)} %get-tuple-element.92), channel_id=1, source_target_pairs={{0,2},{2,0},{4,6},{6,4},{8,10},{10,8},{12,14},{14,12},{1,3},{3,1},... | collective-permute-start | bytes 589832 | tf_op jit(solution)/shard_map/ppermute | solution.py:209
  137.1 14.3 %collective-permute-start.28 = (bf16[6,128,128]{2,1,0:T(8,128)(2,1)S(1)}, bf16[6,128,128]{2,1,0:T(8,128)(2,1)S(1)}, u32[]{:S(2)}, u32[]{:S(2)}) collective-permute-start(bf16[6,128,128]{2,1,0:T(8,128)(2,1)S(1)} %get-tuple-element.99), channel_id=1, source_target_pairs={{0,12},{2,14},{4,8},{6,10},{8,4},{10,6},{12,0},{14,2},{1,13},{3,15... | collective-permute-start | bytes 589832 | tf_op jit(solution)/shard_map/ppermute | solution.py:209
  147.3 7.8 %collective-permute-start.24 = (bf16[6,128,128]{2,1,0:T(8,128)(2,1)S(1)}, bf16[6,128,128]{2,1,0:T(8,128)(2,1)S(1)}, u32[]{:S(2)}, u32[]{:S(2)}) collective-permute-start(bf16[6,128,128]{2,1,0:T(8,128)(2,1)S(1)} %get-tuple-element.93), channel_id=1, source_target_pairs={{0,4},{2,6},{4,0},{6,2},{8,12},{10,14},{12,8},{14,10},{1,5},{3,7},... | collective-permute-start | bytes 589832 | tf_op jit(solution)/shard_map/ppermute | solution.py:209
  147.9 11.5 %collective-permute-start.25 = (bf16[6,128,128]{2,1,0:T(8,128)(2,1)S(1)}, bf16[6,128,128]{2,1,0:T(8,128)(2,1)S(1)}, u32[]{:S(2)}, u32[]{:S(2)}) collective-permute-start(bf16[6,128,128]{2,1,0:T(8,128)(2,1)S(1)} %get-tuple-element.94), channel_id=1, source_target_pairs={{0,6},{2,4},{4,2},{6,0},{8,14},{10,12},{12,10},{14,8},{1,7},{3,5},... | collective-permute-start | bytes 589832 | tf_op jit(solution)/shard_map/ppermute | solution.py:209
  148.7 17.0 %collective-permute-start.29 = (bf16[6,128,128]{2,1,0:T(8,128)(2,1)S(1)}, bf16[6,128,128]{2,1,0:T(8,128)(2,1)S(1)}, u32[]{:S(2)}, u32[]{:S(2)}) collective-permute-start(bf16[6,128,128]{2,1,0:T(8,128)(2,1)S(1)} %get-tuple-element.101), channel_id=1, source_target_pairs={{0,14},{2,12},{4,10},{6,8},{8,6},{10,4},{12,2},{14,0},{1,15},{3,13... | collective-permute-start | bytes 589832 | tf_op jit(solution)/shard_map/ppermute | solution.py:209
  (11 other events, 110.2 us)

commit v17 on v16

--- a/solution.py
+++ b/solution.py
@@ -272,7 +272,7 @@
     in_table = ints([slots(*home_rows, me), slots(*mirror_rows, me)])
 
     bits = [1 << j for j in range(n.bit_length() - 1)]
-    orders = (bits[1::-1] + bits[2:], bits)
+    orders = (bits, bits[1::-1] + bits[2:])
 
     def fit(value, bits, ready=()):
         return call(
@@ -288,41 +288,38 @@
             ready,
         )
 
-    def step_together(states):
-        flat, tree = jax.tree.flatten(states)
-        return jax.tree.unflatten(tree, lax.optimization_barrier(flat))
-
-    def totals(states):
+    def totals(parts):
         last = len(bits) - 1
-        for j in range(last):
-            states = step_together(states)
-            found = []
-            for (keep, send), order in zip(states, orders):
-                value = keep + flip(send, order[j]).astype(f32)
+        parts, marks = list(parts), ([], [])
+        relative = [[0, order[last]] for order in orders]
+        for j in range(2 * last + 1):
+            for c, order in enumerate(orders):
+                lag = j - 2 + c
+                bit = order[min(j, 2 * last - j)]
+                ready = [marks[1 - c][lag]] if lag >= 0 else [parts[1][1]] if lag == -1 and j else []
+                if j <= last:
+                    keep, send = parts[c]
+                    value = keep + flip(after(send, *ready), bit).astype(f32)
                 if j < last - 1:
-                    found.append((value[0::2], value[1::2].astype(bf16)))
+                    parts[c] = (value[0::2], value[1::2].astype(bf16))
+                elif j == last - 1:
+                    turned = jnp.concatenate([value[1:], value[:1]], axis=0)
+                    parts[c] = (value, turned.astype(bf16))
+                elif j == last:
+                    parts[c] = (None, value.astype(bf16))
                 else:
-                    turned = jnp.concatenate([value[1:], value[:1]], axis=0)
-                    found.append((value, turned.astype(bf16)))
-            states = found
-        states = step_together(states)
-        states = [
-            (keep + flip(send, order[last]).astype(f32)).astype(bf16)
-            for (keep, send), order in zip(states, orders)
-        ]
-        relative = [[0, order[last]] for order in orders]
-        for j in reversed(range(last)):
-            states = step_together(states)
-            fars = [flip(near, order[j]) for near, order in zip(states, orders)]
-            relative = [r + [e ^ order[j] for e in r] for r, order in zip(relative, orders)]
-            if j == 0:
-                return [(*pair, r) for pair, r in zip(zip(states, fars), relative)]
-            states = [jnp.concatenate(pair, axis=0) for pair in zip(states, fars)]
-
-    fit_own = fit(own, orders[1])
-    fit_other = fit(other, orders[0], fit_own[:1])
-    (near_other, far_other, order_other), (near_own, far_own, order_own) = totals(
-        [tuple(fit_other), tuple(fit_own)]
+                    near = after(parts[c][1], *ready)
+                    far = flip(near, bit)
+                    relative[c] = relative[c] + [e ^ bit for e in relative[c]]
+                    both = (near, far) if j == 2 * last else (jnp.concatenate([near, far], axis=0),)
+                    parts[c] = (both[0], both[-1])
+                marks[c].append(parts[c][1])
+        return [(*pair, order) for pair, order in zip(parts, relative)]
+
+    fit_own = fit(own, orders[0])
+    fit_other = fit(other, orders[1], fit_own[:1])
+    (near_own, far_own, order_own), (near_other, far_other, order_other) = totals(
+        [tuple(fit_own), tuple(fit_other)]
     )
 
     mine, theirs = call(

time: 169 us -> 166 us (0.982)
  waiting for transfers between devices: 88.6 us -> 85.5 us
    ppermute x21, waiting for transfers between devices: 76.1 us -> 73 us  [flip(): return lax.ppermute(x, 'pair', [(s, s ^ bit) for s in range(n)])]
    unnamed x10 -> x11, local copies, waits for them, and re-layouts: 6.69 us -> 6.7 us
  transfers between devices with their start and end apart: 30 -> 30, of which waited for: 22 -> 20; matrix products, arithmetic and copies ran while one was open for 1% -> 1% of each run, Pallas kernels for 3% -> 4%
where the time goes in v17:
time: 166 us
  waiting for transfers between devices  85.5 us (52%)
  starting transfers between devices  51.3 us (31%)
  Pallas kernels  17.9 us (11%)
  local copies, waits for them, and re-layouts  6.78 us (4%)
  other arithmetic  3.73 us (2%)
    ppermute x21, waiting for transfers between devices, flip(): return lax.ppermute(x, 'pair', [(s, s ^ bit) for s in range(n)])  73 us
    ppermute x21, starting transfers between devices, flip(): return lax.ppermute(x, 'pair', [(s, s ^ bit) for s in range(n)])  35.2 us
    pallas_call x7, Pallas kernels, call(): pl.pallas_call(kernel, out_shape=out_shape, grid_spec=pltpu.PrefetchScala...  16 us
    ppermute x7, starting transfers between devices, shift(): return lax.ppermute(x, 'pair', [(s, (s + d) % n) for s in range(n)])  15.9 us
    ppermute x7, waiting for transfers between devices, shift(): return lax.ppermute(x, 'pair', [(s, (s + d) % n) for s in range(n)])  10.6 us
    unnamed x11, local copies, waits for them, and re-layouts  6.7 us
  transfers between devices with their start and end apart: 30, of which 20 were waited for; matrix products, arithmetic and copies ran while one was open for 1% of the time, Pallas kernels for 4%

profile of v17, /device:TPU:0, one launch (start us, length us, event | category | flops | bytes accessed | tf_op | source)
XLA Modules:
  0.0 166.2 jit_solution(2148521745710135721)
XLA Ops:
  5.1 6.1 %collective-permute-start.1 = (bf16[3,128,256]{2,1,0:T(8,128)(2,1)S(1)}, bf16[3,128,256]{2,1,0:T(8,128)(2,1)S(1)}, u32[]{:S(2)}, u32[]{:S(2)}) collective-permute-start(bf16[3,128,256]{2,1,0:T(8,128)(2,1)S(1)} %get-tuple-element.45), channel_id=1, source_target_pairs={{0,14},{2,0},{4,2},{6,4},{8,6},{10,8},{12,10},{14,12},{1,15},{3,1}... | collective-permute-start | bytes 589832 | tf_op jit(solution)/shard_map/ppermute | solution.py:206
  11.2 5.2 %collective-permute-start.3 = (bf16[3,128,256]{2,1,0:T(8,128)(2,1)S(1)}, bf16[3,128,256]{2,1,0:T(8,128)(2,1)S(1)}, u32[]{:S(2)}, u32[]{:S(2)}) collective-permute-start(bf16[3,128,256]{2,1,0:T(8,128)(2,1)S(1)} %get-tuple-element.47), channel_id=1, source_target_pairs={{0,6},{2,8},{4,10},{6,12},{8,14},{10,0},{12,2},{14,4},{1,7},{3,9},... | collective-permute-start | bytes 589832 | tf_op jit(solution)/shard_map/ppermute | solution.py:206
  16.5 4.6 %collective-permute-start.6 = (bf16[3,128,256]{2,1,0:T(8,128)(2,1)S(1)}, bf16[3,128,256]{2,1,0:T(8,128)(2,1)S(1)}, u32[]{:S(2)}, u32[]{:S(2)}) collective-permute-start(bf16[3,128,256]{2,1,0:T(8,128)(2,1)S(1)} %get-tuple-element.52), channel_id=1, source_target_pairs={{0,12},{2,14},{4,0},{6,2},{8,4},{10,6},{12,8},{14,10},{1,13},{3,15... | collective-permute-start | bytes 589832 | tf_op jit(solution)/shard_map/ppermute | solution.py:206
  21.8 5.2 %copy-done = bf16[14,256,2048]{2,1,0:T(8,128)(2,1)S(1)} copy-done((bf16[14,256,2048]{2,1,0:T(8,128)(2,1)S(1)}, bf16[14,256,2048]{2,1,0:T(8,128)(2,1)}, u32[]{:S(2)}) %copy-start) | copy-done | bytes 14680088
  28.0 5.7 %collective-permute-done.2.rest_2_ = bf16[3,128,256]{2,1,0:T(8,128)(2,1)S(1)} collective-permute-done((bf16[3,128,256]{2,1,0:T(8,128)(2,1)S(1)}, bf16[3,128,256]{2,1,0:T(8,128)(2,1)S(1)}, u32[]{:S(2)}, u32[]{:S(2)}) %collective-permute-start.2) | collective-permute-done | bytes 196640 | tf_op jit(solution)/shard_map/ppermute | solution.py:206
  33.7 2.7 %collective-permute-done.3.rest_3_ = bf16[3,128,256]{2,1,0:T(8,128)(2,1)S(1)} collective-permute-done((bf16[3,128,256]{2,1,0:T(8,128)(2,1)S(1)}, bf16[3,128,256]{2,1,0:T(8,128)(2,1)S(1)}, u32[]{:S(2)}, u32[]{:S(2)}) %collective-permute-start.3) | collective-permute-done | bytes 196640 | tf_op jit(solution)/shard_map/ppermute | solution.py:206
  38.9 2.8 %fit.2 = (f32[4,128,256]{2,1,0:T(8,128)S(1)}, bf16[4,128,256]{2,1,0:T(8,128)(2,1)S(1)}) custom-call(s32[8]{0:T(128)S(1)} %iota_xor_fusion.table, bf16[14,1,256]{2,1,0:T(2,128)(2,1)S(1)} %copy.10.factor, bf16[14,128,256]{2,1,0:T(8,128)(2,1)S(1)} %gather_density.1.density, bf16[14,256,2048]{2,1,0:T(8,128)(2,1)S(1)} %load_integrals.1.rest_8_.integrals), custom_call_target="tpu_custom_call" | custom-call | tf_op jit(solution)/shard_map/fit/pallas_call | solution.py:191
  41.7 5.2 %collective-permute-start.7 = (bf16[4,128,256]{2,1,0:T(8,128)(2,1)S(1)}, bf16[4,128,256]{2,1,0:T(8,128)(2,1)S(1)}, u32[]{:S(2)}, u32[]{:S(2)}) collective-permute-start(bf16[4,128,256]{2,1,0:T(8,128)(2,1)S(1)} %get-tuple-element.56), channel_id=1, source_target_pairs={{0,2},{2,0},{4,6},{6,4},{8,10},{10,8},{12,14},{14,12},{1,3},{3,1},... | collective-permute-start | bytes 786440 | tf_op jit(solution)/shard_map/ppermute | solution.py:209
  46.9 2.7 %fit.3 = (f32[4,128,256]{2,1,0:T(8,128)S(1)}, bf16[4,128,256]{2,1,0:T(8,128)(2,1)S(1)}) custom-call(s32[8]{0:T(128)S(1)} %iota_xor_fusion.table, bf16[14,1,256]{2,1,0:T(2,128)(2,1)S(1)} %copy.10.factor, bf16[14,128,256]{2,1,0:T(8,128)(2,1)S(1)} %collective-permute-done.8.density, bf16[14,256,2048]{2,1,0:T(8,128)(2,1)S(1)} %load_integrals.1.rest_8_.integrals, ...), custom_call_target="tpu_custom_call" | custom-call | tf_op jit(solution)/shard_map/fit/pallas_call | solution.py:191
  49.6 5.2 %collective-permute-start.9 = (bf16[4,128,256]{2,1,0:T(8,128)(2,1)S(1)}, bf16[4,128,256]{2,1,0:T(8,128)(2,1)S(1)}, u32[]{:S(2)}, u32[]{:S(2)}) collective-permute-start(bf16[4,128,256]{2,1,0:T(8,128)(2,1)S(1)} %get-tuple-element.58), channel_id=1, source_target_pairs={{0,4},{2,6},{4,0},{6,2},{8,12},{10,14},{12,8},{14,10},{1,5},{3,7},... | collective-permute-start | bytes 786440 | tf_op jit(solution)/shard_map/ppermute | solution.py:209
  54.9 6.6 %collective-permute-done.9 = bf16[4,128,256]{2,1,0:T(8,128)(2,1)S(1)} collective-permute-done((bf16[4,128,256]{2,1,0:T(8,128)(2,1)S(1)}, bf16[4,128,256]{2,1,0:T(8,128)(2,1)S(1)}, u32[]{:S(2)}, u32[]{:S(2)}) %collective-permute-start.9) | collective-permute-done | bytes 262176 | tf_op jit(solution)/shard_map/ppermute | solution.py:209
  63.7 3.0 %collective-permute-done.10 = bf16[2,128,256]{2,1,0:T(8,128)(2,1)S(1)} collective-permute-done((bf16[2,128,256]{2,1,0:T(8,128)(2,1)S(1)}, bf16[2,128,256]{2,1,0:T(8,128)(2,1)S(1)}, u32[]{:S(2)}, u32[]{:S(2)}) %collective-permute-start.10) | collective-permute-done | bytes 131104 | tf_op jit(solution)/shard_map/ppermute | solution.py:209
  70.0 8.3 %collective-permute-done.11 = bf16[2,128,256]{2,1,0:T(8,128)(2,1)S(1)} collective-permute-done((bf16[2,128,256]{2,1,0:T(8,128)(2,1)S(1)}, bf16[2,128,256]{2,1,0:T(8,128)(2,1)S(1)}, u32[]{:S(2)}, u32[]{:S(2)}) %collective-permute-start.11) | collective-permute-done | bytes 131104 | tf_op jit(solution)/shard_map/ppermute | solution.py:209
  86.6 5.5 %collective-permute-done.15.far = bf16[4,128,256]{2,1,0:T(8,128)(2,1)S(1)} collective-permute-done((bf16[4,128,256]{2,1,0:T(8,128)(2,1)S(1)}, bf16[4,128,256]{2,1,0:T(8,128)(2,1)S(1)}, u32[]{:S(2)}, u32[]{:S(2)}) %collective-permute-start.15) | collective-permute-done | bytes 262176 | tf_op jit(solution)/shard_map/ppermute | solution.py:209
  92.8 5.0 %apply.1 = (f32[14,128,256]{2,1,0:T(8,128)S(1)}, bf16[14,128,256]{2,1,0:T(8,128)(2,1)S(1)}) custom-call(s32[8]{0:T(128)S(1)} %iota_xor_fusion.table, bf16[14,256,2048]{2,1,0:T(8,128)(2,1)S(1)} %load_integrals.1.rest_8_.integrals, bf16[4,128,256]{2,1,0:T(8,128)(2,1)S(1)} %constant_dynamic-update-slice_fusion.near, ...), custom_call_target="tpu_custom_call" | custom-call | tf_op jit(solution)/shard_map/apply/pallas_call | solution.py:191
  106.5 7.1 %collective-permute-done.19.rest_0_.rest_1_ = bf16[6,128,256]{2,1,0:T(8,128)(2,1)S(1)} collective-permute-done((bf16[6,128,256]{2,1,0:T(8,128)(2,1)S(1)}, bf16[6,128,256]{2,1,0:T(8,128)(2,1)S(1)}, u32[]{:S(2)}, u32[]{:S(2)}) %collective-permute-start.19) | collective-permute-done | bytes 393248 | tf_op jit(solution)/shard_map/ppermute | solution.py:209
  113.5 2.6 %collective-permute-start.27 = (bf16[6,128,128]{2,1,0:T(8,128)(2,1)S(1)}, bf16[6,128,128]{2,1,0:T(8,128)(2,1)S(1)}, u32[]{:S(2)}, u32[]{:S(2)}) collective-permute-start(bf16[6,128,128]{2,1,0:T(8,128)(2,1)S(1)} %get-tuple-element.81), channel_id=1, source_target_pairs={{0,10},{2,8},{4,14},{6,12},{8,2},{10,0},{12,6},{14,4},{1,11},{3,9}... | collective-permute-start | bytes 589832 | tf_op jit(solution)/shard_map/ppermute | solution.py:209
  116.1 5.7 %collective-permute-done.20.rest_1_.rest_2_ = bf16[6,128,256]{2,1,0:T(8,128)(2,1)S(1)} collective-permute-done((bf16[6,128,256]{2,1,0:T(8,128)(2,1)S(1)}, bf16[6,128,256]{2,1,0:T(8,128)(2,1)S(1)}, u32[]{:S(2)}, u32[]{:S(2)}) %collective-permute-start.20) | collective-permute-done | bytes 393248 | tf_op jit(solution)/shard_map/ppermute | solution.py:209
  124.2 9.0 %collective-permute-done.22.whole = bf16[14,128,128]{2,1,0:T(8,128)(2,1)S(1)} collective-permute-done((bf16[14,128,128]{2,1,0:T(8,128)(2,1)S(1)}, bf16[14,128,128]{2,1,0:T(8,128)(2,1)S(1)}, u32[]{:S(2)}, u32[]{:S(2)}) %collective-permute-start.22) | collective-permute-done | bytes 458784 | tf_op jit(solution)/shard_map/ppermute | solution.py:209
  136.5 7.2 %collective-permute-done.23.rest_5_ = bf16[6,128,128]{2,1,0:T(8,128)(2,1)S(1)} collective-permute-done((bf16[6,128,128]{2,1,0:T(8,128)(2,1)S(1)}, bf16[6,128,128]{2,1,0:T(8,128)(2,1)S(1)}, u32[]{:S(2)}, u32[]{:S(2)}) %collective-permute-start.23) | collective-permute-done | bytes 196640 | tf_op jit(solution)/shard_map/ppermute | solution.py:209
  146.7 2.7 %collective-permute-start.29 = (bf16[6,128,128]{2,1,0:T(8,128)(2,1)S(1)}, bf16[6,128,128]{2,1,0:T(8,128)(2,1)S(1)}, u32[]{:S(2)}, u32[]{:S(2)}) collective-permute-start(bf16[6,128,128]{2,1,0:T(8,128)(2,1)S(1)} %get-tuple-element.85), channel_id=1, source_target_pairs={{0,14},{2,12},{4,10},{6,8},{8,6},{10,4},{12,2},{14,0},{1,15},{3,13... | collective-permute-start | bytes 589832 | tf_op jit(solution)/shard_map/ppermute | solution.py:209
  151.5 5.4 %collective-permute-done.25.rest_7_ = bf16[6,128,128]{2,1,0:T(8,128)(2,1)S(1)} collective-permute-done((bf16[6,128,128]{2,1,0:T(8,128)(2,1)S(1)}, bf16[6,128,128]{2,1,0:T(8,128)(2,1)S(1)}, u32[]{:S(2)}, u32[]{:S(2)}) %collective-permute-start.25) | collective-permute-done | bytes 196640 | tf_op jit(solution)/shard_map/ppermute | solution.py:209
  156.9 6.2 %collective-permute-done.29.rest_11_ = bf16[6,128,128]{2,1,0:T(8,128)(2,1)S(1)} collective-permute-done((bf16[6,128,128]{2,1,0:T(8,128)(2,1)S(1)}, bf16[6,128,128]{2,1,0:T(8,128)(2,1)S(1)}, u32[]{:S(2)}, u32[]{:S(2)}) %collective-permute-start.29) | collective-permute-done | bytes 196640 | tf_op jit(solution)/shard_map/ppermute | solution.py:209
  163.1 3.1 %gather_coulomb.1 = (bf16[14,256,128]{2,1,0:T(8,128)(2,1)}, bf16[14,256,128]{2,1,0:T(8,128)(2,1)}) custom-call(s32[48]{0:T(128)S(1)} %pad_add_fusion.1.table, bf16[6,128,256]{2,1,0:T(8,128)(2,1)S(1)} %get-tuple-element.69.rest_0_, bf16[6,128,256]{2,1,0:T(8,128)(2,1)S(1)} %collective-permute-done.19.rest_0_.rest_1_, ...), custom_call_target="tpu_custom_call" | custom-call | tf_op jit(solution)/shard_map/gather_coulomb/pallas_call | solution.py:191
  (99 shorter events, 42.5 us)
Async XLA Ops:
  5.1 11.4 %collective-permute-start.1 = (bf16[3,128,256]{2,1,0:T(8,128)(2,1)S(1)}, bf16[3,128,256]{2,1,0:T(8,128)(2,1)S(1)}, u32[]{:S(2)}, u32[]{:S(2)}) collective-permute-start(bf16[3,128,256]{2,1,0:T(8,128)(2,1)S(1)} %get-tuple-element.45), channel_id=1, source_target_pairs={{0,14},{2,0},{4,2},{6,4},{8,6},{10,8},{12,10},{14,12},{1,15},{3,1}... | collective-permute-start | bytes 589832 | tf_op jit(solution)/shard_map/ppermute | solution.py:206
  11.1 10.6 %collective-permute-start = (bf16[3,128,256]{2,1,0:T(8,128)(2,1)S(1)}, bf16[3,128,256]{2,1,0:T(8,128)(2,1)S(1)}, u32[]{:S(2)}, u32[]{:S(2)}) collective-permute-start(bf16[3,128,256]{2,1,0:T(8,128)(2,1)S(1)} %get-tuple-element.44), channel_id=1, source_target_pairs={{0,2},{2,4},{4,6},{6,8},{8,10},{10,12},{12,14},{14,0},{1,3},{3,5},... | collective-permute-start | bytes 589832 | tf_op jit(solution)/shard_map/ppermute | solution.py:206
  11.2 22.6 %collective-permute-start.2 = (bf16[3,128,256]{2,1,0:T(8,128)(2,1)S(1)}, bf16[3,128,256]{2,1,0:T(8,128)(2,1)S(1)}, u32[]{:S(2)}, u32[]{:S(2)}) collective-permute-start(bf16[3,128,256]{2,1,0:T(8,128)(2,1)S(1)} %get-tuple-element.46), channel_id=1, source_target_pairs={{0,8},{2,10},{4,12},{6,14},{8,0},{10,2},{12,4},{14,6},{1,9},{3,11}... | collective-permute-start | bytes 589832 | tf_op jit(solution)/shard_map/ppermute | solution.py:206
  11.2 25.2 %collective-permute-start.3 = (bf16[3,128,256]{2,1,0:T(8,128)(2,1)S(1)}, bf16[3,128,256]{2,1,0:T(8,128)(2,1)S(1)}, u32[]{:S(2)}, u32[]{:S(2)}) collective-permute-start(bf16[3,128,256]{2,1,0:T(8,128)(2,1)S(1)} %get-tuple-element.47), channel_id=1, source_target_pairs={{0,6},{2,8},{4,10},{6,12},{8,14},{10,0},{12,2},{14,4},{1,7},{3,9},... | collective-permute-start | bytes 589832 | tf_op jit(solution)/shard_map/ppermute | solution.py:206
  16.4 20.0 %collective-permute-start.4 = (bf16[3,128,256]{2,1,0:T(8,128)(2,1)S(1)}, bf16[3,128,256]{2,1,0:T(8,128)(2,1)S(1)}, u32[]{:S(2)}, u32[]{:S(2)}) collective-permute-start(bf16[3,128,256]{2,1,0:T(8,128)(2,1)S(1)} %get-tuple-element.48), channel_id=1, source_target_pairs={{0,10},{2,12},{4,14},{6,0},{8,2},{10,4},{12,6},{14,8},{1,11},{3,13... | collective-permute-start | bytes 589832 | tf_op jit(solution)/shard_map/ppermute | solution.py:206
  16.5 20.0 %collective-permute-start.6 = (bf16[3,128,256]{2,1,0:T(8,128)(2,1)S(1)}, bf16[3,128,256]{2,1,0:T(8,128)(2,1)S(1)}, u32[]{:S(2)}, u32[]{:S(2)}) collective-permute-start(bf16[3,128,256]{2,1,0:T(8,128)(2,1)S(1)} %get-tuple-element.52), channel_id=1, source_target_pairs={{0,12},{2,14},{4,0},{6,2},{8,4},{10,6},{12,8},{14,10},{1,13},{3,15... | collective-permute-start | bytes 589832 | tf_op jit(solution)/shard_map/ppermute | solution.py:206
  21.7 16.2 %collective-permute-start.5 = (bf16[3,128,256]{2,1,0:T(8,128)(2,1)S(1)}, bf16[3,128,256]{2,1,0:T(8,128)(2,1)S(1)}, u32[]{:S(2)}, u32[]{:S(2)}) collective-permute-start(bf16[3,128,256]{2,1,0:T(8,128)(2,1)S(1)} %get-tuple-element.50), channel_id=1, source_target_pairs={{0,4},{2,6},{4,8},{6,10},{8,12},{10,14},{12,0},{14,2},{1,5},{3,7},... | collective-permute-start | bytes 589832 | tf_op jit(solution)/shard_map/ppermute | solution.py:206
  38.7 8.2 %collective-permute-start.8 = (bf16[14,128,256]{2,1,0:T(8,128)(2,1)S(1)}, bf16[14,128,256]{2,1,0:T(8,128)(2,1)S(1)}, u32[]{:S(2)}, u32[]{:S(2)}) collective-permute-start(bf16[14,128,256]{2,1,0:T(8,128)(2,1)S(1)} %gather_density.1.density), channel_id=1, source_target_pairs={{0,1},{1,0},{2,3},{3,2},{4,5},{5,4},{6,7},{7,6},{8,9},{9,8},{10,11... | collective-permute-start | bytes 2752520 | tf_op jit(solution)/shard_map/ppermute | solution.py:212
  41.7 13.1 %collective-permute-start.7 = (bf16[4,128,256]{2,1,0:T(8,128)(2,1)S(1)}, bf16[4,128,256]{2,1,0:T(8,128)(2,1)S(1)}, u32[]{:S(2)}, u32[]{:S(2)}) collective-permute-start(bf16[4,128,256]{2,1,0:T(8,128)(2,1)S(1)} %get-tuple-element.56), channel_id=1, source_target_pairs={{0,2},{2,0},{4,6},{6,4},{8,10},{10,8},{12,14},{14,12},{1,3},{3,1},... | collective-permute-start | bytes 786440 | tf_op jit(solution)/shard_map/ppermute | solution.py:209
  49.6 11.9 %collective-permute-start.9 = (bf16[4,128,256]{2,1,0:T(8,128)(2,1)S(1)}, bf16[4,128,256]{2,1,0:T(8,128)(2,1)S(1)}, u32[]{:S(2)}, u32[]{:S(2)}) collective-permute-start(bf16[4,128,256]{2,1,0:T(8,128)(2,1)S(1)} %get-tuple-element.58), channel_id=1, source_target_pairs={{0,4},{2,6},{4,0},{6,2},{8,12},{10,14},{12,8},{14,10},{1,5},{3,7},... | collective-permute-start | bytes 786440 | tf_op jit(solution)/shard_map/ppermute | solution.py:209
  66.8 11.4 %collective-permute-start.11 = (bf16[2,128,256]{2,1,0:T(8,128)(2,1)S(1)}, bf16[2,128,256]{2,1,0:T(8,128)(2,1)S(1)}, u32[]{:S(2)}, u32[]{:S(2)}) collective-permute-start(bf16[2,128,256]{2,1,0:T(8,128)(2,1)S(1)} %pad_maximum_fusion.1), channel_id=1, source_target_pairs={{0,8},{2,10},{4,12},{6,14},{8,0},{10,2},{12,4},{14,6},{1,9},{3,11}... | collective-permute-start | bytes 393224 | tf_op jit(solution)/shard_map/ppermute | solution.py:209
  68.5 11.9 %collective-permute-start.14 = (bf16[2,128,256]{2,1,0:T(8,128)(2,1)S(1)}, bf16[2,128,256]{2,1,0:T(8,128)(2,1)S(1)}, u32[]{:S(2)}, u32[]{:S(2)}) collective-permute-start(bf16[2,128,256]{2,1,0:T(8,128)(2,1)S(1)} %pad_maximum_fusion.2), channel_id=1, source_target_pairs={{0,8},{2,10},{4,12},{6,14},{8,0},{10,2},{12,4},{14,6},{1,9},{3,11}... | collective-permute-start | bytes 393224 | tf_op jit(solution)/shard_map/ppermute | solution.py:209
  85.6 6.5 %collective-permute-start.15 = (bf16[4,128,256]{2,1,0:T(8,128)(2,1)S(1)}, bf16[4,128,256]{2,1,0:T(8,128)(2,1)S(1)}, u32[]{:S(2)}, u32[]{:S(2)}) collective-permute-start(bf16[4,128,256]{2,1,0:T(8,128)(2,1)S(1)} %constant_dynamic-update-slice_fusion.near), channel_id=1, source_target_pairs={{0,2},{2,0},{4,6},{6,4},{8,10},{10,8},{12,14},{14,12},{1,3},{3,1},... | collective-permute-start | bytes 786440 | tf_op jit(solution)/shard_map/ppermute | solution.py:209
  101.4 31.8 %collective-permute-start.22 = (bf16[14,128,128]{2,1,0:T(8,128)(2,1)S(1)}, bf16[14,128,128]{2,1,0:T(8,128)(2,1)S(1)}, u32[]{:S(2)}, u32[]{:S(2)}) collective-permute-start(bf16[14,128,128]{2,1,0:T(8,128)(2,1)S(1)} %get-tuple-element.74), channel_id=1, source_target_pairs={{0,8},{2,10},{4,12},{6,14},{8,0},{10,2},{12,4},{14,6},{1,9},{3,11}... | collective-permute-start | bytes 1376264 | tf_op jit(solution)/shard_map/ppermute | solution.py:209
  102.6 10.9 %collective-permute-start.19 = (bf16[6,128,256]{2,1,0:T(8,128)(2,1)S(1)}, bf16[6,128,256]{2,1,0:T(8,128)(2,1)S(1)}, u32[]{:S(2)}, u32[]{:S(2)}) collective-permute-start(bf16[6,128,256]{2,1,0:T(8,128)(2,1)S(1)} %get-tuple-element.70), channel_id=1, source_target_pairs={{0,2},{2,0},{4,6},{6,4},{8,10},{10,8},{12,14},{14,12},{1,3},{3,1},... | collective-permute-start | bytes 1179656 | tf_op jit(solution)/shard_map/ppermute | solution.py:209
  103.1 18.8 %collective-permute-start.20 = (bf16[6,128,256]{2,1,0:T(8,128)(2,1)S(1)}, bf16[6,128,256]{2,1,0:T(8,128)(2,1)S(1)}, u32[]{:S(2)}, u32[]{:S(2)}) collective-permute-start(bf16[6,128,256]{2,1,0:T(8,128)(2,1)S(1)} %get-tuple-element.71), channel_id=1, source_target_pairs={{0,4},{2,6},{4,0},{6,2},{8,12},{10,14},{12,8},{14,10},{1,5},{3,7},... | collective-permute-start | bytes 1179656 | tf_op jit(solution)/shard_map/ppermute | solution.py:209
  105.3 40.2 %collective-permute-start.26 = (bf16[6,128,128]{2,1,0:T(8,128)(2,1)S(1)}, bf16[6,128,128]{2,1,0:T(8,128)(2,1)S(1)}, u32[]{:S(2)}, u32[]{:S(2)}) collective-permute-start(bf16[6,128,128]{2,1,0:T(8,128)(2,1)S(1)} %get-tuple-element.79), channel_id=1, source_target_pairs={{0,8},{2,10},{4,12},{6,14},{8,0},{10,2},{12,4},{14,6},{1,9},{3,11}... | collective-permute-start | bytes 589832 | tf_op jit(solution)/shard_map/ppermute | solution.py:209
  113.5 33.1 %collective-permute-start.27 = (bf16[6,128,128]{2,1,0:T(8,128)(2,1)S(1)}, bf16[6,128,128]{2,1,0:T(8,128)(2,1)S(1)}, u32[]{:S(2)}, u32[]{:S(2)}) collective-permute-start(bf16[6,128,128]{2,1,0:T(8,128)(2,1)S(1)} %get-tuple-element.81), channel_id=1, source_target_pairs={{0,10},{2,8},{4,14},{6,12},{8,2},{10,0},{12,6},{14,4},{1,11},{3,9}... | collective-permute-start | bytes 589832 | tf_op jit(solution)/shard_map/ppermute | solution.py:209
  121.9 35.0 %collective-permute-start.21 = (bf16[6,128,256]{2,1,0:T(8,128)(2,1)S(1)}, bf16[6,128,256]{2,1,0:T(8,128)(2,1)S(1)}, u32[]{:S(2)}, u32[]{:S(2)}) collective-permute-start(bf16[6,128,256]{2,1,0:T(8,128)(2,1)S(1)} %get-tuple-element.73), channel_id=1, source_target_pairs={{0,6},{2,4},{4,2},{6,0},{8,14},{10,12},{12,10},{14,8},{1,7},{3,5},... | collective-permute-start | bytes 1179656 | tf_op jit(solution)/shard_map/ppermute | solution.py:209
  133.8 9.9 %collective-permute-start.23 = (bf16[6,128,128]{2,1,0:T(8,128)(2,1)S(1)}, bf16[6,128,128]{2,1,0:T(8,128)(2,1)S(1)}, u32[]{:S(2)}, u32[]{:S(2)}) collective-permute-start(bf16[6,128,128]{2,1,0:T(8,128)(2,1)S(1)} %get-tuple-element.76), channel_id=1, source_target_pairs={{0,2},{2,0},{4,6},{6,4},{8,10},{10,8},{12,14},{14,12},{1,3},{3,1},... | collective-permute-start | bytes 589832 | tf_op jit(solution)/shard_map/ppermute | solution.py:209
  134.9 14.6 %collective-permute-start.28 = (bf16[6,128,128]{2,1,0:T(8,128)(2,1)S(1)}, bf16[6,128,128]{2,1,0:T(8,128)(2,1)S(1)}, u32[]{:S(2)}, u32[]{:S(2)}) collective-permute-start(bf16[6,128,128]{2,1,0:T(8,128)(2,1)S(1)} %get-tuple-element.83), channel_id=1, source_target_pairs={{0,12},{2,14},{4,8},{6,10},{8,4},{10,6},{12,0},{14,2},{1,13},{3,15... | collective-permute-start | bytes 589832 | tf_op jit(solution)/shard_map/ppermute | solution.py:209
  143.7 7.8 %collective-permute-start.24 = (bf16[6,128,128]{2,1,0:T(8,128)(2,1)S(1)}, bf16[6,128,128]{2,1,0:T(8,128)(2,1)S(1)}, u32[]{:S(2)}, u32[]{:S(2)}) collective-permute-start(bf16[6,128,128]{2,1,0:T(8,128)(2,1)S(1)} %get-tuple-element.77), channel_id=1, source_target_pairs={{0,4},{2,6},{4,0},{6,2},{8,12},{10,14},{12,8},{14,10},{1,5},{3,7},... | collective-permute-start | bytes 589832 | tf_op jit(solution)/shard_map/ppermute | solution.py:209
  145.4 11.5 %collective-permute-start.25 = (bf16[6,128,128]{2,1,0:T(8,128)(2,1)S(1)}, bf16[6,128,128]{2,1,0:T(8,128)(2,1)S(1)}, u32[]{:S(2)}, u32[]{:S(2)}) collective-permute-start(bf16[6,128,128]{2,1,0:T(8,128)(2,1)S(1)} %get-tuple-element.78), channel_id=1, source_target_pairs={{0,6},{2,4},{4,2},{6,0},{8,14},{10,12},{12,10},{14,8},{1,7},{3,5},... | collective-permute-start | bytes 589832 | tf_op jit(solution)/shard_map/ppermute | solution.py:209
  146.7 16.5 %collective-permute-start.29 = (bf16[6,128,128]{2,1,0:T(8,128)(2,1)S(1)}, bf16[6,128,128]{2,1,0:T(8,128)(2,1)S(1)}, u32[]{:S(2)}, u32[]{:S(2)}) collective-permute-start(bf16[6,128,128]{2,1,0:T(8,128)(2,1)S(1)} %get-tuple-element.85), channel_id=1, source_target_pairs={{0,14},{2,12},{4,10},{6,8},{8,6},{10,4},{12,2},{14,0},{1,15},{3,13... | collective-permute-start | bytes 589832 | tf_op jit(solution)/shard_map/ppermute | solution.py:209
  (11 other events, 105.9 us)

commit v18 on v17

--- a/solution.py
+++ b/solution.py
@@ -361,7 +361,9 @@
         [in_vmem] * (n // 2),
         near[1:3],
     )
-    passed = [passed[0]] + [flip(passed[d], d) for d in range(1, n // 2)]
+    passed = [passed[0], flip(passed[1], 1)] + [
+        flip(after(passed[d], far[min(d - 2, 1)]), d) for d in range(2, n // 2)
+    ]
     for i in range(3, n // 2):
         far.append(direct(i, passed[i - 2]))
     return call(

time: 166 us -> 163 us (0.982)
  starting transfers between devices: 51.3 us -> 48.2 us
    ppermute x21, starting transfers between devices: 35.2 us -> 32.1 us  [flip(): return lax.ppermute(x, 'pair', [(s, s ^ bit) for s in range(n)])]
where the time goes in v18:
time: 163 us; the launch traced here: 162 us
  waiting for transfers between devices  84.8 us (52%)
  starting transfers between devices  48.2 us (30%)
  Pallas kernels  17.9 us (11%)
  local copies, waits for them, and re-layouts  6.78 us (4%)
  other arithmetic  3.73 us (2%)
    ppermute x21, waiting for transfers between devices, flip(): return lax.ppermute(x, 'pair', [(s, s ^ bit) for s in range(n)])  72.3 us
    ppermute x21, starting transfers between devices, flip(): return lax.ppermute(x, 'pair', [(s, s ^ bit) for s in range(n)])  32.1 us
    pallas_call x7, Pallas kernels, call(): pl.pallas_call(kernel, out_shape=out_shape, grid_spec=pltpu.PrefetchScala...  16 us
    ppermute x7, starting transfers between devices, shift(): return lax.ppermute(x, 'pair', [(s, (s + d) % n) for s in range(n)])  15.9 us
    ppermute x7, waiting for transfers between devices, shift(): return lax.ppermute(x, 'pair', [(s, (s + d) % n) for s in range(n)])  10.6 us
    unnamed x11, local copies, waits for them, and re-layouts  6.7 us
  transfers between devices with their start and end apart: 30, of which 20 were waited for; matrix products, arithmetic and copies ran while one was open for 1% of the time, Pallas kernels for 4%

profile of v18, /device:TPU:0, one launch (start us, length us, event | category | flops | bytes accessed | tf_op | source)
XLA Modules:
  0.0 162.4 jit_solution(7320410859969414374)
XLA Ops:
  5.1 6.1 %collective-permute-start.1 = (bf16[3,128,256]{2,1,0:T(8,128)(2,1)S(1)}, bf16[3,128,256]{2,1,0:T(8,128)(2,1)S(1)}, u32[]{:S(2)}, u32[]{:S(2)}) collective-permute-start(bf16[3,128,256]{2,1,0:T(8,128)(2,1)S(1)} %get-tuple-element.47), channel_id=1, source_target_pairs={{0,14},{2,0},{4,2},{6,4},{8,6},{10,8},{12,10},{14,12},{1,15},{3,1}... | collective-permute-start | bytes 589832 | tf_op jit(solution)/shard_map/ppermute | solution.py:206
  11.2 5.2 %collective-permute-start.3 = (bf16[3,128,256]{2,1,0:T(8,128)(2,1)S(1)}, bf16[3,128,256]{2,1,0:T(8,128)(2,1)S(1)}, u32[]{:S(2)}, u32[]{:S(2)}) collective-permute-start(bf16[3,128,256]{2,1,0:T(8,128)(2,1)S(1)} %get-tuple-element.49), channel_id=1, source_target_pairs={{0,6},{2,8},{4,10},{6,12},{8,14},{10,0},{12,2},{14,4},{1,7},{3,9},... | collective-permute-start | bytes 589832 | tf_op jit(solution)/shard_map/ppermute | solution.py:206
  16.5 4.6 %collective-permute-start.6 = (bf16[3,128,256]{2,1,0:T(8,128)(2,1)S(1)}, bf16[3,128,256]{2,1,0:T(8,128)(2,1)S(1)}, u32[]{:S(2)}, u32[]{:S(2)}) collective-permute-start(bf16[3,128,256]{2,1,0:T(8,128)(2,1)S(1)} %get-tuple-element.54), channel_id=1, source_target_pairs={{0,12},{2,14},{4,0},{6,2},{8,4},{10,6},{12,8},{14,10},{1,13},{3,15... | collective-permute-start | bytes 589832 | tf_op jit(solution)/shard_map/ppermute | solution.py:206
  21.8 5.2 %copy-done = bf16[14,256,2048]{2,1,0:T(8,128)(2,1)S(1)} copy-done((bf16[14,256,2048]{2,1,0:T(8,128)(2,1)S(1)}, bf16[14,256,2048]{2,1,0:T(8,128)(2,1)}, u32[]{:S(2)}) %copy-start) | copy-done | bytes 14680088
  28.0 5.7 %collective-permute-done.2.rest_2_ = bf16[3,128,256]{2,1,0:T(8,128)(2,1)S(1)} collective-permute-done((bf16[3,128,256]{2,1,0:T(8,128)(2,1)S(1)}, bf16[3,128,256]{2,1,0:T(8,128)(2,1)S(1)}, u32[]{:S(2)}, u32[]{:S(2)}) %collective-permute-start.2) | collective-permute-done | bytes 196640 | tf_op jit(solution)/shard_map/ppermute | solution.py:206
  33.7 2.7 %collective-permute-done.3.rest_3_ = bf16[3,128,256]{2,1,0:T(8,128)(2,1)S(1)} collective-permute-done((bf16[3,128,256]{2,1,0:T(8,128)(2,1)S(1)}, bf16[3,128,256]{2,1,0:T(8,128)(2,1)S(1)}, u32[]{:S(2)}, u32[]{:S(2)}) %collective-permute-start.3) | collective-permute-done | bytes 196640 | tf_op jit(solution)/shard_map/ppermute | solution.py:206
  38.9 2.8 %fit.2 = (f32[4,128,256]{2,1,0:T(8,128)S(1)}, bf16[4,128,256]{2,1,0:T(8,128)(2,1)S(1)}) custom-call(s32[8]{0:T(128)S(1)} %iota_xor_fusion.table, bf16[14,1,256]{2,1,0:T(2,128)(2,1)S(1)} %copy.10.factor, bf16[14,128,256]{2,1,0:T(8,128)(2,1)S(1)} %gather_density.1.density, bf16[14,256,2048]{2,1,0:T(8,128)(2,1)S(1)} %load_integrals.1.rest_8_.integrals), custom_call_target="tpu_custom_call" | custom-call | tf_op jit(solution)/shard_map/fit/pallas_call | solution.py:191
  41.7 5.2 %collective-permute-start.7 = (bf16[4,128,256]{2,1,0:T(8,128)(2,1)S(1)}, bf16[4,128,256]{2,1,0:T(8,128)(2,1)S(1)}, u32[]{:S(2)}, u32[]{:S(2)}) collective-permute-start(bf16[4,128,256]{2,1,0:T(8,128)(2,1)S(1)} %get-tuple-element.58), channel_id=1, source_target_pairs={{0,2},{2,0},{4,6},{6,4},{8,10},{10,8},{12,14},{14,12},{1,3},{3,1},... | collective-permute-start | bytes 786440 | tf_op jit(solution)/shard_map/ppermute | solution.py:209
  46.9 2.7 %fit.3 = (f32[4,128,256]{2,1,0:T(8,128)S(1)}, bf16[4,128,256]{2,1,0:T(8,128)(2,1)S(1)}) custom-call(s32[8]{0:T(128)S(1)} %iota_xor_fusion.table, bf16[14,1,256]{2,1,0:T(2,128)(2,1)S(1)} %copy.10.factor, bf16[14,128,256]{2,1,0:T(8,128)(2,1)S(1)} %collective-permute-done.8.density, bf16[14,256,2048]{2,1,0:T(8,128)(2,1)S(1)} %load_integrals.1.rest_8_.integrals, ...), custom_call_target="tpu_custom_call" | custom-call | tf_op jit(solution)/shard_map/fit/pallas_call | solution.py:191
  49.6 5.2 %collective-permute-start.9 = (bf16[4,128,256]{2,1,0:T(8,128)(2,1)S(1)}, bf16[4,128,256]{2,1,0:T(8,128)(2,1)S(1)}, u32[]{:S(2)}, u32[]{:S(2)}) collective-permute-start(bf16[4,128,256]{2,1,0:T(8,128)(2,1)S(1)} %get-tuple-element.60), channel_id=1, source_target_pairs={{0,4},{2,6},{4,0},{6,2},{8,12},{10,14},{12,8},{14,10},{1,5},{3,7},... | collective-permute-start | bytes 786440 | tf_op jit(solution)/shard_map/ppermute | solution.py:209
  54.9 6.6 %collective-permute-done.9 = bf16[4,128,256]{2,1,0:T(8,128)(2,1)S(1)} collective-permute-done((bf16[4,128,256]{2,1,0:T(8,128)(2,1)S(1)}, bf16[4,128,256]{2,1,0:T(8,128)(2,1)S(1)}, u32[]{:S(2)}, u32[]{:S(2)}) %collective-permute-start.9) | collective-permute-done | bytes 262176 | tf_op jit(solution)/shard_map/ppermute | solution.py:209
  63.7 3.0 %collective-permute-done.10 = bf16[2,128,256]{2,1,0:T(8,128)(2,1)S(1)} collective-permute-done((bf16[2,128,256]{2,1,0:T(8,128)(2,1)S(1)}, bf16[2,128,256]{2,1,0:T(8,128)(2,1)S(1)}, u32[]{:S(2)}, u32[]{:S(2)}) %collective-permute-start.10) | collective-permute-done | bytes 131104 | tf_op jit(solution)/shard_map/ppermute | solution.py:209
  70.0 8.3 %collective-permute-done.11 = bf16[2,128,256]{2,1,0:T(8,128)(2,1)S(1)} collective-permute-done((bf16[2,128,256]{2,1,0:T(8,128)(2,1)S(1)}, bf16[2,128,256]{2,1,0:T(8,128)(2,1)S(1)}, u32[]{:S(2)}, u32[]{:S(2)}) %collective-permute-start.11) | collective-permute-done | bytes 131104 | tf_op jit(solution)/shard_map/ppermute | solution.py:209
  86.6 5.5 %collective-permute-done.15.far = bf16[4,128,256]{2,1,0:T(8,128)(2,1)S(1)} collective-permute-done((bf16[4,128,256]{2,1,0:T(8,128)(2,1)S(1)}, bf16[4,128,256]{2,1,0:T(8,128)(2,1)S(1)}, u32[]{:S(2)}, u32[]{:S(2)}) %collective-permute-start.15) | collective-permute-done | bytes 262176 | tf_op jit(solution)/shard_map/ppermute | solution.py:209
  92.8 5.0 %apply.1 = (f32[14,128,256]{2,1,0:T(8,128)S(1)}, bf16[14,128,256]{2,1,0:T(8,128)(2,1)S(1)}) custom-call(s32[8]{0:T(128)S(1)} %iota_xor_fusion.table, bf16[14,256,2048]{2,1,0:T(8,128)(2,1)S(1)} %load_integrals.1.rest_8_.integrals, bf16[4,128,256]{2,1,0:T(8,128)(2,1)S(1)} %constant_dynamic-update-slice_fusion.near, ...), custom_call_target="tpu_custom_call" | custom-call | tf_op jit(solution)/shard_map/apply/pallas_call | solution.py:191
  106.5 7.1 %collective-permute-done.19.rest_0_.rest_1_ = bf16[6,128,256]{2,1,0:T(8,128)(2,1)S(1)} collective-permute-done((bf16[6,128,256]{2,1,0:T(8,128)(2,1)S(1)}, bf16[6,128,256]{2,1,0:T(8,128)(2,1)S(1)}, u32[]{:S(2)}, u32[]{:S(2)}) %collective-permute-start.19) | collective-permute-done | bytes 393248 | tf_op jit(solution)/shard_map/ppermute | solution.py:209
  113.5 2.6 %collective-permute-start.26 = (bf16[6,128,128]{2,1,0:T(8,128)(2,1)S(1)}, bf16[6,128,128]{2,1,0:T(8,128)(2,1)S(1)}, u32[]{:S(2)}, u32[]{:S(2)}) collective-permute-start(bf16[6,128,128]{2,1,0:T(8,128)(2,1)S(1)} %get-tuple-element.84), channel_id=1, source_target_pairs={{0,10},{2,8},{4,14},{6,12},{8,2},{10,0},{12,6},{14,4},{1,11},{3,9}... | collective-permute-start | bytes 589832 | tf_op jit(solution)/shard_map/ppermute | solution.py:209
  116.1 5.7 %collective-permute-done.20.rest_1_.rest_2_ = bf16[6,128,256]{2,1,0:T(8,128)(2,1)S(1)} collective-permute-done((bf16[6,128,256]{2,1,0:T(8,128)(2,1)S(1)}, bf16[6,128,256]{2,1,0:T(8,128)(2,1)S(1)}, u32[]{:S(2)}, u32[]{:S(2)}) %collective-permute-start.20) | collective-permute-done | bytes 393248 | tf_op jit(solution)/shard_map/ppermute | solution.py:209
  121.9 2.3 %collective-permute-start.21 = (bf16[6,128,256]{2,1,0:T(8,128)(2,1)S(1)}, bf16[6,128,256]{2,1,0:T(8,128)(2,1)S(1)}, u32[]{:S(2)}, u32[]{:S(2)}) collective-permute-start(bf16[6,128,256]{2,1,0:T(8,128)(2,1)S(1)} %get-tuple-element.75), channel_id=1, source_target_pairs={{0,6},{2,4},{4,2},{6,0},{8,14},{10,12},{12,10},{14,8},{1,7},{3,5},... | collective-permute-start | bytes 1179656 | tf_op jit(solution)/shard_map/ppermute | solution.py:209
  124.2 9.0 %collective-permute-done.22.whole = bf16[14,128,128]{2,1,0:T(8,128)(2,1)S(1)} collective-permute-done((bf16[14,128,128]{2,1,0:T(8,128)(2,1)S(1)}, bf16[14,128,128]{2,1,0:T(8,128)(2,1)S(1)}, u32[]{:S(2)}, u32[]{:S(2)}) %collective-permute-start.22) | collective-permute-done | bytes 458784 | tf_op jit(solution)/shard_map/ppermute | solution.py:209
  137.4 8.9 %collective-permute-done.26.rest_9_ = bf16[6,128,128]{2,1,0:T(8,128)(2,1)S(1)} collective-permute-done((bf16[6,128,128]{2,1,0:T(8,128)(2,1)S(1)}, bf16[6,128,128]{2,1,0:T(8,128)(2,1)S(1)}, u32[]{:S(2)}, u32[]{:S(2)}) %collective-permute-start.26) | collective-permute-done | bytes 196640 | tf_op jit(solution)/shard_map/ppermute | solution.py:209
  146.3 2.5 %collective-permute-start.29 = (bf16[6,128,128]{2,1,0:T(8,128)(2,1)S(1)}, bf16[6,128,128]{2,1,0:T(8,128)(2,1)S(1)}, u32[]{:S(2)}, u32[]{:S(2)}) collective-permute-start(bf16[6,128,128]{2,1,0:T(8,128)(2,1)S(1)} %get-tuple-element.89), channel_id=1, source_target_pairs={{0,14},{2,12},{4,10},{6,8},{8,6},{10,4},{12,2},{14,0},{1,15},{3,13... | collective-permute-start | bytes 589832 | tf_op jit(solution)/shard_map/ppermute | solution.py:209
  150.8 8.5 %collective-permute-done.27.rest_7_ = bf16[6,128,128]{2,1,0:T(8,128)(2,1)S(1)} collective-permute-done((bf16[6,128,128]{2,1,0:T(8,128)(2,1)S(1)}, bf16[6,128,128]{2,1,0:T(8,128)(2,1)S(1)}, u32[]{:S(2)}, u32[]{:S(2)}) %collective-permute-start.27) | collective-permute-done | bytes 196640 | tf_op jit(solution)/shard_map/ppermute | solution.py:209
  159.3 3.1 %gather_coulomb.1 = (bf16[14,256,128]{2,1,0:T(8,128)(2,1)}, bf16[14,256,128]{2,1,0:T(8,128)(2,1)}) custom-call(s32[48]{0:T(128)S(1)} %pad_add_fusion.1.table, bf16[6,128,256]{2,1,0:T(8,128)(2,1)S(1)} %get-tuple-element.71.rest_0_, bf16[6,128,256]{2,1,0:T(8,128)(2,1)S(1)} %collective-permute-done.19.rest_0_.rest_1_, ...), custom_call_target="tpu_custom_call" | custom-call | tf_op jit(solution)/shard_map/gather_coulomb/pallas_call | solution.py:191
  (99 shorter events, 38.0 us)
Async XLA Ops:
  5.1 11.4 %collective-permute-start.1 = (bf16[3,128,256]{2,1,0:T(8,128)(2,1)S(1)}, bf16[3,128,256]{2,1,0:T(8,128)(2,1)S(1)}, u32[]{:S(2)}, u32[]{:S(2)}) collective-permute-start(bf16[3,128,256]{2,1,0:T(8,128)(2,1)S(1)} %get-tuple-element.47), channel_id=1, source_target_pairs={{0,14},{2,0},{4,2},{6,4},{8,6},{10,8},{12,10},{14,12},{1,15},{3,1}... | collective-permute-start | bytes 589832 | tf_op jit(solution)/shard_map/ppermute | solution.py:206
  11.1 10.6 %collective-permute-start = (bf16[3,128,256]{2,1,0:T(8,128)(2,1)S(1)}, bf16[3,128,256]{2,1,0:T(8,128)(2,1)S(1)}, u32[]{:S(2)}, u32[]{:S(2)}) collective-permute-start(bf16[3,128,256]{2,1,0:T(8,128)(2,1)S(1)} %get-tuple-element.46), channel_id=1, source_target_pairs={{0,2},{2,4},{4,6},{6,8},{8,10},{10,12},{12,14},{14,0},{1,3},{3,5},... | collective-permute-start | bytes 589832 | tf_op jit(solution)/shard_map/ppermute | solution.py:206
  11.2 22.6 %collective-permute-start.2 = (bf16[3,128,256]{2,1,0:T(8,128)(2,1)S(1)}, bf16[3,128,256]{2,1,0:T(8,128)(2,1)S(1)}, u32[]{:S(2)}, u32[]{:S(2)}) collective-permute-start(bf16[3,128,256]{2,1,0:T(8,128)(2,1)S(1)} %get-tuple-element.48), channel_id=1, source_target_pairs={{0,8},{2,10},{4,12},{6,14},{8,0},{10,2},{12,4},{14,6},{1,9},{3,11}... | collective-permute-start | bytes 589832 | tf_op jit(solution)/shard_map/ppermute | solution.py:206
  11.2 25.2 %collective-permute-start.3 = (bf16[3,128,256]{2,1,0:T(8,128)(2,1)S(1)}, bf16[3,128,256]{2,1,0:T(8,128)(2,1)S(1)}, u32[]{:S(2)}, u32[]{:S(2)}) collective-permute-start(bf16[3,128,256]{2,1,0:T(8,128)(2,1)S(1)} %get-tuple-element.49), channel_id=1, source_target_pairs={{0,6},{2,8},{4,10},{6,12},{8,14},{10,0},{12,2},{14,4},{1,7},{3,9},... | collective-permute-start | bytes 589832 | tf_op jit(solution)/shard_map/ppermute | solution.py:206
  16.4 20.0 %collective-permute-start.4 = (bf16[3,128,256]{2,1,0:T(8,128)(2,1)S(1)}, bf16[3,128,256]{2,1,0:T(8,128)(2,1)S(1)}, u32[]{:S(2)}, u32[]{:S(2)}) collective-permute-start(bf16[3,128,256]{2,1,0:T(8,128)(2,1)S(1)} %get-tuple-element.50), channel_id=1, source_target_pairs={{0,10},{2,12},{4,14},{6,0},{8,2},{10,4},{12,6},{14,8},{1,11},{3,13... | collective-permute-start | bytes 589832 | tf_op jit(solution)/shard_map/ppermute | solution.py:206
  16.5 20.0 %collective-permute-start.6 = (bf16[3,128,256]{2,1,0:T(8,128)(2,1)S(1)}, bf16[3,128,256]{2,1,0:T(8,128)(2,1)S(1)}, u32[]{:S(2)}, u32[]{:S(2)}) collective-permute-start(bf16[3,128,256]{2,1,0:T(8,128)(2,1)S(1)} %get-tuple-element.54), channel_id=1, source_target_pairs={{0,12},{2,14},{4,0},{6,2},{8,4},{10,6},{12,8},{14,10},{1,13},{3,15... | collective-permute-start | bytes 589832 | tf_op jit(solution)/shard_map/ppermute | solution.py:206
  21.7 16.2 %collective-permute-start.5 = (bf16[3,128,256]{2,1,0:T(8,128)(2,1)S(1)}, bf16[3,128,256]{2,1,0:T(8,128)(2,1)S(1)}, u32[]{:S(2)}, u32[]{:S(2)}) collective-permute-start(bf16[3,128,256]{2,1,0:T(8,128)(2,1)S(1)} %get-tuple-element.52), channel_id=1, source_target_pairs={{0,4},{2,6},{4,8},{6,10},{8,12},{10,14},{12,0},{14,2},{1,5},{3,7},... | collective-permute-start | bytes 589832 | tf_op jit(solution)/shard_map/ppermute | solution.py:206
  38.7 8.2 %collective-permute-start.8 = (bf16[14,128,256]{2,1,0:T(8,128)(2,1)S(1)}, bf16[14,128,256]{2,1,0:T(8,128)(2,1)S(1)}, u32[]{:S(2)}, u32[]{:S(2)}) collective-permute-start(bf16[14,128,256]{2,1,0:T(8,128)(2,1)S(1)} %gather_density.1.density), channel_id=1, source_target_pairs={{0,1},{1,0},{2,3},{3,2},{4,5},{5,4},{6,7},{7,6},{8,9},{9,8},{10,11... | collective-permute-start | bytes 2752520 | tf_op jit(solution)/shard_map/ppermute | solution.py:212
  41.7 13.1 %collective-permute-start.7 = (bf16[4,128,256]{2,1,0:T(8,128)(2,1)S(1)}, bf16[4,128,256]{2,1,0:T(8,128)(2,1)S(1)}, u32[]{:S(2)}, u32[]{:S(2)}) collective-permute-start(bf16[4,128,256]{2,1,0:T(8,128)(2,1)S(1)} %get-tuple-element.58), channel_id=1, source_target_pairs={{0,2},{2,0},{4,6},{6,4},{8,10},{10,8},{12,14},{14,12},{1,3},{3,1},... | collective-permute-start | bytes 786440 | tf_op jit(solution)/shard_map/ppermute | solution.py:209
  49.6 11.9 %collective-permute-start.9 = (bf16[4,128,256]{2,1,0:T(8,128)(2,1)S(1)}, bf16[4,128,256]{2,1,0:T(8,128)(2,1)S(1)}, u32[]{:S(2)}, u32[]{:S(2)}) collective-permute-start(bf16[4,128,256]{2,1,0:T(8,128)(2,1)S(1)} %get-tuple-element.60), channel_id=1, source_target_pairs={{0,4},{2,6},{4,0},{6,2},{8,12},{10,14},{12,8},{14,10},{1,5},{3,7},... | collective-permute-start | bytes 786440 | tf_op jit(solution)/shard_map/ppermute | solution.py:209
  66.8 11.4 %collective-permute-start.11 = (bf16[2,128,256]{2,1,0:T(8,128)(2,1)S(1)}, bf16[2,128,256]{2,1,0:T(8,128)(2,1)S(1)}, u32[]{:S(2)}, u32[]{:S(2)}) collective-permute-start(bf16[2,128,256]{2,1,0:T(8,128)(2,1)S(1)} %pad_maximum_fusion.1), channel_id=1, source_target_pairs={{0,8},{2,10},{4,12},{6,14},{8,0},{10,2},{12,4},{14,6},{1,9},{3,11}... | collective-permute-start | bytes 393224 | tf_op jit(solution)/shard_map/ppermute | solution.py:209
  68.5 11.9 %collective-permute-start.14 = (bf16[2,128,256]{2,1,0:T(8,128)(2,1)S(1)}, bf16[2,128,256]{2,1,0:T(8,128)(2,1)S(1)}, u32[]{:S(2)}, u32[]{:S(2)}) collective-permute-start(bf16[2,128,256]{2,1,0:T(8,128)(2,1)S(1)} %pad_maximum_fusion.2), channel_id=1, source_target_pairs={{0,8},{2,10},{4,12},{6,14},{8,0},{10,2},{12,4},{14,6},{1,9},{3,11}... | collective-permute-start | bytes 393224 | tf_op jit(solution)/shard_map/ppermute | solution.py:209
  85.6 6.5 %collective-permute-start.15 = (bf16[4,128,256]{2,1,0:T(8,128)(2,1)S(1)}, bf16[4,128,256]{2,1,0:T(8,128)(2,1)S(1)}, u32[]{:S(2)}, u32[]{:S(2)}) collective-permute-start(bf16[4,128,256]{2,1,0:T(8,128)(2,1)S(1)} %constant_dynamic-update-slice_fusion.near), channel_id=1, source_target_pairs={{0,2},{2,0},{4,6},{6,4},{8,10},{10,8},{12,14},{14,12},{1,3},{3,1},... | collective-permute-start | bytes 786440 | tf_op jit(solution)/shard_map/ppermute | solution.py:209
  101.4 31.8 %collective-permute-start.22 = (bf16[14,128,128]{2,1,0:T(8,128)(2,1)S(1)}, bf16[14,128,128]{2,1,0:T(8,128)(2,1)S(1)}, u32[]{:S(2)}, u32[]{:S(2)}) collective-permute-start(bf16[14,128,128]{2,1,0:T(8,128)(2,1)S(1)} %get-tuple-element.76), channel_id=1, source_target_pairs={{0,8},{2,10},{4,12},{6,14},{8,0},{10,2},{12,4},{14,6},{1,9},{3,11}... | collective-permute-start | bytes 1376264 | tf_op jit(solution)/shard_map/ppermute | solution.py:209
  102.6 10.9 %collective-permute-start.19 = (bf16[6,128,256]{2,1,0:T(8,128)(2,1)S(1)}, bf16[6,128,256]{2,1,0:T(8,128)(2,1)S(1)}, u32[]{:S(2)}, u32[]{:S(2)}) collective-permute-start(bf16[6,128,256]{2,1,0:T(8,128)(2,1)S(1)} %get-tuple-element.72), channel_id=1, source_target_pairs={{0,2},{2,0},{4,6},{6,4},{8,10},{10,8},{12,14},{14,12},{1,3},{3,1},... | collective-permute-start | bytes 1179656 | tf_op jit(solution)/shard_map/ppermute | solution.py:209
  103.1 18.8 %collective-permute-start.20 = (bf16[6,128,256]{2,1,0:T(8,128)(2,1)S(1)}, bf16[6,128,256]{2,1,0:T(8,128)(2,1)S(1)}, u32[]{:S(2)}, u32[]{:S(2)}) collective-permute-start(bf16[6,128,256]{2,1,0:T(8,128)(2,1)S(1)} %get-tuple-element.73), channel_id=1, source_target_pairs={{0,4},{2,6},{4,0},{6,2},{8,12},{10,14},{12,8},{14,10},{1,5},{3,7},... | collective-permute-start | bytes 1179656 | tf_op jit(solution)/shard_map/ppermute | solution.py:209
  105.3 32.1 %collective-permute-start.24 = (bf16[6,128,128]{2,1,0:T(8,128)(2,1)S(1)}, bf16[6,128,128]{2,1,0:T(8,128)(2,1)S(1)}, u32[]{:S(2)}, u32[]{:S(2)}) collective-permute-start(bf16[6,128,128]{2,1,0:T(8,128)(2,1)S(1)} %get-tuple-element.80), channel_id=1, source_target_pairs={{0,8},{2,10},{4,12},{6,14},{8,0},{10,2},{12,4},{14,6},{1,9},{3,11}... | collective-permute-start | bytes 589832 | tf_op jit(solution)/shard_map/ppermute | solution.py:209
  113.5 32.7 %collective-permute-start.26 = (bf16[6,128,128]{2,1,0:T(8,128)(2,1)S(1)}, bf16[6,128,128]{2,1,0:T(8,128)(2,1)S(1)}, u32[]{:S(2)}, u32[]{:S(2)}) collective-permute-start(bf16[6,128,128]{2,1,0:T(8,128)(2,1)S(1)} %get-tuple-element.84), channel_id=1, source_target_pairs={{0,10},{2,8},{4,14},{6,12},{8,2},{10,0},{12,6},{14,4},{1,11},{3,9}... | collective-permute-start | bytes 589832 | tf_op jit(solution)/shard_map/ppermute | solution.py:209
  121.9 29.0 %collective-permute-start.21 = (bf16[6,128,256]{2,1,0:T(8,128)(2,1)S(1)}, bf16[6,128,256]{2,1,0:T(8,128)(2,1)S(1)}, u32[]{:S(2)}, u32[]{:S(2)}) collective-permute-start(bf16[6,128,256]{2,1,0:T(8,128)(2,1)S(1)} %get-tuple-element.75), channel_id=1, source_target_pairs={{0,6},{2,4},{4,2},{6,0},{8,14},{10,12},{12,10},{14,8},{1,7},{3,5},... | collective-permute-start | bytes 1179656 | tf_op jit(solution)/shard_map/ppermute | solution.py:209
  133.8 12.5 %collective-permute-start.23 = (bf16[6,128,128]{2,1,0:T(8,128)(2,1)S(1)}, bf16[6,128,128]{2,1,0:T(8,128)(2,1)S(1)}, u32[]{:S(2)}, u32[]{:S(2)}) collective-permute-start(bf16[6,128,128]{2,1,0:T(8,128)(2,1)S(1)} %get-tuple-element.78), channel_id=1, source_target_pairs={{0,2},{2,0},{4,6},{6,4},{8,10},{10,8},{12,14},{14,12},{1,3},{3,1},... | collective-permute-start | bytes 589832 | tf_op jit(solution)/shard_map/ppermute | solution.py:209
  134.9 14.1 %collective-permute-start.28 = (bf16[6,128,128]{2,1,0:T(8,128)(2,1)S(1)}, bf16[6,128,128]{2,1,0:T(8,128)(2,1)S(1)}, u32[]{:S(2)}, u32[]{:S(2)}) collective-permute-start(bf16[6,128,128]{2,1,0:T(8,128)(2,1)S(1)} %get-tuple-element.87), channel_id=1, source_target_pairs={{0,12},{2,14},{4,8},{6,10},{8,4},{10,6},{12,0},{14,2},{1,13},{3,15... | collective-permute-start | bytes 589832 | tf_op jit(solution)/shard_map/ppermute | solution.py:209
  137.4 13.4 %collective-permute-start.25 = (bf16[6,128,128]{2,1,0:T(8,128)(2,1)S(1)}, bf16[6,128,128]{2,1,0:T(8,128)(2,1)S(1)}, u32[]{:S(2)}, u32[]{:S(2)}) collective-permute-start(bf16[6,128,128]{2,1,0:T(8,128)(2,1)S(1)} %get-tuple-element.81), channel_id=1, source_target_pairs={{0,4},{2,6},{4,0},{6,2},{8,12},{10,14},{12,8},{14,10},{1,5},{3,7},... | collective-permute-start | bytes 589832 | tf_op jit(solution)/shard_map/ppermute | solution.py:209
  146.3 13.0 %collective-permute-start.27 = (bf16[6,128,128]{2,1,0:T(8,128)(2,1)S(1)}, bf16[6,128,128]{2,1,0:T(8,128)(2,1)S(1)}, u32[]{:S(2)}, u32[]{:S(2)}) collective-permute-start(bf16[6,128,128]{2,1,0:T(8,128)(2,1)S(1)} %get-tuple-element.85), channel_id=1, source_target_pairs={{0,6},{2,4},{4,2},{6,0},{8,14},{10,12},{12,10},{14,8},{1,7},{3,5},... | collective-permute-start | bytes 589832 | tf_op jit(solution)/shard_map/ppermute | solution.py:209
  146.3 13.0 %collective-permute-start.29 = (bf16[6,128,128]{2,1,0:T(8,128)(2,1)S(1)}, bf16[6,128,128]{2,1,0:T(8,128)(2,1)S(1)}, u32[]{:S(2)}, u32[]{:S(2)}) collective-permute-start(bf16[6,128,128]{2,1,0:T(8,128)(2,1)S(1)} %get-tuple-element.89), channel_id=1, source_target_pairs={{0,14},{2,12},{4,10},{6,8},{8,6},{10,4},{12,2},{14,0},{1,15},{3,13... | collective-permute-start | bytes 589832 | tf_op jit(solution)/shard_map/ppermute | solution.py:209
  (11 other events, 105.9 us)

commit v19 on v18

--- a/solution.py
+++ b/solution.py
@@ -79,34 +79,37 @@
             ).astype(out.dtype)
 
 
-def apply_kernel(orders, some, table, integrals, near, far, near_other, far_other, own, other):
-    blocks, pairs, half = integrals.shape[0], integrals.shape[1], own.shape[1]
+def apply_kernel(orders, first, table, integrals, near, far, near_other, far_other, *rest):
+    own, other = rest[-2:]
+    pairs, (some, half) = integrals.shape[1], own.shape[:2]
     count, _, width = near.shape
     chunks = []
     for order, low, high in ((orders[0], near, far), (orders[1], near_other, far_other)):
         chunks.append({e: (low, i) if i < count else (high, i - count) for i, e in enumerate(order)})
-    for first in range(0, blocks, some):
-        total = None
-        for e in range(2 * count):
-            at = pl.ds(pl.multiple_of(table[e] * width, width), width)
-            term = lax.dot_general(
-                integrals[first : first + some, :, at].reshape(some * pairs, width),
-                jnp.concatenate([piece[e][0][piece[e][1]] for piece in chunks], axis=0),
-                (((1,), (1,)), ((), ())),
-                preferred_element_type=jnp.float32,
-            )
-            total = term if total is None else total + term
-        for b in range(some):
-            value = total[b * pairs : (b + 1) * pairs].T
-            own[first + b] = value[:half]
-            other[first + b] = value[half:].astype(other.dtype)
-
-
-def scatter_coulomb_kernel(devices, blocks, cap, table, screen, own, other, *rest):
+    total = None
+    for e in range(2 * count):
+        at = pl.ds(pl.multiple_of(table[e] * width, width), width)
+        term = lax.dot_general(
+            integrals[first : first + some, :, at].reshape(some * pairs, width),
+            jnp.concatenate([piece[e][0][piece[e][1]] for piece in chunks], axis=0),
+            (((1,), (1,)), ((), ())),
+            preferred_element_type=jnp.float32,
+        )
+        total = term if total is None else total + term
+    for b in range(some):
+        value = total[b * pairs : (b + 1) * pairs].T
+        own[b] = value[:half]
+        other[b] = value[half:].astype(other.dtype)
+
+
+def scatter_coulomb_kernel(devices, blocks, cap, table, screen, *rest):
+    sums, rest = rest[:4], rest[4:]
+    some = sums[0].shape[0]
     near, far, whole, ready = rest[: devices // 2], rest[devices // 2 : devices], rest[-2], rest[-1]
     part = whole.shape[2]
     for b in range(blocks):
-        value = (own[b] + other[b].astype(jnp.float32)) * screen[b]
+        own, other = sums[b // some * 2 : b // some * 2 + 2]
+        value = (own[b % some] + other[b % some].astype(jnp.float32)) * screen[b]
         ready[b] = value.astype(jnp.bfloat16)
         whole[b] = ready[b, :, pl.ds(0, part)]
     for group in range(2):
@@ -322,22 +325,26 @@
         [tuple(fit_own), tuple(fit_other)]
     )
 
-    mine, theirs = call(
-        functools.partial(apply_kernel, (order_own, order_other), blocks // 2),
-        "apply",
-        chunk_table,
-        [integrals, near_own, far_own, near_other, far_other],
-        [
-            jax.ShapeDtypeStruct((blocks, half, pairs), f32),
-            jax.ShapeDtypeStruct((blocks, half, pairs), bf16),
-        ],
-        [in_vmem] * 2,
-    )
+    sums = []
+    for first in (0, blocks // 2):
+        mine, theirs = call(
+            functools.partial(apply_kernel, (order_own, order_other), first),
+            "apply",
+            chunk_table,
+            [integrals, near_own, far_own, near_other, far_other],
+            [
+                jax.ShapeDtypeStruct((blocks // 2, half, pairs), f32),
+                jax.ShapeDtypeStruct((blocks // 2, half, pairs), bf16),
+            ],
+            [in_vmem] * 2,
+            sums[:1],
+        )
+        sums += [mine, swap(after(theirs, *sums[1:2]))]
     sends = call(
         functools.partial(scatter_coulomb_kernel, n, blocks, cap),
         "scatter_coulomb",
         out_table,
-        [keeping, mine, swap(theirs)],
+        [keeping, *sums],
         [jax.ShapeDtypeStruct((2 * cap, half, pairs), bf16)] * (n // 2)
         + [jax.ShapeDtypeStruct((2 * cap, half, part), bf16)] * (n // 2)
         + [jax.ShapeDtypeStruct((blocks, half, part), bf16)],

time: 163 us -> 172 us (1.055)
  waiting for transfers between devices: 84.8 us -> 95.1 us
    ppermute x21, waiting for transfers between devices: 72.3 us -> 83.5 us  [flip(): return lax.ppermute(x, 'pair', [(s, s ^ bit) for s in range(n)])]
    ppermute x21, starting transfers between devices: 32.1 us -> 30 us  [flip(): return lax.ppermute(x, 'pair', [(s, s ^ bit) for s in range(n)])]
    pallas_call x7 -> x8, Pallas kernels: 16 us -> 16.5 us  [call(): pl.pallas_call(kernel, out_shape=out_shape, grid_spec=pltpu.PrefetchScala...]
  transfers between devices with their start and end apart: 30 -> 31, of which waited for: 20 -> 21; matrix products, arithmetic and copies ran while one was open for 1% -> 1% of each run, Pallas kernels for 4% -> 6%
where the time goes in v19:
time: 172 us
  waiting for transfers between devices  95.1 us (55%)
  starting transfers between devices  46.7 us (27%)
  Pallas kernels  18.4 us (11%)
  local copies, waits for them, and re-layouts  6.78 us (4%)
  other arithmetic  3.73 us (2%)
    ppermute x21, waiting for transfers between devices, flip(): return lax.ppermute(x, 'pair', [(s, s ^ bit) for s in range(n)])  83.5 us
    ppermute x21, starting transfers between devices, flip(): return lax.ppermute(x, 'pair', [(s, s ^ bit) for s in range(n)])  30 us
    pallas_call x8, Pallas kernels, call(): pl.pallas_call(kernel, out_shape=out_shape, grid_spec=pltpu.PrefetchScala...  16.5 us
    ppermute x7, starting transfers between devices, shift(): return lax.ppermute(x, 'pair', [(s, (s + d) % n) for s in range(n)])  15.9 us
    ppermute x7, waiting for transfers between devices, shift(): return lax.ppermute(x, 'pair', [(s, (s + d) % n) for s in range(n)])  10.5 us
    unnamed x11, local copies, waits for them, and re-layouts  6.7 us
  transfers between devices with their start and end apart: 31, of which 21 were waited for; matrix products, arithmetic and copies ran while one was open for 1% of the time, Pallas kernels for 6%

profile of v19, /device:TPU:0, one launch (start us, length us, event | category | flops | bytes accessed | tf_op | source)
XLA Modules:
  0.0 171.6 jit_solution(3112794909225451819)
XLA Ops:
  5.0 6.1 %collective-permute-start.1 = (bf16[3,128,256]{2,1,0:T(8,128)(2,1)S(1)}, bf16[3,128,256]{2,1,0:T(8,128)(2,1)S(1)}, u32[]{:S(2)}, u32[]{:S(2)}) collective-permute-start(bf16[3,128,256]{2,1,0:T(8,128)(2,1)S(1)} %get-tuple-element.50), channel_id=1, source_target_pairs={{0,14},{2,0},{4,2},{6,4},{8,6},{10,8},{12,10},{14,12},{1,15},{3,1}... | collective-permute-start | bytes 589832 | tf_op jit(solution)/shard_map/ppermute | solution.py:209
  11.1 5.2 %collective-permute-start.3 = (bf16[3,128,256]{2,1,0:T(8,128)(2,1)S(1)}, bf16[3,128,256]{2,1,0:T(8,128)(2,1)S(1)}, u32[]{:S(2)}, u32[]{:S(2)}) collective-permute-start(bf16[3,128,256]{2,1,0:T(8,128)(2,1)S(1)} %get-tuple-element.52), channel_id=1, source_target_pairs={{0,6},{2,8},{4,10},{6,12},{8,14},{10,0},{12,2},{14,4},{1,7},{3,9},... | collective-permute-start | bytes 589832 | tf_op jit(solution)/shard_map/ppermute | solution.py:209
  16.4 4.6 %collective-permute-start.6 = (bf16[3,128,256]{2,1,0:T(8,128)(2,1)S(1)}, bf16[3,128,256]{2,1,0:T(8,128)(2,1)S(1)}, u32[]{:S(2)}, u32[]{:S(2)}) collective-permute-start(bf16[3,128,256]{2,1,0:T(8,128)(2,1)S(1)} %get-tuple-element.57), channel_id=1, source_target_pairs={{0,12},{2,14},{4,0},{6,2},{8,4},{10,6},{12,8},{14,10},{1,13},{3,15... | collective-permute-start | bytes 589832 | tf_op jit(solution)/shard_map/ppermute | solution.py:209
  21.8 5.2 %copy-done = bf16[14,256,2048]{2,1,0:T(8,128)(2,1)S(1)} copy-done((bf16[14,256,2048]{2,1,0:T(8,128)(2,1)S(1)}, bf16[14,256,2048]{2,1,0:T(8,128)(2,1)}, u32[]{:S(2)}) %copy-start) | copy-done | bytes 14680088
  28.0 5.6 %collective-permute-done.2.rest_2_ = bf16[3,128,256]{2,1,0:T(8,128)(2,1)S(1)} collective-permute-done((bf16[3,128,256]{2,1,0:T(8,128)(2,1)S(1)}, bf16[3,128,256]{2,1,0:T(8,128)(2,1)S(1)}, u32[]{:S(2)}, u32[]{:S(2)}) %collective-permute-start.2) | collective-permute-done | bytes 196640 | tf_op jit(solution)/shard_map/ppermute | solution.py:209
  38.8 2.8 %fit.2 = (f32[4,128,256]{2,1,0:T(8,128)S(1)}, bf16[4,128,256]{2,1,0:T(8,128)(2,1)S(1)}) custom-call(s32[8]{0:T(128)S(1)} %iota_xor_fusion.table, bf16[14,1,256]{2,1,0:T(2,128)(2,1)S(1)} %copy.10.factor, bf16[14,128,256]{2,1,0:T(8,128)(2,1)S(1)} %gather_density.1.density, bf16[14,256,2048]{2,1,0:T(8,128)(2,1)S(1)} %load_integrals.1.rest_8_.integrals), custom_call_target="tpu_custom_call" | custom-call | tf_op jit(solution)/shard_map/fit/pallas_call | solution.py:194
  41.6 5.2 %collective-permute-start.7 = (bf16[4,128,256]{2,1,0:T(8,128)(2,1)S(1)}, bf16[4,128,256]{2,1,0:T(8,128)(2,1)S(1)}, u32[]{:S(2)}, u32[]{:S(2)}) collective-permute-start(bf16[4,128,256]{2,1,0:T(8,128)(2,1)S(1)} %get-tuple-element.61), channel_id=1, source_target_pairs={{0,2},{2,0},{4,6},{6,4},{8,10},{10,8},{12,14},{14,12},{1,3},{3,1},... | collective-permute-start | bytes 786440 | tf_op jit(solution)/shard_map/ppermute | solution.py:212
  46.8 2.7 %fit.3 = (f32[4,128,256]{2,1,0:T(8,128)S(1)}, bf16[4,128,256]{2,1,0:T(8,128)(2,1)S(1)}) custom-call(s32[8]{0:T(128)S(1)} %iota_xor_fusion.table, bf16[14,1,256]{2,1,0:T(2,128)(2,1)S(1)} %copy.10.factor, bf16[14,128,256]{2,1,0:T(8,128)(2,1)S(1)} %collective-permute-done.8.density, bf16[14,256,2048]{2,1,0:T(8,128)(2,1)S(1)} %load_integrals.1.rest_8_.integrals, ...), custom_call_target="tpu_custom_call" | custom-call | tf_op jit(solution)/shard_map/fit/pallas_call | solution.py:194
  49.5 5.2 %collective-permute-start.9 = (bf16[4,128,256]{2,1,0:T(8,128)(2,1)S(1)}, bf16[4,128,256]{2,1,0:T(8,128)(2,1)S(1)}, u32[]{:S(2)}, u32[]{:S(2)}) collective-permute-start(bf16[4,128,256]{2,1,0:T(8,128)(2,1)S(1)} %get-tuple-element.63), channel_id=1, source_target_pairs={{0,4},{2,6},{4,0},{6,2},{8,12},{10,14},{12,8},{14,10},{1,5},{3,7},... | collective-permute-start | bytes 786440 | tf_op jit(solution)/shard_map/ppermute | solution.py:212
  54.8 6.6 %collective-permute-done.9 = bf16[4,128,256]{2,1,0:T(8,128)(2,1)S(1)} collective-permute-done((bf16[4,128,256]{2,1,0:T(8,128)(2,1)S(1)}, bf16[4,128,256]{2,1,0:T(8,128)(2,1)S(1)}, u32[]{:S(2)}, u32[]{:S(2)}) %collective-permute-start.9) | collective-permute-done | bytes 262176 | tf_op jit(solution)/shard_map/ppermute | solution.py:212
  63.6 3.1 %collective-permute-done.10 = bf16[2,128,256]{2,1,0:T(8,128)(2,1)S(1)} collective-permute-done((bf16[2,128,256]{2,1,0:T(8,128)(2,1)S(1)}, bf16[2,128,256]{2,1,0:T(8,128)(2,1)S(1)}, u32[]{:S(2)}, u32[]{:S(2)}) %collective-permute-start.10) | collective-permute-done | bytes 131104 | tf_op jit(solution)/shard_map/ppermute | solution.py:212
  69.9 8.3 %collective-permute-done.11 = bf16[2,128,256]{2,1,0:T(8,128)(2,1)S(1)} collective-permute-done((bf16[2,128,256]{2,1,0:T(8,128)(2,1)S(1)}, bf16[2,128,256]{2,1,0:T(8,128)(2,1)S(1)}, u32[]{:S(2)}, u32[]{:S(2)}) %collective-permute-start.11) | collective-permute-done | bytes 131104 | tf_op jit(solution)/shard_map/ppermute | solution.py:212
  86.5 5.6 %collective-permute-done.15.far = bf16[4,128,256]{2,1,0:T(8,128)(2,1)S(1)} collective-permute-done((bf16[4,128,256]{2,1,0:T(8,128)(2,1)S(1)}, bf16[4,128,256]{2,1,0:T(8,128)(2,1)S(1)}, u32[]{:S(2)}, u32[]{:S(2)}) %collective-permute-start.15) | collective-permute-done | bytes 262176 | tf_op jit(solution)/shard_map/ppermute | solution.py:212
  92.7 2.7 %apply.2 = (f32[7,128,256]{2,1,0:T(8,128)S(1)}, bf16[7,128,256]{2,1,0:T(8,128)(2,1)S(1)}) custom-call(s32[8]{0:T(128)S(1)} %iota_xor_fusion.table, bf16[14,256,2048]{2,1,0:T(8,128)(2,1)S(1)} %load_integrals.1.rest_8_.integrals, bf16[4,128,256]{2,1,0:T(8,128)(2,1)S(1)} %constant_dynamic-update-slice_fusion.near, ...), custom_call_target="tpu_custom_call" | custom-call | tf_op jit(solution)/shard_map/apply/pallas_call | solution.py:194
  95.9 2.8 %apply.3 = (f32[7,128,256]{2,1,0:T(8,128)S(1)}, bf16[7,128,256]{2,1,0:T(8,128)(2,1)S(1)}) custom-call(s32[8]{0:T(128)S(1)} %iota_xor_fusion.table, bf16[14,256,2048]{2,1,0:T(8,128)(2,1)S(1)} %load_integrals.1.rest_8_.integrals, bf16[4,128,256]{2,1,0:T(8,128)(2,1)S(1)} %constant_dynamic-update-slice_fusion.near, ...), custom_call_target="tpu_custom_call" | custom-call | tf_op jit(solution)/shard_map/apply/pallas_call | solution.py:194
  106.4 6.8 %collective-permute-done.20.rest_0_.rest_1_ = bf16[6,128,256]{2,1,0:T(8,128)(2,1)S(1)} collective-permute-done((bf16[6,128,256]{2,1,0:T(8,128)(2,1)S(1)}, bf16[6,128,256]{2,1,0:T(8,128)(2,1)S(1)}, u32[]{:S(2)}, u32[]{:S(2)}) %collective-permute-start.20) | collective-permute-done | bytes 393248 | tf_op jit(solution)/shard_map/ppermute | solution.py:212
  114.2 8.5 %collective-permute-done.21.rest_1_.rest_2_ = bf16[6,128,256]{2,1,0:T(8,128)(2,1)S(1)} collective-permute-done((bf16[6,128,256]{2,1,0:T(8,128)(2,1)S(1)}, bf16[6,128,256]{2,1,0:T(8,128)(2,1)S(1)}, u32[]{:S(2)}, u32[]{:S(2)}) %collective-permute-start.21) | collective-permute-done | bytes 393248 | tf_op jit(solution)/shard_map/ppermute | solution.py:212
  122.6 11.8 %collective-permute-done.23.whole = bf16[14,128,128]{2,1,0:T(8,128)(2,1)S(1)} collective-permute-done((bf16[14,128,128]{2,1,0:T(8,128)(2,1)S(1)}, bf16[14,128,128]{2,1,0:T(8,128)(2,1)S(1)}, u32[]{:S(2)}, u32[]{:S(2)}) %collective-permute-start.23) | collective-permute-done | bytes 458784 | tf_op jit(solution)/shard_map/ppermute | solution.py:212
  139.4 4.0 %collective-permute-done.27.rest_9_ = bf16[6,128,128]{2,1,0:T(8,128)(2,1)S(1)} collective-permute-done((bf16[6,128,128]{2,1,0:T(8,128)(2,1)S(1)}, bf16[6,128,128]{2,1,0:T(8,128)(2,1)S(1)}, u32[]{:S(2)}, u32[]{:S(2)}) %collective-permute-start.27) | collective-permute-done | bytes 196640 | tf_op jit(solution)/shard_map/ppermute | solution.py:212
  143.5 6.6 %collective-permute-done.24.rest_5_ = bf16[6,128,128]{2,1,0:T(8,128)(2,1)S(1)} collective-permute-done((bf16[6,128,128]{2,1,0:T(8,128)(2,1)S(1)}, bf16[6,128,128]{2,1,0:T(8,128)(2,1)S(1)}, u32[]{:S(2)}, u32[]{:S(2)}) %collective-permute-start.24) | collective-permute-done | bytes 196640 | tf_op jit(solution)/shard_map/ppermute | solution.py:212
  150.0 3.2 %collective-permute-start.30 = (bf16[6,128,128]{2,1,0:T(8,128)(2,1)S(1)}, bf16[6,128,128]{2,1,0:T(8,128)(2,1)S(1)}, u32[]{:S(2)}, u32[]{:S(2)}) collective-permute-start(bf16[6,128,128]{2,1,0:T(8,128)(2,1)S(1)} %get-tuple-element.95), channel_id=1, source_target_pairs={{0,14},{2,12},{4,10},{6,8},{8,6},{10,4},{12,2},{14,0},{1,15},{3,13... | collective-permute-start | bytes 589832 | tf_op jit(solution)/shard_map/ppermute | solution.py:212
  153.4 6.8 %collective-permute-done.26.rest_6_ = bf16[6,128,128]{2,1,0:T(8,128)(2,1)S(1)} collective-permute-done((bf16[6,128,128]{2,1,0:T(8,128)(2,1)S(1)}, bf16[6,128,128]{2,1,0:T(8,128)(2,1)S(1)}, u32[]{:S(2)}, u32[]{:S(2)}) %collective-permute-start.26) | collective-permute-done | bytes 196640 | tf_op jit(solution)/shard_map/ppermute | solution.py:212
  160.2 8.4 %collective-permute-done.28.rest_7_ = bf16[6,128,128]{2,1,0:T(8,128)(2,1)S(1)} collective-permute-done((bf16[6,128,128]{2,1,0:T(8,128)(2,1)S(1)}, bf16[6,128,128]{2,1,0:T(8,128)(2,1)S(1)}, u32[]{:S(2)}, u32[]{:S(2)}) %collective-permute-start.28) | collective-permute-done | bytes 196640 | tf_op jit(solution)/shard_map/ppermute | solution.py:212
  168.6 3.1 %gather_coulomb.1 = (bf16[14,256,128]{2,1,0:T(8,128)(2,1)}, bf16[14,256,128]{2,1,0:T(8,128)(2,1)}) custom-call(s32[48]{0:T(128)S(1)} %pad_add_fusion.1.table, bf16[6,128,256]{2,1,0:T(8,128)(2,1)S(1)} %get-tuple-element.77.rest_0_, bf16[6,128,256]{2,1,0:T(8,128)(2,1)S(1)} %collective-permute-done.20.rest_0_.rest_1_, ...), custom_call_target="tpu_custom_call" | custom-call | tf_op jit(solution)/shard_map/gather_coulomb/pallas_call | solution.py:194
  (102 shorter events, 40.1 us)
Async XLA Ops:
  5.0 11.4 %collective-permute-start.1 = (bf16[3,128,256]{2,1,0:T(8,128)(2,1)S(1)}, bf16[3,128,256]{2,1,0:T(8,128)(2,1)S(1)}, u32[]{:S(2)}, u32[]{:S(2)}) collective-permute-start(bf16[3,128,256]{2,1,0:T(8,128)(2,1)S(1)} %get-tuple-element.50), channel_id=1, source_target_pairs={{0,14},{2,0},{4,2},{6,4},{8,6},{10,8},{12,10},{14,12},{1,15},{3,1}... | collective-permute-start | bytes 589832 | tf_op jit(solution)/shard_map/ppermute | solution.py:209
  11.1 10.6 %collective-permute-start = (bf16[3,128,256]{2,1,0:T(8,128)(2,1)S(1)}, bf16[3,128,256]{2,1,0:T(8,128)(2,1)S(1)}, u32[]{:S(2)}, u32[]{:S(2)}) collective-permute-start(bf16[3,128,256]{2,1,0:T(8,128)(2,1)S(1)} %get-tuple-element.49), channel_id=1, source_target_pairs={{0,2},{2,4},{4,6},{6,8},{8,10},{10,12},{12,14},{14,0},{1,3},{3,5},... | collective-permute-start | bytes 589832 | tf_op jit(solution)/shard_map/ppermute | solution.py:209
  11.1 22.6 %collective-permute-start.2 = (bf16[3,128,256]{2,1,0:T(8,128)(2,1)S(1)}, bf16[3,128,256]{2,1,0:T(8,128)(2,1)S(1)}, u32[]{:S(2)}, u32[]{:S(2)}) collective-permute-start(bf16[3,128,256]{2,1,0:T(8,128)(2,1)S(1)} %get-tuple-element.51), channel_id=1, source_target_pairs={{0,8},{2,10},{4,12},{6,14},{8,0},{10,2},{12,4},{14,6},{1,9},{3,11}... | collective-permute-start | bytes 589832 | tf_op jit(solution)/shard_map/ppermute | solution.py:209
  11.1 25.2 %collective-permute-start.3 = (bf16[3,128,256]{2,1,0:T(8,128)(2,1)S(1)}, bf16[3,128,256]{2,1,0:T(8,128)(2,1)S(1)}, u32[]{:S(2)}, u32[]{:S(2)}) collective-permute-start(bf16[3,128,256]{2,1,0:T(8,128)(2,1)S(1)} %get-tuple-element.52), channel_id=1, source_target_pairs={{0,6},{2,8},{4,10},{6,12},{8,14},{10,0},{12,2},{14,4},{1,7},{3,9},... | collective-permute-start | bytes 589832 | tf_op jit(solution)/shard_map/ppermute | solution.py:209
  16.4 20.0 %collective-permute-start.4 = (bf16[3,128,256]{2,1,0:T(8,128)(2,1)S(1)}, bf16[3,128,256]{2,1,0:T(8,128)(2,1)S(1)}, u32[]{:S(2)}, u32[]{:S(2)}) collective-permute-start(bf16[3,128,256]{2,1,0:T(8,128)(2,1)S(1)} %get-tuple-element.53), channel_id=1, source_target_pairs={{0,10},{2,12},{4,14},{6,0},{8,2},{10,4},{12,6},{14,8},{1,11},{3,13... | collective-permute-start | bytes 589832 | tf_op jit(solution)/shard_map/ppermute | solution.py:209
  16.4 20.0 %collective-permute-start.6 = (bf16[3,128,256]{2,1,0:T(8,128)(2,1)S(1)}, bf16[3,128,256]{2,1,0:T(8,128)(2,1)S(1)}, u32[]{:S(2)}, u32[]{:S(2)}) collective-permute-start(bf16[3,128,256]{2,1,0:T(8,128)(2,1)S(1)} %get-tuple-element.57), channel_id=1, source_target_pairs={{0,12},{2,14},{4,0},{6,2},{8,4},{10,6},{12,8},{14,10},{1,13},{3,15... | collective-permute-start | bytes 589832 | tf_op jit(solution)/shard_map/ppermute | solution.py:209
  21.7 16.2 %collective-permute-start.5 = (bf16[3,128,256]{2,1,0:T(8,128)(2,1)S(1)}, bf16[3,128,256]{2,1,0:T(8,128)(2,1)S(1)}, u32[]{:S(2)}, u32[]{:S(2)}) collective-permute-start(bf16[3,128,256]{2,1,0:T(8,128)(2,1)S(1)} %get-tuple-element.55), channel_id=1, source_target_pairs={{0,4},{2,6},{4,8},{6,10},{8,12},{10,14},{12,0},{14,2},{1,5},{3,7},... | collective-permute-start | bytes 589832 | tf_op jit(solution)/shard_map/ppermute | solution.py:209
  38.6 8.2 %collective-permute-start.8 = (bf16[14,128,256]{2,1,0:T(8,128)(2,1)S(1)}, bf16[14,128,256]{2,1,0:T(8,128)(2,1)S(1)}, u32[]{:S(2)}, u32[]{:S(2)}) collective-permute-start(bf16[14,128,256]{2,1,0:T(8,128)(2,1)S(1)} %gather_density.1.density), channel_id=1, source_target_pairs={{0,1},{1,0},{2,3},{3,2},{4,5},{5,4},{6,7},{7,6},{8,9},{9,8},{10,11... | collective-permute-start | bytes 2752520 | tf_op jit(solution)/shard_map/ppermute | solution.py:215
  41.6 13.1 %collective-permute-start.7 = (bf16[4,128,256]{2,1,0:T(8,128)(2,1)S(1)}, bf16[4,128,256]{2,1,0:T(8,128)(2,1)S(1)}, u32[]{:S(2)}, u32[]{:S(2)}) collective-permute-start(bf16[4,128,256]{2,1,0:T(8,128)(2,1)S(1)} %get-tuple-element.61), channel_id=1, source_target_pairs={{0,2},{2,0},{4,6},{6,4},{8,10},{10,8},{12,14},{14,12},{1,3},{3,1},... | collective-permute-start | bytes 786440 | tf_op jit(solution)/shard_map/ppermute | solution.py:212
  49.5 11.9 %collective-permute-start.9 = (bf16[4,128,256]{2,1,0:T(8,128)(2,1)S(1)}, bf16[4,128,256]{2,1,0:T(8,128)(2,1)S(1)}, u32[]{:S(2)}, u32[]{:S(2)}) collective-permute-start(bf16[4,128,256]{2,1,0:T(8,128)(2,1)S(1)} %get-tuple-element.63), channel_id=1, source_target_pairs={{0,4},{2,6},{4,0},{6,2},{8,12},{10,14},{12,8},{14,10},{1,5},{3,7},... | collective-permute-start | bytes 786440 | tf_op jit(solution)/shard_map/ppermute | solution.py:212
  66.8 11.4 %collective-permute-start.11 = (bf16[2,128,256]{2,1,0:T(8,128)(2,1)S(1)}, bf16[2,128,256]{2,1,0:T(8,128)(2,1)S(1)}, u32[]{:S(2)}, u32[]{:S(2)}) collective-permute-start(bf16[2,128,256]{2,1,0:T(8,128)(2,1)S(1)} %pad_maximum_fusion.1), channel_id=1, source_target_pairs={{0,8},{2,10},{4,12},{6,14},{8,0},{10,2},{12,4},{14,6},{1,9},{3,11}... | collective-permute-start | bytes 393224 | tf_op jit(solution)/shard_map/ppermute | solution.py:212
  68.5 11.9 %collective-permute-start.14 = (bf16[2,128,256]{2,1,0:T(8,128)(2,1)S(1)}, bf16[2,128,256]{2,1,0:T(8,128)(2,1)S(1)}, u32[]{:S(2)}, u32[]{:S(2)}) collective-permute-start(bf16[2,128,256]{2,1,0:T(8,128)(2,1)S(1)} %pad_maximum_fusion.2), channel_id=1, source_target_pairs={{0,8},{2,10},{4,12},{6,14},{8,0},{10,2},{12,4},{14,6},{1,9},{3,11}... | collective-permute-start | bytes 393224 | tf_op jit(solution)/shard_map/ppermute | solution.py:212
  85.5 6.5 %collective-permute-start.15 = (bf16[4,128,256]{2,1,0:T(8,128)(2,1)S(1)}, bf16[4,128,256]{2,1,0:T(8,128)(2,1)S(1)}, u32[]{:S(2)}, u32[]{:S(2)}) collective-permute-start(bf16[4,128,256]{2,1,0:T(8,128)(2,1)S(1)} %constant_dynamic-update-slice_fusion.near), channel_id=1, source_target_pairs={{0,2},{2,0},{4,6},{6,4},{8,10},{10,8},{12,14},{14,12},{1,3},{3,1},... | collective-permute-start | bytes 786440 | tf_op jit(solution)/shard_map/ppermute | solution.py:212
  101.7 11.5 %collective-permute-start.20 = (bf16[6,128,256]{2,1,0:T(8,128)(2,1)S(1)}, bf16[6,128,256]{2,1,0:T(8,128)(2,1)S(1)}, u32[]{:S(2)}, u32[]{:S(2)}) collective-permute-start(bf16[6,128,256]{2,1,0:T(8,128)(2,1)S(1)} %get-tuple-element.78), channel_id=1, source_target_pairs={{0,2},{2,0},{4,6},{6,4},{8,10},{10,8},{12,14},{14,12},{1,3},{3,1},... | collective-permute-start | bytes 1179656 | tf_op jit(solution)/shard_map/ppermute | solution.py:212
  103.1 31.3 %collective-permute-start.23 = (bf16[14,128,128]{2,1,0:T(8,128)(2,1)S(1)}, bf16[14,128,128]{2,1,0:T(8,128)(2,1)S(1)}, u32[]{:S(2)}, u32[]{:S(2)}) collective-permute-start(bf16[14,128,128]{2,1,0:T(8,128)(2,1)S(1)} %get-tuple-element.82), channel_id=1, source_target_pairs={{0,8},{2,10},{4,12},{6,14},{8,0},{10,2},{12,4},{14,6},{1,9},{3,11}... | collective-permute-start | bytes 1376264 | tf_op jit(solution)/shard_map/ppermute | solution.py:212
  103.3 19.3 %collective-permute-start.21 = (bf16[6,128,256]{2,1,0:T(8,128)(2,1)S(1)}, bf16[6,128,256]{2,1,0:T(8,128)(2,1)S(1)}, u32[]{:S(2)}, u32[]{:S(2)}) collective-permute-start(bf16[6,128,256]{2,1,0:T(8,128)(2,1)S(1)} %get-tuple-element.79), channel_id=1, source_target_pairs={{0,4},{2,6},{4,0},{6,2},{8,12},{10,14},{12,8},{14,10},{1,5},{3,7},... | collective-permute-start | bytes 1179656 | tf_op jit(solution)/shard_map/ppermute | solution.py:212
  105.2 33.4 %collective-permute-start.25 = (bf16[6,128,128]{2,1,0:T(8,128)(2,1)S(1)}, bf16[6,128,128]{2,1,0:T(8,128)(2,1)S(1)}, u32[]{:S(2)}, u32[]{:S(2)}) collective-permute-start(bf16[6,128,128]{2,1,0:T(8,128)(2,1)S(1)} %get-tuple-element.86), channel_id=1, source_target_pairs={{0,8},{2,10},{4,12},{6,14},{8,0},{10,2},{12,4},{14,6},{1,9},{3,11}... | collective-permute-start | bytes 589832 | tf_op jit(solution)/shard_map/ppermute | solution.py:212
  113.2 30.3 %collective-permute-start.27 = (bf16[6,128,128]{2,1,0:T(8,128)(2,1)S(1)}, bf16[6,128,128]{2,1,0:T(8,128)(2,1)S(1)}, u32[]{:S(2)}, u32[]{:S(2)}) collective-permute-start(bf16[6,128,128]{2,1,0:T(8,128)(2,1)S(1)} %get-tuple-element.90), channel_id=1, source_target_pairs={{0,10},{2,8},{4,14},{6,12},{8,2},{10,0},{12,6},{14,4},{1,11},{3,9}... | collective-permute-start | bytes 589832 | tf_op jit(solution)/shard_map/ppermute | solution.py:212
  135.0 15.0 %collective-permute-start.24 = (bf16[6,128,128]{2,1,0:T(8,128)(2,1)S(1)}, bf16[6,128,128]{2,1,0:T(8,128)(2,1)S(1)}, u32[]{:S(2)}, u32[]{:S(2)}) collective-permute-start(bf16[6,128,128]{2,1,0:T(8,128)(2,1)S(1)} %get-tuple-element.84), channel_id=1, source_target_pairs={{0,2},{2,0},{4,6},{6,4},{8,10},{10,8},{12,14},{14,12},{1,3},{3,1},... | collective-permute-start | bytes 589832 | tf_op jit(solution)/shard_map/ppermute | solution.py:212
  136.1 24.1 %collective-permute-start.22 = (bf16[6,128,256]{2,1,0:T(8,128)(2,1)S(1)}, bf16[6,128,256]{2,1,0:T(8,128)(2,1)S(1)}, u32[]{:S(2)}, u32[]{:S(2)}) collective-permute-start(bf16[6,128,256]{2,1,0:T(8,128)(2,1)S(1)} %get-tuple-element.81), channel_id=1, source_target_pairs={{0,6},{2,4},{4,2},{6,0},{8,14},{10,12},{12,10},{14,8},{1,7},{3,5},... | collective-permute-start | bytes 1179656 | tf_op jit(solution)/shard_map/ppermute | solution.py:212
  136.2 17.1 %collective-permute-start.29 = (bf16[6,128,128]{2,1,0:T(8,128)(2,1)S(1)}, bf16[6,128,128]{2,1,0:T(8,128)(2,1)S(1)}, u32[]{:S(2)}, u32[]{:S(2)}) collective-permute-start(bf16[6,128,128]{2,1,0:T(8,128)(2,1)S(1)} %get-tuple-element.93), channel_id=1, source_target_pairs={{0,12},{2,14},{4,8},{6,10},{8,4},{10,6},{12,0},{14,2},{1,13},{3,15... | collective-permute-start | bytes 589832 | tf_op jit(solution)/shard_map/ppermute | solution.py:212
  138.6 21.6 %collective-permute-start.26 = (bf16[6,128,128]{2,1,0:T(8,128)(2,1)S(1)}, bf16[6,128,128]{2,1,0:T(8,128)(2,1)S(1)}, u32[]{:S(2)}, u32[]{:S(2)}) collective-permute-start(bf16[6,128,128]{2,1,0:T(8,128)(2,1)S(1)} %get-tuple-element.87), channel_id=1, source_target_pairs={{0,4},{2,6},{4,0},{6,2},{8,12},{10,14},{12,8},{14,10},{1,5},{3,7},... | collective-permute-start | bytes 589832 | tf_op jit(solution)/shard_map/ppermute | solution.py:212
  143.5 25.1 %collective-permute-start.28 = (bf16[6,128,128]{2,1,0:T(8,128)(2,1)S(1)}, bf16[6,128,128]{2,1,0:T(8,128)(2,1)S(1)}, u32[]{:S(2)}, u32[]{:S(2)}) collective-permute-start(bf16[6,128,128]{2,1,0:T(8,128)(2,1)S(1)} %get-tuple-element.91), channel_id=1, source_target_pairs={{0,6},{2,4},{4,2},{6,0},{8,14},{10,12},{12,10},{14,8},{1,7},{3,5},... | collective-permute-start | bytes 589832 | tf_op jit(solution)/shard_map/ppermute | solution.py:212
  150.0 18.5 %collective-permute-start.30 = (bf16[6,128,128]{2,1,0:T(8,128)(2,1)S(1)}, bf16[6,128,128]{2,1,0:T(8,128)(2,1)S(1)}, u32[]{:S(2)}, u32[]{:S(2)}) collective-permute-start(bf16[6,128,128]{2,1,0:T(8,128)(2,1)S(1)} %get-tuple-element.95), channel_id=1, source_target_pairs={{0,14},{2,12},{4,10},{6,8},{8,6},{10,4},{12,2},{14,0},{1,15},{3,13... | collective-permute-start | bytes 589832 | tf_op jit(solution)/shard_map/ppermute | solution.py:212
  (12 other events, 106.0 us)

commit v20 on v18

--- a/solution.py
+++ b/solution.py
@@ -351,7 +351,7 @@
     near = [sends[0], flip(sends[1], 1), flip(sends[2], 2)]
     for d in range(3, n // 2):
         near.append(flip(after(sends[d], near[d - 1]), d))
-    far = [direct(0), direct(1, near[1]), direct(2, near[2])]
+    far = [direct(0), direct(1, near[2]), direct(2, near[2])]
     passed = call(
         functools.partial(pass_on_kernel, n, cap),
         "pass_on",

time: 163 us -> 165 us (1.012)
  waiting for transfers between devices: 84.8 us -> 89 us
  starting transfers between devices: 48.2 us -> 46.5 us
    ppermute x21, waiting for transfers between devices: 72.3 us -> 76.5 us  [flip(): return lax.ppermute(x, 'pair', [(s, s ^ bit) for s in range(n)])]
    ppermute x21, starting transfers between devices: 32.1 us -> 30.4 us  [flip(): return lax.ppermute(x, 'pair', [(s, s ^ bit) for s in range(n)])]
  transfers between devices with their start and end apart: 30 -> 30, of which waited for: 20 -> 19; matrix products, arithmetic and copies ran while one was open for 1% -> 1% of each run, Pallas kernels for 4% -> 4%
where the time goes in v20:
time: 165 us
  waiting for transfers between devices  89 us (54%)
  starting transfers between devices  46.5 us (28%)
  Pallas kernels  17.9 us (11%)
  local copies, waits for them, and re-layouts  6.78 us (4%)
  other arithmetic  3.73 us (2%)
    ppermute x21, waiting for transfers between devices, flip(): return lax.ppermute(x, 'pair', [(s, s ^ bit) for s in range(n)])  76.5 us
    ppermute x21, starting transfers between devices, flip(): return lax.ppermute(x, 'pair', [(s, s ^ bit) for s in range(n)])  30.4 us
    pallas_call x7, Pallas kernels, call(): pl.pallas_call(kernel, out_shape=out_shape, grid_spec=pltpu.PrefetchScala...  16 us
    ppermute x7, starting transfers between devices, shift(): return lax.ppermute(x, 'pair', [(s, (s + d) % n) for s in range(n)])  15.9 us
    ppermute x7, waiting for transfers between devices, shift(): return lax.ppermute(x, 'pair', [(s, (s + d) % n) for s in range(n)])  10.6 us
    unnamed x11, local copies, waits for them, and re-layouts  6.7 us
  transfers between devices with their start and end apart: 30, of which 19 were waited for; matrix products, arithmetic and copies ran while one was open for 1% of the time, Pallas kernels for 4%

profile of v20, /device:TPU:0, one launch (start us, length us, event | category | flops | bytes accessed | tf_op | source)
XLA Modules:
  0.0 164.9 jit_solution(15412026802015209780)
XLA Ops:
  5.1 6.1 %collective-permute-start.1 = (bf16[3,128,256]{2,1,0:T(8,128)(2,1)S(1)}, bf16[3,128,256]{2,1,0:T(8,128)(2,1)S(1)}, u32[]{:S(2)}, u32[]{:S(2)}) collective-permute-start(bf16[3,128,256]{2,1,0:T(8,128)(2,1)S(1)} %get-tuple-element.47), channel_id=1, source_target_pairs={{0,14},{2,0},{4,2},{6,4},{8,6},{10,8},{12,10},{14,12},{1,15},{3,1}... | collective-permute-start | bytes 589832 | tf_op jit(solution)/shard_map/ppermute | solution.py:206
  11.2 5.2 %collective-permute-start.3 = (bf16[3,128,256]{2,1,0:T(8,128)(2,1)S(1)}, bf16[3,128,256]{2,1,0:T(8,128)(2,1)S(1)}, u32[]{:S(2)}, u32[]{:S(2)}) collective-permute-start(bf16[3,128,256]{2,1,0:T(8,128)(2,1)S(1)} %get-tuple-element.49), channel_id=1, source_target_pairs={{0,6},{2,8},{4,10},{6,12},{8,14},{10,0},{12,2},{14,4},{1,7},{3,9},... | collective-permute-start | bytes 589832 | tf_op jit(solution)/shard_map/ppermute | solution.py:206
  16.5 4.6 %collective-permute-start.6 = (bf16[3,128,256]{2,1,0:T(8,128)(2,1)S(1)}, bf16[3,128,256]{2,1,0:T(8,128)(2,1)S(1)}, u32[]{:S(2)}, u32[]{:S(2)}) collective-permute-start(bf16[3,128,256]{2,1,0:T(8,128)(2,1)S(1)} %get-tuple-element.54), channel_id=1, source_target_pairs={{0,12},{2,14},{4,0},{6,2},{8,4},{10,6},{12,8},{14,10},{1,13},{3,15... | collective-permute-start | bytes 589832 | tf_op jit(solution)/shard_map/ppermute | solution.py:206
  21.8 5.2 %copy-done = bf16[14,256,2048]{2,1,0:T(8,128)(2,1)S(1)} copy-done((bf16[14,256,2048]{2,1,0:T(8,128)(2,1)S(1)}, bf16[14,256,2048]{2,1,0:T(8,128)(2,1)}, u32[]{:S(2)}) %copy-start) | copy-done | bytes 14680088
  28.0 5.7 %collective-permute-done.2.rest_2_ = bf16[3,128,256]{2,1,0:T(8,128)(2,1)S(1)} collective-permute-done((bf16[3,128,256]{2,1,0:T(8,128)(2,1)S(1)}, bf16[3,128,256]{2,1,0:T(8,128)(2,1)S(1)}, u32[]{:S(2)}, u32[]{:S(2)}) %collective-permute-start.2) | collective-permute-done | bytes 196640 | tf_op jit(solution)/shard_map/ppermute | solution.py:206
  33.7 2.7 %collective-permute-done.3.rest_3_ = bf16[3,128,256]{2,1,0:T(8,128)(2,1)S(1)} collective-permute-done((bf16[3,128,256]{2,1,0:T(8,128)(2,1)S(1)}, bf16[3,128,256]{2,1,0:T(8,128)(2,1)S(1)}, u32[]{:S(2)}, u32[]{:S(2)}) %collective-permute-start.3) | collective-permute-done | bytes 196640 | tf_op jit(solution)/shard_map/ppermute | solution.py:206
  38.9 2.8 %fit.2 = (f32[4,128,256]{2,1,0:T(8,128)S(1)}, bf16[4,128,256]{2,1,0:T(8,128)(2,1)S(1)}) custom-call(s32[8]{0:T(128)S(1)} %iota_xor_fusion.table, bf16[14,1,256]{2,1,0:T(2,128)(2,1)S(1)} %copy.10.factor, bf16[14,128,256]{2,1,0:T(8,128)(2,1)S(1)} %gather_density.1.density, bf16[14,256,2048]{2,1,0:T(8,128)(2,1)S(1)} %load_integrals.1.rest_8_.integrals), custom_call_target="tpu_custom_call" | custom-call | tf_op jit(solution)/shard_map/fit/pallas_call | solution.py:191
  41.7 5.2 %collective-permute-start.7 = (bf16[4,128,256]{2,1,0:T(8,128)(2,1)S(1)}, bf16[4,128,256]{2,1,0:T(8,128)(2,1)S(1)}, u32[]{:S(2)}, u32[]{:S(2)}) collective-permute-start(bf16[4,128,256]{2,1,0:T(8,128)(2,1)S(1)} %get-tuple-element.58), channel_id=1, source_target_pairs={{0,2},{2,0},{4,6},{6,4},{8,10},{10,8},{12,14},{14,12},{1,3},{3,1},... | collective-permute-start | bytes 786440 | tf_op jit(solution)/shard_map/ppermute | solution.py:209
  46.9 2.7 %fit.3 = (f32[4,128,256]{2,1,0:T(8,128)S(1)}, bf16[4,128,256]{2,1,0:T(8,128)(2,1)S(1)}) custom-call(s32[8]{0:T(128)S(1)} %iota_xor_fusion.table, bf16[14,1,256]{2,1,0:T(2,128)(2,1)S(1)} %copy.10.factor, bf16[14,128,256]{2,1,0:T(8,128)(2,1)S(1)} %collective-permute-done.8.density, bf16[14,256,2048]{2,1,0:T(8,128)(2,1)S(1)} %load_integrals.1.rest_8_.integrals, ...), custom_call_target="tpu_custom_call" | custom-call | tf_op jit(solution)/shard_map/fit/pallas_call | solution.py:191
  49.6 5.2 %collective-permute-start.9 = (bf16[4,128,256]{2,1,0:T(8,128)(2,1)S(1)}, bf16[4,128,256]{2,1,0:T(8,128)(2,1)S(1)}, u32[]{:S(2)}, u32[]{:S(2)}) collective-permute-start(bf16[4,128,256]{2,1,0:T(8,128)(2,1)S(1)} %get-tuple-element.60), channel_id=1, source_target_pairs={{0,4},{2,6},{4,0},{6,2},{8,12},{10,14},{12,8},{14,10},{1,5},{3,7},... | collective-permute-start | bytes 786440 | tf_op jit(solution)/shard_map/ppermute | solution.py:209
  54.9 6.6 %collective-permute-done.9 = bf16[4,128,256]{2,1,0:T(8,128)(2,1)S(1)} collective-permute-done((bf16[4,128,256]{2,1,0:T(8,128)(2,1)S(1)}, bf16[4,128,256]{2,1,0:T(8,128)(2,1)S(1)}, u32[]{:S(2)}, u32[]{:S(2)}) %collective-permute-start.9) | collective-permute-done | bytes 262176 | tf_op jit(solution)/shard_map/ppermute | solution.py:209
  63.7 3.0 %collective-permute-done.10 = bf16[2,128,256]{2,1,0:T(8,128)(2,1)S(1)} collective-permute-done((bf16[2,128,256]{2,1,0:T(8,128)(2,1)S(1)}, bf16[2,128,256]{2,1,0:T(8,128)(2,1)S(1)}, u32[]{:S(2)}, u32[]{:S(2)}) %collective-permute-start.10) | collective-permute-done | bytes 131104 | tf_op jit(solution)/shard_map/ppermute | solution.py:209
  70.0 8.3 %collective-permute-done.11 = bf16[2,128,256]{2,1,0:T(8,128)(2,1)S(1)} collective-permute-done((bf16[2,128,256]{2,1,0:T(8,128)(2,1)S(1)}, bf16[2,128,256]{2,1,0:T(8,128)(2,1)S(1)}, u32[]{:S(2)}, u32[]{:S(2)}) %collective-permute-start.11) | collective-permute-done | bytes 131104 | tf_op jit(solution)/shard_map/ppermute | solution.py:209
  83.3 2.2 %collective-permute-done.16 = bf16[2,128,256]{2,1,0:T(8,128)(2,1)S(1)} collective-permute-done((bf16[2,128,256]{2,1,0:T(8,128)(2,1)S(1)}, bf16[2,128,256]{2,1,0:T(8,128)(2,1)S(1)}, u32[]{:S(2)}, u32[]{:S(2)}) %collective-permute-start.16) | collective-permute-done | bytes 131104 | tf_op jit(solution)/shard_map/ppermute | solution.py:209
  86.6 5.5 %collective-permute-done.15.far = bf16[4,128,256]{2,1,0:T(8,128)(2,1)S(1)} collective-permute-done((bf16[4,128,256]{2,1,0:T(8,128)(2,1)S(1)}, bf16[4,128,256]{2,1,0:T(8,128)(2,1)S(1)}, u32[]{:S(2)}, u32[]{:S(2)}) %collective-permute-start.15) | collective-permute-done | bytes 262176 | tf_op jit(solution)/shard_map/ppermute | solution.py:209
  92.8 5.0 %apply.1 = (f32[14,128,256]{2,1,0:T(8,128)S(1)}, bf16[14,128,256]{2,1,0:T(8,128)(2,1)S(1)}) custom-call(s32[8]{0:T(128)S(1)} %iota_xor_fusion.table, bf16[14,256,2048]{2,1,0:T(8,128)(2,1)S(1)} %load_integrals.1.rest_8_.integrals, bf16[4,128,256]{2,1,0:T(8,128)(2,1)S(1)} %constant_dynamic-update-slice_fusion.near, ...), custom_call_target="tpu_custom_call" | custom-call | tf_op jit(solution)/shard_map/apply/pallas_call | solution.py:191
  106.5 15.4 %collective-permute-done.20.rest_1_.rest_2_ = bf16[6,128,256]{2,1,0:T(8,128)(2,1)S(1)} collective-permute-done((bf16[6,128,256]{2,1,0:T(8,128)(2,1)S(1)}, bf16[6,128,256]{2,1,0:T(8,128)(2,1)S(1)}, u32[]{:S(2)}, u32[]{:S(2)}) %collective-permute-start.20) | collective-permute-done | bytes 393248 | tf_op jit(solution)/shard_map/ppermute | solution.py:209
  121.9 3.2 %collective-permute-start.26 = (bf16[6,128,128]{2,1,0:T(8,128)(2,1)S(1)}, bf16[6,128,128]{2,1,0:T(8,128)(2,1)S(1)}, u32[]{:S(2)}, u32[]{:S(2)}) collective-permute-start(bf16[6,128,128]{2,1,0:T(8,128)(2,1)S(1)} %get-tuple-element.84), channel_id=1, source_target_pairs={{0,10},{2,8},{4,14},{6,12},{8,2},{10,0},{12,6},{14,4},{1,11},{3,9}... | collective-permute-start | bytes 589832 | tf_op jit(solution)/shard_map/ppermute | solution.py:209
  125.1 8.1 %collective-permute-done.22.whole = bf16[14,128,128]{2,1,0:T(8,128)(2,1)S(1)} collective-permute-done((bf16[14,128,128]{2,1,0:T(8,128)(2,1)S(1)}, bf16[14,128,128]{2,1,0:T(8,128)(2,1)S(1)}, u32[]{:S(2)}, u32[]{:S(2)}) %collective-permute-start.22) | collective-permute-done | bytes 458784 | tf_op jit(solution)/shard_map/ppermute | solution.py:209
  137.4 8.8 %collective-permute-done.26.rest_9_ = bf16[6,128,128]{2,1,0:T(8,128)(2,1)S(1)} collective-permute-done((bf16[6,128,128]{2,1,0:T(8,128)(2,1)S(1)}, bf16[6,128,128]{2,1,0:T(8,128)(2,1)S(1)}, u32[]{:S(2)}, u32[]{:S(2)}) %collective-permute-start.26) | collective-permute-done | bytes 196640 | tf_op jit(solution)/shard_map/ppermute | solution.py:209
  146.3 2.6 %collective-permute-start.29 = (bf16[6,128,128]{2,1,0:T(8,128)(2,1)S(1)}, bf16[6,128,128]{2,1,0:T(8,128)(2,1)S(1)}, u32[]{:S(2)}, u32[]{:S(2)}) collective-permute-start(bf16[6,128,128]{2,1,0:T(8,128)(2,1)S(1)} %get-tuple-element.89), channel_id=1, source_target_pairs={{0,14},{2,12},{4,10},{6,8},{8,6},{10,4},{12,2},{14,0},{1,15},{3,13... | collective-permute-start | bytes 589832 | tf_op jit(solution)/shard_map/ppermute | solution.py:209
  149.0 10.4 %collective-permute-done.25.rest_6_ = bf16[6,128,128]{2,1,0:T(8,128)(2,1)S(1)} collective-permute-done((bf16[6,128,128]{2,1,0:T(8,128)(2,1)S(1)}, bf16[6,128,128]{2,1,0:T(8,128)(2,1)S(1)}, u32[]{:S(2)}, u32[]{:S(2)}) %collective-permute-start.25) | collective-permute-done | bytes 196640 | tf_op jit(solution)/shard_map/ppermute | solution.py:209
  159.4 2.4 %collective-permute-done.27.rest_7_ = bf16[6,128,128]{2,1,0:T(8,128)(2,1)S(1)} collective-permute-done((bf16[6,128,128]{2,1,0:T(8,128)(2,1)S(1)}, bf16[6,128,128]{2,1,0:T(8,128)(2,1)S(1)}, u32[]{:S(2)}, u32[]{:S(2)}) %collective-permute-start.27) | collective-permute-done | bytes 196640 | tf_op jit(solution)/shard_map/ppermute | solution.py:209
  161.8 3.1 %gather_coulomb.1 = (bf16[14,256,128]{2,1,0:T(8,128)(2,1)}, bf16[14,256,128]{2,1,0:T(8,128)(2,1)}) custom-call(s32[48]{0:T(128)S(1)} %pad_add_fusion.1.table, bf16[6,128,256]{2,1,0:T(8,128)(2,1)S(1)} %get-tuple-element.71.rest_0_, bf16[6,128,256]{2,1,0:T(8,128)(2,1)S(1)} %collective-permute-done.19.rest_0_.rest_1_, ...), custom_call_target="tpu_custom_call" | custom-call | tf_op jit(solution)/shard_map/gather_coulomb/pallas_call | solution.py:191
  (99 shorter events, 33.9 us)
Async XLA Ops:
  5.1 11.4 %collective-permute-start.1 = (bf16[3,128,256]{2,1,0:T(8,128)(2,1)S(1)}, bf16[3,128,256]{2,1,0:T(8,128)(2,1)S(1)}, u32[]{:S(2)}, u32[]{:S(2)}) collective-permute-start(bf16[3,128,256]{2,1,0:T(8,128)(2,1)S(1)} %get-tuple-element.47), channel_id=1, source_target_pairs={{0,14},{2,0},{4,2},{6,4},{8,6},{10,8},{12,10},{14,12},{1,15},{3,1}... | collective-permute-start | bytes 589832 | tf_op jit(solution)/shard_map/ppermute | solution.py:206
  11.1 10.6 %collective-permute-start = (bf16[3,128,256]{2,1,0:T(8,128)(2,1)S(1)}, bf16[3,128,256]{2,1,0:T(8,128)(2,1)S(1)}, u32[]{:S(2)}, u32[]{:S(2)}) collective-permute-start(bf16[3,128,256]{2,1,0:T(8,128)(2,1)S(1)} %get-tuple-element.46), channel_id=1, source_target_pairs={{0,2},{2,4},{4,6},{6,8},{8,10},{10,12},{12,14},{14,0},{1,3},{3,5},... | collective-permute-start | bytes 589832 | tf_op jit(solution)/shard_map/ppermute | solution.py:206
  11.2 22.6 %collective-permute-start.2 = (bf16[3,128,256]{2,1,0:T(8,128)(2,1)S(1)}, bf16[3,128,256]{2,1,0:T(8,128)(2,1)S(1)}, u32[]{:S(2)}, u32[]{:S(2)}) collective-permute-start(bf16[3,128,256]{2,1,0:T(8,128)(2,1)S(1)} %get-tuple-element.48), channel_id=1, source_target_pairs={{0,8},{2,10},{4,12},{6,14},{8,0},{10,2},{12,4},{14,6},{1,9},{3,11}... | collective-permute-start | bytes 589832 | tf_op jit(solution)/shard_map/ppermute | solution.py:206
  11.2 25.2 %collective-permute-start.3 = (bf16[3,128,256]{2,1,0:T(8,128)(2,1)S(1)}, bf16[3,128,256]{2,1,0:T(8,128)(2,1)S(1)}, u32[]{:S(2)}, u32[]{:S(2)}) collective-permute-start(bf16[3,128,256]{2,1,0:T(8,128)(2,1)S(1)} %get-tuple-element.49), channel_id=1, source_target_pairs={{0,6},{2,8},{4,10},{6,12},{8,14},{10,0},{12,2},{14,4},{1,7},{3,9},... | collective-permute-start | bytes 589832 | tf_op jit(solution)/shard_map/ppermute | solution.py:206
  16.4 20.0 %collective-permute-start.4 = (bf16[3,128,256]{2,1,0:T(8,128)(2,1)S(1)}, bf16[3,128,256]{2,1,0:T(8,128)(2,1)S(1)}, u32[]{:S(2)}, u32[]{:S(2)}) collective-permute-start(bf16[3,128,256]{2,1,0:T(8,128)(2,1)S(1)} %get-tuple-element.50), channel_id=1, source_target_pairs={{0,10},{2,12},{4,14},{6,0},{8,2},{10,4},{12,6},{14,8},{1,11},{3,13... | collective-permute-start | bytes 589832 | tf_op jit(solution)/shard_map/ppermute | solution.py:206
  16.5 20.0 %collective-permute-start.6 = (bf16[3,128,256]{2,1,0:T(8,128)(2,1)S(1)}, bf16[3,128,256]{2,1,0:T(8,128)(2,1)S(1)}, u32[]{:S(2)}, u32[]{:S(2)}) collective-permute-start(bf16[3,128,256]{2,1,0:T(8,128)(2,1)S(1)} %get-tuple-element.54), channel_id=1, source_target_pairs={{0,12},{2,14},{4,0},{6,2},{8,4},{10,6},{12,8},{14,10},{1,13},{3,15... | collective-permute-start | bytes 589832 | tf_op jit(solution)/shard_map/ppermute | solution.py:206
  21.7 16.2 %collective-permute-start.5 = (bf16[3,128,256]{2,1,0:T(8,128)(2,1)S(1)}, bf16[3,128,256]{2,1,0:T(8,128)(2,1)S(1)}, u32[]{:S(2)}, u32[]{:S(2)}) collective-permute-start(bf16[3,128,256]{2,1,0:T(8,128)(2,1)S(1)} %get-tuple-element.52), channel_id=1, source_target_pairs={{0,4},{2,6},{4,8},{6,10},{8,12},{10,14},{12,0},{14,2},{1,5},{3,7},... | collective-permute-start | bytes 589832 | tf_op jit(solution)/shard_map/ppermute | solution.py:206
  38.7 8.2 %collective-permute-start.8 = (bf16[14,128,256]{2,1,0:T(8,128)(2,1)S(1)}, bf16[14,128,256]{2,1,0:T(8,128)(2,1)S(1)}, u32[]{:S(2)}, u32[]{:S(2)}) collective-permute-start(bf16[14,128,256]{2,1,0:T(8,128)(2,1)S(1)} %gather_density.1.density), channel_id=1, source_target_pairs={{0,1},{1,0},{2,3},{3,2},{4,5},{5,4},{6,7},{7,6},{8,9},{9,8},{10,11... | collective-permute-start | bytes 2752520 | tf_op jit(solution)/shard_map/ppermute | solution.py:212
  41.7 13.1 %collective-permute-start.7 = (bf16[4,128,256]{2,1,0:T(8,128)(2,1)S(1)}, bf16[4,128,256]{2,1,0:T(8,128)(2,1)S(1)}, u32[]{:S(2)}, u32[]{:S(2)}) collective-permute-start(bf16[4,128,256]{2,1,0:T(8,128)(2,1)S(1)} %get-tuple-element.58), channel_id=1, source_target_pairs={{0,2},{2,0},{4,6},{6,4},{8,10},{10,8},{12,14},{14,12},{1,3},{3,1},... | collective-permute-start | bytes 786440 | tf_op jit(solution)/shard_map/ppermute | solution.py:209
  49.6 11.9 %collective-permute-start.9 = (bf16[4,128,256]{2,1,0:T(8,128)(2,1)S(1)}, bf16[4,128,256]{2,1,0:T(8,128)(2,1)S(1)}, u32[]{:S(2)}, u32[]{:S(2)}) collective-permute-start(bf16[4,128,256]{2,1,0:T(8,128)(2,1)S(1)} %get-tuple-element.60), channel_id=1, source_target_pairs={{0,4},{2,6},{4,0},{6,2},{8,12},{10,14},{12,8},{14,10},{1,5},{3,7},... | collective-permute-start | bytes 786440 | tf_op jit(solution)/shard_map/ppermute | solution.py:209
  66.8 11.4 %collective-permute-start.11 = (bf16[2,128,256]{2,1,0:T(8,128)(2,1)S(1)}, bf16[2,128,256]{2,1,0:T(8,128)(2,1)S(1)}, u32[]{:S(2)}, u32[]{:S(2)}) collective-permute-start(bf16[2,128,256]{2,1,0:T(8,128)(2,1)S(1)} %pad_maximum_fusion.1), channel_id=1, source_target_pairs={{0,8},{2,10},{4,12},{6,14},{8,0},{10,2},{12,4},{14,6},{1,9},{3,11}... | collective-permute-start | bytes 393224 | tf_op jit(solution)/shard_map/ppermute | solution.py:209
  68.5 11.9 %collective-permute-start.14 = (bf16[2,128,256]{2,1,0:T(8,128)(2,1)S(1)}, bf16[2,128,256]{2,1,0:T(8,128)(2,1)S(1)}, u32[]{:S(2)}, u32[]{:S(2)}) collective-permute-start(bf16[2,128,256]{2,1,0:T(8,128)(2,1)S(1)} %pad_maximum_fusion.2), channel_id=1, source_target_pairs={{0,8},{2,10},{4,12},{6,14},{8,0},{10,2},{12,4},{14,6},{1,9},{3,11}... | collective-permute-start | bytes 393224 | tf_op jit(solution)/shard_map/ppermute | solution.py:209
  85.6 6.5 %collective-permute-start.15 = (bf16[4,128,256]{2,1,0:T(8,128)(2,1)S(1)}, bf16[4,128,256]{2,1,0:T(8,128)(2,1)S(1)}, u32[]{:S(2)}, u32[]{:S(2)}) collective-permute-start(bf16[4,128,256]{2,1,0:T(8,128)(2,1)S(1)} %constant_dynamic-update-slice_fusion.near), channel_id=1, source_target_pairs={{0,2},{2,0},{4,6},{6,4},{8,10},{10,8},{12,14},{14,12},{1,3},{3,1},... | collective-permute-start | bytes 786440 | tf_op jit(solution)/shard_map/ppermute | solution.py:209
  101.4 31.8 %collective-permute-start.22 = (bf16[14,128,128]{2,1,0:T(8,128)(2,1)S(1)}, bf16[14,128,128]{2,1,0:T(8,128)(2,1)S(1)}, u32[]{:S(2)}, u32[]{:S(2)}) collective-permute-start(bf16[14,128,128]{2,1,0:T(8,128)(2,1)S(1)} %get-tuple-element.76), channel_id=1, source_target_pairs={{0,8},{2,10},{4,12},{6,14},{8,0},{10,2},{12,4},{14,6},{1,9},{3,11}... | collective-permute-start | bytes 1376264 | tf_op jit(solution)/shard_map/ppermute | solution.py:209
  102.6 22.5 %collective-permute-start.19 = (bf16[6,128,256]{2,1,0:T(8,128)(2,1)S(1)}, bf16[6,128,256]{2,1,0:T(8,128)(2,1)S(1)}, u32[]{:S(2)}, u32[]{:S(2)}) collective-permute-start(bf16[6,128,256]{2,1,0:T(8,128)(2,1)S(1)} %get-tuple-element.72), channel_id=1, source_target_pairs={{0,2},{2,0},{4,6},{6,4},{8,10},{10,8},{12,14},{14,12},{1,3},{3,1},... | collective-permute-start | bytes 1179656 | tf_op jit(solution)/shard_map/ppermute | solution.py:209
  103.1 18.8 %collective-permute-start.20 = (bf16[6,128,256]{2,1,0:T(8,128)(2,1)S(1)}, bf16[6,128,256]{2,1,0:T(8,128)(2,1)S(1)}, u32[]{:S(2)}, u32[]{:S(2)}) collective-permute-start(bf16[6,128,256]{2,1,0:T(8,128)(2,1)S(1)} %get-tuple-element.73), channel_id=1, source_target_pairs={{0,4},{2,6},{4,0},{6,2},{8,12},{10,14},{12,8},{14,10},{1,5},{3,7},... | collective-permute-start | bytes 1179656 | tf_op jit(solution)/shard_map/ppermute | solution.py:209
  105.3 32.2 %collective-permute-start.24 = (bf16[6,128,128]{2,1,0:T(8,128)(2,1)S(1)}, bf16[6,128,128]{2,1,0:T(8,128)(2,1)S(1)}, u32[]{:S(2)}, u32[]{:S(2)}) collective-permute-start(bf16[6,128,128]{2,1,0:T(8,128)(2,1)S(1)} %get-tuple-element.80), channel_id=1, source_target_pairs={{0,8},{2,10},{4,12},{6,14},{8,0},{10,2},{12,4},{14,6},{1,9},{3,11}... | collective-permute-start | bytes 589832 | tf_op jit(solution)/shard_map/ppermute | solution.py:209
  121.9 24.4 %collective-permute-start.26 = (bf16[6,128,128]{2,1,0:T(8,128)(2,1)S(1)}, bf16[6,128,128]{2,1,0:T(8,128)(2,1)S(1)}, u32[]{:S(2)}, u32[]{:S(2)}) collective-permute-start(bf16[6,128,128]{2,1,0:T(8,128)(2,1)S(1)} %get-tuple-element.84), channel_id=1, source_target_pairs={{0,10},{2,8},{4,14},{6,12},{8,2},{10,0},{12,6},{14,4},{1,11},{3,9}... | collective-permute-start | bytes 589832 | tf_op jit(solution)/shard_map/ppermute | solution.py:209
  125.1 34.4 %collective-permute-start.21 = (bf16[6,128,256]{2,1,0:T(8,128)(2,1)S(1)}, bf16[6,128,256]{2,1,0:T(8,128)(2,1)S(1)}, u32[]{:S(2)}, u32[]{:S(2)}) collective-permute-start(bf16[6,128,256]{2,1,0:T(8,128)(2,1)S(1)} %get-tuple-element.75), channel_id=1, source_target_pairs={{0,6},{2,4},{4,2},{6,0},{8,14},{10,12},{12,10},{14,8},{1,7},{3,5},... | collective-permute-start | bytes 1179656 | tf_op jit(solution)/shard_map/ppermute | solution.py:209
  133.8 12.5 %collective-permute-start.23 = (bf16[6,128,128]{2,1,0:T(8,128)(2,1)S(1)}, bf16[6,128,128]{2,1,0:T(8,128)(2,1)S(1)}, u32[]{:S(2)}, u32[]{:S(2)}) collective-permute-start(bf16[6,128,128]{2,1,0:T(8,128)(2,1)S(1)} %get-tuple-element.78), channel_id=1, source_target_pairs={{0,2},{2,0},{4,6},{6,4},{8,10},{10,8},{12,14},{14,12},{1,3},{3,1},... | collective-permute-start | bytes 589832 | tf_op jit(solution)/shard_map/ppermute | solution.py:209
  134.9 14.1 %collective-permute-start.28 = (bf16[6,128,128]{2,1,0:T(8,128)(2,1)S(1)}, bf16[6,128,128]{2,1,0:T(8,128)(2,1)S(1)}, u32[]{:S(2)}, u32[]{:S(2)}) collective-permute-start(bf16[6,128,128]{2,1,0:T(8,128)(2,1)S(1)} %get-tuple-element.87), channel_id=1, source_target_pairs={{0,12},{2,14},{4,8},{6,10},{8,4},{10,6},{12,0},{14,2},{1,13},{3,15... | collective-permute-start | bytes 589832 | tf_op jit(solution)/shard_map/ppermute | solution.py:209
  137.4 22.0 %collective-permute-start.25 = (bf16[6,128,128]{2,1,0:T(8,128)(2,1)S(1)}, bf16[6,128,128]{2,1,0:T(8,128)(2,1)S(1)}, u32[]{:S(2)}, u32[]{:S(2)}) collective-permute-start(bf16[6,128,128]{2,1,0:T(8,128)(2,1)S(1)} %get-tuple-element.81), channel_id=1, source_target_pairs={{0,4},{2,6},{4,0},{6,2},{8,12},{10,14},{12,8},{14,10},{1,5},{3,7},... | collective-permute-start | bytes 589832 | tf_op jit(solution)/shard_map/ppermute | solution.py:209
  146.3 15.5 %collective-permute-start.27 = (bf16[6,128,128]{2,1,0:T(8,128)(2,1)S(1)}, bf16[6,128,128]{2,1,0:T(8,128)(2,1)S(1)}, u32[]{:S(2)}, u32[]{:S(2)}) collective-permute-start(bf16[6,128,128]{2,1,0:T(8,128)(2,1)S(1)} %get-tuple-element.85), channel_id=1, source_target_pairs={{0,6},{2,4},{4,2},{6,0},{8,14},{10,12},{12,10},{14,8},{1,7},{3,5},... | collective-permute-start | bytes 589832 | tf_op jit(solution)/shard_map/ppermute | solution.py:209
  146.3 15.5 %collective-permute-start.29 = (bf16[6,128,128]{2,1,0:T(8,128)(2,1)S(1)}, bf16[6,128,128]{2,1,0:T(8,128)(2,1)S(1)}, u32[]{:S(2)}, u32[]{:S(2)}) collective-permute-start(bf16[6,128,128]{2,1,0:T(8,128)(2,1)S(1)} %get-tuple-element.89), channel_id=1, source_target_pairs={{0,14},{2,12},{4,10},{6,8},{8,6},{10,4},{12,2},{14,0},{1,15},{3,13... | collective-permute-start | bytes 589832 | tf_op jit(solution)/shard_map/ppermute | solution.py:209
  (11 other events, 105.9 us)
